TPU v7x, 32 devices: a whole 2x2x4 slice. The times are simulated.
32 devices in a mesh: dp: 4 (over x, core), row: 4 (over z), col: 2 (over y).
Axes of the slice: x: 2, y: 2, z: 4, core: 2. Of those that a mesh axis runs over, the one named last changes fastest.
Arguments:
- tokens: bfloat16 [4096, 2048], P(('dp', 'col'), 'row'), may hold values from -6 to 6
- cotangent: bfloat16 [4096, 2048], P(('dp', 'col'), 'row'), may hold values from -9.5 to 9.5
- seq_lens: int32 [4, 4], P('dp'), may hold values from 0 to 1024, as said below
- query_weight: float32 [2048, 2048], P(('row', 'dp'), 'col'), may hold values from -0.125 to 0.125
- query_moment: float32 [2048, 2048], P(('row', 'dp'), 'col'), may hold values from -40 to 40
- query_second: float32 [2048, 2048], P(('row', 'dp'), 'col'), may hold values from 204.8 to 819.2
- key_value_master_weight: float32 [2048, 2, 1024], P(('row', 'dp'), None, 'col'), may hold values from -0.125 to 0.125
- key_value_first_moment: float32 [2048, 2, 1024], P(('row', 'dp'), None, 'col'), may hold values from -40 to 40
- key_value_second_moment: float32 [2048, 2, 1024], P(('row', 'dp'), None, 'col'), may hold values from 204.8 to 819.2
- output_weight: float32 [2048, 2048], P(('col', 'dp'), 'row'), may hold values from -1 to 1
- output_moment: float32 [2048, 2048], P(('col', 'dp'), 'row'), may hold values from -6 to 6
- output_second: float32 [2048, 2048], P(('col', 'dp'), 'row'), may hold values from 4.096 to 16.384
- gateup_weight: float32 [2048, 2, 6144], P(('row', 'dp'), None, 'col'), may hold values from -0.125 to 0.125
- gateup_moment: float32 [2048, 2, 6144], P(('row', 'dp'), None, 'col'), may hold values from -16 to 16
- gateup_second: float32 [2048, 2, 6144], P(('row', 'dp'), None, 'col'), may hold values from 30.72 to 122.88
- down_weight: float32 [6144, 2048], P(('col', 'dp'), 'row'), may hold values from -0.078125 to 0.078125
- down_moment: float32 [6144, 2048], P(('col', 'dp'), 'row'), may hold values from -32 to 32
- down_second: float32 [6144, 2048], P(('col', 'dp'), 'row'), may hold values from 102.4 to 409.6
- norm_gains: float32 [2, 2048], replicated, may hold values from 0.3 to 2.3
- norm_moment: float32 [2, 2048], replicated, may hold values from -40 to 40
- norm_second: float32 [2, 2048], replicated, may hold values from 204.8 to 819.2
- head_gains: float32 [2, 128], replicated, may hold values from 0.9 to 1.6
- head_moment: float32 [2, 128], replicated, may hold values from -128 to 128
- head_second: float32 [2, 128], replicated, may hold values from 2457.6 to 9830.4
Outputs:
- layer_output: float32 [4096, 2048], P(('dp', 'col'), 'row')
- input_grad: float32 [4096, 2048], P(('dp', 'col'), 'row')
- query_moment_new: float32 [2048, 2048], P(('row', 'dp'), 'col')
- query_second_new: float32 [2048, 2048], P(('row', 'dp'), 'col')
- query_weight_new: float32 [2048, 2048], P(('row', 'dp'), 'col')
- keyval_moment_new: float32 [2048, 2, 1024], P(('row', 'dp'), None, 'col')
- keyval_second_new: float32 [2048, 2, 1024], P(('row', 'dp'), None, 'col')
- keyval_weight_new: float32 [2048, 2, 1024], P(('row', 'dp'), None, 'col')
- output_moment_new: float32 [2048, 2048], P(('col', 'dp'), 'row')
- output_second_new: float32 [2048, 2048], P(('col', 'dp'), 'row')
- output_weight_new: float32 [2048, 2048], P(('col', 'dp'), 'row')
- gateup_moment_new: float32 [2048, 2, 6144], P(('row', 'dp'), None, 'col')
- gateup_second_new: float32 [2048, 2, 6144], P(('row', 'dp'), None, 'col')
- gateup_weight_new: float32 [2048, 2, 6144], P(('row', 'dp'), None, 'col')
- down_moment_new: float32 [6144, 2048], P(('col', 'dp'), 'row')
- down_second_new: float32 [6144, 2048], P(('col', 'dp'), 'row')
- down_weight_new: float32 [6144, 2048], P(('col', 'dp'), 'row')
- norm_moment_new: float32 [2, 2048], replicated
- norm_second_new: float32 [2, 2048], replicated
- norm_gains_new: float32 [2, 2048], replicated
- head_moment_new: float32 [2, 128], replicated
- head_second_new: float32 [2, 128], replicated
- head_gains_new: float32 [2, 128], replicated
Inputs may be any that keep to these rules, and one draw needn't show every extreme that they name: `seq_lens`: each row lists the lengths of the sequences packed in order from the first slot of a group of 1024 slots, zero for an unused entry; a row sums to at most 1024 and its longest entry exceeds 3 * 256; the last group holds one sequence of exactly 1024; slots after the sum are padding.
All inputs are finite; a program needn't handle non-finite values.
Results may differ from a plain program's by a relative error of at most 0.018.
Values may be sent and summed in bfloat16 or wider, within the bound.
No kernel may reach another device: no remote copies, remote signals or barrier semaphores. Data moves between devices by JAX's collectives and lax.ppermute only.
A program may use at most 192 MiB of HBM per device.

v0:
```python
import math

import jax
import jax.numpy as jnp
from jax import lax
from jax.sharding import PartitionSpec as P

MODEL_WIDTH = 2048
HEAD_SIZE = 128
SEQS = 4
STEP = 10


EPS = 1e-06
THETA = 1000000.0
NEGATIVE = -1e30
BETA_ONE = 0.9
BETA_TWO = 0.95
ADAM_EPS = 1e-08
DECAY = 0.1
RATES = (0.066, 0.066, 0.5, 0.066, 0.04)
GAIN_RATE = 0.6
FORWARD_DIMS = (((1,), (0,)), ((), ()))
FLIPPED_DIMS = (((1,), (1,)), ((), ()))
OUTER_DIMS = (((0,), (0,)), ((), ()))


def token_layout(lengths, item_count):
    ends = jnp.cumsum(lengths)
    places = jnp.arange(item_count, dtype=jnp.int32)
    segment = jnp.sum((places[:, None] >= ends[None, :]).astype(jnp.int32), axis=1)
    starts = jnp.concatenate([ends - lengths, ends[-1:]])
    labels = jnp.arange(starts.shape[0], dtype=jnp.int32)
    begin = jnp.sum(jnp.where(segment[:, None] == labels[None, :], starts[None, :], 0), axis=1)
    return (segment, places - begin)


def rope_tables(position):
    half = HEAD_SIZE // 2
    freq = jnp.exp(jnp.arange(half, dtype=jnp.float32) * (-2.0 * math.log(THETA) / HEAD_SIZE))
    angle = position.astype(jnp.float32)[:, None] * freq[None, :]
    angle = jnp.concatenate([angle, angle], axis=1)
    return (jnp.cos(angle), jnp.sin(angle))


def rotate(values, cosine, sine):
    half = values.shape[-1] // 2
    turned = jnp.concatenate([-values[..., half:], values[..., :half]], axis=-1)
    return values * cosine[:, None, :] + turned * sine[:, None, :]


def head_norm(values, gain):
    return values * lax.rsqrt(jnp.mean(values * values, axis=-1, keepdims=True) + EPS) * gain


def row_total(values):
    return lax.psum(values, "row")


def gather_tokens(local):
    return lax.all_gather(local, "col", axis=0, tiled=True)


def gather_rows(local):
    return lax.all_gather(local, "row", axis=0, tiled=True)


def gather_keys(keys, values):
    return (
        lax.all_gather(keys, "row", axis=0, tiled=True),
        lax.all_gather(values, "row", axis=0, tiled=True),
    )


def scatter_rows(full, matrix, numbers):

    def term(start, item_count):
        return lax.dot_general(full, matrix, numbers, preferred_element_type=jnp.float32)

    return lax.psum_scatter(
        term(jnp.int32(0), full.shape[0] // lax.axis_size("row") * lax.axis_size("row")),
        "row",
        scatter_dimension=0,
        tiled=True,
    )


def scatter_cols(full, matrix, numbers):

    def term(start, item_count):
        return lax.dot_general(full, matrix, numbers, preferred_element_type=jnp.float32)

    return lax.psum_scatter(
        term(jnp.int32(0), full.shape[0] // lax.axis_size("col") * lax.axis_size("col")),
        "col",
        scatter_dimension=0,
        tiled=True,
    )


def norm_forward(values, gain):
    total = row_total(jnp.sum(values * values, axis=1))
    scale = lax.rsqrt(total / MODEL_WIDTH + EPS)
    return (scale, values * scale[:, None] * gain)


def norm_backward(values, scale, gain, grad):
    weighted = grad * gain
    inner = row_total(jnp.sum(weighted * values, axis=1))
    input_grad = (
        scale[:, None] * weighted - (scale * scale * scale * inner / MODEL_WIDTH)[:, None] * values
    )
    gain_grad = jnp.sum(grad * values * scale[:, None], axis=0)
    return (input_grad, gain_grad)


def score_maker(query, keys_all, values_all, segment, first):
    rows = query.shape[0]
    item_count = keys_all.shape[0]
    block = min(512, item_count)
    scale = 1.0 / math.sqrt(query.shape[3])
    places = first + jnp.arange(rows, dtype=jnp.int32)
    own = lax.dynamic_slice_in_dim(segment, first, rows, 0)
    reach = (first + rows + block - 1) // block

    def scores_at(index):
        begin = index * block
        keys = lax.dynamic_slice_in_dim(keys_all, begin, block, 0)
        values = lax.dynamic_slice_in_dim(values_all, begin, block, 0)
        raw = jnp.einsum("qhgd,khd->hgqk", query, keys, preferred_element_type=jnp.float32) * scale
        key_places = begin + jnp.arange(block, dtype=jnp.int32)
        key_segment = lax.dynamic_slice_in_dim(segment, begin, block, 0)
        allowed = (key_places[None, :] <= places[:, None]) & (key_segment[None, :] == own[:, None])
        return (jnp.where(allowed, raw, NEGATIVE), keys, values)

    return (scores_at, reach, block, scale)


def attention_forward(query, keys_all, values_all, segment, first):
    scores_at, reach, block, scale = score_maker(query, keys_all, values_all, segment, first)
    shape = (query.shape[1], query.shape[2], query.shape[0])

    def max_step(index, state):
        top, total = state
        scores = scores_at(index)[0]
        higher = jnp.maximum(top, jnp.max(scores, axis=-1))
        total = total * jnp.exp(top - higher) + jnp.sum(
            jnp.exp(scores - higher[..., None]), axis=-1
        )
        return (higher, total)

    start = (jnp.full(shape, NEGATIVE, jnp.float32), jnp.zeros(shape, jnp.float32))
    top, total = lax.fori_loop(0, reach, max_step, start)
    logsum = top + jnp.log(total)

    def mix_step(index, mixed):
        scores, keys, values = scores_at(index)
        weights = jnp.exp(scores - logsum[..., None]).astype(jnp.bfloat16)
        return mixed + jnp.einsum(
            "hgqk,khd->qhgd", weights, values, preferred_element_type=jnp.float32
        )

    mixed = lax.fori_loop(0, reach, mix_step, jnp.zeros(query.shape, jnp.float32))
    return (mixed, logsum)


def attention_backward(query, keys_all, values_all, segment, first, logsum, mixed_grad):
    scores_at, reach, block, scale = score_maker(query, keys_all, values_all, segment, first)
    shape = (query.shape[1], query.shape[2], query.shape[0])

    def probs_at(index):
        scores, keys, values = scores_at(index)
        probs = jnp.exp(scores - logsum[..., None])
        dots = jnp.einsum("qhgd,khd->hgqk", mixed_grad, values, preferred_element_type=jnp.float32)
        return (probs, dots, keys)

    def delta_step(index, delta):
        probs, dots, keys = probs_at(index)
        return delta + jnp.sum(probs * dots, axis=-1)

    delta = lax.fori_loop(0, reach, delta_step, jnp.zeros(shape, jnp.float32))

    def grad_step(index, state):
        query_grad, key_grad, value_grad = state
        probs, dots, keys = probs_at(index)
        begin = index * block
        score_grad = (probs * (dots - delta[..., None])).astype(jnp.bfloat16)
        query_grad = query_grad + jnp.einsum(
            "hgqk,khd->qhgd", score_grad, keys, preferred_element_type=jnp.float32
        )
        key_part = jnp.einsum(
            "hgqk,qhgd->khd", score_grad, query, preferred_element_type=jnp.float32
        )
        value_part = jnp.einsum(
            "hgqk,qhgd->khd",
            probs.astype(jnp.bfloat16),
            mixed_grad,
            preferred_element_type=jnp.float32,
        )
        key_grad = lax.dynamic_update_slice_in_dim(
            key_grad, lax.dynamic_slice_in_dim(key_grad, begin, block, 0) + key_part, begin, 0
        )
        value_grad = lax.dynamic_update_slice_in_dim(
            value_grad, lax.dynamic_slice_in_dim(value_grad, begin, block, 0) + value_part, begin, 0
        )
        return (query_grad, key_grad, value_grad)

    start = (
        jnp.zeros(query.shape, jnp.float32),
        jnp.zeros(keys_all.shape, jnp.float32),
        jnp.zeros(values_all.shape, jnp.float32),
    )
    query_grad, key_grad, value_grad = lax.fori_loop(0, reach, grad_step, start)
    return (query_grad * scale, key_grad * scale, value_grad)


def adamw(weight, moment, second, grad, rate, decay):
    moment_new = BETA_ONE * moment + (1.0 - BETA_ONE) * grad
    second_new = BETA_TWO * second + (1.0 - BETA_TWO) * grad * grad
    first_hat = moment_new / (1.0 - BETA_ONE**STEP)
    second_hat = second_new / (1.0 - BETA_TWO**STEP)
    weight_new = weight - rate * (first_hat / (jnp.sqrt(second_hat) + ADAM_EPS) + decay * weight)
    return (moment_new, second_new, weight_new)


def swiglu(gate, up):
    return jax.nn.silu(gate) * up


def body(
    tokens,
    cotangent,
    seq_lens,
    query_weight,
    query_moment,
    query_second,
    key_value_master_weight,
    key_value_first_moment,
    key_value_second_moment,
    output_weight,
    output_moment,
    output_second,
    gateup_weight,
    gateup_moment,
    gateup_second,
    down_weight,
    down_moment,
    down_second,
    norm_gains,
    norm_moment,
    norm_second,
    head_gains,
    head_moment,
    head_second,
):
    query_block, keyval_block, output_block, gateup_block, down_block = (
        lax.all_gather(query_weight.astype(jnp.bfloat16), "dp", axis=0, tiled=True),
        lax.all_gather(key_value_master_weight.astype(jnp.bfloat16), "dp", axis=0, tiled=True),
        lax.all_gather(output_weight.astype(jnp.bfloat16), "dp", axis=0, tiled=True),
        lax.all_gather(gateup_weight.astype(jnp.bfloat16), "dp", axis=0, tiled=True),
        lax.all_gather(down_weight.astype(jnp.bfloat16), "dp", axis=0, tiled=True),
    )
    half_rows, width = tokens.shape
    item_count = half_rows * lax.axis_size("col")
    quarter = item_count // lax.axis_size("row")
    row_index = lax.axis_index("row")
    col_index = lax.axis_index("col")
    head_width = query_block.shape[1]
    kv_width = keyval_block.shape[2]
    ff_width = down_block.shape[0]
    heads_local = head_width // HEAD_SIZE
    kv_heads = kv_width // HEAD_SIZE
    groups = heads_local // kv_heads
    in_matrix = jnp.concatenate([query_block, keyval_block.reshape(width, 2 * kv_width)], axis=1)
    gateup_matrix = gateup_block.reshape(width, 2 * ff_width)
    segment, position = token_layout(seq_lens[0], item_count)
    first = row_index * quarter
    cosine, sine = rope_tables(lax.dynamic_slice_in_dim(position, first, quarter, 0))
    valid = (lax.dynamic_slice_in_dim(segment, col_index * half_rows, half_rows, 0) < SEQS).astype(
        jnp.float32
    )
    inputs = tokens.astype(jnp.float32)
    attention_gain = lax.dynamic_slice_in_dim(norm_gains[0], row_index * width, width, 0)
    feedforward_gain = lax.dynamic_slice_in_dim(norm_gains[1], row_index * width, width, 0)
    first_scale, first_normed = norm_forward(inputs, attention_gain)
    first_low = first_normed.astype(jnp.bfloat16)
    first_full = gather_tokens(first_low)
    projected = scatter_rows(first_full, in_matrix, FORWARD_DIMS)
    query_raw = projected[:, :head_width].reshape(quarter, heads_local, HEAD_SIZE)
    key_unrotated = projected[:, head_width : head_width + kv_width].reshape(
        quarter, kv_heads, HEAD_SIZE
    )
    value_unprojected = projected[:, head_width + kv_width :].reshape(quarter, kv_heads, HEAD_SIZE)

    def head_path(raw, gain):
        return rotate(head_norm(raw, gain), cosine, sine)

    query_rot, query_pull = jax.vjp(head_path, query_raw, head_gains[0])
    key_rot, key_pull = jax.vjp(head_path, key_unrotated, head_gains[1])
    query = query_rot.astype(jnp.bfloat16).reshape(quarter, kv_heads, groups, HEAD_SIZE)
    keys = key_rot.astype(jnp.bfloat16)
    values = value_unprojected.astype(jnp.bfloat16)
    keys_all, values_all = gather_keys(keys, values)
    mixed, logsum = attention_forward(query, keys_all, values_all, segment, first)
    mixed_low = mixed.reshape(quarter, head_width).astype(jnp.bfloat16)
    mixed_full = gather_rows(mixed_low)
    hidden = inputs + scatter_cols(mixed_full, output_block, FORWARD_DIMS)
    second_scale, second_normed = norm_forward(hidden, feedforward_gain)
    second_low = second_normed.astype(jnp.bfloat16)
    second_full = gather_tokens(second_low)
    gateup = scatter_rows(second_full, gateup_matrix, FORWARD_DIMS)
    active, swiglu_pull = jax.vjp(swiglu, gateup[:, :ff_width], gateup[:, ff_width:])
    active_low = active.astype(jnp.bfloat16)
    active_full = gather_rows(active_low)
    layer_output = hidden + scatter_cols(active_full, down_block, FORWARD_DIMS)
    out_grad = cotangent.astype(jnp.float32) * valid[:, None]
    down_grad_full = gather_tokens(out_grad.astype(jnp.bfloat16))
    active_grad = scatter_rows(down_grad_full, down_block, FLIPPED_DIMS)
    down_weight_grad = lax.dot_general(
        active_full, down_grad_full, OUTER_DIMS, preferred_element_type=jnp.float32
    )
    gate_grad, up_grad = swiglu_pull(active_grad)
    gateup_grad_full = gather_rows(
        jnp.concatenate([gate_grad, up_grad], axis=1).astype(jnp.bfloat16)
    )
    gateup_weight_grad = lax.dot_general(
        second_full, gateup_grad_full, OUTER_DIMS, preferred_element_type=jnp.float32
    ).reshape(width, 2, ff_width)
    second_normed_grad = scatter_cols(gateup_grad_full, gateup_matrix, FLIPPED_DIMS)
    hidden_norm_grad, second_gain_grad = norm_backward(
        hidden, second_scale, feedforward_gain, second_normed_grad
    )
    hidden_grad = out_grad + hidden_norm_grad
    hidden_grad_full = gather_tokens(hidden_grad.astype(jnp.bfloat16))
    mixed_grad = scatter_rows(hidden_grad_full, output_block, FLIPPED_DIMS)
    output_weight_grad = lax.dot_general(
        mixed_full, hidden_grad_full, OUTER_DIMS, preferred_element_type=jnp.float32
    )
    mixed_grad_low = mixed_grad.astype(jnp.bfloat16).reshape(quarter, kv_heads, groups, HEAD_SIZE)
    query_grad, key_grad_all, value_grad_all = attention_backward(
        query, keys_all, values_all, segment, first, logsum, mixed_grad_low
    )
    key_grad, value_grad = (
        lax.psum_scatter(key_grad_all, "row", scatter_dimension=0, tiled=True),
        lax.psum_scatter(value_grad_all, "row", scatter_dimension=0, tiled=True),
    )
    query_raw_grad, query_gain_grad = query_pull(
        query_grad.reshape(quarter, heads_local, HEAD_SIZE)
    )
    key_raw_grad, key_gain_grad = key_pull(key_grad)
    in_grad = jnp.concatenate(
        [
            query_raw_grad.reshape(quarter, head_width),
            key_raw_grad.reshape(quarter, kv_width),
            value_grad.reshape(quarter, kv_width),
        ],
        axis=1,
    ).astype(jnp.bfloat16)
    in_grad_full = gather_rows(in_grad)
    in_weight_grad = lax.dot_general(
        first_full, in_grad_full, OUTER_DIMS, preferred_element_type=jnp.float32
    )
    first_normed_grad = scatter_cols(in_grad_full, in_matrix, FLIPPED_DIMS)
    inputs_norm_grad, first_gain_grad = norm_backward(
        inputs, first_scale, attention_gain, first_normed_grad
    )
    input_grad = hidden_grad + inputs_norm_grad
    norm_part = lax.dynamic_update_slice_in_dim(
        jnp.zeros((2, MODEL_WIDTH), jnp.float32),
        jnp.stack([first_gain_grad, second_gain_grad]),
        row_index * width,
        1,
    )
    head_part = jnp.stack([query_gain_grad, key_gain_grad])
    norm_total, head_total = lax.psum((norm_part, head_part), ("dp", "row", "col"))
    query_weight_grad = in_weight_grad[:, :head_width]
    keyval_weight_grad = in_weight_grad[:, head_width:].reshape(width, 2, kv_width)
    query_reduced, keyval_reduced, output_reduced, gateup_reduced, down_reduced = (
        lax.psum_scatter(query_weight_grad, "dp", scatter_dimension=0, tiled=True),
        lax.psum_scatter(keyval_weight_grad, "dp", scatter_dimension=0, tiled=True),
        lax.psum_scatter(output_weight_grad, "dp", scatter_dimension=0, tiled=True),
        lax.psum_scatter(gateup_weight_grad, "dp", scatter_dimension=0, tiled=True),
        lax.psum_scatter(down_weight_grad, "dp", scatter_dimension=0, tiled=True),
    )
    query_new = adamw(query_weight, query_moment, query_second, query_reduced, RATES[0], DECAY)
    keyval_new = adamw(
        key_value_master_weight,
        key_value_first_moment,
        key_value_second_moment,
        keyval_reduced,
        RATES[1],
        DECAY,
    )
    output_new = adamw(output_weight, output_moment, output_second, output_reduced, RATES[2], DECAY)
    gateup_new = adamw(gateup_weight, gateup_moment, gateup_second, gateup_reduced, RATES[3], DECAY)
    down_new = adamw(down_weight, down_moment, down_second, down_reduced, RATES[4], DECAY)
    norm_new = adamw(norm_gains, norm_moment, norm_second, norm_total, GAIN_RATE, 0.0)
    head_new = adamw(head_gains, head_moment, head_second, head_total, GAIN_RATE, 0.0)
    return (
        layer_output,
        input_grad,
        query_new[0],
        query_new[1],
        query_new[2],
        keyval_new[0],
        keyval_new[1],
        keyval_new[2],
        output_new[0],
        output_new[1],
        output_new[2],
        gateup_new[0],
        gateup_new[1],
        gateup_new[2],
        down_new[0],
        down_new[1],
        down_new[2],
        norm_new[0],
        norm_new[1],
        norm_new[2],
        head_new[0],
        head_new[1],
        head_new[2],
    )


def solution(mesh):
    placed = (
        P(("dp", "col"), "row"),
        P(("dp", "col"), "row"),
        P("dp", None),
        P(("row", "dp"), "col"),
        P(("row", "dp"), "col"),
        P(("row", "dp"), "col"),
        P(("row", "dp"), None, "col"),
        P(("row", "dp"), None, "col"),
        P(("row", "dp"), None, "col"),
        P(("col", "dp"), "row"),
        P(("col", "dp"), "row"),
        P(("col", "dp"), "row"),
        P(("row", "dp"), None, "col"),
        P(("row", "dp"), None, "col"),
        P(("row", "dp"), None, "col"),
        P(("col", "dp"), "row"),
        P(("col", "dp"), "row"),
        P(("col", "dp"), "row"),
        P(),
        P(),
        P(),
        P(),
        P(),
        P(),
    )
    return jax.shard_map(
        body,
        mesh=mesh,
        in_specs=placed,
        out_specs=(
            P(("dp", "col"), "row"),
            P(("dp", "col"), "row"),
            P(("row", "dp"), "col"),
            P(("row", "dp"), "col"),
            P(("row", "dp"), "col"),
            P(("row", "dp"), None, "col"),
            P(("row", "dp"), None, "col"),
            P(("row", "dp"), None, "col"),
            P(("col", "dp"), "row"),
            P(("col", "dp"), "row"),
            P(("col", "dp"), "row"),
            P(("row", "dp"), None, "col"),
            P(("row", "dp"), None, "col"),
            P(("row", "dp"), None, "col"),
            P(("col", "dp"), "row"),
            P(("col", "dp"), "row"),
            P(("col", "dp"), "row"),
            P(),
            P(),
            P(),
            P(),
            P(),
            P(),
        ),
        check_vma=False,
    )
```

profile of v0, /device:TPU:0, one launch (start us, length us, event | category | flops | bytes accessed | tf_op | source)
XLA Modules:
  0.0 2368.7 jit_solution(10633256953461352103)
XLA Ops:
  12.3 13.5 psum.42
  31.1 17.4 all-gather.18.cloned.1.call-done
  51.8 20.2 all-gather.16.cloned.1.call-done
  72.0 7.6 fusion.123
  82.6 141.7 %reduce-scatter.14.cloned.1.call-done = f32[256,2048]{1,0:T(8,128)} async-done(((f32[1024,2048]{1,0:T(8,128)}), f32[256,2048]{1,0:T(8,128)}) %reduce-scatter.14.cloned.1.call-update) | async-done | bytes 2097168 | tf_op jit(solution)/shard_map/reduce_scatter | solution.py:80
  238.3 19.9 all-gather.24.cloned.1.call-done
  260.6 3.1 while.50
  263.7 22.9 all-gather.22.cloned.1.call-done
  286.7 3.4 while.51
  287.2 2.8 fusion.202
  291.0 14.0 all-gather.28.cloned.1.call-done
  305.0 48.4 %all-gather.26.cloned.1.call-done = bf16[1024,1024]{0,1:T(8,128)(2,1)} async-done(((bf16[256,1024]{0,1:T(8,128)(2,1)}), bf16[1024,1024]{0,1:T(8,128)(2,1)}) %all-gather.26.cloned.1.call-update) | async-done | bytes 2097168 | tf_op jit(solution)/shard_map/all_gather | solution.py:65
  353.4 4.5 fusion.124
  360.5 4.4 convert_element_type.89
  365.0 23.0 reduce-scatter.16.cloned.1.call-done
  389.5 11.7 psum.43
  402.2 9.2 all-gather.38.cloned.1.call-done
  411.5 30.8 %all-gather.36.cloned.1.call-done = bf16[3072,512]{1,0:T(8,128)(2,1)} async-done(((bf16[768,512]{1,0:T(8,128)(2,1)}), bf16[3072,512]{1,0:T(8,128)(2,1)}) %all-gather.36.cloned.1.call-update) | async-done | bytes 3145744 | tf_op jit(solution)/shard_map/all_gather | solution.py:261
  442.2 11.0 fusion.127
  453.3 37.4 %all-gather.32.cloned.1.call-done = bf16[512,2,3072]{2,1,0:T(2,128)(2,1)} async-done(((bf16[128,2,3072]{2,1,0:T(2,128)(2,1)}), bf16[512,2,3072]{2,1,0:T(2,128)(2,1)}) %all-gather.32.cloned.1.call-update) | async-done | bytes 6291472 | tf_op jit(solution)/shard_map/all_gather | solution.py:260
  490.7 7.2 copy.248
  497.9 16.3 all-gather.30.cloned.1.call-done
  514.3 14.7 fusion.125
  529.5 199.0 %reduce-scatter.22.cloned.1.call-done = f32[256,3072]{1,0:T(8,128)} async-done(((f32[1024,3072]{1,0:T(8,128)}), f32[256,3072]{1,0:T(8,128)}) %reduce-scatter.22.cloned.1.call-update) | async-done | bytes 3145744 | tf_op jit(solution)/shard_map/reduce_scatter | solution.py:80
  728.5 417.8 %reduce-scatter.18.cloned.1.call-done = f32[256,6144]{1,0:T(8,128)} async-done(((f32[1024,6144]{1,0:T(8,128)}), f32[256,6144]{1,0:T(8,128)}) %reduce-scatter.18.cloned.1.call-update) | async-done | bytes 6291472 | tf_op jit(solution)/shard_map/reduce_scatter | solution.py:80
  1146.3 5.7 fusion.72
  1154.5 219.5 %all-gather.40.cloned.1.call-done = bf16[1024,6144]{1,0:T(8,128)(2,1)} async-done(((bf16[256,6144]{1,0:T(8,128)(2,1)}), bf16[1024,6144]{1,0:T(8,128)(2,1)}) %all-gather.40.cloned.1.call-update) | async-done | bytes 12582928 | tf_op jit(solution)/shard_map/all_gather | solution.py:65
  1374.1 12.5 fusion.128
  1386.6 103.0 %all-gather.34.cloned.1.call-done = bf16[1024,3072]{1,0:T(8,128)(2,1)} async-done(((bf16[256,3072]{1,0:T(8,128)(2,1)}), bf16[1024,3072]{1,0:T(8,128)(2,1)}) %all-gather.34.cloned.1.call-update) | async-done | bytes 6291472 | tf_op jit(solution)/shard_map/all_gather | solution.py:65
  1489.6 8.4 fusion.126
  1498.1 24.3 %reduce-scatter.24.cloned.1.call-done = f32[512,512]{1,0:T(8,128)} async-done(((f32[1024,512]{1,0:T(8,128)}), f32[512,512]{1,0:T(8,128)}) %reduce-scatter.24.cloned.1.call-update) | async-done | bytes 1048592 | tf_op jit(solution)/shard_map/reduce_scatter | solution.py:93
  1524.5 11.7 psum.44
  1536.2 21.0 reduce-scatter.20.cloned.1.call-done
  1557.2 3.4 fusion.118
  1560.6 21.4 all-gather.42.cloned.1.call-done
  1582.0 4.8 fusion.129
  1587.0 76.9 %reduce-scatter.26.cloned.1.call-done = f32[256,1024]{1,0:T(8,128)} async-done(((f32[1024,1024]{1,0:T(8,128)}), f32[256,1024]{1,0:T(8,128)}) %reduce-scatter.26.cloned.1.call-update) | async-done | bytes 1048592 | tf_op jit(solution)/shard_map/reduce_scatter | solution.py:80
  1666.4 4.6 while.52
  1675.2 32.9 %while.53 = (s32[]{:T(128)}, f32[256,4,2,128]{0,3,2,1:T(8,128)}, f32[1024,4,128]{0,2,1:T(8,128)}, f32[1024,4,128]{0,2,1:T(8,128)}, s32[]{:T(128)}, /*index=5*/bf...) while((s32[]{:T(128)}, f32[256,4,2,128]{0,3,2,1:T(8,128)}, ...), condition=%wide.region_28.29_spmd.clone, body=%wide.region_27.28_spmd.clone.sunk | while | flops 1353843456 | bytes 71210280 | solution.py:213
  1677.4 3.5 fusion.220
  1684.6 2.9 fusion.223
  1695.0 4.7 fusion.222
  1702.2 3.0 constant_dynamic-update-slice_fusion.5
  1705.2 2.9 fusion.221
  1708.1 3.3 broadcast_multiply_fusion
  1714.9 78.4 %reduce-scatter.28.cloned.1.call-done = f32[256,4,128]{0,2,1:T(8,128)} async-done(((f32[1024,4,128]{0,2,1:T(8,128)}), f32[256,4,128]{0,2,1:T(8,128)}) %reduce-scatter.28.cloned.1.call-update) | async-done | bytes 524304 | tf_op jit(solution)/shard_map/reduce_scatter | solution.py:344
  1795.8 43.5 %reduce-scatter.30.cloned.1.call-done = f32[256,4,128]{0,2,1:T(8,128)} async-done(((f32[1024,4,128]{0,2,1:T(8,128)}), f32[256,4,128]{0,2,1:T(8,128)}) %reduce-scatter.30.cloned.1.call-update) | async-done | bytes 524304 | tf_op jit(solution)/shard_map/reduce_scatter | solution.py:345
  1841.5 8.3 fusion.134
  1851.5 3.8 fusion.132
  1855.6 65.9 %all-gather.44.cloned.1.call-done = bf16[1024,2048]{0,1:T(8,128)(2,1)} async-done(((bf16[256,2048]{0,1:T(8,128)(2,1)}), bf16[1024,2048]{0,1:T(8,128)(2,1)}) %all-gather.44.cloned.1.call-update) | async-done | bytes 4194320 | tf_op jit(solution)/shard_map/all_gather | solution.py:65
  1921.5 6.6 fusion.130
  1928.2 5.0 fusion.131
  1935.0 13.0 fusion.133
  1948.1 16.6 reshape.262
  1969.4 11.4 reduce-scatter.38.cloned.1.call-done
  1980.8 5.4 multiply_subtract_fusion.1
  1986.3 28.4 %reduce-scatter.36.cloned.1.call-done = f32[256,512]{1,0:T(8,128)} async-done(((f32[1024,512]{1,0:T(8,128)}), f32[256,512]{1,0:T(8,128)}) %reduce-scatter.36.cloned.1.call-update) | async-done | bytes 524304 | tf_op jit(solution)/shard_map/reduce_scatter | solution.py:381
  2017.5 31.8 %reduce-scatter.32.cloned.1.call-done = f32[512,512]{1,0:T(8,128)} async-done(((f32[1024,512]{1,0:T(8,128)}), f32[512,512]{1,0:T(8,128)}) %reduce-scatter.32.cloned.1.call-update) | async-done | bytes 1048592 | tf_op jit(solution)/shard_map/reduce_scatter | solution.py:93
  2051.1 11.7 psum.45
  2062.8 37.6 %all-reduce.6 = (f32[2,2048]{1,0:T(2,128)S(1)}, f32[2,128]{1,0:T(2,128)S(1)}) all-reduce(f32[2,2048]{1,0:T(2,128)S(1)} %maximum_dynamic-update-slice_fusion, f32[2,128]{1,0:T(2,128)S(1)} %pad_maximum_fusion.3), channel_id=1, replica_groups=mesh['dp'=4,'row'=4,'col'=2] {'dp','row','col'}, use_global_device_ids=true, to_apply=%region_43.44 | all-reduce | flops 4352 | bytes 34816 | tf_op jit(solution)/shard_map/psum | solution.py:375
  2101.1 2.9 multiply_subtract_fusion.4
  2105.9 237.0 %all-reduce.10.cloned.1.call-done = (f32[512,2,512]{2,1,0:T(2,128)}, f32[512,2,3072]{2,1,0:T(2,128)}) async-done(((f32[512,2,512]{2,1,0:T(2,128)}, f32[512,2,3072]{2,1,0:T(2,128)}), (f32[512,2,512]{2,1,0:T(2,128)}, f32[512,2,3072]{2,1,0:T(2,128)})) %all-reduce.10.cloned.1.call-update) | async-done | bytes 14680080
  2342.9 14.9 multiply_subtract_fusion
  2357.9 3.9 multiply_subtract_fusion.3
  (296 shorter events, 97.6 us)
Async XLA Ops:
  7.2 22.4 all-gather.20.cloned.1.call-start
  9.2 39.3 %all-gather.18.cloned.1.call-start = ((), (), s32[]{:S(2)}) async-start(), calls=%async_computation.14 | async-start | bytes 1310720 | tf_op jit(solution)/shard_map/all_gather | solution.py:257
  11.0 60.9 %all-gather.16.cloned.1.call-start = ((), (), s32[]{:S(2)}) async-start(), calls=%async_computation.13 | async-start | bytes 1572864 | tf_op jit(solution)/shard_map/all_gather | solution.py:61
  25.8 26.0 %copy-start.37 = (f32[512]{0:T(512)}, f32[512]{0:T(512)S(1)}, u32[]{:S(2)}) copy-start(f32[512]{0:T(512)S(1)} %psum.42) | copy-start | bytes 6148
  26.6 25.2 %copy-start.33 = (f32[1,512]{1,0:T(1,128)}, f32[1,512]{1,0:T(1,128)S(1)}, u32[]{:S(2)}) copy-start(f32[1,512]{1,0:T(1,128)S(1)} %constant_dynamic-slice_fusion.3) | copy-start | bytes 6148
  26.6 25.2 %copy-start.35 = (f32[512]{0:T(512)}, f32[512]{0:T(512)S(1)}, u32[]{:S(2)}) copy-start(f32[512]{0:T(512)S(1)} %add_rsqrt_fusion.1) | copy-start | bytes 6148
  28.7 195.5 %reduce-scatter.14.cloned.1.call-start = ((), (), s32[]{:S(2)}) async-start(), calls=%async_computation.16 | async-start | bytes 10485760 | tf_op jit(solution)/shard_map/reduce_scatter | solution.py:80
  79.6 178.7 %all-gather.24.cloned.1.call-start = ((), (), s32[]{:S(2)}) async-start(), calls=%async_computation.18 | async-start | bytes 1310720 | tf_op jit(solution)/shard_map/all_gather | solution.py:70
  82.5 147.4 %copy-start.13 = (f32[256,128]{0,1:T(8,128)}, f32[256,128]{0,1:T(8,128)S(1)}, u32[]{:S(2)}) copy-start(f32[256,128]{0,1:T(8,128)S(1)} %get-tuple-element.769) | copy-start | bytes 393220
  82.5 147.5 %copy-start.15 = (f32[256,128]{0,1:T(8,128)}, f32[256,128]{0,1:T(8,128)S(1)}, u32[]{:S(2)}) copy-start(f32[256,128]{0,1:T(8,128)S(1)} %get-tuple-element.770) | copy-start | bytes 393220
  82.6 144.6 %copy-start.41 = (f32[128]{0:T(128)}, f32[128]{0:T(128)S(1)}, u32[]{:S(2)}) copy-start(f32[128]{0:T(128)S(1)} %get-tuple-element.774) | copy-start | bytes 1540
  82.6 153.9 %copy-start.43 = (f32[128]{0:T(128)}, f32[128]{0:T(128)S(1)}, u32[]{:S(2)}) copy-start(f32[128]{0:T(128)S(1)} %get-tuple-element.773) | copy-start | bytes 1540
  226.1 4.1 copy-start.4
  227.2 59.3 %all-gather.22.cloned.1.call-start = ((), (), s32[]{:S(2)}) async-start(), calls=%async_computation.17 | async-start | bytes 1310720 | tf_op jit(solution)/shard_map/all_gather | solution.py:71
  229.1 75.9 %all-gather.28.cloned.1.call-start = ((), (), s32[]{:S(2)}) async-start(), calls=%async_computation.20 | async-start | bytes 1310720 | tf_op jit(solution)/shard_map/all_gather | solution.py:259
  229.9 123.5 %all-gather.26.cloned.1.call-start = ((), (), s32[]{:S(2)}) async-start(), calls=%async_computation.19 | async-start | bytes 2621440 | tf_op jit(solution)/shard_map/all_gather | solution.py:65
  290.9 67.1 %copy-start.17 = (bf16[512,512]{1,0:T(8,128)(2,1)S(1)}, bf16[512,512]{1,0:T(8,128)(2,1)}, u32[]{:S(2)}) copy-start(bf16[512,512]{1,0:T(8,128)(2,1)} %param.33) | copy-start | bytes 1572868
  290.9 97.2 %reduce-scatter.16.cloned.1.call-start = ((), (), s32[]{:S(2)}) async-start(), calls=%async_computation.21 | async-start | bytes 3145728 | tf_op jit(solution)/shard_map/reduce_scatter | solution.py:93
  357.9 53.6 %all-gather.38.cloned.1.call-start = ((), (), s32[]{:S(2)}) async-start(), calls=%async_computation.28 | async-start | bytes 1572864 | tf_op jit(solution)/shard_map/all_gather | solution.py:61
  359.0 83.3 %all-gather.36.cloned.1.call-start = ((), (), s32[]{:S(2)}) async-start(), calls=%async_computation.26 | async-start | bytes 3932160 | tf_op jit(solution)/shard_map/all_gather | solution.py:261
  360.4 27.6 %copy-start.6 = (bf16[512,512]{1,0:T(8,128)(2,1)S(1)}, bf16[512,512]{1,0:T(8,128)(2,1)}, u32[]{:S(2)}) copy-start(bf16[512,512]{1,0:T(8,128)(2,1)} %param.32) | copy-start | bytes 1572868
  360.4 130.3 %all-gather.32.cloned.1.call-start = ((), (), s32[]{:S(2)}) async-start(), calls=%async_computation.23 | async-start | bytes 7864320 | tf_op jit(solution)/shard_map/all_gather | solution.py:260
  365.0 149.3 %all-gather.30.cloned.1.call-start = ((), (), s32[]{:S(2)}) async-start(), calls=%async_computation.22 | async-start | bytes 1572864 | tf_op jit(solution)/shard_map/all_gather | solution.py:61
  402.2 326.3 %reduce-scatter.22.cloned.1.call-start = ((), (), s32[]{:S(2)}) async-start(), calls=%async_computation.29 | async-start | bytes 15728640 | tf_op jit(solution)/shard_map/reduce_scatter | solution.py:80
  453.3 693.0 %reduce-scatter.18.cloned.1.call-start = ((), (), s32[]{:S(2)}) async-start(), calls=%async_computation.24 | async-start | bytes 31457280 | tf_op jit(solution)/shard_map/reduce_scatter | solution.py:80
  529.0 845.0 %all-gather.40.cloned.1.call-start = ((), (), s32[]{:S(2)}) async-start(), calls=%async_computation.30 | async-start | bytes 15728640 | tf_op jit(solution)/shard_map/all_gather | solution.py:65
  1153.9 335.7 %all-gather.34.cloned.1.call-start = ((), (), s32[]{:S(2)}) async-start(), calls=%async_computation.25 | async-start | bytes 7864320 | tf_op jit(solution)/shard_map/all_gather | solution.py:65
  1154.5 367.9 %reduce-scatter.24.cloned.1.call-start = ((), (), s32[]{:S(2)}) async-start(), calls=%async_computation.31 | async-start | bytes 3145728 | tf_op jit(solution)/shard_map/reduce_scatter | solution.py:93
  1386.6 170.6 %reduce-scatter.20.cloned.1.call-start = ((), (), s32[]{:S(2)}) async-start(), calls=%async_computation.27 | async-start | bytes 3145728 | tf_op jit(solution)/shard_map/reduce_scatter | solution.py:93
  1498.1 84.0 %all-gather.42.cloned.1.call-start = ((), (), s32[]{:S(2)}) async-start(), calls=%async_computation.32 | async-start | bytes 1572864 | tf_op jit(solution)/shard_map/all_gather | solution.py:61
  1560.6 103.3 %reduce-scatter.26.cloned.1.call-start = ((), (), s32[]{:S(2)}) async-start(), calls=%async_computation.33 | async-start | bytes 5242880 | tf_op jit(solution)/shard_map/reduce_scatter | solution.py:80
  1586.9 206.3 %reduce-scatter.28.cloned.1.call-start = ((), (), s32[]{:S(2)}) async-start(), calls=%async_computation.34 | async-start | bytes 2621440 | tf_op jit(solution)/shard_map/reduce_scatter | solution.py:344
  1711.4 127.9 %reduce-scatter.30.cloned.1.call-start = ((), (), s32[]{:S(2)}) async-start(), calls=%async_computation.35 | async-start | bytes 2621440 | tf_op jit(solution)/shard_map/reduce_scatter | solution.py:345
  1712.1 209.4 %all-gather.44.cloned.1.call-start = ((), (), s32[]{:S(2)}) async-start(), calls=%async_computation.36 | async-start | bytes 5242880 | tf_op jit(solution)/shard_map/all_gather | solution.py:65
  1714.3 80.0 %copy-start.5 = (f32[256,4,128]{0,2,1:T(8,128)S(1)}, f32[256,4,128]{0,2,1:T(8,128)}, u32[]{:S(2)}) copy-start(f32[256,4,128]{0,2,1:T(8,128)} %copy-done.4) | copy-start | bytes 1572868
  1714.4 80.0 %copy-start.27 = (f32[256,4]{0,1:T(4,128)S(1)}, f32[256,4]{0,1:T(4,128)}, u32[]{:S(2)}) copy-start(f32[256,4]{0,1:T(4,128)} %copy-done.26) | copy-start | bytes 12292
  1714.4 80.0 %copy-start.42 = (f32[128]{0:T(128)S(1)}, f32[128]{0:T(128)}, u32[]{:S(2)}) copy-start(f32[128]{0:T(128)} %copy-done.41) | copy-start | bytes 1540
  1714.6 81.1 %copy-start.32 = (f32[256,4]{0,1:T(4,128)S(1)}, f32[256,4]{0,1:T(4,128)}, u32[]{:S(2)}) copy-start(f32[256,4]{0,1:T(4,128)} %copy-done.31) | copy-start | bytes 12292
  1795.7 45.9 %copy-start.52 = (bf16[1024,512]{1,0:T(8,128)(2,1)S(1)}, bf16[1024,512]{1,0:T(8,128)(2,1)}, u32[]{:S(2)}) copy-start(bf16[1024,512]{1,0:T(8,128)(2,1)} %all-gather.38.cloned.1.call-done) | copy-start | bytes 3145732
  1841.5 139.3 %reduce-scatter.38.cloned.1.call-start = ((), (), s32[]{:S(2)}) async-start(), calls=%async_computation.40 | async-start | bytes 7864320 | tf_op jit(solution)/shard_map/reduce_scatter | solution.py:383
  1849.9 164.8 %reduce-scatter.36.cloned.1.call-start = ((), (), s32[]{:S(2)}) async-start(), calls=%async_computation.39 | async-start | bytes 2621440 | tf_op jit(solution)/shard_map/reduce_scatter | solution.py:381
  1855.3 72.9 %copy-start.51 = (bf16[1024,512]{1,0:T(8,128)(2,1)S(1)}, bf16[1024,512]{1,0:T(8,128)(2,1)}, u32[]{:S(2)}) copy-start(bf16[1024,512]{1,0:T(8,128)(2,1)} %all-gather.16.cloned.1.call-done) | copy-start | bytes 3145732
  1855.3 193.9 %reduce-scatter.32.cloned.1.call-start = ((), (), s32[]{:S(2)}) async-start(), calls=%async_computation.37 | async-start | bytes 3145728 | tf_op jit(solution)/shard_map/reduce_scatter | solution.py:93
  1928.2 172.9 %reduce-scatter.34.cloned.1.call-start = ((), (), s32[]{:S(2)}) async-start(), calls=%async_computation.38 | async-start | bytes 2621440 | tf_op jit(solution)/shard_map/reduce_scatter | solution.py:379
  1935.0 407.9 %all-reduce.10.cloned.1.call-start = ((), (), s32[]{:S(2)}) async-start(), calls=%async_computation.41 | async-start | bytes 29360128
  1967.5 13.3 copy-start.9
  1969.4 45.3 %copy-start.19 = (f32[256,512]{1,0:T(8,128)S(1)}, f32[256,512]{1,0:T(8,128)}, u32[]{:S(2)}) copy-start(f32[256,512]{1,0:T(8,128)} %param.41) | copy-start | bytes 1572868
  1986.2 63.1 %copy-start.7 = (bf16[512,512]{1,0:T(8,128)(2,1)S(1)}, bf16[512,512]{1,0:T(8,128)(2,1)}, u32[]{:S(2)}) copy-start(bf16[512,512]{1,0:T(8,128)(2,1)} %param.32) | copy-start | bytes 1572868
  1986.2 63.1 %copy-start.34 = (f32[1,512]{1,0:T(1,128)S(1)}, f32[1,512]{1,0:T(1,128)}, u32[]{:S(2)}) copy-start(f32[1,512]{1,0:T(1,128)} %copy-done.33) | copy-start | bytes 6148
  1986.2 63.1 %copy-start.36 = (f32[512]{0:T(512)S(1)}, f32[512]{0:T(512)}, u32[]{:S(2)}) copy-start(f32[512]{0:T(512)} %copy-done.35) | copy-start | bytes 6148
  1986.2 76.6 %copy-start.45 = (f32[512]{0:T(512)S(1)}, f32[512]{0:T(512)}, u32[]{:S(2)}) copy-start(f32[512]{0:T(512)} %get-tuple-element.624) | copy-start | bytes 6148
  1986.2 114.2 %copy-start.38 = (f32[512]{0:T(512)S(1)}, f32[512]{0:T(512)}, u32[]{:S(2)}) copy-start(f32[512]{0:T(512)} %copy-done.37) | copy-start | bytes 6148
  1986.2 114.2 %copy-start.47 = (f32[2,128]{1,0:T(2,128)S(1)}, f32[2,128]{1,0:T(2,128)}, u32[]{:S(2)}) copy-start(f32[2,128]{1,0:T(2,128)} %param.53) | copy-start | bytes 3076
  1986.2 114.2 %copy-start.48 = (f32[2,128]{1,0:T(2,128)S(1)}, f32[2,128]{1,0:T(2,128)}, u32[]{:S(2)}) copy-start(f32[2,128]{1,0:T(2,128)} %param.55) | copy-start | bytes 3076
  1986.3 114.2 %copy-start.49 = (f32[2,128]{1,0:T(2,128)S(1)}, f32[2,128]{1,0:T(2,128)}, u32[]{:S(2)}) copy-start(f32[2,128]{1,0:T(2,128)} %param.54) | copy-start | bytes 3076
  1986.3 114.8 %copy-start.20 = (f32[128,1024]{1,0:T(8,128)S(1)}, f32[128,1024]{1,0:T(8,128)}, u32[]{:S(2)}) copy-start(f32[128,1024]{1,0:T(8,128)} %param.35) | copy-start | bytes 1572868
  2017.5 86.5 %copy-start.12 = (f32[512,512]{1,0:T(8,128)S(1)}, f32[512,512]{1,0:T(8,128)}, u32[]{:S(2)}) copy-start(f32[512,512]{1,0:T(8,128)} %get-tuple-element.748) | copy-start | bytes 3145732
  2049.3 54.7 %copy-start.10 = (f32[512,512]{1,0:T(8,128)S(1)}, f32[512,512]{1,0:T(8,128)}, u32[]{:S(2)}) copy-start(f32[512,512]{1,0:T(8,128)} %reduce-scatter.32.cloned.1.call-done) | copy-start | bytes 3145732
  2101.1 4.1 copy-start.30
  2101.1 4.1 copy-start.39
  2101.1 4.1 copy-start.40
  2342.9 14.9 copy-start.21
  2342.9 14.9 copy-start.22
  2342.9 14.9 copy-start.23
  (20 other events, 41.8 us)
Sparse Core Ops, SparseCore 0:
  10.2 19.4 all-gather.19
  31.7 16.7 all-gather.17
  50.6 21.3 all-gather.15
  79.7 144.4 reduce-scatter.13
  227.4 30.9 all-gather.23
  260.3 26.2 all-gather.21
  288.7 16.2 all-gather.27
  307.1 46.2 all-gather.25
  358.0 30.0 reduce-scatter.15
  390.1 21.3 all-gather.37
  413.7 28.5 all-gather.35
  444.3 46.3 all-gather.31
  492.9 21.3 all-gather.29
  516.6 211.8 reduce-scatter.21
  730.8 415.4 reduce-scatter.17
  1154.0 220.0 all-gather.39
  1376.1 113.5 all-gather.33
  1492.3 30.0 reduce-scatter.23
  1525.3 31.8 reduce-scatter.19
  1560.7 21.3 all-gather.41
  1587.0 76.7 reduce-scatter.25
  1711.5 81.6 reduce-scatter.27
  1796.1 43.1 reduce-scatter.29
  1841.6 79.8 all-gather.43
  1924.2 56.5 reduce-scatter.37
  1983.2 31.4 reduce-scatter.35
  2017.4 31.8 reduce-scatter.31
  2052.4 31.6 reduce-scatter.33
  2087.4 255.4 all-reduce.9
where the time goes:
time: 2380 us; the launch traced here: 2370 us
  waiting for transfers between devices  1980 us (83%)
  matrix products  125 us (5%)
  blocking collectives  86.2 us (4%)
  other arithmetic  83.3 us (4%)
  local copies, waits for them, and re-layouts  72.9 us (3%)
    reduce_scatter x4, waiting for transfers between devices, scatter_rows(): lax.psum_scatter(term(jnp.int32(0), full.shape[0] // lax.axis_size('row')...  835 us
    all_gather x4, waiting for transfers between devices, gather_rows(): return lax.all_gather(local, 'row', axis=0, tiled=True)  437 us
    unnamed x30, waiting for transfers between devices  239 us
    reduce_scatter x4, waiting for transfers between devices, scatter_cols(): lax.psum_scatter(term(jnp.int32(0), full.shape[0] // lax.axis_size('col')...  100 us
    reduce_scatter x1, waiting for transfers between devices, body(): lax.psum_scatter(key_grad_all, 'row', scatter_dimension=0, tiled=True)  78.4 us
    dot_general x8, matrix products, term(): lax.dot_general(full, matrix, numbers, preferred_element_type=jnp.float32)  70.1 us
    all_gather x4, waiting for transfers between devices, gather_tokens(): return lax.all_gather(local, 'col', axis=0, tiled=True)  67.1 us
    psum x4, blocking collectives, row_total(): return lax.psum(values, 'row')  48.5 us
  transfers between devices with their start and end apart: 29, of which 28 were waited for; matrix products, arithmetic and copies ran while one was open for 7% of the time, Pallas kernels for 0%

commit v1 on v0

v1 whole, which is shorter than its diff:
```python
import functools
import math

import jax
import jax.numpy as jnp
from jax import lax
from jax.experimental import pallas as pl
from jax.experimental.pallas import tpu as pltpu
from jax.sharding import PartitionSpec as P

MODEL_WIDTH = 2048
HEAD_SIZE = 128
SEQS = 4
STEP = 10

EPS = 1e-06
THETA = 1000000.0
NEGATIVE = -1e30
BETA_ONE = 0.9
BETA_TWO = 0.95
ADAM_EPS = 1e-08
DECAY = 0.1
RATES = (0.066, 0.066, 0.5, 0.066, 0.04)
GAIN_RATE = 0.6
BF = jnp.bfloat16
F32 = jnp.float32
SCALE = 1.0 / math.sqrt(HEAD_SIZE)


def dot(a, b, kind="nn"):
    dims = {"nn": ((1,), (0,)), "nt": ((1,), (1,)), "tn": ((0,), (0,))}[kind]
    return lax.dot_general(a, b, (dims, ((), ())), preferred_element_type=F32)


def token_layout(lengths, item_count):
    ends = jnp.cumsum(lengths)
    places = jnp.arange(item_count, dtype=jnp.int32)
    segment = jnp.sum((places[:, None] >= ends[None, :]).astype(jnp.int32), axis=1)
    starts = jnp.concatenate([ends - lengths, ends[-1:]])
    labels = jnp.arange(starts.shape[0], dtype=jnp.int32)
    begin = jnp.sum(jnp.where(segment[:, None] == labels[None, :], starts[None, :], 0), axis=1)
    return (segment, places - begin)


def rope_tables(position):
    half = HEAD_SIZE // 2
    freq = jnp.exp(jnp.arange(half, dtype=F32) * (-2.0 * math.log(THETA) / HEAD_SIZE))
    angle = position.astype(F32)[:, None] * freq[None, :]
    angle = jnp.concatenate([angle, angle], axis=1)
    return (jnp.cos(angle), jnp.sin(angle))


def block_masks(own_col, own_row, prev_row, later):
    rows = own_col.shape[0]
    r = lax.broadcasted_iota(jnp.int32, (rows, rows), 0)
    c = lax.broadcasted_iota(jnp.int32, (rows, rows), 1)
    own = (c <= r) & (own_col == own_row)
    prev = (own_col == prev_row) & (later > 0)
    return own, prev


def forward_kernel(later, own_col, own_row, prev_row, q, k, v, kp, vp, o, lse):
    own, prev = block_masks(own_col[...], own_row[...], prev_row[...], later[0])
    s_own = jnp.where(own, dot(q[...], k[...], "nt") * SCALE, NEGATIVE)
    s_prev = jnp.where(prev, dot(q[...], kp[...], "nt") * SCALE, NEGATIVE)
    top = jnp.maximum(
        jnp.max(s_own, axis=1, keepdims=True), jnp.max(s_prev, axis=1, keepdims=True)
    )
    total = jnp.sum(jnp.exp(s_own - top), axis=1, keepdims=True) + jnp.sum(
        jnp.exp(s_prev - top), axis=1, keepdims=True
    )
    logsum = top + jnp.log(total)
    p_own = jnp.exp(s_own - logsum).astype(BF)
    p_prev = jnp.exp(s_prev - logsum).astype(BF)
    o[...] = (dot(p_own, v[...]) + dot(p_prev, vp[...])).astype(BF)
    lse[0] = logsum


def attention_forward(later, own_col, own_row, prev_row, q, kv, before, after):
    rows, width = q.shape
    heads = width // HEAD_SIZE
    groups = 2 * width // kv.shape[1]
    inputs = (later, own_col, own_row, prev_row, q, kv, kv, before, before)

    def kernel(*refs):
        forward_kernel(*refs[: len(inputs)], *refs[len(inputs) + len(after) :])

    mine = pl.BlockSpec((rows, HEAD_SIZE), lambda h: (0, h))
    key = pl.BlockSpec((rows, HEAD_SIZE), lambda h: (0, 2 * (h // groups)))
    value = pl.BlockSpec((rows, HEAD_SIZE), lambda h: (0, 2 * (h // groups) + 1))
    column = pl.BlockSpec((rows, 1), lambda h: (0, 0))
    line = pl.BlockSpec((1, rows), lambda h: (0, 0))
    return pl.pallas_call(
        kernel,
        grid=(heads,),
        in_specs=[pl.BlockSpec(memory_space=pltpu.SMEM), column, line, line, mine]
        + [key, value] * 2
        + [pl.BlockSpec(memory_space=pl.ANY)] * len(after),
        out_specs=[mine, pl.BlockSpec((1, rows, 1), lambda h: (h, 0, 0))],
        out_shape=[
            jax.ShapeDtypeStruct((rows, width), BF),
            jax.ShapeDtypeStruct((heads, rows, 1), F32),
        ],
        compiler_params=pltpu.CompilerParams(vmem_limit_bytes=32 * 2**20),
    )(*inputs, *after)


def backward_kernel(
    later, own_col, own_row, prev_row, q, k, v, kp, vp, do, lse, dq, dk, dv, far, total
):
    own, prev = block_masks(own_col[...], own_row[...], prev_row[...], later[0])
    logsum = lse[0]
    p_own = jnp.exp(jnp.where(own, dot(q[...], k[...], "nt") * SCALE, NEGATIVE) - logsum)
    p_prev = jnp.exp(jnp.where(prev, dot(q[...], kp[...], "nt") * SCALE, NEGATIVE) - logsum)
    d_own = dot(do[...], v[...], "nt")
    d_prev = dot(do[...], vp[...], "nt")
    delta = jnp.sum(p_own * d_own, axis=1, keepdims=True) + jnp.sum(
        p_prev * d_prev, axis=1, keepdims=True
    )
    g_own = (p_own * (d_own - delta)).astype(BF)
    g_prev = (p_prev * (d_prev - delta)).astype(BF)
    dq[...] = (dot(g_own, k[...]) + dot(g_prev, kp[...])) * SCALE
    near = ((dk, dot(g_own, q[...], "tn") * SCALE), (dv, dot(p_own.astype(BF), do[...], "tn")))
    dkp = dot(g_prev, q[...], "tn") * SCALE
    dvp = dot(p_prev.astype(BF), do[...], "tn")
    group = pl.program_id(1)

    @pl.when(group == 0)
    def _():
        for ref, value in near:
            ref[...] = value
        total[:, :HEAD_SIZE] = dkp
        total[:, HEAD_SIZE:] = dvp

    @pl.when(group > 0)
    def _():
        for ref, value in near:
            ref[...] += value
        total[:, :HEAD_SIZE] += dkp
        total[:, HEAD_SIZE:] += dvp

    @pl.when(group == pl.num_programs(1) - 1)
    def _():
        far[...] = total[...].astype(BF)


def attention_backward(later, own_col, own_row, prev_row, q, kv, before, do, lse, after):
    rows, width = q.shape
    kv_heads = kv.shape[1] // (2 * HEAD_SIZE)
    groups = 2 * width // kv.shape[1]
    inputs = (later, own_col, own_row, prev_row, q, kv, kv, before, before, do, lse)

    def kernel(*refs):
        backward_kernel(*refs[: len(inputs)], *refs[len(inputs) + len(after) :])

    mine = pl.BlockSpec((rows, HEAD_SIZE), lambda h, g: (0, h * groups + g))
    shared = pl.BlockSpec((rows, HEAD_SIZE), lambda h, g: (0, h))
    key = pl.BlockSpec((rows, HEAD_SIZE), lambda h, g: (0, 2 * h))
    value = pl.BlockSpec((rows, HEAD_SIZE), lambda h, g: (0, 2 * h + 1))
    column = pl.BlockSpec((rows, 1), lambda h, g: (0, 0))
    line = pl.BlockSpec((1, rows), lambda h, g: (0, 0))
    near = jax.ShapeDtypeStruct((rows, kv_heads * HEAD_SIZE), F32)
    return pl.pallas_call(
        kernel,
        grid=(kv_heads, groups),
        in_specs=[pl.BlockSpec(memory_space=pltpu.SMEM), column, line, line, mine]
        + [key, value] * 2
        + [mine, pl.BlockSpec((1, rows, 1), lambda h, g: (h * groups + g, 0, 0))]
        + [pl.BlockSpec(memory_space=pl.ANY)] * len(after),
        out_specs=[mine, shared, shared, pl.BlockSpec((rows, 2 * HEAD_SIZE), lambda h, g: (0, h))],
        out_shape=[
            jax.ShapeDtypeStruct((rows, width), F32),
            near,
            near,
            jax.ShapeDtypeStruct((rows, kv.shape[1]), BF),
        ],
        scratch_shapes=[pltpu.VMEM((rows, 2 * HEAD_SIZE), F32)],
        compiler_params=pltpu.CompilerParams(vmem_limit_bytes=32 * 2**20),
    )(*inputs, *after)


def call(
    kernel,
    out,
    inputs,
    scalars=(),
    grid=(1,),
    in_specs=None,
    out_specs=None,
    scratch=(),
    vmem=20,
    after=(),
    alias=None,
    hbm=4 * 2**20,
):
    def whole(a):
        return pl.BlockSpec(a.shape, lambda *_: (0,) * len(a.shape))

    in_specs = [s or whole(a) for s, a in zip(in_specs or [None] * len(inputs), inputs)]
    out_specs = [s or whole(a) for s, a in zip(out_specs or [None] * len(out), out)]
    alias = alias or {}

    def held(a, least):
        if a.size * a.dtype.itemsize < least:
            return a
        return pltpu.with_memory_space_constraint(a, pltpu.HBM)

    inputs = [held(a, hbm) for a in inputs]
    after = [held(a, hbm) for a in alias.values()] + [held(a, 2**20) for a in after]
    first = len(scalars) + len(inputs)

    def run(*refs):
        kernel(*refs[:first], *refs[first + len(after) :])

    return pl.pallas_call(
        run,
        grid_spec=pltpu.PrefetchScalarGridSpec(
            num_scalar_prefetch=len(scalars),
            grid=grid,
            in_specs=in_specs + [pl.BlockSpec(memory_space=pl.ANY)] * len(after),
            out_specs=out_specs,
            scratch_shapes=list(scratch),
        ),
        out_shape=list(out),
        compiler_params=pltpu.CompilerParams(vmem_limit_bytes=vmem * 2**20),
        input_output_aliases={first + i: place for i, place in enumerate(alias)},
        cost_estimate=pl.CostEstimate(flops=0, bytes_accessed=0, transcendentals=0),
    )(*[s.astype(jnp.int32).reshape(1) for s in scalars], *inputs, *after)


def in_hbm(dims, dtype):
    return pltpu.HBM(tuple(dims), dtype)


def shape(dims, dtype):
    return jax.ShapeDtypeStruct(tuple(dims), dtype)


def blocked(dims, index):
    return pl.BlockSpec(dims, index)


COLUMNS = 512


def other(index, k):
    return lax.bitwise_xor(index, jnp.int32(k))


def partners(z, size):
    return lax.bitwise_xor(z, jnp.arange(size, dtype=jnp.int32))


def ahead(index, k, size):
    return lax.bitwise_and(index + jnp.int32(k), jnp.int32(size - 1))


def behind(index, k, size):
    return lax.bitwise_and(index + jnp.int32(size) - jnp.int32(k), jnp.int32(size - 1))


def out_rows(ref):
    cols, dp, rows, width = ref.shape
    size = 4
    if dp == size:
        return ref[...].reshape(cols * dp * rows, width)
    per = dp // size
    order = [(c, q * per + r) for c in range(cols) for r in range(per) for q in range(size)]
    return jnp.concatenate([ref[c, d] for c, d in order])


def assemble(pieces, z, rolled, direct, after=()):
    def place_of(z, k):
        return behind(z, k, len(pieces)) if direct else other(z, k)

    size, dp = lax.axis_size("row"), lax.axis_size("dp")
    rows, width = pieces[0].shape
    rest = width // dp
    block = rows // size
    if rest % 128:
        out = jnp.stack([p.reshape(rows, dp, rest) for p in pieces], axis=2)
        order = behind(z, jnp.arange(size), size) if direct else partners(z, size)
        out = jnp.take(out, order, axis=2).reshape(rows, -1)
        if rolled:
            out = jnp.concatenate(
                [
                    lax.dynamic_slice_in_dim(out, other(z, k) * block, block, 0)
                    for k in range(size)
                ]
            )
        return out

    def kernel(z, *refs):
        out = refs[-1]
        for k in range(size):
            piece = refs[k][...]
            for d in range(dp):
                place = pl.multiple_of((d * size + place_of(z[0], k)) * rest, rest)
                out[:, pl.ds(place, rest)] = piece[:, d * rest : (d + 1) * rest]

    def index(i, z):
        return (lax.bitwise_xor(z[0], jnp.int32(i)) if rolled else i, 0)

    return call(
        kernel,
        [shape((rows, size * width), pieces[0].dtype)],
        list(pieces),
        [z],
        (size,),
        [blocked((block, width), index)] * size,
        [blocked((block, size * width), lambda i, z: (i, 0))],
        after=after,
    )[0]


def take_apart(full, z, rolled, after=()):
    size, dp = lax.axis_size("row"), lax.axis_size("dp")
    rows, width = full.shape
    rest = width // (size * dp)
    block = rows // size
    if rest % 128:
        if rolled:
            full = jnp.concatenate(
                [
                    lax.dynamic_slice_in_dim(full, other(z, i) * block, block, 0)
                    for i in range(size)
                ]
            )
        split = full.reshape(rows, dp, size, rest)
        split = jnp.take(split, partners(z, size), axis=2)
        return [split[:, :, k].reshape(rows, dp * rest) for k in range(size)]

    def kernel(z, full, *outs):
        for k in range(size):
            for d in range(dp):
                place = pl.multiple_of((d * size + other(z[0], k)) * rest, rest)
                outs[k][:, d * rest : (d + 1) * rest] = full[:, pl.ds(place, rest)]

    def index(i, z):
        return (lax.bitwise_xor(z[0], jnp.int32(i)) if rolled else i, 0)

    return call(
        kernel,
        [shape((rows, dp * rest), full.dtype)] * size,
        [full],
        [z],
        (size,),
        [blocked((block, width), lambda i, z: (i, 0))],
        [blocked((block, dp * rest), index)] * size,
        after=after,
    )


def project_kernel(x, gain, weight, cosine, sine, head_gain, a, scale, qr, kr, qn, kv):
    rows = x.shape[0]
    heads = qr.shape[1] // HEAD_SIZE
    kv_heads = kr.shape[1] // HEAD_SIZE

    @pl.when(pl.program_id(0) == 0)
    def _():
        for first in range(0, rows, 128):
            s = slice(first, first + 128)
            xf = x[s, :].astype(F32)
            r = lax.rsqrt(jnp.mean(xf * xf, axis=1, keepdims=True) + EPS)
            a[s, :] = (xf * r * gain[...]).astype(BF)
            scale[s, :] = r

    raw = dot(a[...], weight[0].reshape(MODEL_WIDTH, COLUMNS))

    def turn(values, gains):
        normed = (
            values
            * lax.rsqrt(jnp.mean(values * values, axis=-1, keepdims=True) + EPS)
            * gains
        )
        half = HEAD_SIZE // 2
        turned = jnp.concatenate([-normed[:, half:], normed[:, :half]], axis=-1)
        return (normed * cosine[...] + turned * sine[...]).astype(BF)

    for h in range(heads):
        s = slice(h * HEAD_SIZE, (h + 1) * HEAD_SIZE)
        qr[:, s] = raw[:, s]
        qn[:, s] = turn(raw[:, s], head_gain[0:1, :])
    first = heads * HEAD_SIZE
    for h in range(kv_heads):
        s = slice(h * HEAD_SIZE, (h + 1) * HEAD_SIZE)
        values = raw[:, first + h * HEAD_SIZE : first + (h + 1) * HEAD_SIZE]
        kr[:, s] = values
        kv[:, s] = turn(values, head_gain[1:2, :])
    kv[:, kv_heads * HEAD_SIZE :] = raw[:, first + kv_heads * HEAD_SIZE :].astype(BF)


def project(x, gain, weight, cosine, sine, head_gain, head_width, kv_width, after):
    rows = x.shape[0]
    cols, dp, _, width = weight.shape
    q = blocked((rows, head_width), lambda c: (0, c))
    k = blocked((rows, kv_width), lambda c: (0, c))
    return call(
        project_kernel,
        [
            shape(x.shape, BF),
            shape((rows, 1), F32),
            shape((rows, cols * head_width), F32),
            shape((rows, cols * kv_width), F32),
            shape((rows, cols * head_width), BF),
            shape((rows, 2 * cols * kv_width), BF),
        ],
        [x, gain, weight, cosine, sine, head_gain],
        (),
        (cols,),
        [None, None, blocked((1, dp, MODEL_WIDTH // dp, width), lambda c: (c, 0, 0, 0)), None, None, None],
        [None, None, q, k, q, blocked((rows, 2 * kv_width), lambda c: (0, c))],
        after=after,
    )


def mixed_parts(mixed, weight, z, base, after):
    size = lax.axis_size("row")
    cols, dp, total_rows, _ = weight.shape
    rows = mixed.shape[0]
    inner = mixed.shape[1] // (cols * dp)
    part = rows // size
    steps = MODEL_WIDTH // COLUMNS

    def kernel(z, mixed, weight, *refs):
        *outs, total = refs
        total[...] = dot(mixed[...], out_rows(weight))
        for k in range(size):
            first = pl.multiple_of(other(z[0], k) * part, part)
            outs[k][...] = total[pl.ds(first, part), :].astype(outs[k].dtype)

    return call(
        kernel,
        [shape((part, MODEL_WIDTH), BF if k else F32) for k in range(size)],
        [mixed, weight],
        [z],
        (steps,),
        [None, blocked((cols, dp, inner, COLUMNS), lambda c, z: (0, 0, base + c, 0))],
        [blocked((part, COLUMNS), lambda c, z: (0, c))] * size,
        scratch=[pltpu.VMEM((rows, COLUMNS), F32)],
        after=after,
    )


def mixed_back(chunks, weight, z, base, inner, after):
    size = len(chunks)
    cols, dp, _, _ = weight.shape
    part, width = chunks[0].shape
    rows = size * part
    heads = cols * dp * inner
    steps = width // COLUMNS

    def kernel(z, *refs):
        *ins, weight, full, out, total = refs
        for k in range(size):
            first = pl.multiple_of(other(z[0], k) * part, part)
            full[pl.ds(first, part), :] = ins[k][...]
        term = dot(full[...], out_rows(weight), "nt")
        c = pl.program_id(0)

        @pl.when(c == 0)
        def _():
            total[...] = term

        @pl.when(c > 0)
        def _():
            total[...] += term

        @pl.when(c == steps - 1)
        def _():
            out[...] = total[...].astype(BF)

    return call(
        kernel,
        [shape((rows, width), BF), shape((rows, heads), BF)],
        list(chunks) + [weight],
        [z],
        (steps,),
        [blocked((part, COLUMNS), lambda c, z: (0, c))] * size
        + [blocked((cols, dp, inner, COLUMNS), lambda c, z: (0, 0, base + c, 0))],
        [blocked((rows, COLUMNS), lambda c, z: (0, c)), None],
        scratch=[pltpu.VMEM((rows, heads), F32)],
        after=after,
    )


def masked(values, valid, after):
    def kernel(values, valid, out):
        out[...] = jnp.where(valid[...] > 0, values[...], jnp.zeros_like(values))

    return call(kernel, [shape(values.shape, values.dtype)], [values, valid], after=after)[0]


def add_parts(parts, dtype, after=()):
    def kernel(*refs):
        total = refs[0][...].astype(F32)
        for ref in refs[1:-1]:
            total = total + ref[...].astype(F32)
        refs[-1][...] = total.astype(dtype)

    return call(kernel, [shape(parts[0].shape, dtype)], list(parts), after=after)[0]


def hidden_norm(parts, x, gain, z, after=()):
    rows, width = parts[0].shape

    def kernel(z, *refs):
        *ps, x, gain, h, scale, a = refs
        total = x[...].astype(F32)
        for p in ps:
            total = total + p[...].astype(F32)
        r = lax.rsqrt(jnp.mean(total * total, axis=1, keepdims=True) + EPS)
        h[...] = total
        scale[...] = r
        a[...] = (total * r * gain[...]).astype(BF)

    return call(
        kernel,
        [shape((rows, width), F32), shape((rows, 1), F32), shape((rows, width), BF)],
        list(parts) + [x, gain],
        [z],
        (1,),
        [None] * len(parts) + [blocked((rows, width), lambda i, z: (z[0], 0)), None],
        after=after,
    )


def gateup_chunk(parts, weight, grad, index, hidden, news):
    part, width = parts[0].shape
    rows = part * len(parts)
    cols, dp, _, _ = weight.shape
    steps = 2 * hidden // (cols * COLUMNS)
    half = COLUMNS // 2

    def kernel(*refs):
        *ins, weight, grad, act, out, a = refs

        @pl.when((pl.program_id(0) == 0) & (pl.program_id(1) == 0))
        def _():
            for i, ref in enumerate(ins):
                a[i * part : (i + 1) * part, :] = ref[...]

        p = dot(a[...], weight[0].reshape(width, COLUMNS))
        for j in range(half // 128):
            gate, up = p[:, j * 256 : j * 256 + 128], p[:, j * 256 + 128 : j * 256 + 256]
            s = slice(j * 128, (j + 1) * 128)
            spread = 1.0 / (1.0 + jnp.exp(-gate))
            silu = gate * spread
            act[:, s] = (silu * up).astype(BF)
            g = grad[:, s]
            out[:, j * 256 : j * 256 + 128] = (g * up * (spread + silu * (1.0 - spread))).astype(BF)
            out[:, j * 256 + 128 : j * 256 + 256] = (g * silu).astype(BF)

    def place(c, t):
        return (index, c * steps + t)

    total = grad.shape[0]
    return call(
        kernel,
        [shape((total, hidden), BF), shape((total, 2 * hidden), BF)],
        list(parts) + [weight, grad],
        (),
        (cols, steps),
        [None] * len(parts)
        + [
            blocked((1, dp, width // dp, COLUMNS), lambda c, t: (c, 0, t, 0)),
            blocked((rows, half), place),
        ],
        [blocked((rows, half), place), blocked((rows, COLUMNS), place)],
        scratch=[pltpu.VMEM((rows, width), BF)],
        alias=dict(enumerate(news or ())),
    )


def gateup_back(grad, weight, index, kinds):
    cols, dp, _, _ = weight.shape
    both = grad.shape[1]
    block = MODEL_WIDTH // dp
    terms = both // COLUMNS
    per = terms // cols
    part = grad.shape[0] // 4
    rows = part * len(kinds)

    def kernel(grad, weight, *outs):
        total = None
        for t in range(terms):
            right = weight[t // per, 0, (t % per) * block : (t % per + 1) * block, :]
            term = dot(grad[:, t * COLUMNS : (t + 1) * COLUMNS], right, "nt")
            total = term if total is None else total + term
        for i, (out, kind) in enumerate(zip(outs, kinds)):
            out[...] = total[i * part : (i + 1) * part, :].astype(kind)

    return call(
        kernel,
        [shape((part, MODEL_WIDTH), kind) for kind in kinds],
        [grad, weight],
        (),
        (dp,),
        [
            blocked((rows, both), lambda n: (index, 0)),
            blocked((cols, 1, per * block, COLUMNS), lambda n: (0, n, 0, 0)),
        ],
        [blocked((part, block), lambda n: (0, n))] * len(kinds),
    )


def down_back(out_low, weight, base, inner, after):
    cols, dp, _, _ = weight.shape
    rows, width = out_low.shape
    hidden = cols * dp * inner

    def kernel(low, weight, out):
        term = dot(low[...], out_rows(weight), "nt")

        @pl.when(pl.program_id(0) == 0)
        def _():
            out[...] = term

        @pl.when(pl.program_id(0) > 0)
        def _():
            out[...] += term

    return call(
        kernel,
        [shape((rows, hidden), F32)],
        [out_low, weight],
        (),
        (width // COLUMNS,),
        [
            blocked((rows, COLUMNS), lambda c: (0, c)),
            blocked((cols, dp, inner, COLUMNS), lambda c: (0, 0, base + c, 0)),
        ],
        [None],
        vmem=24,
        after=after,
    )[0]


def down_forward(active, hidden, weight, base, inner, after):
    cols, dp, _, _ = weight.shape
    rows, width = active.shape
    part = hidden.shape[0]

    def kernel(active, hidden, weight, out):
        p = dot(active[...], out_rows(weight))
        out[:part, :] = (p[:part, :] + hidden[...]).astype(BF)
        out[part:, :] = p[part:, :].astype(BF)

    return call(
        kernel,
        [shape((rows, MODEL_WIDTH), BF)],
        [active, hidden, weight],
        (),
        (MODEL_WIDTH // COLUMNS,),
        [
            None,
            blocked((part, COLUMNS), lambda c: (0, c)),
            blocked((cols, dp, inner, COLUMNS), lambda c: (0, 0, base + c, 0)),
        ],
        [blocked((rows, COLUMNS), lambda c: (0, c))],
        after=after,
    )[0]


def hidden_back(parts, h, scale, gain, out_low, after):
    rows, width = h.shape

    def kernel(*refs):
        *ps, h, scale, gain, dy, dh, low, gain_grad = refs
        grad = ps[0][...].astype(F32)
        for p in ps[1:]:
            grad = grad + p[...].astype(F32)
        hidden, r = h[...], scale[...]
        weighted = grad * gain[...]
        inner = jnp.sum(weighted * hidden, axis=1, keepdims=True)
        total = dy[...].astype(F32) + r * weighted - (r * r * r * inner / MODEL_WIDTH) * hidden
        dh[...] = total
        low[...] = total.astype(BF)
        gain_grad[...] = jnp.sum(grad * hidden * r, axis=0, keepdims=True)

    return call(
        kernel,
        [shape((rows, width), F32), shape((rows, width), BF), shape((1, width), F32)],
        list(parts) + [h, scale, gain, out_low],
        (),
        (1,),
        [None] * (len(parts) + 3) + [blocked((rows, width), lambda i: (0, 0))],
        after=after,
    )


def heads_back_kernel(
    qr, kr, dqn, dkn, dv, far, cosine, sine, head_gain, out, gain_grad
):
    heads = qr.shape[1] // HEAD_SIZE
    kv_heads = kr.shape[1] // HEAD_SIZE
    half = HEAD_SIZE // 2

    def back(raw, grad, gains):
        turned = grad * sine[...]
        turned = jnp.concatenate([turned[:, half:], -turned[:, :half]], axis=-1)
        g = grad * cosine[...] + turned
        r = lax.rsqrt(jnp.mean(raw * raw, axis=-1, keepdims=True) + EPS)
        weighted = g * gains
        inner = jnp.sum(weighted * raw, axis=-1, keepdims=True)
        low = (r * weighted - (r * r * r * inner / HEAD_SIZE) * raw).astype(BF)
        return low, jnp.sum(g * raw * r, axis=0, keepdims=True)

    @pl.when(pl.program_id(0) == 0)
    def _():
        gain_grad[...] = jnp.zeros_like(gain_grad)

    for h in range(heads):
        s = slice(h * HEAD_SIZE, (h + 1) * HEAD_SIZE)
        low, total = back(qr[:, s], dqn[:, s], head_gain[0:1, :])
        out[:, s] = low
        gain_grad[0:1, :] += total
    first = heads * HEAD_SIZE
    for h in range(kv_heads):
        s = slice(h * HEAD_SIZE, (h + 1) * HEAD_SIZE)
        low, total = back(kr[:, s], dkn[:, s] + far[:, s].astype(F32), head_gain[1:2, :])
        out[:, first + h * HEAD_SIZE : first + (h + 1) * HEAD_SIZE] = low
        gain_grad[1:2, :] += total
    first += kv_heads * HEAD_SIZE
    out[:, first:] = (dv[...] + far[:, kv_heads * HEAD_SIZE :].astype(F32)).astype(BF)


def heads_back(qr, kr, dqn, dkn, dv, far, cosine, sine, head_gain, cols, after):
    rows = qr.shape[0]
    head_width, kv_width = qr.shape[1] // cols, kr.shape[1] // cols
    q = blocked((rows, head_width), lambda c: (0, c))
    k = blocked((rows, kv_width), lambda c: (0, c))
    far_kv = blocked((rows, 2 * kv_width), lambda c: (0, c))
    width = head_width + 2 * kv_width
    return call(
        heads_back_kernel,
        [shape((rows, cols * width), BF), shape((2, HEAD_SIZE), F32)],
        [qr, kr, dqn, dkn, dv, far, cosine, sine, head_gain],
        (),
        (cols,),
        [q, k, q, k, k, far_kv, None, None, None],
        [blocked((rows, width), lambda c: (0, c)), None],
        after=after,
    )


def input_back(grads, weight, x, scale, gain, dh, z, after):
    cols, steps, _, width = weight.shape
    rows = grads.shape[0]
    model = MODEL_WIDTH
    part = dh.shape[0]

    def kernel(z, grads, weight, x, scale, gain, dh, out, c1, gain_grad):
        total = dot(grads[:, :width], weight[0, 0], "nt")
        for c in range(1, cols):
            total = total + dot(grads[:, c * width : (c + 1) * width], weight[c, 0], "nt")
        r = scale[...]
        xf = x[...].astype(F32)
        weighted = total * gain[...]
        moved = weighted * xf
        gain_grad[...] = jnp.sum(total * xf * r, axis=0, keepdims=True)
        out[...] = (r * weighted).astype(BF)
        first = pl.multiple_of(z[0] * part, part)
        own = pl.ds(first, part)
        out[own, :] = (out[own, :].astype(F32) + dh[...]).astype(BF)

        @pl.when(pl.program_id(0) == 0)
        def _():
            c1[...] = jnp.zeros_like(c1)

        c1[...] += jnp.sum(moved, axis=1, keepdims=True)

    block = model // steps
    wide = blocked((rows, block), lambda n, z: (0, n))
    return call(
        kernel,
        [shape((rows, model), BF), shape((rows, 1), F32), shape((1, model), F32)],
        [grads, weight, x, scale, gain, dh],
        [z],
        (steps,),
        [
            None,
            blocked((cols, 1, block, width), lambda n, z: (0, n, 0, 0)),
            wide,
            None,
            blocked((1, block), lambda n, z: (0, n)),
            blocked((part, block), lambda n, z: (0, n)),
        ],
        [wide, None, blocked((1, block), lambda n, z: (0, n))],
        after=after,
    )


def weight_grads(lefts, right, out_left, out_right, cols, after=()):
    size, dp = lax.axis_size("row"), lax.axis_size("dp")
    rows = right.shape[0]
    block = MODEL_WIDTH // dp
    n = right.shape[1] // cols
    part = rows // len(lefts)
    m = out_left.shape[1] // cols
    inner = m // dp
    terms = n // COLUMNS
    total = terms * block + MODEL_WIDTH // COLUMNS * inner

    def kernel(*refs):
        *ins, right, out_left, out_right, out = refs
        left = jnp.concatenate([ref[...] for ref in ins]) if len(ins) > 1 else ins[0][...]
        for t in range(terms):
            term = dot(left, right[:, t * COLUMNS : (t + 1) * COLUMNS], "tn")
            out[0, 0, t * block : (t + 1) * block, :] = term.astype(BF)
        for d in range(dp):
            q, r = d // (dp // size), d % (dp // size)
            first = (r * size + q) * inner

            @pl.when(pl.program_id(1) == d)
            def _():
                term = dot(out_left[:, first : first + inner], out_right[...], "tn").astype(BF)
                for c in range(MODEL_WIDTH // COLUMNS):
                    place = terms * block + c * inner
                    piece = term[:, c * COLUMNS : (c + 1) * COLUMNS]
                    out[0, 0, place : place + inner, :] = piece

    return call(
        kernel,
        [in_hbm((cols, dp, total, COLUMNS), BF)],
        list(lefts) + [right, out_left, out_right],
        (),
        (cols, dp),
        [blocked((part, block), lambda c, d: (0, d))] * len(lefts)
        + [
            blocked((rows, n), lambda c, d: (0, c)),
            blocked((rows, m), lambda c, d: (0, c)),
            None,
        ],
        [blocked((1, 1, total, COLUMNS), lambda c, d: (c, d, 0, 0))],
        after=after,
        vmem=28,
    )[0]


def swap(value, axis, step):
    return lax.ppermute(value, axis, [(i, i ^ step) for i in range(lax.axis_size(axis))])


def gather_pieces(own, beside=None):
    two = swap(own, "row", 2)
    if beside is not None:
        two, beside = lax.optimization_barrier((two, beside))
    pieces = [own, swap(own, "row", 1), two, swap(two, "row", 1)]
    return pieces if beside is None else (pieces, beside)


def gather_direct(own):
    return along_row([own] * lax.axis_size("row"), True)


def scatter_pieces(pieces):
    sent = add_parts([pieces[2], swap(pieces[3], "row", 1)], BF)
    direct, sent = lax.optimization_barrier((pieces[1], sent))
    return [pieces[0], swap(direct, "row", 1), swap(sent, "row", 2)], sent


def add_along(value, axes):
    for axis in axes:
        step = 1
        while step < lax.axis_size(axis):
            value = value + swap(value, axis, step)
            step *= 2
    return value


def along_row(pieces, forward):
    size = len(pieces)
    sign = 1 if forward else -1
    return [pieces[0]] + [
        lax.ppermute(p, "row", [(i, (i + sign * k) % size) for i in range(size)])
        for k, p in enumerate(pieces)
        if k
    ]


def along_quarters(pieces, forward):
    size = len(pieces)
    per = lax.axis_size("dp") // size
    sign = 1 if forward else -1

    def pairs(k):
        places = [(q, r) for q in range(size) for r in range(per)]
        return [(q * per + r, (q + sign * k) % size * per + r) for q, r in places]

    return [pieces[0]] + [lax.ppermute(p, "dp", pairs(k)) for k, p in enumerate(pieces) if k]


def gather_shard(shard):
    full = lax.all_gather(shard, ("col", "dp"), axis=0)
    return full.reshape(lax.axis_size("col"), lax.axis_size("dp"), *shard.shape)


def scatter_shard(full):
    flat_rows = full.reshape(-1, full.shape[-1])
    return lax.psum_scatter(flat_rows, ("col", "dp"), scatter_dimension=0, tiled=True)


def quarter_index():
    return lax.axis_index("dp") // (lax.axis_size("dp") // lax.axis_size("row"))


def pack_attention(query, keyval, z):
    size = lax.axis_size("row")
    rows = query.shape[0]
    hw, kw = query.shape[1] // size, keyval.shape[2] // size

    def kernel(z, query, keyval, *outs):
        for k in range(size):
            at = ahead(z[0], k, size)
            out = outs[k]
            out[:, :hw] = query[:, pl.ds(pl.multiple_of(at * hw, hw), hw)].astype(BF)
            for s in range(2):
                part = keyval[:, s, pl.ds(pl.multiple_of(at * kw, kw), kw)]
                out[:, hw + s * kw : hw + (s + 1) * kw] = part.astype(BF)

    return call(kernel, [shape((rows, hw + 2 * kw), BF)] * size, [query, keyval], [z], hbm=0)


def pack_feed(gateup, downs, z, after):
    size = lax.axis_size("row")
    rows = gateup.shape[0]
    fw = gateup.shape[2] // size
    terms = 2 * fw // COLUMNS
    inner = downs[0].shape[0]

    def kernel(z, gateup, *refs):
        for k in range(size):
            at = ahead(z[0], k, size)
            out = refs[size + k]
            for s in range(2):
                for j in range(fw // 128):
                    first = pl.multiple_of(at * fw + j * 128, 128)
                    place = (2 * j + s) * 128
                    t, lane = place // COLUMNS, place % COLUMNS
                    part = gateup[:, s, pl.ds(first, 128)].astype(BF)
                    out[t * rows : (t + 1) * rows, lane : lane + 128] = part
            out[terms * rows :, :] = refs[k][...]

    return call(
        kernel,
        [shape((terms * rows + inner, COLUMNS), BF)] * size,
        [gateup, *downs],
        [z],
        after=after,
        vmem=32,
    )


def pack_out(blocks, after=()):
    size = lax.axis_size("row")
    rows = [b.shape[0] // size for b in blocks]

    def kernel(q, *refs):
        for k in range(size):
            place = 0
            for ref, n in zip(refs, rows):
                first = pl.multiple_of(ahead(q[0], k, size) * n, n)
                refs[len(rows) + k][place : place + n, :] = ref[pl.ds(first, n), :].astype(BF)
                place += n

    return call(
        kernel,
        [shape((sum(rows), blocks[0].shape[1]), BF)] * size,
        blocks,
        [quarter_index()],
        after=after,
        hbm=0,
    )


def regroup(parts, source, target, cuts, after=()):
    size = len(parts)
    sources = [source(k) for k in range(size)]
    targets = [target(k) for k in range(size)]
    starts = [sum(cuts[:i]) for i in range(len(cuts))]

    def kernel(*refs):
        places, ins = refs[: 2 * size], refs[2 * size : 3 * size]
        outs, held = refs[3 * size : -1], refs[-1]
        for k in range(size):
            held[places[k][0]] = ins[k][...]
        for i, (first, n) in enumerate(zip(starts, cuts)):
            for k in range(size):
                outs[i * size + k][...] = held[places[size + k][0], first : first + n]

    rows, width = parts[0].shape
    outs = call(
        kernel,
        [shape((n, width), BF) for n in cuts for _ in range(size)],
        parts,
        sources + targets,
        scratch=[pltpu.VMEM((size, rows, width), BF)],
        after=after,
    )
    return [outs[i * size : (i + 1) * size] for i in range(len(cuts))]


def make_shard(in_parts, out_parts, z, after=()):
    size, dp = len(in_parts), lax.axis_size("dp")
    rest = MODEL_WIDTH // (size * dp)
    steps = MODEL_WIDTH // COLUMNS
    rows = MODEL_WIDTH // (size * dp)
    if isinstance(out_parts, int):
        inner, joined = out_parts, True
        terms = (in_parts[0].shape[0] - inner) // rows
    else:
        inner, joined = out_parts[0].shape[0], False
        terms = in_parts[0].shape[0] // rows
    base = terms * size * rows
    if rest % 128:
        order = behind(z, jnp.arange(size), size)
        if joined:
            out_parts = [p[terms * rows :] for p in in_parts]
            in_parts = [p[: terms * rows] for p in in_parts]
        full = jnp.take(jnp.stack(in_parts), order, axis=0).reshape(size, terms, rows, COLUMNS)
        ins = full.transpose(1, 0, 2, 3).reshape(base, COLUMNS)
        full = jnp.stack([p.reshape(inner, dp, rest) for p in out_parts], axis=2)
        full = jnp.take(full, order, axis=2).reshape(inner, steps, COLUMNS)
        return jnp.concatenate([ins, full.transpose(1, 0, 2).reshape(-1, COLUMNS)])

    def kernel(z, *refs):
        out = refs[-1]
        for k in range(size):
            at = behind(z[0], k, size)
            for t in range(terms):
                first = pl.multiple_of((t * size + at) * rows, rows)
                out[pl.ds(first, rows), :] = refs[k][t * rows : (t + 1) * rows, :]
            place = pl.multiple_of(at * rest, rest)
            ref = refs[k] if joined else refs[size + k]
            top = terms * rows if joined else 0
            for d in range(dp):
                first = base + d * inner
                part = ref[top : top + inner, d * rest : (d + 1) * rest]
                out[first : first + inner, pl.ds(place, rest)] = part

    parts = list(in_parts) if joined else list(in_parts) + list(out_parts)
    out = shape((base + steps * inner, COLUMNS), BF)
    return call(kernel, [out], parts, [z], after=after)[0]


def split_shard(shard, terms, rows, inner, z, after=()):
    size, dp = lax.axis_size("row"), lax.axis_size("dp")
    rest = MODEL_WIDTH // (size * dp)
    steps = MODEL_WIDTH // COLUMNS
    base = terms * size * rows
    if rest % 128:
        ins = shard[:base].reshape(terms, size, rows, COLUMNS).transpose(1, 0, 2, 3)
        ins = jnp.take(ins, behind(z, jnp.arange(size), size), axis=0)
        outs = shard[base:].reshape(steps, inner, COLUMNS).transpose(1, 0, 2)
        outs = outs.reshape(inner, dp, size, rest)
        outs = jnp.take(outs, behind(z, jnp.arange(size), size), axis=2)
        return [
            jnp.concatenate([ins[k].reshape(-1, COLUMNS), outs[:, :, k].reshape(inner, COLUMNS)])
            for k in range(size)
        ]

    def kernel(z, full, *outs):
        for k in range(size):
            at = behind(z[0], k, size)
            for t in range(terms):
                first = pl.multiple_of((t * size + at) * rows, rows)
                outs[k][t * rows : (t + 1) * rows, :] = full[pl.ds(first, rows), :]
            place = pl.multiple_of(at * rest, rest)
            for d in range(dp):
                part = full[base + d * inner : base + (d + 1) * inner, pl.ds(place, rest)]
                outs[k][terms * rows :, d * rest : (d + 1) * rest] = part

    return call(
        kernel,
        [shape((terms * rows + inner, COLUMNS), BF)] * size,
        [shard],
        [z],
        after=after,
    )


def out_pieces(messages, inner, z):
    size = len(messages)
    quarter = quarter_index()
    parts = regroup(
        [m[-inner:] for m in messages],
        lambda k: ahead(z, k, size),
        lambda k: ahead(quarter, k, size),
        [inner],
    )[0]
    return along_quarters(parts, True)


def update(refs, grad, rate):
    weight, moment, second, weight_new, moment_new, second_new = refs
    m, v, w = adamw(weight[...], moment[...], second[...], grad, rate, DECAY)
    moment_new[...] = m
    second_new[...] = v
    weight_new[...] = w


def update_out(state, pieces, rate):
    size = len(pieces)
    rows, width = pieces[0].shape

    def kernel(q, *refs):
        k = pl.program_id(0)
        for i in range(size):

            @pl.when(k == i)
            def _():
                update(refs[size:], refs[i][...].astype(F32), rate)

    spec = blocked((rows, width), lambda k, q: (lax.bitwise_and(q[0] + size - k, size - 1), 0))
    w, m, v = call(
        kernel,
        [shape(state[0].shape, F32)] * 3,
        list(pieces) + list(state),
        [quarter_index()],
        (size,),
        [None] * size + [spec] * 3,
        [spec] * 3,
        hbm=2**19,
    )
    return m, v, w


def place_columns(messages, rows, cuts, z):
    size = len(messages)

    def kernel(z, *refs):
        for out, cut in zip(refs[size:], cuts):
            width = sum(w for _, _, w in cut)
            for k in range(size):
                at = ahead(z[0], k, size) * width
                for t, first, w in cut:
                    place = pl.multiple_of(at, 128)
                    part = refs[k][t * rows : (t + 1) * rows, first : first + w]
                    out[:, pl.ds(place, w)] = part
                    at = at + w

    out = [shape((rows, size * sum(w for _, _, w in cut)), BF) for cut in cuts]
    return call(kernel, out, messages, [z])


def flat(values):
    rows, two, width = values.shape
    return values.reshape(rows, two, width // 128, 128).transpose(0, 2, 1, 3).reshape(-1, 128)


def update_pair(state, grad, rate):
    rows, two, width = state[0].shape
    total = rows * two * width // 128
    steps = 4 if total % 64 == 0 else 1

    def kernel(grad, *refs):
        update(refs, grad[...].astype(F32), rate)

    spec = blocked((total // steps, 128), lambda i: (i, 0))
    news = call(
        kernel,
        [shape((total, 128), F32)] * 3,
        [grad.reshape(-1, 128)] + [flat(s) for s in state],
        (),
        (steps,),
        [spec] * 4,
        [spec] * 3,
        hbm=2**19,
    )
    w, m, v = [
        n.reshape(rows, width // 128, two, 128).transpose(0, 2, 1, 3).reshape(rows, two, width)
        for n in news
    ]
    return (m, v, w), news[0]


def adamw(weight, moment, second, grad, rate, decay):
    moment_new = BETA_ONE * moment + (1.0 - BETA_ONE) * grad
    second_new = BETA_TWO * second + (1.0 - BETA_TWO) * grad * grad
    first_hat = moment_new / (1.0 - BETA_ONE**STEP)
    second_hat = second_new / (1.0 - BETA_TWO**STEP)
    weight_new = weight - rate * (first_hat / (jnp.sqrt(second_hat) + ADAM_EPS) + decay * weight)
    return (moment_new, second_new, weight_new)


def body(
    tokens,
    cotangent,
    seq_lens,
    query_weight,
    query_moment,
    query_second,
    key_value_master_weight,
    key_value_first_moment,
    key_value_second_moment,
    output_weight,
    output_moment,
    output_second,
    gateup_weight,
    gateup_moment,
    gateup_second,
    down_weight,
    down_moment,
    down_second,
    norm_gains,
    norm_moment,
    norm_second,
    head_gains,
    head_moment,
    head_second,
):
    size, dp, cols = lax.axis_size("row"), lax.axis_size("dp"), lax.axis_size("col")
    z, y = lax.axis_index("row"), lax.axis_index("col")
    rows = tokens.shape[0]
    quarter = rows // size
    item_count = rows * cols
    rest = MODEL_WIDTH // (size * dp)
    head_width = query_weight.shape[1] // size
    kv_width = key_value_master_weight.shape[2] // size

    gains = norm_gains.reshape(2, size, dp, rest).transpose(0, 2, 1, 3).reshape(2, MODEL_WIDTH)
    first_gain, second_gain = gains[0:1], gains[1:2]

    segment, position = token_layout(seq_lens[0], item_count)
    first = y * rows
    own_segment = lax.dynamic_slice_in_dim(segment, first, rows, 0)
    cosine, sine = rope_tables(lax.dynamic_slice_in_dim(position, first, rows, 0))
    valid = (own_segment < SEQS).astype(jnp.int32)[:, None]

    hidden_width = gateup_weight.shape[2] // size * cols

    in_rows = query_weight.shape[0]
    output_inner, down_inner = output_weight.shape[0] // size, down_weight.shape[0] // size
    gateup_terms = 2 * hidden_width // (cols * COLUMNS)
    steps = MODEL_WIDTH // COLUMNS
    down_base = gateup_terms * size * in_rows // down_inner
    output_base = size * in_rows // output_inner
    quarter_place = quarter_index()
    input_chunks = gather_pieces(tokens)
    attention_pieces = pack_attention(query_weight, key_value_master_weight, z)
    out_pieces_sent = pack_out([down_weight, output_weight], attention_pieces[:1])
    down_parts, output_parts = regroup(
        along_quarters(out_pieces_sent, True),
        lambda k: behind(quarter_place, k, size),
        lambda k: ahead(z, k, size),
        [down_inner, output_inner],
    )
    feed_pieces = pack_feed(gateup_weight, down_parts, z, output_parts[:1])
    attention_shard = make_shard(
        along_row(attention_pieces, True),
        along_row(output_parts, True),
        z,
        [feed_pieces[0], input_chunks[2]],
    )
    attention_full = gather_shard(attention_shard)
    inputs = assemble(input_chunks, z, False, False, [attention_shard])
    feed_shard = make_shard(along_row(feed_pieces, True), down_inner, z, [inputs])
    feed_full = gather_shard(feed_shard)
    out_own = masked(cotangent, valid, [feed_shard])
    out_chunks = gather_pieces(out_own)

    first_low, first_scale, query_raw, key_raw, query, keys_values = project(
        inputs,
        first_gain,
        attention_full,
        cosine,
        sine,
        head_gains,
        head_width,
        kv_width,
        [out_own],
    )
    before = lax.ppermute(keys_values, "col", [(i, i + 1) for i in range(cols - 1)])
    masks = (
        y.astype(jnp.int32).reshape(1),
        own_segment.reshape(rows, 1),
        own_segment.reshape(1, rows),
        segment[:rows].reshape(1, rows),
    )
    mixed, logsum = attention_forward(*masks, query, keys_values, before, [])
    out_low = assemble(out_chunks, z, True, False, [mixed])
    hidden_pieces = mixed_parts(mixed, attention_full, z, output_base, [out_low])
    hidden_parts, _ = scatter_pieces(hidden_pieces)
    hidden, second_scale, second_low = hidden_norm(hidden_parts, inputs, second_gain, z)

    second_chunks = gather_pieces(second_low)
    active_grad = down_back(out_low, feed_full, down_base, down_inner, second_chunks[3:])
    far_news = gateup_chunk(second_chunks[2:], feed_full, active_grad, 1, hidden_width, None)
    far_parts = gateup_back(far_news[1], feed_full, 1, (BF, BF))
    active, pair_grad = gateup_chunk(
        second_chunks[:2], feed_full, active_grad, 0, hidden_width, far_news
    )
    near_parts = gateup_back(pair_grad, feed_full, 0, (F32, BF))
    second_parts, sent = scatter_pieces(near_parts + far_parts)
    feed_grads = weight_grads(
        second_chunks, pair_grad, active, out_low, cols, [sent, *near_parts]
    )
    feed_grads, second_parts[1], second_parts[2] = lax.optimization_barrier(
        (feed_grads, second_parts[1], second_parts[2])
    )
    feed_total = scatter_shard(feed_grads)
    hidden_grad, hidden_low, second_gain_grad = hidden_back(
        second_parts, hidden, second_scale, second_gain, out_low, [feed_grads]
    )

    layer_part = down_forward(active, hidden, feed_full, down_base, down_inner, [hidden_low])
    hidden_all, mixed_grad = mixed_back(
        gather_pieces(hidden_low), attention_full, z, output_base, output_inner, [layer_part]
    )
    layer_pieces = take_apart(layer_part, z, True, [hidden_all])
    query_grad, key_grad, value_grad, far_sent = attention_backward(
        *masks, query, keys_values, before, mixed_grad, logsum, layer_pieces[:1]
    )
    far = lax.ppermute(far_sent, "col", [(i + 1, i) for i in range(cols - 1)])
    layer_parts, _ = scatter_pieces(layer_pieces)
    layer_output = add_parts(layer_parts, F32)
    raw_grad, head_part = heads_back(
        query_raw,
        key_raw,
        query_grad,
        key_grad,
        value_grad,
        far,
        cosine,
        sine,
        head_gains,
        cols,
        [layer_output],
    )
    attention_grads = weight_grads([first_low], raw_grad, mixed, hidden_all, cols)
    input_part, inner_part, first_gain_grad = input_back(
        raw_grad,
        attention_full,
        inputs,
        first_scale,
        first_gain,
        hidden_grad,
        z,
        [attention_grads],
    )
    input_pieces = take_apart(input_part, z, False)
    input_parts, _ = scatter_pieces(input_pieces)
    norm_part = jnp.concatenate([first_gain_grad, second_gain_grad])
    norm_part = norm_part.reshape(2, dp, size, rest).transpose(0, 2, 1, 3).reshape(2, MODEL_WIDTH)
    small = jnp.concatenate([norm_part.reshape(-1), head_part.reshape(-1), inner_part.reshape(-1)])
    small, input_parts[0] = lax.optimization_barrier((small, input_parts[0]))
    small = add_along(small.reshape(-1, 128), ("row",)).reshape(-1)
    gain_count = norm_part.size + head_part.size
    inner = small[gain_count:][:, None]
    gain_total = add_along(small[:gain_count].reshape(-1, 128), ("dp", "col")).reshape(-1)
    attention_grads, feed_total, input_parts[1], input_parts[2], gain_total = (
        lax.optimization_barrier(
            (attention_grads, feed_total, input_parts[1], input_parts[2], gain_total)
        )
    )
    norm_total = gain_total[: norm_part.size].reshape(norm_part.shape)
    head_total = gain_total[norm_part.size :].reshape(head_part.shape)
    attention_total = scatter_shard(attention_grads)

    feed_messages = along_row(
        split_shard(feed_total, gateup_terms, in_rows, down_inner, z), False
    )
    down_new = update_out(
        (down_weight, down_moment, down_second),
        out_pieces(feed_messages, down_inner, z),
        RATES[4],
    )
    cut = [(t, 0, COLUMNS) for t in range(gateup_terms)]
    (gateup_total,) = place_columns(feed_messages, in_rows, [cut], z)
    gateup_new, gateup_flat = update_pair(
        (gateup_weight, gateup_moment, gateup_second), gateup_total, RATES[3]
    )
    input_grad = add_parts(input_parts, F32) - (
        first_scale * first_scale * first_scale * inner / MODEL_WIDTH
    ) * tokens.astype(F32)
    attention_messages = along_row(
        split_shard(attention_total, 1, in_rows, output_inner, z, [gateup_flat]), False
    )
    output_new = update_out(
        (output_weight, output_moment, output_second),
        out_pieces(attention_messages, output_inner, z),
        RATES[2],
    )
    query_total, keyval_total = place_columns(
        attention_messages,
        in_rows,
        [[(0, 0, head_width)], [(0, head_width, 2 * kv_width)]],
        z,
    )
    query_new = adamw(
        query_weight, query_moment, query_second, query_total.astype(F32), RATES[0], DECAY
    )
    keyval_new, _ = update_pair(
        (key_value_master_weight, key_value_first_moment, key_value_second_moment),
        keyval_total,
        RATES[1],
    )
    norm_new = adamw(norm_gains, norm_moment, norm_second, norm_total, GAIN_RATE, 0.0)
    head_new = adamw(head_gains, head_moment, head_second, head_total, GAIN_RATE, 0.0)
    return (
        layer_output,
        input_grad,
        *query_new,
        *keyval_new,
        *output_new,
        *gateup_new,
        *down_new,
        *norm_new,
        *head_new,
    )


def solution(mesh):
    items = P(("dp", "col"), "row")
    inward = P(("row", "dp"), "col")
    inward_pair = P(("row", "dp"), None, "col")
    outward = P(("col", "dp"), "row")
    weights = (
        (inward,) * 3 + (inward_pair,) * 3 + (outward,) * 3 + (inward_pair,) * 3 + (outward,) * 3
    )
    return jax.shard_map(
        body,
        mesh=mesh,
        in_specs=(items, items, P("dp", None)) + weights + (P(),) * 6,
        out_specs=(items, items) + weights + (P(),) * 6,
        check_vma=False,
    )
```

time: 2380 us -> 592 us (0.25)
  waiting for transfers between devices: 1980 us -> 270 us
  Pallas kernels: 0 us -> 162 us
  matrix products: 125 us -> 0 us
  blocking collectives: 86.2 us -> 0 us
  starting transfers between devices: 1.82 us -> 87.2 us
  other arithmetic: 83.3 us -> 6.67 us
  local copies, waits for them, and re-layouts: 72.9 us -> 43.2 us
    reduce_scatter x13 -> x2, waiting for transfers between devices: 1100 us -> 0.02 us  [scatter_shard(): lax.psum_scatter(flat_rows, ('col', 'dp'), scatter_dimension=0, tiled=True)]
    all_gather x15 -> x2, waiting for transfers between devices: 647 us -> 0.02 us  [gather_shard(): full = lax.all_gather(shard, ('col', 'dp'), axis=0)]
    ppermute x0 -> x55, waiting for transfers between devices: none -> 269 us  [the longest x29 179 us: swap(): lax.ppermute(value, axis, [(i, i ^ step) for i in range(lax.axis_size(axi...]
    unnamed x30 -> x4, waiting for transfers between devices: 239 us -> 0.07 us
    pallas_call x0 -> x44, Pallas kernels: none -> 162 us  [the longest x42 145 us: call(): pl.pallas_call(run, grid_spec=pltpu.PrefetchScalarGridSpec(num_scalar_pre...]
    dot_general x21 -> x0, matrix products: 125 us -> none  [the longest x8 70.1 us: term(): lax.dot_general(full, matrix, numbers, preferred_element_type=jnp.float32)]
    ppermute x0 -> x55, starting transfers between devices: none -> 86.8 us  [the longest x29 43.9 us: swap(): lax.ppermute(value, axis, [(i, i ^ step) for i in range(lax.axis_size(axi...]
    psum x5 -> x0, blocking collectives: 86.2 us -> none  [the longest x4 48.5 us: row_total(): return lax.psum(values, 'row')]
  transfers between devices with their start and end apart: 29 -> 59, of which waited for: 28 -> 25; matrix products, arithmetic and copies ran while one was open for 7% -> 2% of each run, Pallas kernels for 0% -> 27%
where the time goes in v1:
time: 592 us; the launch traced here: 584 us
  waiting for transfers between devices  270 us (46%)
  Pallas kernels  162 us (27%)
  starting transfers between devices  87.2 us (15%)
  local copies, waits for them, and re-layouts  43.2 us (7%)
  between operations  15.3 us (3%)
  other arithmetic  6.67 us (1%)
    ppermute x29, waiting for transfers between devices, swap(): lax.ppermute(value, axis, [(i, i ^ step) for i in range(lax.axis_size(axi...  179 us
    pallas_call x42, Pallas kernels, call(): pl.pallas_call(run, grid_spec=pltpu.PrefetchScalarGridSpec(num_scalar_pre...  145 us
    ppermute x15, waiting for transfers between devices, along_row(): lax.ppermute(p, 'row', [(i, (i + sign * k) % size) for i in range(size)])  61 us
    ppermute x29, starting transfers between devices, swap(): lax.ppermute(value, axis, [(i, i ^ step) for i in range(lax.axis_size(axi...  43.9 us
    unnamed x166, local copies, waits for them, and re-layouts  40.2 us
    ppermute x15, starting transfers between devices, along_row(): lax.ppermute(p, 'row', [(i, (i + sign * k) % size) for i in range(size)])  29.2 us
    ppermute x1, waiting for transfers between devices, body(): lax.ppermute(keys_values, 'col', [(i, i + 1) for i in range(cols - 1)])  15.1 us
  transfers between devices with their start and end apart: 59, of which 25 were waited for; matrix products, arithmetic and copies ran while one was open for 2% of the time, Pallas kernels for 27%

profile of v1, /device:TPU:0, one launch (start us, length us, event | category | flops | bytes accessed | tf_op | source)
XLA Modules:
  0.0 583.5 jit_solution(4506404285151602653)
XLA Ops:
  7.2 4.1 collective-permute-start.1
  11.3 2.4 shard_map.407
  13.8 2.3 shard_map.408
  20.6 3.5 collective-permute-done.6.refs_9_
  25.9 3.5 collective-permute-start.5
  32.8 3.6 collective-permute-start.11
  36.4 9.1 %collective-permute-done.4.refs_3_ = bf16[128,512]{1,0:T(8,128)(2,1)} collective-permute-done((bf16[128,512]{1,0:T(8,128)(2,1)}, bf16[128,512]{1,0:T(8,128)(2,1)}, u32[]{:S(2)}, u32[]{:S(2)}) %collective-permute-start.4) | collective-permute-done | bytes 131104 | tf_op jit(solution)/shard_map/ppermute | solution.py:876
  45.5 4.2 collective-permute-start.9
  49.7 3.1 shard_map.410
  55.3 2.1 shard_map.411.refs_5_
  58.5 3.4 collective-permute-start.13
  61.9 2.8 collective-permute-start.14
  64.7 2.0 collective-permute-start.2
  66.8 44.9 %collective-permute-done.refs_2_ = bf16[512,512]{1,0:T(8,128)(2,1)S(1)} collective-permute-done((bf16[512,512]{1,0:T(8,128)(2,1)S(1)}, bf16[512,512]{1,0:T(8,128)(2,1)S(1)}, u32[]{:S(2)}, u32[]{:S(2)}) %collective-permute-start) | collective-permute-done | bytes 524320 | tf_op jit(solution)/shard_map/ppermute | solution.py:842
  111.6 11.1 %collective-permute-done.2.refs_4_ = bf16[512,512]{1,0:T(8,128)(2,1)S(1)} collective-permute-done((bf16[512,512]{1,0:T(8,128)(2,1)}, bf16[512,512]{1,0:T(8,128)(2,1)S(1)}, u32[]{:S(2)}, u32[]{:S(2)}) %collective-permute-start.2) | collective-permute-done | bytes 524320 | tf_op jit(solution)/shard_map/ppermute | solution.py:842
  122.8 2.2 shard_map.412.refs_5_.refs_0_.refs_4_.refs_3_
  133.7 7.8 %shard_map.415 = (bf16[512,2048]{1,0:T(8,128)(2,1)S(1)}, f32[512,1]{1,0:T(8,128)S(1)}, f32[512,512]{1,0:T(8,128)S(1)}, f32[512,256]{1,0:T(8,128)S(1)}, bf16[512,...) custom-call(bf16[512,2048]{1,0:T(8,128)(2,1)S(1)} %copy-done.3, f32[1,2048]{1,0:T(1,128)S(1)} %bitcast.113, ...), custom_call_target="tpu_custom_call" | custom-call | tf_op jit(solution)/shard_map/pallas_call | solution.py:215
  146.1 3.6 collective-permute-start.15
  151.0 6.1 %collective-permute-done.17.refs_3_ = bf16[512,512]{1,0:T(8,128)(2,1)} collective-permute-done((bf16[512,512]{1,0:T(8,128)(2,1)}, bf16[512,512]{1,0:T(8,128)(2,1)}, u32[]{:S(2)}, u32[]{:S(2)}) %collective-permute-start.17) | collective-permute-done | bytes 524320 | tf_op jit(solution)/shard_map/ppermute | solution.py:842
  157.3 15.1 %collective-permute-done.15.refs_7_.refs_8_ = bf16[512,512]{1,0:T(8,128)(2,1)S(1)} collective-permute-done((bf16[512,512]{1,0:T(8,128)(2,1)S(1)}, bf16[512,512]{1,0:T(8,128)(2,1)S(1)}, u32[]{:S(2)}, u32[]{:S(2)}) %collective-permute-start.15) | collective-permute-done | bytes 524320 | tf_op jit(solution)/shard_map/ppermute | solution.py:1274
  173.5 7.3 %shard_map.416 = (bf16[512,512]{1,0:T(8,128)(2,1)S(1)}, f32[4,512,1]{2,1,0:T(8,128)S(1)}) custom-call(s32[1]{0:T(128)} %bitcast.1.refs_0_, s32[512,1]{1,0:T(8,128)S(1)} %copy.82.refs_1_, s32[1,512]{1,0:T(1,128)S(1)} %bitcast.116, s32[1,512]{1,0:T(1,128)S(1)} %bitcast.118, bf16[512,512]{1,0:T(8,128)(2,1)S(1)} %copy-done.33, ...), custom_call_target="tpu_custom_call" | custom-call | tf_op jit(solution)/shard_map/pallas_call | solution.py:93
  180.8 3.3 shard_map.417.refs_3_.refs_0_.refs_6_
  185.5 3.9 shard_map.418
  190.6 11.2 %collective-permute-done.19.refs_1_ = bf16[128,2048]{1,0:T(8,128)(2,1)S(1)} collective-permute-done((bf16[128,2048]{1,0:T(8,128)(2,1)S(1)}, bf16[128,2048]{1,0:T(8,128)(2,1)S(1)}, u32[]{:S(2)}, u32[]{:S(2)}) %collective-permute-start.19) | collective-permute-done | bytes 524320 | tf_op jit(solution)/shard_map/ppermute | solution.py:842
  202.3 2.9 collective-permute-start.21
  205.2 19.5 %collective-permute-done.20.refs_2_ = bf16[128,2048]{1,0:T(8,128)(2,1)S(1)} collective-permute-done((bf16[128,2048]{1,0:T(8,128)(2,1)S(1)}, bf16[128,2048]{1,0:T(8,128)(2,1)S(1)}, u32[]{:S(2)}, u32[]{:S(2)}) %collective-permute-start.20) | collective-permute-done | bytes 524320 | tf_op jit(solution)/shard_map/ppermute | solution.py:842
  228.2 19.8 %collective-permute-done.23.refs_0_.refs_2_ = bf16[128,2048]{1,0:T(8,128)(2,1)S(1)} collective-permute-done((bf16[128,2048]{1,0:T(8,128)(2,1)}, bf16[128,2048]{1,0:T(8,128)(2,1)S(1)}, u32[]{:S(2)}, u32[]{:S(2)}) %collective-permute-start.23) | collective-permute-done | bytes 524320 | tf_op jit(solution)/shard_map/ppermute | solution.py:842
  248.1 7.0 %collective-permute-start.24 = (bf16[128,2048]{1,0:T(8,128)(2,1)S(1)}, bf16[128,2048]{1,0:T(8,128)(2,1)S(1)}, u32[]{:S(2)}, u32[]{:S(2)}) collective-permute-start(bf16[128,2048]{1,0:T(8,128)(2,1)S(1)} %collective-permute-done.23.refs_0_.refs_2_), channel_id=1, source_target_pairs={{0,2},{2,0},{4,6},{6,4},{1,3},{3,1},{5,7},{7,5},{8,10},{10,8},{12,... | collective-permute-start | bytes 1572872 | tf_op jit(solution)/shard_map/ppermute | solution.py:842
  255.8 7.5 %collective-permute-done.24.refs_2_.refs_1_.refs_3_ = bf16[128,2048]{1,0:T(8,128)(2,1)S(1)} collective-permute-done((bf16[128,2048]{1,0:T(8,128)(2,1)S(1)}, bf16[128,2048]{1,0:T(8,128)(2,1)S(1)}, u32[]{:S(2)}, u32[]{:S(2)}) %collective-permute-start.24) | collective-permute-done | bytes 524320 | tf_op jit(solution)/shard_map/ppermute | solution.py:842
  265.2 6.8 %shard_map.421.refs_3_ = f32[512,1536]{1,0:T(8,128)S(1)} custom-call(bf16[512,2048]{1,0:T(8,128)(2,1)S(1)} %copy-done.1, bf16[2,4,2304,512]{3,2,1,0:T(8,128)(2,1)} %bitcast.121, bf16[128,2048]{1,0:T(8,128)(2,1)S(1)} %copy-done.14), custom_call_target="tpu_custom_call" | custom-call | tf_op jit(solution)/shard_map/pallas_call | solution.py:215
  272.0 8.6 %shard_map.422 = (bf16[512,1536]{1,0:T(8,128)(2,1)S(1)}, bf16[512,3072]{1,0:T(8,128)(2,1)S(1)}) custom-call(bf16[128,2048]{1,0:T(8,128)(2,1)S(1)} %copy-done.31, bf16[128,2048]{1,0:T(8,128)(2,1)S(1)} %copy-done.14, bf16[2,4,2304,512]{3,2,1,0:T(8,128)(2,1)} %bitcast.122, f32[512,1536]{1,0:T(8,128)S(1)} %shard_map.421.refs_3_), custom_call_target="tpu_custom_call" | custom-call | tf_op jit(solution)/shard_map/pallas_call | solution.py:215
  280.6 7.1 %shard_map.425 = (bf16[128,2048]{1,0:T(8,128)(2,1)S(1)}, bf16[128,2048]{1,0:T(8,128)(2,1)S(1)}) custom-call(bf16[512,3072]{1,0:T(8,128)(2,1)S(1)} %get-tuple-element.167.refs_5_.refs_0_, bf16[2,4,2304,512]{3,2,1,0:T(8,128)(2,1)} %bitcast.123), custom_call_target="tpu_custom_call" | custom-call | tf_op jit(solution)/shard_map/pallas_call | solution.py:215
  288.7 8.8 %shard_map.423 = (bf16[512,1536]{1,0:T(8,128)(2,1)S(1)}, bf16[512,3072]{1,0:T(8,128)(2,1)S(1)}) custom-call(bf16[128,2048]{1,0:T(8,128)(2,1)} %get-tuple-element.165.refs_0_, bf16[128,2048]{1,0:T(8,128)(2,1)} %collective-permute-done.22.refs_1_, bf16[2,4,2304,512]{3,2,1,0:T(8,128)(2,1)} %bitcast.124, ...), custom_call_target="tpu_custom_call", output_to_operand_aliasing={{0}: (4, {}), {1}: (5, {})} | custom-call | tf_op jit(solution)/shard_map/pallas_call | solution.py:215
  297.6 7.7 %shard_map.424 = (f32[128,2048]{1,0:T(8,128)S(1)}, bf16[128,2048]{1,0:T(8,128)(2,1)S(1)}) custom-call(bf16[512,3072]{1,0:T(8,128)(2,1)S(1)} %get-tuple-element.170.refs_0_.refs_4_, bf16[2,4,2304,512]{3,2,1,0:T(8,128)(2,1)} %bitcast.125), custom_call_target="tpu_custom_call" | custom-call | tf_op jit(solution)/shard_map/pallas_call | solution.py:215
  307.6 4.3 collective-permute-start.27
  311.9 16.5 %shard_map.427.refs_7_ = bf16[2,4,2304,512]{3,2,1,0:T(8,128)(2,1)} custom-call(bf16[128,2048]{1,0:T(8,128)(2,1)} %get-tuple-element.165.refs_0_, bf16[128,2048]{1,0:T(8,128)(2,1)} %collective-permute-done.22.refs_1_, bf16[128,2048]{1,0:T(8,128)(2,1)S(1)} %copy-done.31, bf16[128,2048]{1,0:T(8,128)(2,1)S(1)} %copy-done.15, ...), custom_call_target="tpu_custom_call" | custom-call | tf_op jit(solution)/shard_map/pallas_call | solution.py:215
  335.7 2.4 collective-permute-start.28
  338.1 15.7 %collective-permute-done.29.refs_3_ = bf16[128,2048]{1,0:T(8,128)(2,1)S(1)} collective-permute-done((bf16[128,2048]{1,0:T(8,128)(2,1)S(1)}, bf16[128,2048]{1,0:T(8,128)(2,1)S(1)}, u32[]{:S(2)}, u32[]{:S(2)}) %collective-permute-start.29) | collective-permute-done | bytes 524320 | tf_op jit(solution)/shard_map/ppermute | solution.py:842
  353.8 6.7 %shard_map.429.refs_6_.refs_1_ = bf16[512,2048]{1,0:T(8,128)(2,1)S(1)} custom-call(bf16[512,1536]{1,0:T(8,128)(2,1)S(1)} %copy-done.9, f32[128,2048]{1,0:T(8,128)S(1)} %copy-done.20, bf16[2,4,2304,512]{3,2,1,0:T(8,128)(2,1)} %bitcast.126, bf16[128,2048]{1,0:T(8,128)(2,1)S(1)} %get-tuple-element.181.refs_3_.refs_1_), custom_call_target="tpu_custom_call" | custom-call | tf_op jit(solution)/shard_map/pallas_call | solution.py:215
  361.8 3.3 collective-permute-done.30.refs_4_
  365.1 4.1 shard_map.430
  372.0 9.2 %shard_map.434 = (f32[512,512]{1,0:T(8,128)S(1)}, f32[512,256]{1,0:T(8,128)S(1)}, f32[512,256]{1,0:T(8,128)S(1)}, bf16[512,512]{1,0:T(8,128)(2,1)S(1)}) custom-call(s32[1]{0:T(128)} %bitcast.1.refs_0_, s32[512,1]{1,0:T(8,128)S(1)} %copy-done.26, s32[1,512]{1,0:T(1,128)S(1)} %bitcast.117, s32[1,512]{1,0:T(1,128)S(1)} %bitcast.119, ...), custom_call_target="tpu_custom_call" | custom-call | tf_op jit(solution)/shard_map/pallas_call | solution.py:163
  382.8 6.5 %collective-permute-start.33 = (bf16[512,512]{1,0:T(8,128)(2,1)S(1)}, bf16[512,512]{1,0:T(8,128)(2,1)S(1)}, u32[]{:S(2)}, u32[]{:S(2)}) collective-permute-start(bf16[512,512]{1,0:T(8,128)(2,1)S(1)} %shard_map.432), channel_id=1, source_target_pairs={{0,4},{2,6},{4,0},{6,2},{1,5},{3,7},{5,1},{7,3},{8,12},{10,14},{12... | collective-permute-start | bytes 1572872 | tf_op jit(solution)/shard_map/ppermute | solution.py:842
  390.6 13.5 %collective-permute-done.32.refs_1_ = bf16[512,512]{1,0:T(8,128)(2,1)S(1)} collective-permute-done((bf16[512,512]{1,0:T(8,128)(2,1)S(1)}, bf16[512,512]{1,0:T(8,128)(2,1)S(1)}, u32[]{:S(2)}, u32[]{:S(2)}) %collective-permute-start.32) | collective-permute-done | bytes 524320 | tf_op jit(solution)/shard_map/ppermute | solution.py:842
  405.3 10.2 %collective-permute-done.34.refs_5_ = bf16[512,512]{1,0:T(8,128)(2,1)S(1)} collective-permute-done((bf16[512,512]{1,0:T(8,128)(2,1)S(1)}, bf16[512,512]{1,0:T(8,128)(2,1)S(1)}, u32[]{:S(2)}, u32[]{:S(2)}) %collective-permute-start.34) | collective-permute-done | bytes 524320 | tf_op jit(solution)/shard_map/ppermute | solution.py:1315
  415.5 2.6 shard_map.435
  418.2 9.7 %shard_map.436.refs_7_ = bf16[2,4,768,512]{3,2,1,0:T(8,128)(2,1)} custom-call(bf16[512,2048]{1,0:T(8,128)(2,1)S(1)} %copy-done.38, bf16[512,1024]{1,0:T(8,128)(2,1)S(1)} %get-tuple-element.197.refs_1_, bf16[512,512]{1,0:T(8,128)(2,1)S(1)} %copy-done.17, bf16[512,2048]{1,0:T(8,128)(2,1)S(1)} %copy-done.12), custom_call_target="tpu_custom_call" | custom-call | tf_op jit(solution)/shard_map/pallas_call | solution.py:215
  427.9 5.8 %shard_map.437 = (bf16[512,2048]{1,0:T(8,128)(2,1)S(1)}, f32[512,1]{1,0:T(8,128)S(1)}, f32[1,2048]{1,0:T(1,128)S(1)}) custom-call(s32[1]{0:T(128)} %bitcast.refs_0_, bf16[512,1024]{1,0:T(8,128)(2,1)S(1)} %get-tuple-element.197.refs_1_, bf16[2,4,768,512]{3,2,1,0:T(8,128)(2,1)} %bitcast.131, bf16[512,2048]{1,0:T(8,128)(2,1)S(1)} %copy-done.5, ...), custom_call_target="tpu_custom_call" | custom-call | tf_op jit(solution)/shard_map/pallas_call | solution.py:215
  435.6 1.9 collective-permute-start.38
  437.5 15.5 %collective-permute-done.38 = f32[38,128]{1,0:T(8,128)S(1)} collective-permute-done((f32[38,128]{1,0:T(8,128)S(1)}, f32[38,128]{1,0:T(8,128)S(1)}, u32[]{:S(2)}, u32[]{:S(2)}) %collective-permute-start.38) | collective-permute-done | bytes 19488 | tf_op jit(solution)/shard_map/ppermute | solution.py:842
  453.3 3.0 collective-permute-start.37
  459.0 2.3 collective-permute-start.41
  461.3 2.2 collective-permute-done.41
  463.5 4.0 collective-permute-done.42
  472.9 4.3 collective-permute-start.43
  482.5 8.9 %collective-permute-done.43.refs_2_ = bf16[576,512]{1,0:T(8,128)(2,1)S(1)} collective-permute-done((bf16[576,512]{1,0:T(8,128)(2,1)}, bf16[576,512]{1,0:T(8,128)(2,1)S(1)}, u32[]{:S(2)}, u32[]{:S(2)}) %collective-permute-start.43) | collective-permute-done | bytes 589856 | tf_op jit(solution)/shard_map/ppermute | solution.py:876
  491.4 34.9 %collective-permute-done.44.refs_3_ = bf16[576,512]{1,0:T(8,128)(2,1)S(1)} collective-permute-done((bf16[576,512]{1,0:T(8,128)(2,1)}, bf16[576,512]{1,0:T(8,128)(2,1)S(1)}, u32[]{:S(2)}, u32[]{:S(2)}) %collective-permute-start.44) | collective-permute-done | bytes 589856 | tf_op jit(solution)/shard_map/ppermute | solution.py:876
  535.6 8.1 %shard_map.443 = (f32[6144,128]{1,0:T(8,128)}, f32[6144,128]{1,0:T(8,128)}, f32[6144,128]{1,0:T(8,128)}) custom-call(bf16[6144,128]{1,0:T(8,128)(2,1)} %reshape.293.refs_0_, f32[6144,128]{1,0:T(8,128)} %bitcast.110, f32[6144,128]{1,0:T(8,128)} %bitcast.134, f32[6144,128]{1,0:T(8,128)} %bitcast.135), custom_call_target="tpu_custom_call" | custom-call | tf_op jit(solution)/shard_map/pallas_call | solution.py:215
  545.0 2.7 collective-permute-start.47
  547.7 1.9 collective-permute-start.48
  550.3 6.0 %shard_map.450 = (f32[768,512]{1,0:T(8,128)}, f32[768,512]{1,0:T(8,128)}, f32[768,512]{1,0:T(8,128)}) custom-call(s32[1]{0:T(128)} %bitcast.15.refs_0_, bf16[192,512]{1,0:T(8,128)(2,1)S(1)} %get-tuple-element.241.refs_1_, bf16[192,512]{1,0:T(8,128)(2,1)S(1)} %collective-permute-done.52.refs_2_, bf16[192,512]{1,0:T(8,128)(2,1)S(1)} %collective-permute-done.53.refs_3_, ...), custom_call_target="tpu_custom_call" | custom-call | tf_op jit(solution)/shard_map/pallas_call | solution.py:215
  556.3 8.1 %collective-permute-done.47.refs_3_ = bf16[192,512]{1,0:T(8,128)(2,1)S(1)} collective-permute-done((bf16[192,512]{1,0:T(8,128)(2,1)S(1)}, bf16[192,512]{1,0:T(8,128)(2,1)S(1)}, u32[]{:S(2)}, u32[]{:S(2)}) %collective-permute-start.47) | collective-permute-done | bytes 196640 | tf_op jit(solution)/shard_map/ppermute | solution.py:876
  568.9 3.7 shard_map.446
  572.6 3.9 shard_map.448
  (315 shorter events, 87.5 us)
Async XLA Ops:
  7.2 126.5 %all-gather.5.cloned.1.call-start = ((), (), s32[]{:S(2)}) async-start(), calls=%async_computation.4 | async-start | bytes 7077888 | tf_op jit(solution)/shard_map/all_gather | solution.py:895
  7.2 48.1 %collective-permute-start.1 = (bf16[512,512]{1,0:T(8,128)(2,1)}, bf16[512,512]{1,0:T(8,128)(2,1)}, u32[]{:S(2)}, u32[]{:S(2)}) collective-permute-start(bf16[512,512]{1,0:T(8,128)(2,1)} %refs_1_.7), channel_id=1, source_target_pairs={{0,4},{2,6},{4,0},{6,2},{1,5},{3,7},{5,1},{7,3},{8,12},{10,14},{12... | collective-permute-start | bytes 1572872 | tf_op jit(solution)/shard_map/ppermute | solution.py:842
  11.3 38.3 %copy-start.10 = (f32[128,2,3072]{2,1,0:T(2,128)S(1)}, f32[128,2,3072]{2,1,0:T(2,128)}, u32[]{:S(2)}) copy-start(f32[128,2,3072]{2,1,0:T(2,128)} %refs_1_.6) | copy-start | bytes 9437188
  16.1 8.1 %collective-permute-start.6 = (bf16[256,512]{1,0:T(8,128)(2,1)S(1)}, bf16[256,512]{1,0:T(8,128)(2,1)S(1)}, u32[]{:S(2)}, u32[]{:S(2)}) collective-permute-start(bf16[256,512]{1,0:T(8,128)(2,1)S(1)} %get-tuple-element.141), channel_id=1, source_target_pairs={{0,8},{8,16},{16,24},{24,0},{1,9},{9,17},{17,25},{25,1},{2,10},{10... | collective-permute-start | bytes 786440 | tf_op jit(solution)/shard_map/ppermute | solution.py:891
  16.1 9.2 %collective-permute-start.7 = (bf16[256,512]{1,0:T(8,128)(2,1)S(1)}, bf16[256,512]{1,0:T(8,128)(2,1)S(1)}, u32[]{:S(2)}, u32[]{:S(2)}) collective-permute-start(bf16[256,512]{1,0:T(8,128)(2,1)S(1)} %get-tuple-element.142), channel_id=1, source_target_pairs={{0,16},{8,24},{16,0},{24,8},{1,17},{9,25},{17,1},{25,9},{2,18},{10... | collective-permute-start | bytes 786440 | tf_op jit(solution)/shard_map/ppermute | solution.py:891
  17.6 11.9 %collective-permute-start.8 = (bf16[256,512]{1,0:T(8,128)(2,1)}, bf16[256,512]{1,0:T(8,128)(2,1)}, u32[]{:S(2)}, u32[]{:S(2)}) collective-permute-start(bf16[256,512]{1,0:T(8,128)(2,1)} %get-tuple-element.143), channel_id=1, source_target_pairs={{0,24},{8,0},{16,8},{24,16},{1,25},{9,1},{17,9},{25,17},{2,26},{10... | collective-permute-start | bytes 786440 | tf_op jit(solution)/shard_map/ppermute | solution.py:891
  19.0 13.8 %collective-permute-start.3 = (bf16[128,512]{1,0:T(8,128)(2,1)}, bf16[128,512]{1,0:T(8,128)(2,1)}, u32[]{:S(2)}, u32[]{:S(2)}) collective-permute-start(bf16[128,512]{1,0:T(8,128)(2,1)} %get-tuple-element.137), channel_id=1, source_target_pairs={{0,2},{2,4},{4,6},{6,0},{1,3},{3,5},{5,7},{7,1},{8,10},{10,12},{12... | collective-permute-start | bytes 393224 | tf_op jit(solution)/shard_map/ppermute | solution.py:876
  24.8 20.7 %collective-permute-start.4 = (bf16[128,512]{1,0:T(8,128)(2,1)}, bf16[128,512]{1,0:T(8,128)(2,1)}, u32[]{:S(2)}, u32[]{:S(2)}) collective-permute-start(bf16[128,512]{1,0:T(8,128)(2,1)} %get-tuple-element.138), channel_id=1, source_target_pairs={{0,4},{2,6},{4,0},{6,2},{1,5},{3,7},{5,1},{7,3},{8,12},{10,14},{12... | collective-permute-start | bytes 393224 | tf_op jit(solution)/shard_map/ppermute | solution.py:876
  25.9 29.3 %collective-permute-start.5 = (bf16[128,512]{1,0:T(8,128)(2,1)}, bf16[128,512]{1,0:T(8,128)(2,1)}, u32[]{:S(2)}, u32[]{:S(2)}) collective-permute-start(bf16[128,512]{1,0:T(8,128)(2,1)} %get-tuple-element.139), channel_id=1, source_target_pairs={{0,6},{2,0},{4,2},{6,4},{1,7},{3,1},{5,3},{7,5},{8,14},{10,8},{12,... | collective-permute-start | bytes 393224 | tf_op jit(solution)/shard_map/ppermute | solution.py:876
  32.5 22.8 %collective-permute-start.10 = (bf16[64,512]{1,0:T(8,128)(2,1)S(1)}, bf16[64,512]{1,0:T(8,128)(2,1)S(1)}, u32[]{:S(2)}, u32[]{:S(2)}) collective-permute-start(bf16[64,512]{1,0:T(8,128)(2,1)S(1)} %get-tuple-element.146), channel_id=1, source_target_pairs={{0,4},{2,6},{4,0},{6,2},{1,5},{3,7},{5,1},{7,3},{8,12},{10,14},{12... | collective-permute-start | bytes 196616 | tf_op jit(solution)/shard_map/ppermute | solution.py:876
  32.8 22.5 %collective-permute-start.11 = (bf16[64,512]{1,0:T(8,128)(2,1)S(1)}, bf16[64,512]{1,0:T(8,128)(2,1)S(1)}, u32[]{:S(2)}, u32[]{:S(2)}) collective-permute-start(bf16[64,512]{1,0:T(8,128)(2,1)S(1)} %get-tuple-element.147), channel_id=1, source_target_pairs={{0,6},{2,0},{4,2},{6,4},{1,7},{3,1},{5,3},{7,5},{8,14},{10,8},{12,... | collective-permute-start | bytes 196616 | tf_op jit(solution)/shard_map/ppermute | solution.py:876
  45.5 9.8 %collective-permute-start.9 = (bf16[64,512]{1,0:T(8,128)(2,1)S(1)}, bf16[64,512]{1,0:T(8,128)(2,1)S(1)}, u32[]{:S(2)}, u32[]{:S(2)}) collective-permute-start(bf16[64,512]{1,0:T(8,128)(2,1)S(1)} %get-tuple-element.145), channel_id=1, source_target_pairs={{0,2},{2,4},{4,6},{6,0},{1,3},{3,5},{5,7},{7,1},{8,10},{10,12},{12... | collective-permute-start | bytes 196616 | tf_op jit(solution)/shard_map/ppermute | solution.py:876
  58.3 205.8 %all-gather.7.cloned.1.call-start = ((), (), s32[]{:S(2)}) async-start(), calls=%async_computation.5 | async-start | bytes 21233664 | tf_op jit(solution)/shard_map/all_gather | solution.py:895
  58.4 68.0 %collective-permute-start.12 = (bf16[576,512]{1,0:T(8,128)(2,1)S(1)}, bf16[576,512]{1,0:T(8,128)(2,1)S(1)}, u32[]{:S(2)}, u32[]{:S(2)}) collective-permute-start(bf16[576,512]{1,0:T(8,128)(2,1)S(1)} %copy-done.73), channel_id=1, source_target_pairs={{0,2},{2,4},{4,6},{6,0},{1,3},{3,5},{5,7},{7,1},{8,10},{10,12},{12... | collective-permute-start | bytes 1769480 | tf_op jit(solution)/shard_map/ppermute | solution.py:876
  58.5 67.9 %collective-permute-start.13 = (bf16[576,512]{1,0:T(8,128)(2,1)S(1)}, bf16[576,512]{1,0:T(8,128)(2,1)S(1)}, u32[]{:S(2)}, u32[]{:S(2)}) collective-permute-start(bf16[576,512]{1,0:T(8,128)(2,1)S(1)} %copy-done.71), channel_id=1, source_target_pairs={{0,4},{2,6},{4,0},{6,2},{1,5},{3,7},{5,1},{7,3},{8,12},{10,14},{12... | collective-permute-start | bytes 1769480 | tf_op jit(solution)/shard_map/ppermute | solution.py:876
  61.9 64.4 %copy-start.29 = (bf16[576,512]{1,0:T(8,128)(2,1)S(1)}, bf16[576,512]{1,0:T(8,128)(2,1)}, u32[]{:S(2)}) copy-start(bf16[576,512]{1,0:T(8,128)(2,1)} %copy-done.28) | copy-start | bytes 1769476
  61.9 64.4 %collective-permute-start.14 = (bf16[576,512]{1,0:T(8,128)(2,1)S(1)}, bf16[576,512]{1,0:T(8,128)(2,1)S(1)}, u32[]{:S(2)}, u32[]{:S(2)}) collective-permute-start(bf16[576,512]{1,0:T(8,128)(2,1)S(1)} %copy-done.69), channel_id=1, source_target_pairs={{0,6},{2,0},{4,2},{6,4},{1,7},{3,1},{5,3},{7,5},{8,14},{10,8},{12,... | collective-permute-start | bytes 1769480 | tf_op jit(solution)/shard_map/ppermute | solution.py:876
  64.7 46.9 %collective-permute-start = (bf16[512,512]{1,0:T(8,128)(2,1)S(1)}, bf16[512,512]{1,0:T(8,128)(2,1)S(1)}, u32[]{:S(2)}, u32[]{:S(2)}) collective-permute-start(bf16[512,512]{1,0:T(8,128)(2,1)S(1)} %copy-done.35), channel_id=1, source_target_pairs={{0,2},{2,0},{4,6},{6,4},{1,3},{3,1},{5,7},{7,5},{8,10},{10,8},{12,... | collective-permute-start | bytes 1572872 | tf_op jit(solution)/shard_map/ppermute | solution.py:842
  64.7 58.0 %collective-permute-start.2 = (bf16[512,512]{1,0:T(8,128)(2,1)}, bf16[512,512]{1,0:T(8,128)(2,1)S(1)}, u32[]{:S(2)}, u32[]{:S(2)}) collective-permute-start(bf16[512,512]{1,0:T(8,128)(2,1)} %collective-permute-done.1.refs_10_.refs_3_), channel_id=1, source_target_pairs={{0,2},{2,0},{4,6},{6,4},{1,3},{3,1},{5,7},{7,5},{8,10},{10,8},{12,... | collective-permute-start | bytes 1572872 | tf_op jit(solution)/shard_map/ppermute | solution.py:842
  128.0 341.8 %reduce-scatter.3.cloned.1.call-start = ((), (), s32[]{:S(2)}) async-start(), calls=%async_computation.2 | async-start | bytes 21233664 | tf_op jit(solution)/shard_map/reduce_scatter | solution.py:901
  131.7 25.5 %collective-permute-start.17 = (bf16[512,512]{1,0:T(8,128)(2,1)}, bf16[512,512]{1,0:T(8,128)(2,1)}, u32[]{:S(2)}, u32[]{:S(2)}) collective-permute-start(bf16[512,512]{1,0:T(8,128)(2,1)} %shard_map.414.refs_6_.refs_1_), channel_id=1, source_target_pairs={{0,4},{2,6},{4,0},{6,2},{1,5},{3,7},{5,1},{7,3},{8,12},{10,14},{12... | collective-permute-start | bytes 1572872 | tf_op jit(solution)/shard_map/ppermute | solution.py:842
  146.1 26.3 %collective-permute-start.15 = (bf16[512,512]{1,0:T(8,128)(2,1)S(1)}, bf16[512,512]{1,0:T(8,128)(2,1)S(1)}, u32[]{:S(2)}, u32[]{:S(2)}) collective-permute-start(bf16[512,512]{1,0:T(8,128)(2,1)S(1)} %get-tuple-element.157.refs_5_.refs_6_), channel_id=1, source_target_pairs={{0,1},{2,3},{4,5},{6,7},{8,9},{10,11},{12,13},{14,15},{16,17},{18,... | collective-permute-start | bytes 1572872 | tf_op jit(solution)/shard_map/ppermute | solution.py:1274
  149.7 31.1 %collective-permute-start.16 = (bf16[512,512]{1,0:T(8,128)(2,1)}, bf16[512,512]{1,0:T(8,128)(2,1)S(1)}, u32[]{:S(2)}, u32[]{:S(2)}) collective-permute-start(bf16[512,512]{1,0:T(8,128)(2,1)} %shard_map.414.refs_6_.refs_1_), channel_id=1, source_target_pairs={{0,2},{2,0},{4,6},{6,4},{1,3},{3,1},{5,7},{7,5},{8,10},{10,8},{12,... | collective-permute-start | bytes 1572872 | tf_op jit(solution)/shard_map/ppermute | solution.py:842
  157.1 23.7 %collective-permute-start.18 = (bf16[512,512]{1,0:T(8,128)(2,1)}, bf16[512,512]{1,0:T(8,128)(2,1)}, u32[]{:S(2)}, u32[]{:S(2)}) collective-permute-start(bf16[512,512]{1,0:T(8,128)(2,1)} %collective-permute-done.17.refs_3_), channel_id=1, source_target_pairs={{0,2},{2,0},{4,6},{6,4},{1,3},{3,1},{5,7},{7,5},{8,10},{10,8},{12,... | collective-permute-start | bytes 1572872 | tf_op jit(solution)/shard_map/ppermute | solution.py:842
  185.5 39.2 %copy-start.4 = (bf16[512,2048]{1,0:T(8,128)(2,1)S(1)}, bf16[512,2048]{1,0:T(8,128)(2,1)}, u32[]{:S(2)}) copy-start(bf16[512,2048]{1,0:T(8,128)(2,1)} %copy-done.2) | copy-start | bytes 6291460
  189.5 12.3 %collective-permute-start.19 = (bf16[128,2048]{1,0:T(8,128)(2,1)S(1)}, bf16[128,2048]{1,0:T(8,128)(2,1)S(1)}, u32[]{:S(2)}, u32[]{:S(2)}) collective-permute-start(bf16[128,2048]{1,0:T(8,128)(2,1)S(1)} %get-tuple-element.162), channel_id=1, source_target_pairs={{0,2},{2,0},{4,6},{6,4},{1,3},{3,1},{5,7},{7,5},{8,10},{10,8},{12,... | collective-permute-start | bytes 1572872 | tf_op jit(solution)/shard_map/ppermute | solution.py:842
  201.9 22.8 %collective-permute-start.20 = (bf16[128,2048]{1,0:T(8,128)(2,1)S(1)}, bf16[128,2048]{1,0:T(8,128)(2,1)S(1)}, u32[]{:S(2)}, u32[]{:S(2)}) collective-permute-start(bf16[128,2048]{1,0:T(8,128)(2,1)S(1)} %get-tuple-element.163), channel_id=1, source_target_pairs={{0,2},{2,0},{4,6},{6,4},{1,3},{3,1},{5,7},{7,5},{8,10},{10,8},{12,... | collective-permute-start | bytes 1572872 | tf_op jit(solution)/shard_map/ppermute | solution.py:842
  202.3 22.4 %collective-permute-start.21 = (bf16[128,2048]{1,0:T(8,128)(2,1)S(1)}, bf16[128,2048]{1,0:T(8,128)(2,1)S(1)}, u32[]{:S(2)}, u32[]{:S(2)}) collective-permute-start(bf16[128,2048]{1,0:T(8,128)(2,1)S(1)} %shard_map.419), channel_id=1, source_target_pairs={{0,4},{2,6},{4,0},{6,2},{1,5},{3,7},{5,1},{7,3},{8,12},{10,14},{12... | collective-permute-start | bytes 1572872 | tf_op jit(solution)/shard_map/ppermute | solution.py:842
  224.7 39.4 %copy-start.1 = (bf16[512,2048]{1,0:T(8,128)(2,1)S(1)}, bf16[512,2048]{1,0:T(8,128)(2,1)}, u32[]{:S(2)}) copy-start(bf16[512,2048]{1,0:T(8,128)(2,1)} %copy-done) | copy-start | bytes 6291460
  227.0 21.1 %collective-permute-start.23 = (bf16[128,2048]{1,0:T(8,128)(2,1)}, bf16[128,2048]{1,0:T(8,128)(2,1)S(1)}, u32[]{:S(2)}, u32[]{:S(2)}) collective-permute-start(bf16[128,2048]{1,0:T(8,128)(2,1)} %get-tuple-element.165.refs_0_), channel_id=1, source_target_pairs={{0,4},{2,6},{4,0},{6,2},{1,5},{3,7},{5,1},{7,3},{8,12},{10,14},{12... | collective-permute-start | bytes 1572872 | tf_op jit(solution)/shard_map/ppermute | solution.py:842
  248.1 15.3 %collective-permute-start.24 = (bf16[128,2048]{1,0:T(8,128)(2,1)S(1)}, bf16[128,2048]{1,0:T(8,128)(2,1)S(1)}, u32[]{:S(2)}, u32[]{:S(2)}) collective-permute-start(bf16[128,2048]{1,0:T(8,128)(2,1)S(1)} %collective-permute-done.23.refs_0_.refs_2_), channel_id=1, source_target_pairs={{0,2},{2,0},{4,6},{6,4},{1,3},{3,1},{5,7},{7,5},{8,10},{10,8},{12,... | collective-permute-start | bytes 1572872 | tf_op jit(solution)/shard_map/ppermute | solution.py:842
  255.8 32.9 %collective-permute-start.22 = (bf16[128,2048]{1,0:T(8,128)(2,1)}, bf16[128,2048]{1,0:T(8,128)(2,1)}, u32[]{:S(2)}, u32[]{:S(2)}) collective-permute-start(bf16[128,2048]{1,0:T(8,128)(2,1)} %get-tuple-element.165.refs_0_), channel_id=1, source_target_pairs={{0,2},{2,0},{4,6},{6,4},{1,3},{3,1},{5,7},{7,5},{8,10},{10,8},{12,... | collective-permute-start | bytes 1572872 | tf_op jit(solution)/shard_map/ppermute | solution.py:842
  287.7 18.5 %collective-permute-start.25 = (bf16[128,2048]{1,0:T(8,128)(2,1)S(1)}, bf16[128,2048]{1,0:T(8,128)(2,1)S(1)}, u32[]{:S(2)}, u32[]{:S(2)}) collective-permute-start(bf16[128,2048]{1,0:T(8,128)(2,1)S(1)} %get-tuple-element.174), channel_id=1, source_target_pairs={{0,2},{2,0},{4,6},{6,4},{1,3},{3,1},{5,7},{7,5},{8,10},{10,8},{12,... | collective-permute-start | bytes 1572872 | tf_op jit(solution)/shard_map/ppermute | solution.py:842
  306.4 22.0 %collective-permute-start.26 = (bf16[128,2048]{1,0:T(8,128)(2,1)S(1)}, bf16[128,2048]{1,0:T(8,128)(2,1)S(1)}, u32[]{:S(2)}, u32[]{:S(2)}) collective-permute-start(bf16[128,2048]{1,0:T(8,128)(2,1)S(1)} %get-tuple-element.176.refs_9_), channel_id=1, source_target_pairs={{0,2},{2,0},{4,6},{6,4},{1,3},{3,1},{5,7},{7,5},{8,10},{10,8},{12,... | collective-permute-start | bytes 1572872 | tf_op jit(solution)/shard_map/ppermute | solution.py:842
  307.6 21.6 %collective-permute-start.27 = (bf16[128,2048]{1,0:T(8,128)(2,1)S(1)}, bf16[128,2048]{1,0:T(8,128)(2,1)S(1)}, u32[]{:S(2)}, u32[]{:S(2)}) collective-permute-start(bf16[128,2048]{1,0:T(8,128)(2,1)S(1)} %shard_map.426.refs_7_), channel_id=1, source_target_pairs={{0,4},{2,6},{4,0},{6,2},{1,5},{3,7},{5,1},{7,3},{8,12},{10,14},{12... | collective-permute-start | bytes 1572872 | tf_op jit(solution)/shard_map/ppermute | solution.py:842
  330.0 213.7 %reduce-scatter.5.cloned.1.call-start = ((), (), s32[]{:S(2)}) async-start(), calls=%async_computation.3 | async-start | bytes 7077888 | tf_op jit(solution)/shard_map/reduce_scatter | solution.py:901
  335.6 18.2 %collective-permute-start.29 = (bf16[128,2048]{1,0:T(8,128)(2,1)S(1)}, bf16[128,2048]{1,0:T(8,128)(2,1)S(1)}, u32[]{:S(2)}, u32[]{:S(2)}) collective-permute-start(bf16[128,2048]{1,0:T(8,128)(2,1)S(1)} %get-tuple-element.181.refs_3_.refs_1_), channel_id=1, source_target_pairs={{0,4},{2,6},{4,0},{6,2},{1,5},{3,7},{5,1},{7,3},{8,12},{10,14},{12... | collective-permute-start | bytes 1572872 | tf_op jit(solution)/shard_map/ppermute | solution.py:842
  335.7 26.1 %collective-permute-start.28 = (bf16[128,2048]{1,0:T(8,128)(2,1)S(1)}, bf16[128,2048]{1,0:T(8,128)(2,1)S(1)}, u32[]{:S(2)}, u32[]{:S(2)}) collective-permute-start(bf16[128,2048]{1,0:T(8,128)(2,1)S(1)} %get-tuple-element.181.refs_3_.refs_1_), channel_id=1, source_target_pairs={{0,2},{2,0},{4,6},{6,4},{1,3},{3,1},{5,7},{7,5},{8,10},{10,8},{12,... | collective-permute-start | bytes 1572872 | tf_op jit(solution)/shard_map/ppermute | solution.py:842
  353.8 11.3 %collective-permute-start.30 = (bf16[128,2048]{1,0:T(8,128)(2,1)S(1)}, bf16[128,2048]{1,0:T(8,128)(2,1)S(1)}, u32[]{:S(2)}, u32[]{:S(2)}) collective-permute-start(bf16[128,2048]{1,0:T(8,128)(2,1)S(1)} %collective-permute-done.29.refs_3_), channel_id=1, source_target_pairs={{0,2},{2,0},{4,6},{6,4},{1,3},{3,1},{5,7},{7,5},{8,10},{10,8},{12,... | collective-permute-start | bytes 1572872 | tf_op jit(solution)/shard_map/ppermute | solution.py:842
  371.2 11.4 %collective-permute-start.31 = (bf16[512,512]{1,0:T(8,128)(2,1)S(1)}, bf16[512,512]{1,0:T(8,128)(2,1)S(1)}, u32[]{:S(2)}, u32[]{:S(2)}) collective-permute-start(bf16[512,512]{1,0:T(8,128)(2,1)S(1)} %get-tuple-element.186), channel_id=1, source_target_pairs={{0,2},{2,0},{4,6},{6,4},{1,3},{3,1},{5,7},{7,5},{8,10},{10,8},{12,... | collective-permute-start | bytes 1572872 | tf_op jit(solution)/shard_map/ppermute | solution.py:842
  382.7 21.4 %collective-permute-start.32 = (bf16[512,512]{1,0:T(8,128)(2,1)S(1)}, bf16[512,512]{1,0:T(8,128)(2,1)S(1)}, u32[]{:S(2)}, u32[]{:S(2)}) collective-permute-start(bf16[512,512]{1,0:T(8,128)(2,1)S(1)} %get-tuple-element.187), channel_id=1, source_target_pairs={{0,2},{2,0},{4,6},{6,4},{1,3},{3,1},{5,7},{7,5},{8,10},{10,8},{12,... | collective-permute-start | bytes 1572872 | tf_op jit(solution)/shard_map/ppermute | solution.py:842
  382.8 21.3 %collective-permute-start.33 = (bf16[512,512]{1,0:T(8,128)(2,1)S(1)}, bf16[512,512]{1,0:T(8,128)(2,1)S(1)}, u32[]{:S(2)}, u32[]{:S(2)}) collective-permute-start(bf16[512,512]{1,0:T(8,128)(2,1)S(1)} %shard_map.432), channel_id=1, source_target_pairs={{0,4},{2,6},{4,0},{6,2},{1,5},{3,7},{5,1},{7,3},{8,12},{10,14},{12... | collective-permute-start | bytes 1572872 | tf_op jit(solution)/shard_map/ppermute | solution.py:842
  389.3 26.2 %collective-permute-start.34 = (bf16[512,512]{1,0:T(8,128)(2,1)S(1)}, bf16[512,512]{1,0:T(8,128)(2,1)S(1)}, u32[]{:S(2)}, u32[]{:S(2)}) collective-permute-start(bf16[512,512]{1,0:T(8,128)(2,1)S(1)} %get-tuple-element.196), channel_id=1, source_target_pairs={{1,0},{3,2},{5,4},{7,6},{9,8},{11,10},{13,12},{15,14},{17,16},{19,... | collective-permute-start | bytes 1572872 | tf_op jit(solution)/shard_map/ppermute | solution.py:1315
  435.2 17.9 %collective-permute-start.35 = (bf16[512,512]{1,0:T(8,128)(2,1)S(1)}, bf16[512,512]{1,0:T(8,128)(2,1)S(1)}, u32[]{:S(2)}, u32[]{:S(2)}) collective-permute-start(bf16[512,512]{1,0:T(8,128)(2,1)S(1)} %get-tuple-element.210), channel_id=1, source_target_pairs={{0,2},{2,0},{4,6},{6,4},{1,3},{3,1},{5,7},{7,5},{8,10},{10,8},{12,... | collective-permute-start | bytes 1572872 | tf_op jit(solution)/shard_map/ppermute | solution.py:842
  435.6 17.4 %collective-permute-start.38 = (f32[38,128]{1,0:T(8,128)S(1)}, f32[38,128]{1,0:T(8,128)S(1)}, u32[]{:S(2)}, u32[]{:S(2)}) collective-permute-start(f32[38,128]{1,0:T(8,128)S(1)} %bitcast.139), channel_id=1, source_target_pairs={{0,2},{2,0},{4,6},{6,4},{1,3},{3,1},{5,7},{7,5},{8,10},{10,8},{12,... | collective-permute-start | bytes 58376 | tf_op jit(solution)/shard_map/ppermute | solution.py:842
  453.0 4.8 collective-permute-start.39
  453.2 15.1 %collective-permute-start.36 = (bf16[512,512]{1,0:T(8,128)(2,1)S(1)}, bf16[512,512]{1,0:T(8,128)(2,1)S(1)}, u32[]{:S(2)}, u32[]{:S(2)}) collective-permute-start(bf16[512,512]{1,0:T(8,128)(2,1)S(1)} %get-tuple-element.211), channel_id=1, source_target_pairs={{0,2},{2,0},{4,6},{6,4},{1,3},{3,1},{5,7},{7,5},{8,10},{10,8},{12,... | collective-permute-start | bytes 1572872 | tf_op jit(solution)/shard_map/ppermute | solution.py:842
  453.3 15.8 %collective-permute-start.37 = (bf16[512,512]{1,0:T(8,128)(2,1)S(1)}, bf16[512,512]{1,0:T(8,128)(2,1)S(1)}, u32[]{:S(2)}, u32[]{:S(2)}) collective-permute-start(bf16[512,512]{1,0:T(8,128)(2,1)S(1)} %shard_map.439), channel_id=1, source_target_pairs={{0,4},{2,6},{4,0},{6,2},{1,5},{3,7},{5,1},{7,3},{8,12},{10,14},{12... | collective-permute-start | bytes 1572872 | tf_op jit(solution)/shard_map/ppermute | solution.py:842
  457.8 1.2 collective-permute-start.40
  459.0 4.5 collective-permute-start.41
  463.5 4.0 collective-permute-start.42
  472.9 18.4 %collective-permute-start.43 = (bf16[576,512]{1,0:T(8,128)(2,1)}, bf16[576,512]{1,0:T(8,128)(2,1)S(1)}, u32[]{:S(2)}, u32[]{:S(2)}) collective-permute-start(bf16[576,512]{1,0:T(8,128)(2,1)} %get-tuple-element.219), channel_id=1, source_target_pairs={{0,6},{2,0},{4,2},{6,4},{1,7},{3,1},{5,3},{7,5},{8,14},{10,8},{12,... | collective-permute-start | bytes 1769480 | tf_op jit(solution)/shard_map/ppermute | solution.py:876
  477.2 49.1 %collective-permute-start.44 = (bf16[576,512]{1,0:T(8,128)(2,1)}, bf16[576,512]{1,0:T(8,128)(2,1)S(1)}, u32[]{:S(2)}, u32[]{:S(2)}) collective-permute-start(bf16[576,512]{1,0:T(8,128)(2,1)} %get-tuple-element.220), channel_id=1, source_target_pairs={{0,4},{2,6},{4,0},{6,2},{1,5},{3,7},{5,1},{7,3},{8,12},{10,14},{12... | collective-permute-start | bytes 1769480 | tf_op jit(solution)/shard_map/ppermute | solution.py:876
  477.2 49.1 %collective-permute-start.45 = (bf16[576,512]{1,0:T(8,128)(2,1)}, bf16[576,512]{1,0:T(8,128)(2,1)S(1)}, u32[]{:S(2)}, u32[]{:S(2)}) collective-permute-start(bf16[576,512]{1,0:T(8,128)(2,1)} %get-tuple-element.221), channel_id=1, source_target_pairs={{0,2},{2,4},{4,6},{6,0},{1,3},{3,5},{5,7},{7,1},{8,10},{10,12},{12... | collective-permute-start | bytes 1769480 | tf_op jit(solution)/shard_map/ppermute | solution.py:876
  481.6 46.1 %copy-start.36 = (bf16[512,512]{1,0:T(8,128)(2,1)S(1)}, bf16[512,512]{1,0:T(8,128)(2,1)}, u32[]{:S(2)}) copy-start(bf16[512,512]{1,0:T(8,128)(2,1)} %refs_1_.7) | copy-start | bytes 1572868
  527.5 20.2 %collective-permute-start.52 = (bf16[192,512]{1,0:T(8,128)(2,1)}, bf16[192,512]{1,0:T(8,128)(2,1)S(1)}, u32[]{:S(2)}, u32[]{:S(2)}) collective-permute-start(bf16[192,512]{1,0:T(8,128)(2,1)} %get-tuple-element.242), channel_id=1, source_target_pairs={{0,8},{8,16},{16,24},{24,0},{1,9},{9,17},{17,25},{25,1},{2,10},{10... | collective-permute-start | bytes 589832 | tf_op jit(solution)/shard_map/ppermute | solution.py:891
  528.9 21.3 %collective-permute-start.53 = (bf16[192,512]{1,0:T(8,128)(2,1)}, bf16[192,512]{1,0:T(8,128)(2,1)S(1)}, u32[]{:S(2)}, u32[]{:S(2)}) collective-permute-start(bf16[192,512]{1,0:T(8,128)(2,1)} %get-tuple-element.243), channel_id=1, source_target_pairs={{0,16},{8,24},{16,0},{24,8},{1,17},{9,25},{17,1},{25,9},{2,18},{10... | collective-permute-start | bytes 589832 | tf_op jit(solution)/shard_map/ppermute | solution.py:891
  530.3 20.0 %collective-permute-start.54 = (bf16[192,512]{1,0:T(8,128)(2,1)}, bf16[192,512]{1,0:T(8,128)(2,1)}, u32[]{:S(2)}, u32[]{:S(2)}) collective-permute-start(bf16[192,512]{1,0:T(8,128)(2,1)} %get-tuple-element.244), channel_id=1, source_target_pairs={{0,24},{8,0},{16,8},{24,16},{1,25},{9,1},{17,9},{25,17},{2,26},{10... | collective-permute-start | bytes 589832 | tf_op jit(solution)/shard_map/ppermute | solution.py:891
  545.0 11.3 %collective-permute-start.46 = (bf16[192,512]{1,0:T(8,128)(2,1)S(1)}, bf16[192,512]{1,0:T(8,128)(2,1)S(1)}, u32[]{:S(2)}, u32[]{:S(2)}) collective-permute-start(bf16[192,512]{1,0:T(8,128)(2,1)S(1)} %get-tuple-element.224), channel_id=1, source_target_pairs={{0,6},{2,0},{4,2},{6,4},{1,7},{3,1},{5,3},{7,5},{8,14},{10,8},{12,... | collective-permute-start | bytes 589832 | tf_op jit(solution)/shard_map/ppermute | solution.py:876
  545.0 19.4 %collective-permute-start.47 = (bf16[192,512]{1,0:T(8,128)(2,1)S(1)}, bf16[192,512]{1,0:T(8,128)(2,1)S(1)}, u32[]{:S(2)}, u32[]{:S(2)}) collective-permute-start(bf16[192,512]{1,0:T(8,128)(2,1)S(1)} %get-tuple-element.225), channel_id=1, source_target_pairs={{0,4},{2,6},{4,0},{6,2},{1,5},{3,7},{5,1},{7,3},{8,12},{10,14},{12... | collective-permute-start | bytes 589832 | tf_op jit(solution)/shard_map/ppermute | solution.py:876
  547.7 16.7 %collective-permute-start.48 = (bf16[192,512]{1,0:T(8,128)(2,1)S(1)}, bf16[192,512]{1,0:T(8,128)(2,1)S(1)}, u32[]{:S(2)}, u32[]{:S(2)}) collective-permute-start(bf16[192,512]{1,0:T(8,128)(2,1)S(1)} %get-tuple-element.226), channel_id=1, source_target_pairs={{0,2},{2,4},{4,6},{6,0},{1,3},{3,5},{5,7},{7,1},{8,10},{10,12},{12... | collective-permute-start | bytes 589832 | tf_op jit(solution)/shard_map/ppermute | solution.py:876
  564.4 8.2 %collective-permute-start.49 = (bf16[64,512]{1,0:T(8,128)(2,1)S(1)}, bf16[64,512]{1,0:T(8,128)(2,1)S(1)}, u32[]{:S(2)}, u32[]{:S(2)}) collective-permute-start(bf16[64,512]{1,0:T(8,128)(2,1)S(1)} %get-tuple-element.233), channel_id=1, source_target_pairs={{0,8},{8,16},{16,24},{24,0},{1,9},{9,17},{17,25},{25,1},{2,10},{10... | collective-permute-start | bytes 196616 | tf_op jit(solution)/shard_map/ppermute | solution.py:891
  564.5 8.1 %collective-permute-start.50 = (bf16[64,512]{1,0:T(8,128)(2,1)S(1)}, bf16[64,512]{1,0:T(8,128)(2,1)S(1)}, u32[]{:S(2)}, u32[]{:S(2)}) collective-permute-start(bf16[64,512]{1,0:T(8,128)(2,1)S(1)} %get-tuple-element.234), channel_id=1, source_target_pairs={{0,16},{8,24},{16,0},{24,8},{1,17},{9,25},{17,1},{25,9},{2,18},{10... | collective-permute-start | bytes 196616 | tf_op jit(solution)/shard_map/ppermute | solution.py:891
  565.9 6.7 %collective-permute-start.51 = (bf16[64,512]{1,0:T(8,128)(2,1)S(1)}, bf16[64,512]{1,0:T(8,128)(2,1)S(1)}, u32[]{:S(2)}, u32[]{:S(2)}) collective-permute-start(bf16[64,512]{1,0:T(8,128)(2,1)S(1)} %get-tuple-element.235), channel_id=1, source_target_pairs={{0,24},{8,0},{16,8},{24,16},{1,25},{9,1},{17,9},{25,17},{2,26},{10... | collective-permute-start | bytes 196616 | tf_op jit(solution)/shard_map/ppermute | solution.py:891
  (78 other events, 421.2 us)
Sparse Core Ops, SparseCore 0:
  58.4 46.5 all-gather.4
  128.1 109.0 all-gather.6
  330.1 138.9 reduce-scatter.2
  472.4 63.2 reduce-scatter.4

commit v2 on v1

--- a/solution.py
+++ b/solution.py
@@ -525,7 +525,7 @@
     )
 
 
-def gateup_chunk(parts, weight, grad, index, hidden, news):
+def gateup_chunk(parts, weight, grad, hidden):
     part, width = parts[0].shape
     rows = part * len(parts)
     cols, dp, _, _ = weight.shape
@@ -552,7 +552,7 @@
             out[:, j * 256 + 128 : j * 256 + 256] = (g * silu).astype(BF)
 
     def place(c, t):
-        return (index, c * steps + t)
+        return (0, c * steps + t)
 
     total = grad.shape[0]
     return call(
@@ -568,18 +568,18 @@
         ],
         [blocked((rows, half), place), blocked((rows, COLUMNS), place)],
         scratch=[pltpu.VMEM((rows, width), BF)],
-        alias=dict(enumerate(news or ())),
-    )
-
-
-def gateup_back(grad, weight, index, kinds):
+        vmem=24,
+    )
+
+
+def gateup_back(grad, weight, kinds):
     cols, dp, _, _ = weight.shape
     both = grad.shape[1]
     block = MODEL_WIDTH // dp
     terms = both // COLUMNS
     per = terms // cols
-    part = grad.shape[0] // 4
-    rows = part * len(kinds)
+    rows = grad.shape[0]
+    part = rows // len(kinds)
 
     def kernel(grad, weight, *outs):
         total = None
@@ -597,10 +597,11 @@
         (),
         (dp,),
         [
-            blocked((rows, both), lambda n: (index, 0)),
+            None,
             blocked((cols, 1, per * block, COLUMNS), lambda n: (0, n, 0, 0)),
         ],
         [blocked((part, block), lambda n: (0, n))] * len(kinds),
+        vmem=24,
     )
 
 
@@ -686,6 +687,7 @@
         (1,),
         [None] * (len(parts) + 3) + [blocked((rows, width), lambda i: (0, 0))],
         after=after,
+        hbm=2**17,
     )
 
 
@@ -1279,22 +1281,18 @@
         segment[:rows].reshape(1, rows),
     )
     mixed, logsum = attention_forward(*masks, query, keys_values, before, [])
-    out_low = assemble(out_chunks, z, True, False, [mixed])
-    hidden_pieces = mixed_parts(mixed, attention_full, z, output_base, [out_low])
+    hidden_pieces = mixed_parts(mixed, attention_full, z, output_base, out_chunks[1:])
+    out_low = assemble(out_chunks, z, True, False, hidden_pieces[1:2])
     hidden_parts, _ = scatter_pieces(hidden_pieces)
     hidden, second_scale, second_low = hidden_norm(hidden_parts, inputs, second_gain, z)
 
     second_chunks = gather_pieces(second_low)
-    active_grad = down_back(out_low, feed_full, down_base, down_inner, second_chunks[3:])
-    far_news = gateup_chunk(second_chunks[2:], feed_full, active_grad, 1, hidden_width, None)
-    far_parts = gateup_back(far_news[1], feed_full, 1, (BF, BF))
-    active, pair_grad = gateup_chunk(
-        second_chunks[:2], feed_full, active_grad, 0, hidden_width, far_news
-    )
-    near_parts = gateup_back(pair_grad, feed_full, 0, (F32, BF))
-    second_parts, sent = scatter_pieces(near_parts + far_parts)
+    active_grad = down_back(out_low, feed_full, down_base, down_inner, second_chunks[2:3])
+    active, pair_grad = gateup_chunk(second_chunks, feed_full, active_grad, hidden_width)
+    second_parts = gateup_back(pair_grad, feed_full, (F32, BF, BF, BF))
+    second_parts, sent = scatter_pieces(second_parts)
     feed_grads = weight_grads(
-        second_chunks, pair_grad, active, out_low, cols, [sent, *near_parts]
+        second_chunks, pair_grad, active, out_low, cols, [sent]
     )
     feed_grads, second_parts[1], second_parts[2] = lax.optimization_barrier(
         (feed_grads, second_parts[1], second_parts[2])
@@ -1368,14 +1366,14 @@
     )
     cut = [(t, 0, COLUMNS) for t in range(gateup_terms)]
     (gateup_total,) = place_columns(feed_messages, in_rows, [cut], z)
-    gateup_new, gateup_flat = update_pair(
+    gateup_new, _ = update_pair(
         (gateup_weight, gateup_moment, gateup_second), gateup_total, RATES[3]
     )
     input_grad = add_parts(input_parts, F32) - (
         first_scale * first_scale * first_scale * inner / MODEL_WIDTH
     ) * tokens.astype(F32)
     attention_messages = along_row(
-        split_shard(attention_total, 1, in_rows, output_inner, z, [gateup_flat]), False
+        split_shard(attention_total, 1, in_rows, output_inner, z), False
     )
     output_new = update_out(
         (output_weight, output_moment, output_second),

time: 592 us -> 585 us (0.988)
  starting transfers between devices: 87.2 us -> 102 us
  waiting for transfers between devices: 270 us -> 259 us
  Pallas kernels: 162 us -> 154 us
    ppermute x15, waiting for transfers between devices: 61 us -> 45 us  [along_row(): lax.ppermute(p, 'row', [(i, (i + sign * k) % size) for i in range(size)])]
    ppermute x29, starting transfers between devices: 43.9 us -> 52.4 us  [swap(): lax.ppermute(value, axis, [(i, i ^ step) for i in range(lax.axis_size(axi...]
    pallas_call x42 -> x40, Pallas kernels: 145 us -> 138 us  [call(): pl.pallas_call(run, grid_spec=pltpu.PrefetchScalarGridSpec(num_scalar_pre...]
    ppermute x15, starting transfers between devices: 29.2 us -> 35.3 us  [along_row(): lax.ppermute(p, 'row', [(i, (i + sign * k) % size) for i in range(size)])]
    unnamed x166 -> x154, local copies, waits for them, and re-layouts: 40.2 us -> 34.6 us
  transfers between devices with their start and end apart: 59 -> 59, of which waited for: 25 -> 27; matrix products, arithmetic and copies ran while one was open for 2% -> 2% of each run, Pallas kernels for 27% -> 22%
where the time goes in v2:
time: 585 us; the launch traced here: 576 us
  waiting for transfers between devices  259 us (44%)
  Pallas kernels  154 us (26%)
  starting transfers between devices  102 us (17%)
  local copies, waits for them, and re-layouts  39.1 us (7%)
  between operations  15.3 us (3%)
  other arithmetic  6.65 us (1%)
    ppermute x29, waiting for transfers between devices, swap(): lax.ppermute(value, axis, [(i, i ^ step) for i in range(lax.axis_size(axi...  180 us
    pallas_call x40, Pallas kernels, call(): pl.pallas_call(run, grid_spec=pltpu.PrefetchScalarGridSpec(num_scalar_pre...  138 us
    ppermute x29, starting transfers between devices, swap(): lax.ppermute(value, axis, [(i, i ^ step) for i in range(lax.axis_size(axi...  52.4 us
    ppermute x15, waiting for transfers between devices, along_row(): lax.ppermute(p, 'row', [(i, (i + sign * k) % size) for i in range(size)])  45 us
    ppermute x15, starting transfers between devices, along_row(): lax.ppermute(p, 'row', [(i, (i + sign * k) % size) for i in range(size)])  35.3 us
    unnamed x154, local copies, waits for them, and re-layouts  34.6 us
    ppermute x1, waiting for transfers between devices, body(): lax.ppermute(keys_values, 'col', [(i, i + 1) for i in range(cols - 1)])  14.9 us
  transfers between devices with their start and end apart: 59, of which 27 were waited for; matrix products, arithmetic and copies ran while one was open for 2% of the time, Pallas kernels for 22%

profile of v2, /device:TPU:0, one launch (start us, length us, event | category | flops | bytes accessed | tf_op | source)
XLA Modules:
  0.0 575.9 jit_solution(8814523686268066365)
XLA Ops:
  7.2 4.1 collective-permute-start.1
  11.3 2.4 shard_map.407
  13.8 2.3 shard_map.408
  20.6 3.5 collective-permute-done.6.refs_9_
  25.9 3.5 collective-permute-start.5
  34.0 12.0 %collective-permute-start.10 = (bf16[64,512]{1,0:T(8,128)(2,1)S(1)}, bf16[64,512]{1,0:T(8,128)(2,1)S(1)}, u32[]{:S(2)}, u32[]{:S(2)}) collective-permute-start(bf16[64,512]{1,0:T(8,128)(2,1)S(1)} %get-tuple-element.144), channel_id=1, source_target_pairs={{0,4},{2,6},{4,0},{6,2},{1,5},{3,7},{5,1},{7,3},{8,12},{10,14},{12... | collective-permute-start | bytes 196616 | tf_op jit(solution)/shard_map/ppermute | solution.py:878
  46.0 3.7 collective-permute-start.11
  49.7 3.1 shard_map.410
  55.4 2.1 shard_map.411.refs_5_
  59.4 2.9 collective-permute-start.14
  64.4 46.5 %collective-permute-done.refs_2_ = bf16[512,512]{1,0:T(8,128)(2,1)S(1)} collective-permute-done((bf16[512,512]{1,0:T(8,128)(2,1)S(1)}, bf16[512,512]{1,0:T(8,128)(2,1)S(1)}, u32[]{:S(2)}, u32[]{:S(2)}) %collective-permute-start) | collective-permute-done | bytes 524320 | tf_op jit(solution)/shard_map/ppermute | solution.py:844
  111.0 11.1 %collective-permute-done.2.refs_4_ = bf16[512,512]{1,0:T(8,128)(2,1)S(1)} collective-permute-done((bf16[512,512]{1,0:T(8,128)(2,1)}, bf16[512,512]{1,0:T(8,128)(2,1)S(1)}, u32[]{:S(2)}, u32[]{:S(2)}) %collective-permute-start.2) | collective-permute-done | bytes 524320 | tf_op jit(solution)/shard_map/ppermute | solution.py:844
  122.1 2.2 shard_map.412.refs_5_.refs_0_.refs_4_.refs_3_
  125.7 1.6 shard_map.413.refs_2_
  133.7 7.8 %shard_map.415 = (bf16[512,2048]{1,0:T(8,128)(2,1)S(1)}, f32[512,1]{1,0:T(8,128)S(1)}, f32[512,512]{1,0:T(8,128)S(1)}, f32[512,256]{1,0:T(8,128)S(1)}, bf16[512,...) custom-call(bf16[512,2048]{1,0:T(8,128)(2,1)S(1)} %copy-done.1, f32[1,2048]{1,0:T(1,128)S(1)} %bitcast.113, ...), custom_call_target="tpu_custom_call" | custom-call | tf_op jit(solution)/shard_map/pallas_call | solution.py:215
  146.2 3.6 collective-permute-start.15
  149.9 6.5 %collective-permute-done.17.refs_4_.refs_3_ = bf16[512,512]{1,0:T(8,128)(2,1)} collective-permute-done((bf16[512,512]{1,0:T(8,128)(2,1)}, bf16[512,512]{1,0:T(8,128)(2,1)}, u32[]{:S(2)}, u32[]{:S(2)}) %collective-permute-start.17) | collective-permute-done | bytes 524320 | tf_op jit(solution)/shard_map/ppermute | solution.py:844
  157.3 14.9 %collective-permute-done.15.refs_7_.refs_8_ = bf16[512,512]{1,0:T(8,128)(2,1)S(1)} collective-permute-done((bf16[512,512]{1,0:T(8,128)(2,1)S(1)}, bf16[512,512]{1,0:T(8,128)(2,1)S(1)}, u32[]{:S(2)}, u32[]{:S(2)}) %collective-permute-start.15) | collective-permute-done | bytes 524320 | tf_op jit(solution)/shard_map/ppermute | solution.py:1276
  174.2 7.3 %shard_map.416 = (bf16[512,512]{1,0:T(8,128)(2,1)S(1)}, f32[4,512,1]{2,1,0:T(8,128)S(1)}) custom-call(s32[1]{0:T(128)} %bitcast.1.refs_0_, s32[512,1]{1,0:T(8,128)S(1)} %copy-done.16, s32[1,512]{1,0:T(1,128)S(1)} %bitcast.116, s32[1,512]{1,0:T(1,128)S(1)} %bitcast.118, bf16[512,512]{1,0:T(8,128)(2,1)S(1)} %copy-done.24, ...), custom_call_target="tpu_custom_call" | custom-call | tf_op jit(solution)/shard_map/pallas_call | solution.py:93
  181.6 4.3 shard_map.417
  186.0 11.8 %collective-permute-done.19.refs_1_ = bf16[128,2048]{1,0:T(8,128)(2,1)S(1)} collective-permute-done((bf16[128,2048]{1,0:T(8,128)(2,1)S(1)}, bf16[128,2048]{1,0:T(8,128)(2,1)S(1)}, u32[]{:S(2)}, u32[]{:S(2)}) %collective-permute-start.19) | collective-permute-done | bytes 524320 | tf_op jit(solution)/shard_map/ppermute | solution.py:844
  198.0 3.0 collective-permute-start.21
  201.1 18.8 %collective-permute-done.20.refs_2_ = bf16[128,2048]{1,0:T(8,128)(2,1)S(1)} collective-permute-done((bf16[128,2048]{1,0:T(8,128)(2,1)S(1)}, bf16[128,2048]{1,0:T(8,128)(2,1)S(1)}, u32[]{:S(2)}, u32[]{:S(2)}) %collective-permute-start.20) | collective-permute-done | bytes 524320 | tf_op jit(solution)/shard_map/ppermute | solution.py:844
  223.3 16.4 %collective-permute-start.22 = (bf16[128,2048]{1,0:T(8,128)(2,1)}, bf16[128,2048]{1,0:T(8,128)(2,1)}, u32[]{:S(2)}, u32[]{:S(2)}) collective-permute-start(bf16[128,2048]{1,0:T(8,128)(2,1)} %get-tuple-element.163.refs_0_), channel_id=1, source_target_pairs={{0,2},{2,0},{4,6},{6,4},{1,3},{3,1},{5,7},{7,5},{8,10},{10,8},{12,... | collective-permute-start | bytes 1572872 | tf_op jit(solution)/shard_map/ppermute | solution.py:844
  240.3 9.6 %collective-permute-start.24 = (bf16[128,2048]{1,0:T(8,128)(2,1)}, bf16[128,2048]{1,0:T(8,128)(2,1)}, u32[]{:S(2)}, u32[]{:S(2)}) collective-permute-start(bf16[128,2048]{1,0:T(8,128)(2,1)} %collective-permute-done.23.refs_2_), channel_id=1, source_target_pairs={{0,2},{2,0},{4,6},{6,4},{1,3},{3,1},{5,7},{7,5},{8,10},{10,8},{12,... | collective-permute-start | bytes 1572872 | tf_op jit(solution)/shard_map/ppermute | solution.py:844
  249.9 2.6 shard_map.420.refs_0_.refs_6_
  255.5 6.8 %shard_map.421.refs_5_ = f32[512,1536]{1,0:T(8,128)S(1)} custom-call(bf16[512,2048]{1,0:T(8,128)(2,1)S(1)} %copy-done.3, bf16[2,4,2304,512]{3,2,1,0:T(8,128)(2,1)} %bitcast.121, bf16[128,2048]{1,0:T(8,128)(2,1)} %collective-permute-done.23.refs_2_), custom_call_target="tpu_custom_call" | custom-call | tf_op jit(solution)/shard_map/pallas_call | solution.py:215
  262.3 11.6 %shard_map.422 = (bf16[512,1536]{1,0:T(8,128)(2,1)S(1)}, bf16[512,3072]{1,0:T(8,128)(2,1)S(1)}) custom-call(bf16[128,2048]{1,0:T(8,128)(2,1)} %get-tuple-element.163.refs_0_, bf16[128,2048]{1,0:T(8,128)(2,1)} %collective-permute-done.22.refs_1_, bf16[128,2048]{1,0:T(8,128)(2,1)} %collective-permute-done.23.refs_2_, ...), custom_call_target="tpu_custom_call" | custom-call | tf_op jit(solution)/shard_map/pallas_call | solution.py:215
  273.9 10.0 %shard_map.423 = (f32[128,2048]{1,0:T(8,128)S(1)}, bf16[128,2048]{1,0:T(8,128)(2,1)S(1)}, bf16[128,2048]{1,0:T(8,128)(2,1)S(1)}, bf16[128,2048]{1,0:T(8,128)(2,1)S(1)}) custom-call(bf16[512,3072]{1,0:T(8,128)(2,1)S(1)} %get-tuple-element.166.refs_0_.refs_4_, bf16[2,4,2304,512]{3,2,1,0:T(8,128)(2,1)} %bitcast.123), custom_call_target="tpu_custom_call" | custom-call | tf_op jit(solution)/shard_map/pallas_call | solution.py:215
  284.0 17.9 %collective-permute-done.25.refs_1_ = bf16[128,2048]{1,0:T(8,128)(2,1)S(1)} collective-permute-done((bf16[128,2048]{1,0:T(8,128)(2,1)S(1)}, bf16[128,2048]{1,0:T(8,128)(2,1)S(1)}, u32[]{:S(2)}, u32[]{:S(2)}) %collective-permute-start.25) | collective-permute-done | bytes 524320 | tf_op jit(solution)/shard_map/ppermute | solution.py:844
  302.1 2.3 collective-permute-start.27
  304.3 16.6 %shard_map.425.refs_7_ = bf16[2,4,2304,512]{3,2,1,0:T(8,128)(2,1)} custom-call(bf16[128,2048]{1,0:T(8,128)(2,1)} %get-tuple-element.163.refs_0_, bf16[128,2048]{1,0:T(8,128)(2,1)} %collective-permute-done.22.refs_1_, bf16[128,2048]{1,0:T(8,128)(2,1)} %collective-permute-done.23.refs_2_, bf16[128,2048]{1,0:T(8,128)(2,1)} %collective-permute-done.24.refs_3_, ...), custom_call_target="tpu_custom_call" | custom-call | tf_op jit(solution)/shard_map/pallas_call | solution.py:215
  321.0 3.1 collective-permute-done.27.refs_2_
  325.2 2.8 shard_map.426
  328.1 2.5 collective-permute-start.28
  330.5 12.8 %collective-permute-done.29.refs_3_ = bf16[128,2048]{1,0:T(8,128)(2,1)S(1)} collective-permute-done((bf16[128,2048]{1,0:T(8,128)(2,1)S(1)}, bf16[128,2048]{1,0:T(8,128)(2,1)S(1)}, u32[]{:S(2)}, u32[]{:S(2)}) %collective-permute-start.29) | collective-permute-done | bytes 524320 | tf_op jit(solution)/shard_map/ppermute | solution.py:844
  343.4 6.7 %shard_map.427.refs_6_.refs_1_ = bf16[512,2048]{1,0:T(8,128)(2,1)S(1)} custom-call(bf16[512,1536]{1,0:T(8,128)(2,1)S(1)} %copy-done.11, f32[128,2048]{1,0:T(8,128)S(1)} %copy-done.13, bf16[2,4,2304,512]{3,2,1,0:T(8,128)(2,1)} %bitcast.124, bf16[128,2048]{1,0:T(8,128)(2,1)S(1)} %get-tuple-element.177.refs_3_.refs_1_), custom_call_target="tpu_custom_call" | custom-call | tf_op jit(solution)/shard_map/pallas_call | solution.py:215
  351.4 2.7 collective-permute-done.30.refs_4_
  354.1 4.1 shard_map.428
  361.0 9.2 %shard_map.432 = (f32[512,512]{1,0:T(8,128)S(1)}, f32[512,256]{1,0:T(8,128)S(1)}, f32[512,256]{1,0:T(8,128)S(1)}, bf16[512,512]{1,0:T(8,128)(2,1)S(1)}) custom-call(s32[1]{0:T(128)} %bitcast.1.refs_0_, s32[512,1]{1,0:T(8,128)S(1)} %copy-done.17, s32[1,512]{1,0:T(1,128)S(1)} %bitcast.117, s32[1,512]{1,0:T(1,128)S(1)} %bitcast.119, ...), custom_call_target="tpu_custom_call" | custom-call | tf_op jit(solution)/shard_map/pallas_call | solution.py:163
  370.3 6.7 %collective-permute-done.31.refs_1_ = bf16[512,512]{1,0:T(8,128)(2,1)S(1)} collective-permute-done((bf16[512,512]{1,0:T(8,128)(2,1)S(1)}, bf16[512,512]{1,0:T(8,128)(2,1)S(1)}, u32[]{:S(2)}, u32[]{:S(2)}) %collective-permute-start.31) | collective-permute-done | bytes 524320 | tf_op jit(solution)/shard_map/ppermute | solution.py:844
  377.2 2.6 collective-permute-start.33
  381.1 10.0 %collective-permute-done.32.refs_1_ = bf16[512,512]{1,0:T(8,128)(2,1)S(1)} collective-permute-done((bf16[512,512]{1,0:T(8,128)(2,1)S(1)}, bf16[512,512]{1,0:T(8,128)(2,1)S(1)}, u32[]{:S(2)}, u32[]{:S(2)}) %collective-permute-start.32) | collective-permute-done | bytes 524320 | tf_op jit(solution)/shard_map/ppermute | solution.py:844
  391.1 1.9 collective-permute-done.33.refs_2_
  394.2 10.5 %collective-permute-done.34.refs_5_ = bf16[512,512]{1,0:T(8,128)(2,1)S(1)} collective-permute-done((bf16[512,512]{1,0:T(8,128)(2,1)S(1)}, bf16[512,512]{1,0:T(8,128)(2,1)S(1)}, u32[]{:S(2)}, u32[]{:S(2)}) %collective-permute-start.34) | collective-permute-done | bytes 524320 | tf_op jit(solution)/shard_map/ppermute | solution.py:1313
  404.8 2.6 shard_map.433
  407.4 9.7 %shard_map.434.refs_7_ = bf16[2,4,768,512]{3,2,1,0:T(8,128)(2,1)} custom-call(bf16[512,2048]{1,0:T(8,128)(2,1)S(1)} %copy-done.29, bf16[512,1024]{1,0:T(8,128)(2,1)S(1)} %get-tuple-element.193.refs_1_, bf16[512,512]{1,0:T(8,128)(2,1)S(1)} %copy-done.22, bf16[512,2048]{1,0:T(8,128)(2,1)S(1)} %copy-done.9), custom_call_target="tpu_custom_call" | custom-call | tf_op jit(solution)/shard_map/pallas_call | solution.py:215
  417.2 5.8 %shard_map.435 = (bf16[512,2048]{1,0:T(8,128)(2,1)S(1)}, f32[512,1]{1,0:T(8,128)S(1)}, f32[1,2048]{1,0:T(1,128)S(1)}) custom-call(s32[1]{0:T(128)} %bitcast.refs_0_, bf16[512,1024]{1,0:T(8,128)(2,1)S(1)} %get-tuple-element.193.refs_1_, bf16[2,4,768,512]{3,2,1,0:T(8,128)(2,1)} %bitcast.129, bf16[512,2048]{1,0:T(8,128)(2,1)S(1)} %copy-done.1, ...), custom_call_target="tpu_custom_call" | custom-call | tf_op jit(solution)/shard_map/pallas_call | solution.py:215
  425.0 1.7 collective-permute-start.38
  426.7 17.0 %collective-permute-done.38 = f32[38,128]{1,0:T(8,128)S(1)} collective-permute-done((f32[38,128]{1,0:T(8,128)S(1)}, f32[38,128]{1,0:T(8,128)S(1)}, u32[]{:S(2)}, u32[]{:S(2)}) %collective-permute-start.38) | collective-permute-done | bytes 19488 | tf_op jit(solution)/shard_map/ppermute | solution.py:844
  443.9 1.9 collective-permute-start.36
  451.1 2.8 collective-permute-done.41
  453.9 4.2 collective-permute-done.42
  459.4 2.1 collective-permute-done.37.refs_2_
  462.3 1.6 copy-done.18
  465.4 2.5 collective-permute-start.49
  473.6 8.4 %collective-permute-done.49.refs_2_ = bf16[576,512]{1,0:T(8,128)(2,1)S(1)} collective-permute-done((bf16[576,512]{1,0:T(8,128)(2,1)}, bf16[576,512]{1,0:T(8,128)(2,1)S(1)}, u32[]{:S(2)}, u32[]{:S(2)}) %collective-permute-start.49) | collective-permute-done | bytes 589856 | tf_op jit(solution)/shard_map/ppermute | solution.py:878
  482.0 36.6 %collective-permute-done.50.refs_3_ = bf16[576,512]{1,0:T(8,128)(2,1)S(1)} collective-permute-done((bf16[576,512]{1,0:T(8,128)(2,1)}, bf16[576,512]{1,0:T(8,128)(2,1)S(1)}, u32[]{:S(2)}, u32[]{:S(2)}) %collective-permute-start.50) | collective-permute-done | bytes 589856 | tf_op jit(solution)/shard_map/ppermute | solution.py:878
  523.8 4.4 reduce-scatter.5.cloned.1.call-done.refs_1_
  530.1 4.8 collective-permute-start.43
  540.6 8.2 %shard_map.446 = (f32[6144,128]{1,0:T(8,128)}, f32[6144,128]{1,0:T(8,128)}, f32[6144,128]{1,0:T(8,128)}) custom-call(bf16[6144,128]{1,0:T(8,128)(2,1)} %reshape.307.refs_0_, f32[6144,128]{1,0:T(8,128)} %bitcast.110, f32[6144,128]{1,0:T(8,128)} %bitcast.131, f32[6144,128]{1,0:T(8,128)} %bitcast.132), custom_call_target="tpu_custom_call" | custom-call | tf_op jit(solution)/shard_map/pallas_call | solution.py:215
  548.9 6.1 %shard_map.448 = (f32[768,512]{1,0:T(8,128)}, f32[768,512]{1,0:T(8,128)}, f32[768,512]{1,0:T(8,128)}) custom-call(s32[1]{0:T(128)} %bitcast.15.refs_0_, bf16[192,512]{1,0:T(8,128)(2,1)S(1)} %copy-done.56, bf16[192,512]{1,0:T(8,128)(2,1)S(1)} %copy-done.58, bf16[192,512]{1,0:T(8,128)(2,1)} %collective-permute-done.53.refs_3_, ...), custom_call_target="tpu_custom_call" | custom-call | tf_op jit(solution)/shard_map/pallas_call | solution.py:215
  561.3 3.7 shard_map.441
  565.0 3.9 shard_map.443
  (301 shorter events, 83.7 us)
Async XLA Ops:
  7.2 126.5 %all-gather.5.cloned.1.call-start = ((), (), s32[]{:S(2)}) async-start(), calls=%async_computation.4 | async-start | bytes 7077888 | tf_op jit(solution)/shard_map/all_gather | solution.py:897
  7.2 48.1 %collective-permute-start.1 = (bf16[512,512]{1,0:T(8,128)(2,1)}, bf16[512,512]{1,0:T(8,128)(2,1)}, u32[]{:S(2)}, u32[]{:S(2)}) collective-permute-start(bf16[512,512]{1,0:T(8,128)(2,1)} %refs_1_.7), channel_id=1, source_target_pairs={{0,4},{2,6},{4,0},{6,2},{1,5},{3,7},{5,1},{7,3},{8,12},{10,14},{12... | collective-permute-start | bytes 1572872 | tf_op jit(solution)/shard_map/ppermute | solution.py:844
  11.3 38.4 %copy-start.7 = (f32[128,2,3072]{2,1,0:T(2,128)S(1)}, f32[128,2,3072]{2,1,0:T(2,128)}, u32[]{:S(2)}) copy-start(f32[128,2,3072]{2,1,0:T(2,128)} %refs_1_.6) | copy-start | bytes 9437188
  16.1 8.1 %collective-permute-start.6 = (bf16[256,512]{1,0:T(8,128)(2,1)S(1)}, bf16[256,512]{1,0:T(8,128)(2,1)S(1)}, u32[]{:S(2)}, u32[]{:S(2)}) collective-permute-start(bf16[256,512]{1,0:T(8,128)(2,1)S(1)} %get-tuple-element.139), channel_id=1, source_target_pairs={{0,8},{8,16},{16,24},{24,0},{1,9},{9,17},{17,25},{25,1},{2,10},{10... | collective-permute-start | bytes 786440 | tf_op jit(solution)/shard_map/ppermute | solution.py:893
  16.1 9.2 %collective-permute-start.7 = (bf16[256,512]{1,0:T(8,128)(2,1)S(1)}, bf16[256,512]{1,0:T(8,128)(2,1)S(1)}, u32[]{:S(2)}, u32[]{:S(2)}) collective-permute-start(bf16[256,512]{1,0:T(8,128)(2,1)S(1)} %get-tuple-element.140), channel_id=1, source_target_pairs={{0,16},{8,24},{16,0},{24,8},{1,17},{9,25},{17,1},{25,9},{2,18},{10... | collective-permute-start | bytes 786440 | tf_op jit(solution)/shard_map/ppermute | solution.py:893
  17.6 11.9 %collective-permute-start.8 = (bf16[256,512]{1,0:T(8,128)(2,1)}, bf16[256,512]{1,0:T(8,128)(2,1)}, u32[]{:S(2)}, u32[]{:S(2)}) collective-permute-start(bf16[256,512]{1,0:T(8,128)(2,1)} %get-tuple-element.141), channel_id=1, source_target_pairs={{0,24},{8,0},{16,8},{24,16},{1,25},{9,1},{17,9},{25,17},{2,26},{10... | collective-permute-start | bytes 786440 | tf_op jit(solution)/shard_map/ppermute | solution.py:893
  19.0 15.0 %collective-permute-start.3 = (bf16[128,512]{1,0:T(8,128)(2,1)}, bf16[128,512]{1,0:T(8,128)(2,1)}, u32[]{:S(2)}, u32[]{:S(2)}) collective-permute-start(bf16[128,512]{1,0:T(8,128)(2,1)} %get-tuple-element.135), channel_id=1, source_target_pairs={{0,2},{2,4},{4,6},{6,0},{1,3},{3,5},{5,7},{7,1},{8,10},{10,12},{12... | collective-permute-start | bytes 393224 | tf_op jit(solution)/shard_map/ppermute | solution.py:878
  24.8 21.2 %collective-permute-start.4 = (bf16[128,512]{1,0:T(8,128)(2,1)}, bf16[128,512]{1,0:T(8,128)(2,1)}, u32[]{:S(2)}, u32[]{:S(2)}) collective-permute-start(bf16[128,512]{1,0:T(8,128)(2,1)} %get-tuple-element.136), channel_id=1, source_target_pairs={{0,4},{2,6},{4,0},{6,2},{1,5},{3,7},{5,1},{7,3},{8,12},{10,14},{12... | collective-permute-start | bytes 393224 | tf_op jit(solution)/shard_map/ppermute | solution.py:878
  25.9 29.4 %collective-permute-start.5 = (bf16[128,512]{1,0:T(8,128)(2,1)}, bf16[128,512]{1,0:T(8,128)(2,1)}, u32[]{:S(2)}, u32[]{:S(2)}) collective-permute-start(bf16[128,512]{1,0:T(8,128)(2,1)} %get-tuple-element.137), channel_id=1, source_target_pairs={{0,6},{2,0},{4,2},{6,4},{1,7},{3,1},{5,3},{7,5},{8,14},{10,8},{12,... | collective-permute-start | bytes 393224 | tf_op jit(solution)/shard_map/ppermute | solution.py:878
  32.5 22.9 %collective-permute-start.9 = (bf16[64,512]{1,0:T(8,128)(2,1)S(1)}, bf16[64,512]{1,0:T(8,128)(2,1)S(1)}, u32[]{:S(2)}, u32[]{:S(2)}) collective-permute-start(bf16[64,512]{1,0:T(8,128)(2,1)S(1)} %get-tuple-element.143), channel_id=1, source_target_pairs={{0,2},{2,4},{4,6},{6,0},{1,3},{3,5},{5,7},{7,1},{8,10},{10,12},{12... | collective-permute-start | bytes 196616 | tf_op jit(solution)/shard_map/ppermute | solution.py:878
  34.0 21.3 %collective-permute-start.10 = (bf16[64,512]{1,0:T(8,128)(2,1)S(1)}, bf16[64,512]{1,0:T(8,128)(2,1)S(1)}, u32[]{:S(2)}, u32[]{:S(2)}) collective-permute-start(bf16[64,512]{1,0:T(8,128)(2,1)S(1)} %get-tuple-element.144), channel_id=1, source_target_pairs={{0,4},{2,6},{4,0},{6,2},{1,5},{3,7},{5,1},{7,3},{8,12},{10,14},{12... | collective-permute-start | bytes 196616 | tf_op jit(solution)/shard_map/ppermute | solution.py:878
  46.0 9.3 %collective-permute-start.11 = (bf16[64,512]{1,0:T(8,128)(2,1)S(1)}, bf16[64,512]{1,0:T(8,128)(2,1)S(1)}, u32[]{:S(2)}, u32[]{:S(2)}) collective-permute-start(bf16[64,512]{1,0:T(8,128)(2,1)S(1)} %get-tuple-element.145), channel_id=1, source_target_pairs={{0,6},{2,0},{4,2},{6,4},{1,7},{3,1},{5,3},{7,5},{8,14},{10,8},{12,... | collective-permute-start | bytes 196616 | tf_op jit(solution)/shard_map/ppermute | solution.py:878
  58.4 195.5 %all-gather.7.cloned.1.call-start = ((), (), s32[]{:S(2)}) async-start(), calls=%async_computation.5 | async-start | bytes 21233664 | tf_op jit(solution)/shard_map/all_gather | solution.py:897
  58.4 67.2 %collective-permute-start.12 = (bf16[576,512]{1,0:T(8,128)(2,1)S(1)}, bf16[576,512]{1,0:T(8,128)(2,1)S(1)}, u32[]{:S(2)}, u32[]{:S(2)}) collective-permute-start(bf16[576,512]{1,0:T(8,128)(2,1)S(1)} %copy-done.65), channel_id=1, source_target_pairs={{0,2},{2,4},{4,6},{6,0},{1,3},{3,5},{5,7},{7,1},{8,10},{10,12},{12... | collective-permute-start | bytes 1769480 | tf_op jit(solution)/shard_map/ppermute | solution.py:878
  58.5 67.1 %collective-permute-start.13 = (bf16[576,512]{1,0:T(8,128)(2,1)S(1)}, bf16[576,512]{1,0:T(8,128)(2,1)S(1)}, u32[]{:S(2)}, u32[]{:S(2)}) collective-permute-start(bf16[576,512]{1,0:T(8,128)(2,1)S(1)} %copy-done.63), channel_id=1, source_target_pairs={{0,4},{2,6},{4,0},{6,2},{1,5},{3,7},{5,1},{7,3},{8,12},{10,14},{12... | collective-permute-start | bytes 1769480 | tf_op jit(solution)/shard_map/ppermute | solution.py:878
  59.4 66.2 %copy-start.20 = (bf16[576,512]{1,0:T(8,128)(2,1)S(1)}, bf16[576,512]{1,0:T(8,128)(2,1)}, u32[]{:S(2)}) copy-start(bf16[576,512]{1,0:T(8,128)(2,1)} %copy-done.19) | copy-start | bytes 1769476
  59.4 66.2 %collective-permute-start.14 = (bf16[576,512]{1,0:T(8,128)(2,1)S(1)}, bf16[576,512]{1,0:T(8,128)(2,1)S(1)}, u32[]{:S(2)}, u32[]{:S(2)}) collective-permute-start(bf16[576,512]{1,0:T(8,128)(2,1)S(1)} %copy-done.61), channel_id=1, source_target_pairs={{0,6},{2,0},{4,2},{6,4},{1,7},{3,1},{5,3},{7,5},{8,14},{10,8},{12,... | collective-permute-start | bytes 1769480 | tf_op jit(solution)/shard_map/ppermute | solution.py:878
  62.4 48.6 %collective-permute-start = (bf16[512,512]{1,0:T(8,128)(2,1)S(1)}, bf16[512,512]{1,0:T(8,128)(2,1)S(1)}, u32[]{:S(2)}, u32[]{:S(2)}) collective-permute-start(bf16[512,512]{1,0:T(8,128)(2,1)S(1)} %copy-done.26), channel_id=1, source_target_pairs={{0,2},{2,0},{4,6},{6,4},{1,3},{3,1},{5,7},{7,5},{8,10},{10,8},{12,... | collective-permute-start | bytes 1572872 | tf_op jit(solution)/shard_map/ppermute | solution.py:844
  62.9 59.1 %collective-permute-start.2 = (bf16[512,512]{1,0:T(8,128)(2,1)}, bf16[512,512]{1,0:T(8,128)(2,1)S(1)}, u32[]{:S(2)}, u32[]{:S(2)}) collective-permute-start(bf16[512,512]{1,0:T(8,128)(2,1)} %collective-permute-done.1.refs_10_.refs_3_), channel_id=1, source_target_pairs={{0,2},{2,0},{4,6},{6,4},{1,3},{3,1},{5,7},{7,5},{8,10},{10,8},{12,... | collective-permute-start | bytes 1572872 | tf_op jit(solution)/shard_map/ppermute | solution.py:844
  127.3 335.0 %reduce-scatter.3.cloned.1.call-start = ((), (), s32[]{:S(2)}) async-start(), calls=%async_computation.2 | async-start | bytes 21233664 | tf_op jit(solution)/shard_map/reduce_scatter | solution.py:903
  130.9 25.5 %collective-permute-start.17 = (bf16[512,512]{1,0:T(8,128)(2,1)}, bf16[512,512]{1,0:T(8,128)(2,1)}, u32[]{:S(2)}, u32[]{:S(2)}) collective-permute-start(bf16[512,512]{1,0:T(8,128)(2,1)} %shard_map.414.refs_6_.refs_1_), channel_id=1, source_target_pairs={{0,4},{2,6},{4,0},{6,2},{1,5},{3,7},{5,1},{7,3},{8,12},{10,14},{12... | collective-permute-start | bytes 1572872 | tf_op jit(solution)/shard_map/ppermute | solution.py:844
  146.2 26.1 %collective-permute-start.15 = (bf16[512,512]{1,0:T(8,128)(2,1)S(1)}, bf16[512,512]{1,0:T(8,128)(2,1)S(1)}, u32[]{:S(2)}, u32[]{:S(2)}) collective-permute-start(bf16[512,512]{1,0:T(8,128)(2,1)S(1)} %get-tuple-element.155.refs_5_.refs_6_), channel_id=1, source_target_pairs={{0,1},{2,3},{4,5},{6,7},{8,9},{10,11},{12,13},{14,15},{16,17},{18,... | collective-permute-start | bytes 1572872 | tf_op jit(solution)/shard_map/ppermute | solution.py:1276
  149.8 31.8 %collective-permute-start.16 = (bf16[512,512]{1,0:T(8,128)(2,1)}, bf16[512,512]{1,0:T(8,128)(2,1)}, u32[]{:S(2)}, u32[]{:S(2)}) collective-permute-start(bf16[512,512]{1,0:T(8,128)(2,1)} %shard_map.414.refs_6_.refs_1_), channel_id=1, source_target_pairs={{0,2},{2,0},{4,6},{6,4},{1,3},{3,1},{5,7},{7,5},{8,10},{10,8},{12,... | collective-permute-start | bytes 1572872 | tf_op jit(solution)/shard_map/ppermute | solution.py:844
  156.4 25.1 %collective-permute-start.18 = (bf16[512,512]{1,0:T(8,128)(2,1)}, bf16[512,512]{1,0:T(8,128)(2,1)}, u32[]{:S(2)}, u32[]{:S(2)}) collective-permute-start(bf16[512,512]{1,0:T(8,128)(2,1)} %collective-permute-done.17.refs_4_.refs_3_), channel_id=1, source_target_pairs={{0,2},{2,0},{4,6},{6,4},{1,3},{3,1},{5,7},{7,5},{8,10},{10,8},{12,... | collective-permute-start | bytes 1572872 | tf_op jit(solution)/shard_map/ppermute | solution.py:844
  186.0 11.9 %collective-permute-start.19 = (bf16[128,2048]{1,0:T(8,128)(2,1)S(1)}, bf16[128,2048]{1,0:T(8,128)(2,1)S(1)}, u32[]{:S(2)}, u32[]{:S(2)}) collective-permute-start(bf16[128,2048]{1,0:T(8,128)(2,1)S(1)} %get-tuple-element.160), channel_id=1, source_target_pairs={{0,2},{2,0},{4,6},{6,4},{1,3},{3,1},{5,7},{7,5},{8,10},{10,8},{12,... | collective-permute-start | bytes 1572872 | tf_op jit(solution)/shard_map/ppermute | solution.py:844
  198.0 21.9 %collective-permute-start.20 = (bf16[128,2048]{1,0:T(8,128)(2,1)S(1)}, bf16[128,2048]{1,0:T(8,128)(2,1)S(1)}, u32[]{:S(2)}, u32[]{:S(2)}) collective-permute-start(bf16[128,2048]{1,0:T(8,128)(2,1)S(1)} %get-tuple-element.161.refs_5_), channel_id=1, source_target_pairs={{0,2},{2,0},{4,6},{6,4},{1,3},{3,1},{5,7},{7,5},{8,10},{10,8},{12,... | collective-permute-start | bytes 1572872 | tf_op jit(solution)/shard_map/ppermute | solution.py:844
  198.0 21.8 %collective-permute-start.21 = (bf16[128,2048]{1,0:T(8,128)(2,1)S(1)}, bf16[128,2048]{1,0:T(8,128)(2,1)S(1)}, u32[]{:S(2)}, u32[]{:S(2)}) collective-permute-start(bf16[128,2048]{1,0:T(8,128)(2,1)S(1)} %shard_map.418), channel_id=1, source_target_pairs={{0,4},{2,6},{4,0},{6,2},{1,5},{3,7},{5,1},{7,3},{8,12},{10,14},{12... | collective-permute-start | bytes 1572872 | tf_op jit(solution)/shard_map/ppermute | solution.py:844
  222.1 18.2 %collective-permute-start.23 = (bf16[128,2048]{1,0:T(8,128)(2,1)}, bf16[128,2048]{1,0:T(8,128)(2,1)}, u32[]{:S(2)}, u32[]{:S(2)}) collective-permute-start(bf16[128,2048]{1,0:T(8,128)(2,1)} %get-tuple-element.163.refs_0_), channel_id=1, source_target_pairs={{0,4},{2,6},{4,0},{6,2},{1,5},{3,7},{5,1},{7,3},{8,12},{10,14},{12... | collective-permute-start | bytes 1572872 | tf_op jit(solution)/shard_map/ppermute | solution.py:844
  223.3 38.9 %collective-permute-start.22 = (bf16[128,2048]{1,0:T(8,128)(2,1)}, bf16[128,2048]{1,0:T(8,128)(2,1)}, u32[]{:S(2)}, u32[]{:S(2)}) collective-permute-start(bf16[128,2048]{1,0:T(8,128)(2,1)} %get-tuple-element.163.refs_0_), channel_id=1, source_target_pairs={{0,2},{2,0},{4,6},{6,4},{1,3},{3,1},{5,7},{7,5},{8,10},{10,8},{12,... | collective-permute-start | bytes 1572872 | tf_op jit(solution)/shard_map/ppermute | solution.py:844
  240.3 22.0 %collective-permute-start.24 = (bf16[128,2048]{1,0:T(8,128)(2,1)}, bf16[128,2048]{1,0:T(8,128)(2,1)}, u32[]{:S(2)}, u32[]{:S(2)}) collective-permute-start(bf16[128,2048]{1,0:T(8,128)(2,1)} %collective-permute-done.23.refs_2_), channel_id=1, source_target_pairs={{0,2},{2,0},{4,6},{6,4},{1,3},{3,1},{5,7},{7,5},{8,10},{10,8},{12,... | collective-permute-start | bytes 1572872 | tf_op jit(solution)/shard_map/ppermute | solution.py:844
  273.9 30.5 %copy-start.10 = (bf16[512,1536]{1,0:T(8,128)(2,1)}, bf16[512,1536]{1,0:T(8,128)(2,1)S(1)}, u32[]{:S(2)}) copy-start(bf16[512,1536]{1,0:T(8,128)(2,1)S(1)} %get-tuple-element.164.refs_5_.refs_0_) | copy-start | bytes 4718596
  283.9 37.1 %copy-start.32 = (f32[128,2048]{1,0:T(8,128)}, f32[128,2048]{1,0:T(8,128)S(1)}, u32[]{:S(2)}) copy-start(f32[128,2048]{1,0:T(8,128)S(1)} %get-tuple-element.167.refs_0_) | copy-start | bytes 3145732
  283.9 17.9 %collective-permute-start.25 = (bf16[128,2048]{1,0:T(8,128)(2,1)S(1)}, bf16[128,2048]{1,0:T(8,128)(2,1)S(1)}, u32[]{:S(2)}, u32[]{:S(2)}) collective-permute-start(bf16[128,2048]{1,0:T(8,128)(2,1)S(1)} %get-tuple-element.170), channel_id=1, source_target_pairs={{0,2},{2,0},{4,6},{6,4},{1,3},{3,1},{5,7},{7,5},{8,10},{10,8},{12,... | collective-permute-start | bytes 1572872 | tf_op jit(solution)/shard_map/ppermute | solution.py:844
  302.0 19.0 %collective-permute-start.26 = (bf16[128,2048]{1,0:T(8,128)(2,1)S(1)}, bf16[128,2048]{1,0:T(8,128)(2,1)S(1)}, u32[]{:S(2)}, u32[]{:S(2)}) collective-permute-start(bf16[128,2048]{1,0:T(8,128)(2,1)S(1)} %get-tuple-element.172), channel_id=1, source_target_pairs={{0,2},{2,0},{4,6},{6,4},{1,3},{3,1},{5,7},{7,5},{8,10},{10,8},{12,... | collective-permute-start | bytes 1572872 | tf_op jit(solution)/shard_map/ppermute | solution.py:844
  302.1 22.0 %collective-permute-start.27 = (bf16[128,2048]{1,0:T(8,128)(2,1)S(1)}, bf16[128,2048]{1,0:T(8,128)(2,1)S(1)}, u32[]{:S(2)}, u32[]{:S(2)}) collective-permute-start(bf16[128,2048]{1,0:T(8,128)(2,1)S(1)} %shard_map.424.refs_7_), channel_id=1, source_target_pairs={{0,4},{2,6},{4,0},{6,2},{1,5},{3,7},{5,1},{7,3},{8,12},{10,14},{12... | collective-permute-start | bytes 1572872 | tf_op jit(solution)/shard_map/ppermute | solution.py:844
  324.9 203.2 %reduce-scatter.5.cloned.1.call-start = ((), (), s32[]{:S(2)}) async-start(), calls=%async_computation.3 | async-start | bytes 7077888 | tf_op jit(solution)/shard_map/reduce_scatter | solution.py:903
  328.0 15.4 %collective-permute-start.29 = (bf16[128,2048]{1,0:T(8,128)(2,1)S(1)}, bf16[128,2048]{1,0:T(8,128)(2,1)S(1)}, u32[]{:S(2)}, u32[]{:S(2)}) collective-permute-start(bf16[128,2048]{1,0:T(8,128)(2,1)S(1)} %get-tuple-element.177.refs_3_.refs_1_), channel_id=1, source_target_pairs={{0,4},{2,6},{4,0},{6,2},{1,5},{3,7},{5,1},{7,3},{8,12},{10,14},{12... | collective-permute-start | bytes 1572872 | tf_op jit(solution)/shard_map/ppermute | solution.py:844
  328.1 23.3 %collective-permute-start.28 = (bf16[128,2048]{1,0:T(8,128)(2,1)S(1)}, bf16[128,2048]{1,0:T(8,128)(2,1)S(1)}, u32[]{:S(2)}, u32[]{:S(2)}) collective-permute-start(bf16[128,2048]{1,0:T(8,128)(2,1)S(1)} %get-tuple-element.177.refs_3_.refs_1_), channel_id=1, source_target_pairs={{0,2},{2,0},{4,6},{6,4},{1,3},{3,1},{5,7},{7,5},{8,10},{10,8},{12,... | collective-permute-start | bytes 1572872 | tf_op jit(solution)/shard_map/ppermute | solution.py:844
  343.3 10.8 %collective-permute-start.30 = (bf16[128,2048]{1,0:T(8,128)(2,1)S(1)}, bf16[128,2048]{1,0:T(8,128)(2,1)S(1)}, u32[]{:S(2)}, u32[]{:S(2)}) collective-permute-start(bf16[128,2048]{1,0:T(8,128)(2,1)S(1)} %collective-permute-done.29.refs_3_), channel_id=1, source_target_pairs={{0,2},{2,0},{4,6},{6,4},{1,3},{3,1},{5,7},{7,5},{8,10},{10,8},{12,... | collective-permute-start | bytes 1572872 | tf_op jit(solution)/shard_map/ppermute | solution.py:844
  360.2 16.8 %collective-permute-start.31 = (bf16[512,512]{1,0:T(8,128)(2,1)S(1)}, bf16[512,512]{1,0:T(8,128)(2,1)S(1)}, u32[]{:S(2)}, u32[]{:S(2)}) collective-permute-start(bf16[512,512]{1,0:T(8,128)(2,1)S(1)} %get-tuple-element.182), channel_id=1, source_target_pairs={{0,2},{2,0},{4,6},{6,4},{1,3},{3,1},{5,7},{7,5},{8,10},{10,8},{12,... | collective-permute-start | bytes 1572872 | tf_op jit(solution)/shard_map/ppermute | solution.py:844
  377.1 14.0 %collective-permute-start.32 = (bf16[512,512]{1,0:T(8,128)(2,1)S(1)}, bf16[512,512]{1,0:T(8,128)(2,1)S(1)}, u32[]{:S(2)}, u32[]{:S(2)}) collective-permute-start(bf16[512,512]{1,0:T(8,128)(2,1)S(1)} %get-tuple-element.183), channel_id=1, source_target_pairs={{0,2},{2,0},{4,6},{6,4},{1,3},{3,1},{5,7},{7,5},{8,10},{10,8},{12,... | collective-permute-start | bytes 1572872 | tf_op jit(solution)/shard_map/ppermute | solution.py:844
  377.2 15.8 %collective-permute-start.33 = (bf16[512,512]{1,0:T(8,128)(2,1)S(1)}, bf16[512,512]{1,0:T(8,128)(2,1)S(1)}, u32[]{:S(2)}, u32[]{:S(2)}) collective-permute-start(bf16[512,512]{1,0:T(8,128)(2,1)S(1)} %shard_map.430), channel_id=1, source_target_pairs={{0,4},{2,6},{4,0},{6,2},{1,5},{3,7},{5,1},{7,3},{8,12},{10,14},{12... | collective-permute-start | bytes 1572872 | tf_op jit(solution)/shard_map/ppermute | solution.py:844
  379.8 25.0 %collective-permute-start.34 = (bf16[512,512]{1,0:T(8,128)(2,1)S(1)}, bf16[512,512]{1,0:T(8,128)(2,1)S(1)}, u32[]{:S(2)}, u32[]{:S(2)}) collective-permute-start(bf16[512,512]{1,0:T(8,128)(2,1)S(1)} %get-tuple-element.192), channel_id=1, source_target_pairs={{1,0},{3,2},{5,4},{7,6},{9,8},{11,10},{13,12},{15,14},{17,16},{19,... | collective-permute-start | bytes 1572872 | tf_op jit(solution)/shard_map/ppermute | solution.py:1313
  424.4 19.3 %collective-permute-start.35 = (bf16[512,512]{1,0:T(8,128)(2,1)S(1)}, bf16[512,512]{1,0:T(8,128)(2,1)S(1)}, u32[]{:S(2)}, u32[]{:S(2)}) collective-permute-start(bf16[512,512]{1,0:T(8,128)(2,1)S(1)} %get-tuple-element.206), channel_id=1, source_target_pairs={{0,2},{2,0},{4,6},{6,4},{1,3},{3,1},{5,7},{7,5},{8,10},{10,8},{12,... | collective-permute-start | bytes 1572872 | tf_op jit(solution)/shard_map/ppermute | solution.py:844
  425.0 18.7 %collective-permute-start.38 = (f32[38,128]{1,0:T(8,128)S(1)}, f32[38,128]{1,0:T(8,128)S(1)}, u32[]{:S(2)}, u32[]{:S(2)}) collective-permute-start(f32[38,128]{1,0:T(8,128)S(1)} %bitcast.136), channel_id=1, source_target_pairs={{0,2},{2,0},{4,6},{6,4},{1,3},{3,1},{5,7},{7,5},{8,10},{10,8},{12,... | collective-permute-start | bytes 58376 | tf_op jit(solution)/shard_map/ppermute | solution.py:844
  443.7 4.8 collective-permute-start.39
  443.9 14.7 %collective-permute-start.36 = (bf16[512,512]{1,0:T(8,128)(2,1)S(1)}, bf16[512,512]{1,0:T(8,128)(2,1)S(1)}, u32[]{:S(2)}, u32[]{:S(2)}) collective-permute-start(bf16[512,512]{1,0:T(8,128)(2,1)S(1)} %get-tuple-element.207), channel_id=1, source_target_pairs={{0,2},{2,0},{4,6},{6,4},{1,3},{3,1},{5,7},{7,5},{8,10},{10,8},{12,... | collective-permute-start | bytes 1572872 | tf_op jit(solution)/shard_map/ppermute | solution.py:844
  445.8 15.7 %collective-permute-start.37 = (bf16[512,512]{1,0:T(8,128)(2,1)S(1)}, bf16[512,512]{1,0:T(8,128)(2,1)S(1)}, u32[]{:S(2)}, u32[]{:S(2)}) collective-permute-start(bf16[512,512]{1,0:T(8,128)(2,1)S(1)} %shard_map.437), channel_id=1, source_target_pairs={{0,4},{2,6},{4,0},{6,2},{1,5},{3,7},{5,1},{7,3},{8,12},{10,14},{12... | collective-permute-start | bytes 1572872 | tf_op jit(solution)/shard_map/ppermute | solution.py:844
  448.5 1.2 collective-permute-start.40
  449.7 4.2 collective-permute-start.41
  453.9 4.2 collective-permute-start.42
  465.4 16.6 %collective-permute-start.49 = (bf16[576,512]{1,0:T(8,128)(2,1)}, bf16[576,512]{1,0:T(8,128)(2,1)S(1)}, u32[]{:S(2)}, u32[]{:S(2)}) collective-permute-start(bf16[576,512]{1,0:T(8,128)(2,1)} %get-tuple-element.231), channel_id=1, source_target_pairs={{0,6},{2,0},{4,2},{6,4},{1,7},{3,1},{5,3},{7,5},{8,14},{10,8},{12,... | collective-permute-start | bytes 1769480 | tf_op jit(solution)/shard_map/ppermute | solution.py:878
  467.9 50.7 %collective-permute-start.50 = (bf16[576,512]{1,0:T(8,128)(2,1)}, bf16[576,512]{1,0:T(8,128)(2,1)S(1)}, u32[]{:S(2)}, u32[]{:S(2)}) collective-permute-start(bf16[576,512]{1,0:T(8,128)(2,1)} %get-tuple-element.232), channel_id=1, source_target_pairs={{0,4},{2,6},{4,0},{6,2},{1,5},{3,7},{5,1},{7,3},{8,12},{10,14},{12... | collective-permute-start | bytes 1769480 | tf_op jit(solution)/shard_map/ppermute | solution.py:878
  467.9 50.7 %collective-permute-start.51 = (bf16[576,512]{1,0:T(8,128)(2,1)}, bf16[576,512]{1,0:T(8,128)(2,1)S(1)}, u32[]{:S(2)}, u32[]{:S(2)}) collective-permute-start(bf16[576,512]{1,0:T(8,128)(2,1)} %get-tuple-element.233), channel_id=1, source_target_pairs={{0,2},{2,4},{4,6},{6,0},{1,3},{3,5},{5,7},{7,1},{8,10},{10,12},{12... | collective-permute-start | bytes 1769480 | tf_op jit(solution)/shard_map/ppermute | solution.py:878
  472.8 47.0 %copy-start.27 = (bf16[512,512]{1,0:T(8,128)(2,1)S(1)}, bf16[512,512]{1,0:T(8,128)(2,1)}, u32[]{:S(2)}) copy-start(bf16[512,512]{1,0:T(8,128)(2,1)} %refs_1_.7) | copy-start | bytes 1572868
  519.5 15.4 %collective-permute-start.52 = (bf16[192,512]{1,0:T(8,128)(2,1)}, bf16[192,512]{1,0:T(8,128)(2,1)S(1)}, u32[]{:S(2)}, u32[]{:S(2)}) collective-permute-start(bf16[192,512]{1,0:T(8,128)(2,1)} %get-tuple-element.238), channel_id=1, source_target_pairs={{0,8},{8,16},{16,24},{24,0},{1,9},{9,17},{17,25},{25,1},{2,10},{10... | collective-permute-start | bytes 589832 | tf_op jit(solution)/shard_map/ppermute | solution.py:893
  520.9 27.8 %collective-permute-start.53 = (bf16[192,512]{1,0:T(8,128)(2,1)}, bf16[192,512]{1,0:T(8,128)(2,1)}, u32[]{:S(2)}, u32[]{:S(2)}) collective-permute-start(bf16[192,512]{1,0:T(8,128)(2,1)} %get-tuple-element.239), channel_id=1, source_target_pairs={{0,16},{8,24},{16,0},{24,8},{1,17},{9,25},{17,1},{25,9},{2,18},{10... | collective-permute-start | bytes 589832 | tf_op jit(solution)/shard_map/ppermute | solution.py:893
  522.3 26.5 %collective-permute-start.54 = (bf16[192,512]{1,0:T(8,128)(2,1)}, bf16[192,512]{1,0:T(8,128)(2,1)}, u32[]{:S(2)}, u32[]{:S(2)}) collective-permute-start(bf16[192,512]{1,0:T(8,128)(2,1)} %get-tuple-element.240), channel_id=1, source_target_pairs={{0,24},{8,0},{16,8},{24,16},{1,25},{9,1},{17,9},{25,17},{2,26},{10... | collective-permute-start | bytes 589832 | tf_op jit(solution)/shard_map/ppermute | solution.py:893
  530.1 24.8 %collective-permute-start.43 = (bf16[192,512]{1,0:T(8,128)(2,1)}, bf16[192,512]{1,0:T(8,128)(2,1)S(1)}, u32[]{:S(2)}, u32[]{:S(2)}) collective-permute-start(bf16[192,512]{1,0:T(8,128)(2,1)} %get-tuple-element.214), channel_id=1, source_target_pairs={{0,6},{2,0},{4,2},{6,4},{1,7},{3,1},{5,3},{7,5},{8,14},{10,8},{12,... | collective-permute-start | bytes 589832 | tf_op jit(solution)/shard_map/ppermute | solution.py:878
  534.9 20.1 %collective-permute-start.44 = (bf16[192,512]{1,0:T(8,128)(2,1)}, bf16[192,512]{1,0:T(8,128)(2,1)S(1)}, u32[]{:S(2)}, u32[]{:S(2)}) collective-permute-start(bf16[192,512]{1,0:T(8,128)(2,1)} %get-tuple-element.215), channel_id=1, source_target_pairs={{0,4},{2,6},{4,0},{6,2},{1,5},{3,7},{5,1},{7,3},{8,12},{10,14},{12... | collective-permute-start | bytes 589832 | tf_op jit(solution)/shard_map/ppermute | solution.py:878
  535.6 19.4 %collective-permute-start.45 = (bf16[192,512]{1,0:T(8,128)(2,1)}, bf16[192,512]{1,0:T(8,128)(2,1)}, u32[]{:S(2)}, u32[]{:S(2)}) collective-permute-start(bf16[192,512]{1,0:T(8,128)(2,1)} %get-tuple-element.216), channel_id=1, source_target_pairs={{0,2},{2,4},{4,6},{6,0},{1,3},{3,5},{5,7},{7,1},{8,10},{10,12},{12... | collective-permute-start | bytes 589832 | tf_op jit(solution)/shard_map/ppermute | solution.py:878
  555.9 9.1 %collective-permute-start.46 = (bf16[64,512]{1,0:T(8,128)(2,1)S(1)}, bf16[64,512]{1,0:T(8,128)(2,1)S(1)}, u32[]{:S(2)}, u32[]{:S(2)}) collective-permute-start(bf16[64,512]{1,0:T(8,128)(2,1)S(1)} %get-tuple-element.223), channel_id=1, source_target_pairs={{0,8},{8,16},{16,24},{24,0},{1,9},{9,17},{17,25},{25,1},{2,10},{10... | collective-permute-start | bytes 196616 | tf_op jit(solution)/shard_map/ppermute | solution.py:893
  556.0 9.1 %collective-permute-start.47 = (bf16[64,512]{1,0:T(8,128)(2,1)S(1)}, bf16[64,512]{1,0:T(8,128)(2,1)S(1)}, u32[]{:S(2)}, u32[]{:S(2)}) collective-permute-start(bf16[64,512]{1,0:T(8,128)(2,1)S(1)} %get-tuple-element.224), channel_id=1, source_target_pairs={{0,16},{8,24},{16,0},{24,8},{1,17},{9,25},{17,1},{25,9},{2,18},{10... | collective-permute-start | bytes 196616 | tf_op jit(solution)/shard_map/ppermute | solution.py:893
  557.4 7.6 %collective-permute-start.48 = (bf16[64,512]{1,0:T(8,128)(2,1)S(1)}, bf16[64,512]{1,0:T(8,128)(2,1)S(1)}, u32[]{:S(2)}, u32[]{:S(2)}) collective-permute-start(bf16[64,512]{1,0:T(8,128)(2,1)S(1)} %get-tuple-element.225), channel_id=1, source_target_pairs={{0,24},{8,0},{16,8},{24,16},{1,25},{9,1},{17,9},{25,17},{2,26},{10... | collective-permute-start | bytes 196616 | tf_op jit(solution)/shard_map/ppermute | solution.py:893
  (72 other events, 376.3 us)
Sparse Core Ops, SparseCore 0:
  58.5 43.7 all-gather.4
  127.5 109.0 all-gather.6
  325.0 136.3 reduce-scatter.2
  464.7 63.4 reduce-scatter.4

commit v3 on v2

--- a/solution.py
+++ b/solution.py
@@ -1082,6 +1082,59 @@
     )
 
 
+def split_attention(shard, terms, rows, inner, z, after=()):
+    size, dp = lax.axis_size("row"), lax.axis_size("dp")
+    rest = MODEL_WIDTH // (size * dp)
+    steps = MODEL_WIDTH // COLUMNS
+    base = terms * size * rows
+    quarter = quarter_index()
+    if rest % 128:
+        ins = shard[:base].reshape(terms, size, rows, COLUMNS).transpose(1, 0, 2, 3)
+        ins = jnp.take(ins, behind(z, jnp.arange(size), size), axis=0)
+        outs = shard[base:].reshape(steps, inner, COLUMNS).transpose(1, 0, 2)
+        outs = outs.reshape(inner, dp, size, rest)
+        outs = jnp.take(outs, ahead(quarter, jnp.arange(size), size), axis=2)
+        return (
+            [ins[k].reshape(-1, COLUMNS) for k in range(size)],
+            [outs[:, :, k].reshape(inner, COLUMNS) for k in range(size)],
+        )
+
+    def kernel(z, quarter, full, *outs):
+        for k in range(size):
+            at = behind(z[0], k, size)
+            for t in range(terms):
+                first = pl.multiple_of((t * size + at) * rows, rows)
+                outs[k][t * rows : (t + 1) * rows, :] = full[pl.ds(first, rows), :]
+            place = pl.multiple_of(ahead(quarter[0], k, size) * rest, rest)
+            for d in range(dp):
+                part = full[base + d * inner : base + (d + 1) * inner, pl.ds(place, rest)]
+                outs[size + k][:, d * rest : (d + 1) * rest] = part
+
+    pieces = call(
+        kernel,
+        [shape((terms * rows, COLUMNS), BF)] * size + [shape((inner, COLUMNS), BF)] * size,
+        [shard],
+        [z, quarter],
+        after=after,
+    )
+    return pieces[:size], pieces[size:]
+
+
+def turned_back(pieces):
+    size = len(pieces)
+    per = lax.axis_size("dp") // size
+    result = []
+    for k, piece in enumerate(pieces):
+        pairs = []
+        for q in range(size):
+            for r in range(per):
+                for z in range(size):
+                    target = (z * per + r) * size + (q + k) % size
+                    pairs.append(((q * per + r) * size + z, target))
+        result.append(lax.ppermute(piece, ("dp", "row"), pairs))
+    return result
+
+
 def out_pieces(messages, inner, z):
     size = len(messages)
     quarter = quarter_index()
@@ -1102,7 +1155,7 @@
     weight_new[...] = w
 
 
-def update_out(state, pieces, rate):
+def update_out(state, pieces, rate, place):
     size = len(pieces)
     rows, width = pieces[0].shape
 
@@ -1119,7 +1172,7 @@
         kernel,
         [shape(state[0].shape, F32)] * 3,
         list(pieces) + list(state),
-        [quarter_index()],
+        [place],
         (size,),
         [None] * size + [spec] * 3,
         [spec] * 3,
@@ -1290,16 +1343,17 @@
     active_grad = down_back(out_low, feed_full, down_base, down_inner, second_chunks[2:3])
     active, pair_grad = gateup_chunk(second_chunks, feed_full, active_grad, hidden_width)
     second_parts = gateup_back(pair_grad, feed_full, (F32, BF, BF, BF))
-    second_parts, sent = scatter_pieces(second_parts)
     feed_grads = weight_grads(
-        second_chunks, pair_grad, active, out_low, cols, [sent]
-    )
-    feed_grads, second_parts[1], second_parts[2] = lax.optimization_barrier(
-        (feed_grads, second_parts[1], second_parts[2])
-    )
+        second_chunks, pair_grad, active, out_low, cols, [second_parts[3]]
+    )
+    passed = swap(second_parts[3], "row", 1)
+    feed_grads, passed = lax.optimization_barrier((feed_grads, passed))
+    sent = add_parts([second_parts[2], passed], BF)
+    direct, sent = lax.optimization_barrier((second_parts[1], sent))
+    second_parts = [second_parts[0], swap(direct, "row", 1), swap(sent, "row", 2)]
     feed_total = scatter_shard(feed_grads)
     hidden_grad, hidden_low, second_gain_grad = hidden_back(
-        second_parts, hidden, second_scale, second_gain, out_low, [feed_grads]
+        second_parts, hidden, second_scale, second_gain, out_low, []
     )
 
     layer_part = down_forward(active, hidden, feed_full, down_base, down_inner, [hidden_low])
@@ -1327,6 +1381,9 @@
         [layer_output],
     )
     attention_grads = weight_grads([first_low], raw_grad, mixed, hidden_all, cols)
+    attention_grads, feed_total = lax.optimization_barrier((attention_grads, feed_total))
+    attention_total = scatter_shard(attention_grads)
+    feed_pieces = split_shard(feed_total, gateup_terms, in_rows, down_inner, z)
     input_part, inner_part, first_gain_grad = input_back(
         raw_grad,
         attention_full,
@@ -1335,50 +1392,40 @@
         first_gain,
         hidden_grad,
         z,
-        [attention_grads],
+        feed_pieces[:1],
     )
     input_pieces = take_apart(input_part, z, False)
     input_parts, _ = scatter_pieces(input_pieces)
+    feed_messages = along_row(feed_pieces, False)
     norm_part = jnp.concatenate([first_gain_grad, second_gain_grad])
     norm_part = norm_part.reshape(2, dp, size, rest).transpose(0, 2, 1, 3).reshape(2, MODEL_WIDTH)
-    small = jnp.concatenate([norm_part.reshape(-1), head_part.reshape(-1), inner_part.reshape(-1)])
-    small, input_parts[0] = lax.optimization_barrier((small, input_parts[0]))
-    small = add_along(small.reshape(-1, 128), ("row",)).reshape(-1)
-    gain_count = norm_part.size + head_part.size
-    inner = small[gain_count:][:, None]
-    gain_total = add_along(small[:gain_count].reshape(-1, 128), ("dp", "col")).reshape(-1)
-    attention_grads, feed_total, input_parts[1], input_parts[2], gain_total = (
-        lax.optimization_barrier(
-            (attention_grads, feed_total, input_parts[1], input_parts[2], gain_total)
-        )
-    )
-    norm_total = gain_total[: norm_part.size].reshape(norm_part.shape)
-    head_total = gain_total[norm_part.size :].reshape(head_part.shape)
-    attention_total = scatter_shard(attention_grads)
-
-    feed_messages = along_row(
-        split_shard(feed_total, gateup_terms, in_rows, down_inner, z), False
-    )
+    gain_part = jnp.concatenate([norm_part.reshape(-1), head_part.reshape(-1)]).reshape(-1, 128)
+    gain_part, feed_messages[1] = lax.optimization_barrier((gain_part, feed_messages[1]))
+    gain_part = add_along(gain_part, ("dp", "col"))
+    small = jnp.concatenate([gain_part, inner_part.reshape(-1, 128)])
+    small = add_along(small, ("row",)).reshape(-1)
+    inner = small[gain_part.size :][:, None]
+    norm_total = small[: norm_part.size].reshape(norm_part.shape)
+    head_total = small[norm_part.size : gain_part.size].reshape(head_part.shape)
+
     down_new = update_out(
         (down_weight, down_moment, down_second),
         out_pieces(feed_messages, down_inner, z),
         RATES[4],
+        quarter_place,
     )
     cut = [(t, 0, COLUMNS) for t in range(gateup_terms)]
     (gateup_total,) = place_columns(feed_messages, in_rows, [cut], z)
-    gateup_new, _ = update_pair(
+    gateup_new, gateup_flat = update_pair(
         (gateup_weight, gateup_moment, gateup_second), gateup_total, RATES[3]
     )
-    input_grad = add_parts(input_parts, F32) - (
-        first_scale * first_scale * first_scale * inner / MODEL_WIDTH
-    ) * tokens.astype(F32)
-    attention_messages = along_row(
-        split_shard(attention_total, 1, in_rows, output_inner, z), False
-    )
+    attention_pieces, output_pieces = split_attention(
+        attention_total, 1, in_rows, output_inner, z, [gateup_flat]
+    )
+    output_pieces = turned_back(output_pieces)
+    attention_messages = along_row(attention_pieces, False)
     output_new = update_out(
-        (output_weight, output_moment, output_second),
-        out_pieces(attention_messages, output_inner, z),
-        RATES[2],
+        (output_weight, output_moment, output_second), output_pieces, RATES[2], z
     )
     query_total, keyval_total = place_columns(
         attention_messages,
@@ -1386,6 +1433,9 @@
         [[(0, 0, head_width)], [(0, head_width, 2 * kv_width)]],
         z,
     )
+    input_grad = add_parts(input_parts, F32, [query_total]) - (
+        first_scale * first_scale * first_scale * inner / MODEL_WIDTH
+    ) * tokens.astype(F32)
     query_new = adamw(
         query_weight, query_moment, query_second, query_total.astype(F32), RATES[0], DECAY
     )

time: 585 us -> 582 us (level)
  waiting for transfers between devices: 259 us -> 229 us
  starting transfers between devices: 102 us -> 124 us
    ppermute x29, waiting for transfers between devices: 180 us -> 155 us  [swap(): lax.ppermute(value, axis, [(i, i ^ step) for i in range(lax.axis_size(axi...]
    ppermute x29, starting transfers between devices: 52.4 us -> 68.3 us  [swap(): lax.ppermute(value, axis, [(i, i ^ step) for i in range(lax.axis_size(axi...]
    ppermute x0 -> x4, starting transfers between devices: none -> 10.3 us  [turned_back(): result.append(lax.ppermute(piece, ('dp', 'row'), pairs))]
    pallas_call x40 -> x39, Pallas kernels: 138 us -> 140 us  [call(): pl.pallas_call(run, grid_spec=pltpu.PrefetchScalarGridSpec(num_scalar_pre...]
    unnamed x154 -> x162, local copies, waits for them, and re-layouts: 34.6 us -> 32.6 us
  transfers between devices with their start and end apart: 59 -> 60, of which waited for: 27 -> 24; matrix products, arithmetic and copies ran while one was open for 2% -> 2% of each run, Pallas kernels for 22% -> 22%
where the time goes in v3:
time: 582 us; the launch traced here: 571 us
  waiting for transfers between devices  229 us (39%)
  Pallas kernels  157 us (27%)
  starting transfers between devices  124 us (21%)
  local copies, waits for them, and re-layouts  39.1 us (7%)
  between operations  15.3 us (3%)
  other arithmetic  6.65 us (1%)
    ppermute x29, waiting for transfers between devices, swap(): lax.ppermute(value, axis, [(i, i ^ step) for i in range(lax.axis_size(axi...  155 us
    pallas_call x39, Pallas kernels, call(): pl.pallas_call(run, grid_spec=pltpu.PrefetchScalarGridSpec(num_scalar_pre...  140 us
    ppermute x29, starting transfers between devices, swap(): lax.ppermute(value, axis, [(i, i ^ step) for i in range(lax.axis_size(axi...  68.3 us
    ppermute x15, waiting for transfers between devices, along_row(): lax.ppermute(p, 'row', [(i, (i + sign * k) % size) for i in range(size)])  39.9 us
    ppermute x15, starting transfers between devices, along_row(): lax.ppermute(p, 'row', [(i, (i + sign * k) % size) for i in range(size)])  35.3 us
    unnamed x162, local copies, waits for them, and re-layouts  32.6 us
    ppermute x1, waiting for transfers between devices, body(): lax.ppermute(keys_values, 'col', [(i, i + 1) for i in range(cols - 1)])  14.9 us
  transfers between devices with their start and end apart: 60, of which 24 were waited for; matrix products, arithmetic and copies ran while one was open for 2% of the time, Pallas kernels for 22%

profile of v3, /device:TPU:0, one launch (start us, length us, event | category | flops | bytes accessed | tf_op | source)
XLA Modules:
  0.0 570.6 jit_solution(294665766088153161)
XLA Ops:
  7.2 4.1 collective-permute-start.1
  11.3 2.4 shard_map.407
  13.8 2.3 shard_map.408
  20.6 3.5 collective-permute-done.6.refs_9_
  25.9 3.5 collective-permute-start.5
  34.0 12.0 %collective-permute-start.10 = (bf16[64,512]{1,0:T(8,128)(2,1)S(1)}, bf16[64,512]{1,0:T(8,128)(2,1)S(1)}, u32[]{:S(2)}, u32[]{:S(2)}) collective-permute-start(bf16[64,512]{1,0:T(8,128)(2,1)S(1)} %get-tuple-element.140), channel_id=1, source_target_pairs={{0,4},{2,6},{4,0},{6,2},{1,5},{3,7},{5,1},{7,3},{8,12},{10,14},{12... | collective-permute-start | bytes 196616 | tf_op jit(solution)/shard_map/ppermute | solution.py:878
  46.0 3.7 collective-permute-start.11
  49.7 3.1 shard_map.410
  55.4 2.1 shard_map.411.refs_5_
  59.4 2.9 collective-permute-start.14
  64.4 46.5 %collective-permute-done.refs_2_ = bf16[512,512]{1,0:T(8,128)(2,1)S(1)} collective-permute-done((bf16[512,512]{1,0:T(8,128)(2,1)S(1)}, bf16[512,512]{1,0:T(8,128)(2,1)S(1)}, u32[]{:S(2)}, u32[]{:S(2)}) %collective-permute-start) | collective-permute-done | bytes 524320 | tf_op jit(solution)/shard_map/ppermute | solution.py:844
  111.0 11.1 %collective-permute-done.2.refs_4_ = bf16[512,512]{1,0:T(8,128)(2,1)S(1)} collective-permute-done((bf16[512,512]{1,0:T(8,128)(2,1)}, bf16[512,512]{1,0:T(8,128)(2,1)S(1)}, u32[]{:S(2)}, u32[]{:S(2)}) %collective-permute-start.2) | collective-permute-done | bytes 524320 | tf_op jit(solution)/shard_map/ppermute | solution.py:844
  122.1 2.2 shard_map.412.refs_5_.refs_0_.refs_4_.refs_3_
  133.7 7.8 %shard_map.415 = (bf16[512,2048]{1,0:T(8,128)(2,1)S(1)}, f32[512,1]{1,0:T(8,128)S(1)}, f32[512,512]{1,0:T(8,128)S(1)}, f32[512,256]{1,0:T(8,128)S(1)}, bf16[512,...) custom-call(bf16[512,2048]{1,0:T(8,128)(2,1)S(1)} %copy-done.1, f32[1,2048]{1,0:T(1,128)S(1)} %bitcast.102, ...), custom_call_target="tpu_custom_call" | custom-call | tf_op jit(solution)/shard_map/pallas_call | solution.py:215
  146.2 3.6 collective-permute-start.15
  149.9 6.5 %collective-permute-done.17.refs_4_.refs_3_ = bf16[512,512]{1,0:T(8,128)(2,1)} collective-permute-done((bf16[512,512]{1,0:T(8,128)(2,1)}, bf16[512,512]{1,0:T(8,128)(2,1)}, u32[]{:S(2)}, u32[]{:S(2)}) %collective-permute-start.17) | collective-permute-done | bytes 524320 | tf_op jit(solution)/shard_map/ppermute | solution.py:844
  157.3 14.9 %collective-permute-done.15.refs_7_.refs_8_ = bf16[512,512]{1,0:T(8,128)(2,1)S(1)} collective-permute-done((bf16[512,512]{1,0:T(8,128)(2,1)S(1)}, bf16[512,512]{1,0:T(8,128)(2,1)S(1)}, u32[]{:S(2)}, u32[]{:S(2)}) %collective-permute-start.15) | collective-permute-done | bytes 524320 | tf_op jit(solution)/shard_map/ppermute | solution.py:1329
  174.2 7.3 %shard_map.416 = (bf16[512,512]{1,0:T(8,128)(2,1)S(1)}, f32[4,512,1]{2,1,0:T(8,128)S(1)}) custom-call(s32[1]{0:T(128)} %bitcast.1.refs_0_, s32[512,1]{1,0:T(8,128)S(1)} %copy-done.18, s32[1,512]{1,0:T(1,128)S(1)} %bitcast.105, s32[1,512]{1,0:T(1,128)S(1)} %bitcast.107, bf16[512,512]{1,0:T(8,128)(2,1)S(1)} %copy-done.26, ...), custom_call_target="tpu_custom_call" | custom-call | tf_op jit(solution)/shard_map/pallas_call | solution.py:93
  181.6 4.4 shard_map.417
  186.0 11.8 %collective-permute-done.19.refs_1_ = bf16[128,2048]{1,0:T(8,128)(2,1)S(1)} collective-permute-done((bf16[128,2048]{1,0:T(8,128)(2,1)S(1)}, bf16[128,2048]{1,0:T(8,128)(2,1)S(1)}, u32[]{:S(2)}, u32[]{:S(2)}) %collective-permute-start.19) | collective-permute-done | bytes 524320 | tf_op jit(solution)/shard_map/ppermute | solution.py:844
  198.0 3.0 collective-permute-start.21
  201.1 18.8 %collective-permute-done.20.refs_2_ = bf16[128,2048]{1,0:T(8,128)(2,1)S(1)} collective-permute-done((bf16[128,2048]{1,0:T(8,128)(2,1)S(1)}, bf16[128,2048]{1,0:T(8,128)(2,1)S(1)}, u32[]{:S(2)}, u32[]{:S(2)}) %collective-permute-start.20) | collective-permute-done | bytes 524320 | tf_op jit(solution)/shard_map/ppermute | solution.py:844
  223.4 16.4 %collective-permute-start.22 = (bf16[128,2048]{1,0:T(8,128)(2,1)}, bf16[128,2048]{1,0:T(8,128)(2,1)}, u32[]{:S(2)}, u32[]{:S(2)}) collective-permute-start(bf16[128,2048]{1,0:T(8,128)(2,1)} %get-tuple-element.159.refs_0_), channel_id=1, source_target_pairs={{0,2},{2,0},{4,6},{6,4},{1,3},{3,1},{5,7},{7,5},{8,10},{10,8},{12,... | collective-permute-start | bytes 1572872 | tf_op jit(solution)/shard_map/ppermute | solution.py:844
  240.3 9.6 %collective-permute-start.24 = (bf16[128,2048]{1,0:T(8,128)(2,1)}, bf16[128,2048]{1,0:T(8,128)(2,1)}, u32[]{:S(2)}, u32[]{:S(2)}) collective-permute-start(bf16[128,2048]{1,0:T(8,128)(2,1)} %collective-permute-done.23.refs_2_), channel_id=1, source_target_pairs={{0,2},{2,0},{4,6},{6,4},{1,3},{3,1},{5,7},{7,5},{8,10},{10,8},{12,... | collective-permute-start | bytes 1572872 | tf_op jit(solution)/shard_map/ppermute | solution.py:844
  249.9 2.6 shard_map.420.refs_0_.refs_6_
  255.4 6.8 %shard_map.421.refs_5_ = f32[512,1536]{1,0:T(8,128)S(1)} custom-call(bf16[512,2048]{1,0:T(8,128)(2,1)S(1)} %copy-done.3, bf16[2,4,2304,512]{3,2,1,0:T(8,128)(2,1)} %bitcast.110, bf16[128,2048]{1,0:T(8,128)(2,1)} %collective-permute-done.23.refs_2_), custom_call_target="tpu_custom_call" | custom-call | tf_op jit(solution)/shard_map/pallas_call | solution.py:215
  262.2 11.6 %shard_map.422 = (bf16[512,1536]{1,0:T(8,128)(2,1)S(1)}, bf16[512,3072]{1,0:T(8,128)(2,1)S(1)}) custom-call(bf16[128,2048]{1,0:T(8,128)(2,1)} %get-tuple-element.159.refs_0_, bf16[128,2048]{1,0:T(8,128)(2,1)} %collective-permute-done.22.refs_1_, bf16[128,2048]{1,0:T(8,128)(2,1)} %collective-permute-done.23.refs_2_, ...), custom_call_target="tpu_custom_call" | custom-call | tf_op jit(solution)/shard_map/pallas_call | solution.py:215
  273.9 10.0 %shard_map.423 = (f32[128,2048]{1,0:T(8,128)S(1)}, bf16[128,2048]{1,0:T(8,128)(2,1)S(1)}, bf16[128,2048]{1,0:T(8,128)(2,1)S(1)}, bf16[128,2048]{1,0:T(8,128)(2,1)S(1)}) custom-call(bf16[512,3072]{1,0:T(8,128)(2,1)S(1)} %get-tuple-element.162.refs_0_.refs_4_, bf16[2,4,2304,512]{3,2,1,0:T(8,128)(2,1)} %bitcast.112), custom_call_target="tpu_custom_call" | custom-call | tf_op jit(solution)/shard_map/pallas_call | solution.py:215
  284.7 17.2 %shard_map.424 = bf16[2,4,2304,512]{3,2,1,0:T(8,128)(2,1)} custom-call(bf16[128,2048]{1,0:T(8,128)(2,1)} %get-tuple-element.159.refs_0_, bf16[128,2048]{1,0:T(8,128)(2,1)} %collective-permute-done.22.refs_1_, bf16[128,2048]{1,0:T(8,128)(2,1)} %collective-permute-done.23.refs_2_, bf16[128,2048]{1,0:T(8,128)(2,1)} %collective-permute-done.24.refs_3_, ...), custom_call_target="tpu_custom_call" | custom-call | tf_op jit(solution)/shard_map/pallas_call | solution.py:215
  306.7 2.3 collective-permute-start.27
  309.1 12.9 %collective-permute-done.26.refs_1_ = bf16[128,2048]{1,0:T(8,128)(2,1)S(1)} collective-permute-done((bf16[128,2048]{1,0:T(8,128)(2,1)}, bf16[128,2048]{1,0:T(8,128)(2,1)S(1)}, u32[]{:S(2)}, u32[]{:S(2)}) %collective-permute-start.26) | collective-permute-done | bytes 524320 | tf_op jit(solution)/shard_map/ppermute | solution.py:844
  322.0 6.6 %collective-permute-done.27.refs_2_ = bf16[128,2048]{1,0:T(8,128)(2,1)S(1)} collective-permute-done((bf16[128,2048]{1,0:T(8,128)(2,1)S(1)}, bf16[128,2048]{1,0:T(8,128)(2,1)S(1)}, u32[]{:S(2)}, u32[]{:S(2)}) %collective-permute-start.27) | collective-permute-done | bytes 524320 | tf_op jit(solution)/shard_map/ppermute | solution.py:844
  329.4 3.5 shard_map.426
  333.0 8.0 %collective-permute-start.28 = (bf16[128,2048]{1,0:T(8,128)(2,1)S(1)}, bf16[128,2048]{1,0:T(8,128)(2,1)S(1)}, u32[]{:S(2)}, u32[]{:S(2)}) collective-permute-start(bf16[128,2048]{1,0:T(8,128)(2,1)S(1)} %get-tuple-element.171.refs_3_.refs_1_), channel_id=1, source_target_pairs={{0,2},{2,0},{4,6},{6,4},{1,3},{3,1},{5,7},{7,5},{8,10},{10,8},{12,... | collective-permute-start | bytes 1572872 | tf_op jit(solution)/shard_map/ppermute | solution.py:844
  341.0 13.4 %collective-permute-done.29.refs_3_ = bf16[128,2048]{1,0:T(8,128)(2,1)S(1)} collective-permute-done((bf16[128,2048]{1,0:T(8,128)(2,1)S(1)}, bf16[128,2048]{1,0:T(8,128)(2,1)S(1)}, u32[]{:S(2)}, u32[]{:S(2)}) %collective-permute-start.29) | collective-permute-done | bytes 524320 | tf_op jit(solution)/shard_map/ppermute | solution.py:844
  354.4 6.0 %shard_map.427.refs_6_.refs_1_ = bf16[512,2048]{1,0:T(8,128)(2,1)S(1)} custom-call(bf16[512,1536]{1,0:T(8,128)(2,1)S(1)} %copy-done.11, f32[128,2048]{1,0:T(8,128)S(1)} %copy-done.13, bf16[2,4,2304,512]{3,2,1,0:T(8,128)(2,1)} %bitcast.113, bf16[128,2048]{1,0:T(8,128)(2,1)S(1)} %get-tuple-element.171.refs_3_.refs_1_), custom_call_target="tpu_custom_call" | custom-call | tf_op jit(solution)/shard_map/pallas_call | solution.py:215
  361.8 3.9 collective-permute-done.30.refs_4_
  365.7 4.2 shard_map.428
  372.7 9.2 %shard_map.432 = (f32[512,512]{1,0:T(8,128)S(1)}, f32[512,256]{1,0:T(8,128)S(1)}, f32[512,256]{1,0:T(8,128)S(1)}, bf16[512,512]{1,0:T(8,128)(2,1)S(1)}) custom-call(s32[1]{0:T(128)} %bitcast.1.refs_0_, s32[512,1]{1,0:T(8,128)S(1)} %copy-done.19, s32[1,512]{1,0:T(1,128)S(1)} %bitcast.106, s32[1,512]{1,0:T(1,128)S(1)} %bitcast.108, ...), custom_call_target="tpu_custom_call" | custom-call | tf_op jit(solution)/shard_map/pallas_call | solution.py:163
  383.5 11.3 %collective-permute-start.33 = (bf16[512,512]{1,0:T(8,128)(2,1)S(1)}, bf16[512,512]{1,0:T(8,128)(2,1)S(1)}, u32[]{:S(2)}, u32[]{:S(2)}) collective-permute-start(bf16[512,512]{1,0:T(8,128)(2,1)S(1)} %shard_map.430), channel_id=1, source_target_pairs={{0,4},{2,6},{4,0},{6,2},{1,5},{3,7},{5,1},{7,3},{8,12},{10,14},{12... | collective-permute-start | bytes 1572872 | tf_op jit(solution)/shard_map/ppermute | solution.py:844
  396.1 6.4 %collective-permute-done.32.refs_1_ = bf16[512,512]{1,0:T(8,128)(2,1)S(1)} collective-permute-done((bf16[512,512]{1,0:T(8,128)(2,1)S(1)}, bf16[512,512]{1,0:T(8,128)(2,1)S(1)}, u32[]{:S(2)}, u32[]{:S(2)}) %collective-permute-start.32) | collective-permute-done | bytes 524320 | tf_op jit(solution)/shard_map/ppermute | solution.py:844
  402.5 4.9 collective-permute-done.33.refs_2_
  408.6 8.6 %collective-permute-done.34.refs_5_ = bf16[512,512]{1,0:T(8,128)(2,1)S(1)} collective-permute-done((bf16[512,512]{1,0:T(8,128)(2,1)S(1)}, bf16[512,512]{1,0:T(8,128)(2,1)S(1)}, u32[]{:S(2)}, u32[]{:S(2)}) %collective-permute-start.34) | collective-permute-done | bytes 524320 | tf_op jit(solution)/shard_map/ppermute | solution.py:1367
  417.3 2.6 shard_map.433
  419.9 9.7 %shard_map.434 = bf16[2,4,768,512]{3,2,1,0:T(8,128)(2,1)} custom-call(bf16[512,2048]{1,0:T(8,128)(2,1)S(1)} %copy-done.31, bf16[512,1024]{1,0:T(8,128)(2,1)S(1)} %get-tuple-element.187.refs_1_, bf16[512,512]{1,0:T(8,128)(2,1)S(1)} %copy-done.24, bf16[512,2048]{1,0:T(8,128)(2,1)S(1)} %copy-done.9), custom_call_target="tpu_custom_call" | custom-call | tf_op jit(solution)/shard_map/pallas_call | solution.py:215
  429.6 6.9 %reduce-scatter.3.cloned.1.call-done.refs_1_ = bf16[2304,512]{1,0:T(8,128)(2,1)} async-done(((bf16[18432,512]{1,0:T(8,128)(2,1)}), bf16[2304,512]{1,0:T(8,128)(2,1)}) %reduce-scatter.3.cloned.1.call-update) | async-done | bytes 2359312 | tf_op jit(solution)/shard_map/reduce_scatter | solution.py:903
  436.6 1.7 copy-done.20
  441.9 6.3 %shard_map.436 = (bf16[512,2048]{1,0:T(8,128)(2,1)S(1)}, f32[512,1]{1,0:T(8,128)S(1)}, f32[1,2048]{1,0:T(1,128)S(1)}) custom-call(s32[1]{0:T(128)} %bitcast.refs_0_, bf16[512,1024]{1,0:T(8,128)(2,1)S(1)} %get-tuple-element.187.refs_1_, bf16[2,4,768,512]{3,2,1,0:T(8,128)(2,1)} %bitcast.117, bf16[512,2048]{1,0:T(8,128)(2,1)S(1)} %copy-done.1, ...), custom_call_target="tpu_custom_call" | custom-call | tf_op jit(solution)/shard_map/pallas_call | solution.py:215
  451.1 2.3 collective-permute-start.35
  453.4 3.0 collective-permute-done.38.refs_2_
  457.4 36.0 %collective-permute-done.39.refs_3_ = bf16[576,512]{1,0:T(8,128)(2,1)} collective-permute-done((bf16[576,512]{1,0:T(8,128)(2,1)}, bf16[576,512]{1,0:T(8,128)(2,1)}, u32[]{:S(2)}, u32[]{:S(2)}) %collective-permute-start.39) | collective-permute-done | bytes 589856 | tf_op jit(solution)/shard_map/ppermute | solution.py:878
  498.3 2.7 collective-permute-done.45
  501.1 3.6 collective-permute-done.46
  504.8 3.8 collective-permute-done.47
  509.2 2.6 collective-permute-start.37
  516.2 8.1 %shard_map.440 = (f32[6144,128]{1,0:T(8,128)}, f32[6144,128]{1,0:T(8,128)}, f32[6144,128]{1,0:T(8,128)}) custom-call(bf16[6144,128]{1,0:T(8,128)(2,1)} %reshape.274.refs_0_, f32[6144,128]{1,0:T(8,128)} %bitcast.99, f32[6144,128]{1,0:T(8,128)} %bitcast.121, f32[6144,128]{1,0:T(8,128)} %bitcast.122), custom_call_target="tpu_custom_call" | custom-call | tf_op jit(solution)/shard_map/pallas_call | solution.py:215
  527.8 3.4 collective-permute-start.50
  532.7 4.8 collective-permute-start.52
  538.2 2.0 collective-permute-start.41
  540.2 2.5 collective-permute-start.42
  542.7 2.2 collective-permute-start.43
  545.0 5.7 %shard_map.447 = (f32[768,512]{1,0:T(8,128)}, f32[768,512]{1,0:T(8,128)}, f32[768,512]{1,0:T(8,128)}) custom-call(s32[1]{0:T(128)} %bitcast.15.refs_0_.refs_1_, bf16[192,512]{1,0:T(8,128)(2,1)S(1)} %get-tuple-element.230.refs_1_, bf16[192,512]{1,0:T(8,128)(2,1)S(1)} %collective-permute-done.53.refs_2_, bf16[192,512]{1,0:T(8,128)(2,1)S(1)} %collective-permute-done.54.refs_3_, ...), custom_call_target="tpu_custom_call" | custom-call | tf_op jit(solution)/shard_map/pallas_call | solution.py:215
  550.7 3.9 shard_map.445
  559.9 3.7 shard_map.444
  (307 shorter events, 84.6 us)
Async XLA Ops:
  7.2 126.5 %all-gather.5.cloned.1.call-start = ((), (), s32[]{:S(2)}) async-start(), calls=%async_computation.4 | async-start | bytes 7077888 | tf_op jit(solution)/shard_map/all_gather | solution.py:897
  7.2 48.1 %collective-permute-start.1 = (bf16[512,512]{1,0:T(8,128)(2,1)}, bf16[512,512]{1,0:T(8,128)(2,1)}, u32[]{:S(2)}, u32[]{:S(2)}) collective-permute-start(bf16[512,512]{1,0:T(8,128)(2,1)} %refs_1_.7), channel_id=1, source_target_pairs={{0,4},{2,6},{4,0},{6,2},{1,5},{3,7},{5,1},{7,3},{8,12},{10,14},{12... | collective-permute-start | bytes 1572872 | tf_op jit(solution)/shard_map/ppermute | solution.py:844
  11.3 38.4 %copy-start.7 = (f32[128,2,3072]{2,1,0:T(2,128)S(1)}, f32[128,2,3072]{2,1,0:T(2,128)}, u32[]{:S(2)}) copy-start(f32[128,2,3072]{2,1,0:T(2,128)} %refs_1_.6) | copy-start | bytes 9437188
  16.1 8.1 %collective-permute-start.6 = (bf16[256,512]{1,0:T(8,128)(2,1)S(1)}, bf16[256,512]{1,0:T(8,128)(2,1)S(1)}, u32[]{:S(2)}, u32[]{:S(2)}) collective-permute-start(bf16[256,512]{1,0:T(8,128)(2,1)S(1)} %get-tuple-element.135), channel_id=1, source_target_pairs={{0,8},{8,16},{16,24},{24,0},{1,9},{9,17},{17,25},{25,1},{2,10},{10... | collective-permute-start | bytes 786440 | tf_op jit(solution)/shard_map/ppermute | solution.py:893
  16.1 9.2 %collective-permute-start.7 = (bf16[256,512]{1,0:T(8,128)(2,1)S(1)}, bf16[256,512]{1,0:T(8,128)(2,1)S(1)}, u32[]{:S(2)}, u32[]{:S(2)}) collective-permute-start(bf16[256,512]{1,0:T(8,128)(2,1)S(1)} %get-tuple-element.136), channel_id=1, source_target_pairs={{0,16},{8,24},{16,0},{24,8},{1,17},{9,25},{17,1},{25,9},{2,18},{10... | collective-permute-start | bytes 786440 | tf_op jit(solution)/shard_map/ppermute | solution.py:893
  17.6 11.9 %collective-permute-start.8 = (bf16[256,512]{1,0:T(8,128)(2,1)}, bf16[256,512]{1,0:T(8,128)(2,1)}, u32[]{:S(2)}, u32[]{:S(2)}) collective-permute-start(bf16[256,512]{1,0:T(8,128)(2,1)} %get-tuple-element.137), channel_id=1, source_target_pairs={{0,24},{8,0},{16,8},{24,16},{1,25},{9,1},{17,9},{25,17},{2,26},{10... | collective-permute-start | bytes 786440 | tf_op jit(solution)/shard_map/ppermute | solution.py:893
  19.0 15.0 %collective-permute-start.3 = (bf16[128,512]{1,0:T(8,128)(2,1)}, bf16[128,512]{1,0:T(8,128)(2,1)}, u32[]{:S(2)}, u32[]{:S(2)}) collective-permute-start(bf16[128,512]{1,0:T(8,128)(2,1)} %get-tuple-element.131), channel_id=1, source_target_pairs={{0,2},{2,4},{4,6},{6,0},{1,3},{3,5},{5,7},{7,1},{8,10},{10,12},{12... | collective-permute-start | bytes 393224 | tf_op jit(solution)/shard_map/ppermute | solution.py:878
  24.8 21.2 %collective-permute-start.4 = (bf16[128,512]{1,0:T(8,128)(2,1)}, bf16[128,512]{1,0:T(8,128)(2,1)}, u32[]{:S(2)}, u32[]{:S(2)}) collective-permute-start(bf16[128,512]{1,0:T(8,128)(2,1)} %get-tuple-element.132), channel_id=1, source_target_pairs={{0,4},{2,6},{4,0},{6,2},{1,5},{3,7},{5,1},{7,3},{8,12},{10,14},{12... | collective-permute-start | bytes 393224 | tf_op jit(solution)/shard_map/ppermute | solution.py:878
  25.9 29.4 %collective-permute-start.5 = (bf16[128,512]{1,0:T(8,128)(2,1)}, bf16[128,512]{1,0:T(8,128)(2,1)}, u32[]{:S(2)}, u32[]{:S(2)}) collective-permute-start(bf16[128,512]{1,0:T(8,128)(2,1)} %get-tuple-element.133), channel_id=1, source_target_pairs={{0,6},{2,0},{4,2},{6,4},{1,7},{3,1},{5,3},{7,5},{8,14},{10,8},{12,... | collective-permute-start | bytes 393224 | tf_op jit(solution)/shard_map/ppermute | solution.py:878
  32.5 22.9 %collective-permute-start.9 = (bf16[64,512]{1,0:T(8,128)(2,1)S(1)}, bf16[64,512]{1,0:T(8,128)(2,1)S(1)}, u32[]{:S(2)}, u32[]{:S(2)}) collective-permute-start(bf16[64,512]{1,0:T(8,128)(2,1)S(1)} %get-tuple-element.139), channel_id=1, source_target_pairs={{0,2},{2,4},{4,6},{6,0},{1,3},{3,5},{5,7},{7,1},{8,10},{10,12},{12... | collective-permute-start | bytes 196616 | tf_op jit(solution)/shard_map/ppermute | solution.py:878
  34.0 21.3 %collective-permute-start.10 = (bf16[64,512]{1,0:T(8,128)(2,1)S(1)}, bf16[64,512]{1,0:T(8,128)(2,1)S(1)}, u32[]{:S(2)}, u32[]{:S(2)}) collective-permute-start(bf16[64,512]{1,0:T(8,128)(2,1)S(1)} %get-tuple-element.140), channel_id=1, source_target_pairs={{0,4},{2,6},{4,0},{6,2},{1,5},{3,7},{5,1},{7,3},{8,12},{10,14},{12... | collective-permute-start | bytes 196616 | tf_op jit(solution)/shard_map/ppermute | solution.py:878
  46.0 9.3 %collective-permute-start.11 = (bf16[64,512]{1,0:T(8,128)(2,1)S(1)}, bf16[64,512]{1,0:T(8,128)(2,1)S(1)}, u32[]{:S(2)}, u32[]{:S(2)}) collective-permute-start(bf16[64,512]{1,0:T(8,128)(2,1)S(1)} %get-tuple-element.141), channel_id=1, source_target_pairs={{0,6},{2,0},{4,2},{6,4},{1,7},{3,1},{5,3},{7,5},{8,14},{10,8},{12,... | collective-permute-start | bytes 196616 | tf_op jit(solution)/shard_map/ppermute | solution.py:878
  58.4 195.5 %all-gather.7.cloned.1.call-start = ((), (), s32[]{:S(2)}) async-start(), calls=%async_computation.5 | async-start | bytes 21233664 | tf_op jit(solution)/shard_map/all_gather | solution.py:897
  58.4 67.2 %collective-permute-start.12 = (bf16[576,512]{1,0:T(8,128)(2,1)S(1)}, bf16[576,512]{1,0:T(8,128)(2,1)S(1)}, u32[]{:S(2)}, u32[]{:S(2)}) collective-permute-start(bf16[576,512]{1,0:T(8,128)(2,1)S(1)} %copy-done.63), channel_id=1, source_target_pairs={{0,2},{2,4},{4,6},{6,0},{1,3},{3,5},{5,7},{7,1},{8,10},{10,12},{12... | collective-permute-start | bytes 1769480 | tf_op jit(solution)/shard_map/ppermute | solution.py:878
  58.5 67.1 %collective-permute-start.13 = (bf16[576,512]{1,0:T(8,128)(2,1)S(1)}, bf16[576,512]{1,0:T(8,128)(2,1)S(1)}, u32[]{:S(2)}, u32[]{:S(2)}) collective-permute-start(bf16[576,512]{1,0:T(8,128)(2,1)S(1)} %copy-done.61), channel_id=1, source_target_pairs={{0,4},{2,6},{4,0},{6,2},{1,5},{3,7},{5,1},{7,3},{8,12},{10,14},{12... | collective-permute-start | bytes 1769480 | tf_op jit(solution)/shard_map/ppermute | solution.py:878
  59.4 66.2 %copy-start.22 = (bf16[576,512]{1,0:T(8,128)(2,1)S(1)}, bf16[576,512]{1,0:T(8,128)(2,1)}, u32[]{:S(2)}) copy-start(bf16[576,512]{1,0:T(8,128)(2,1)} %copy-done.21) | copy-start | bytes 1769476
  59.4 66.2 %collective-permute-start.14 = (bf16[576,512]{1,0:T(8,128)(2,1)S(1)}, bf16[576,512]{1,0:T(8,128)(2,1)S(1)}, u32[]{:S(2)}, u32[]{:S(2)}) collective-permute-start(bf16[576,512]{1,0:T(8,128)(2,1)S(1)} %copy-done.59), channel_id=1, source_target_pairs={{0,6},{2,0},{4,2},{6,4},{1,7},{3,1},{5,3},{7,5},{8,14},{10,8},{12,... | collective-permute-start | bytes 1769480 | tf_op jit(solution)/shard_map/ppermute | solution.py:878
  62.4 48.6 %collective-permute-start = (bf16[512,512]{1,0:T(8,128)(2,1)S(1)}, bf16[512,512]{1,0:T(8,128)(2,1)S(1)}, u32[]{:S(2)}, u32[]{:S(2)}) collective-permute-start(bf16[512,512]{1,0:T(8,128)(2,1)S(1)} %copy-done.28), channel_id=1, source_target_pairs={{0,2},{2,0},{4,6},{6,4},{1,3},{3,1},{5,7},{7,5},{8,10},{10,8},{12,... | collective-permute-start | bytes 1572872 | tf_op jit(solution)/shard_map/ppermute | solution.py:844
  62.9 59.1 %collective-permute-start.2 = (bf16[512,512]{1,0:T(8,128)(2,1)}, bf16[512,512]{1,0:T(8,128)(2,1)S(1)}, u32[]{:S(2)}, u32[]{:S(2)}) collective-permute-start(bf16[512,512]{1,0:T(8,128)(2,1)} %collective-permute-done.1.refs_10_.refs_3_), channel_id=1, source_target_pairs={{0,2},{2,0},{4,6},{6,4},{1,3},{3,1},{5,7},{7,5},{8,10},{10,8},{12,... | collective-permute-start | bytes 1572872 | tf_op jit(solution)/shard_map/ppermute | solution.py:844
  127.3 309.2 %reduce-scatter.3.cloned.1.call-start = ((), (), s32[]{:S(2)}) async-start(), calls=%async_computation.2 | async-start | bytes 21233664 | tf_op jit(solution)/shard_map/reduce_scatter | solution.py:903
  130.9 25.5 %collective-permute-start.17 = (bf16[512,512]{1,0:T(8,128)(2,1)}, bf16[512,512]{1,0:T(8,128)(2,1)}, u32[]{:S(2)}, u32[]{:S(2)}) collective-permute-start(bf16[512,512]{1,0:T(8,128)(2,1)} %shard_map.414.refs_6_.refs_1_), channel_id=1, source_target_pairs={{0,4},{2,6},{4,0},{6,2},{1,5},{3,7},{5,1},{7,3},{8,12},{10,14},{12... | collective-permute-start | bytes 1572872 | tf_op jit(solution)/shard_map/ppermute | solution.py:844
  146.2 26.1 %collective-permute-start.15 = (bf16[512,512]{1,0:T(8,128)(2,1)S(1)}, bf16[512,512]{1,0:T(8,128)(2,1)S(1)}, u32[]{:S(2)}, u32[]{:S(2)}) collective-permute-start(bf16[512,512]{1,0:T(8,128)(2,1)S(1)} %get-tuple-element.151.refs_5_.refs_6_), channel_id=1, source_target_pairs={{0,1},{2,3},{4,5},{6,7},{8,9},{10,11},{12,13},{14,15},{16,17},{18,... | collective-permute-start | bytes 1572872 | tf_op jit(solution)/shard_map/ppermute | solution.py:1329
  149.8 31.7 %collective-permute-start.16 = (bf16[512,512]{1,0:T(8,128)(2,1)}, bf16[512,512]{1,0:T(8,128)(2,1)}, u32[]{:S(2)}, u32[]{:S(2)}) collective-permute-start(bf16[512,512]{1,0:T(8,128)(2,1)} %shard_map.414.refs_6_.refs_1_), channel_id=1, source_target_pairs={{0,2},{2,0},{4,6},{6,4},{1,3},{3,1},{5,7},{7,5},{8,10},{10,8},{12,... | collective-permute-start | bytes 1572872 | tf_op jit(solution)/shard_map/ppermute | solution.py:844
  156.4 25.1 %collective-permute-start.18 = (bf16[512,512]{1,0:T(8,128)(2,1)}, bf16[512,512]{1,0:T(8,128)(2,1)}, u32[]{:S(2)}, u32[]{:S(2)}) collective-permute-start(bf16[512,512]{1,0:T(8,128)(2,1)} %collective-permute-done.17.refs_4_.refs_3_), channel_id=1, source_target_pairs={{0,2},{2,0},{4,6},{6,4},{1,3},{3,1},{5,7},{7,5},{8,10},{10,8},{12,... | collective-permute-start | bytes 1572872 | tf_op jit(solution)/shard_map/ppermute | solution.py:844
  186.0 11.9 %collective-permute-start.19 = (bf16[128,2048]{1,0:T(8,128)(2,1)S(1)}, bf16[128,2048]{1,0:T(8,128)(2,1)S(1)}, u32[]{:S(2)}, u32[]{:S(2)}) collective-permute-start(bf16[128,2048]{1,0:T(8,128)(2,1)S(1)} %get-tuple-element.156), channel_id=1, source_target_pairs={{0,2},{2,0},{4,6},{6,4},{1,3},{3,1},{5,7},{7,5},{8,10},{10,8},{12,... | collective-permute-start | bytes 1572872 | tf_op jit(solution)/shard_map/ppermute | solution.py:844
  197.9 21.9 %collective-permute-start.20 = (bf16[128,2048]{1,0:T(8,128)(2,1)S(1)}, bf16[128,2048]{1,0:T(8,128)(2,1)S(1)}, u32[]{:S(2)}, u32[]{:S(2)}) collective-permute-start(bf16[128,2048]{1,0:T(8,128)(2,1)S(1)} %get-tuple-element.157.refs_5_), channel_id=1, source_target_pairs={{0,2},{2,0},{4,6},{6,4},{1,3},{3,1},{5,7},{7,5},{8,10},{10,8},{12,... | collective-permute-start | bytes 1572872 | tf_op jit(solution)/shard_map/ppermute | solution.py:844
  198.0 21.8 %collective-permute-start.21 = (bf16[128,2048]{1,0:T(8,128)(2,1)S(1)}, bf16[128,2048]{1,0:T(8,128)(2,1)S(1)}, u32[]{:S(2)}, u32[]{:S(2)}) collective-permute-start(bf16[128,2048]{1,0:T(8,128)(2,1)S(1)} %shard_map.418), channel_id=1, source_target_pairs={{0,4},{2,6},{4,0},{6,2},{1,5},{3,7},{5,1},{7,3},{8,12},{10,14},{12... | collective-permute-start | bytes 1572872 | tf_op jit(solution)/shard_map/ppermute | solution.py:844
  222.1 18.2 %collective-permute-start.23 = (bf16[128,2048]{1,0:T(8,128)(2,1)}, bf16[128,2048]{1,0:T(8,128)(2,1)}, u32[]{:S(2)}, u32[]{:S(2)}) collective-permute-start(bf16[128,2048]{1,0:T(8,128)(2,1)} %get-tuple-element.159.refs_0_), channel_id=1, source_target_pairs={{0,4},{2,6},{4,0},{6,2},{1,5},{3,7},{5,1},{7,3},{8,12},{10,14},{12... | collective-permute-start | bytes 1572872 | tf_op jit(solution)/shard_map/ppermute | solution.py:844
  223.4 38.9 %collective-permute-start.22 = (bf16[128,2048]{1,0:T(8,128)(2,1)}, bf16[128,2048]{1,0:T(8,128)(2,1)}, u32[]{:S(2)}, u32[]{:S(2)}) collective-permute-start(bf16[128,2048]{1,0:T(8,128)(2,1)} %get-tuple-element.159.refs_0_), channel_id=1, source_target_pairs={{0,2},{2,0},{4,6},{6,4},{1,3},{3,1},{5,7},{7,5},{8,10},{10,8},{12,... | collective-permute-start | bytes 1572872 | tf_op jit(solution)/shard_map/ppermute | solution.py:844
  240.3 21.9 %collective-permute-start.24 = (bf16[128,2048]{1,0:T(8,128)(2,1)}, bf16[128,2048]{1,0:T(8,128)(2,1)}, u32[]{:S(2)}, u32[]{:S(2)}) collective-permute-start(bf16[128,2048]{1,0:T(8,128)(2,1)} %collective-permute-done.23.refs_2_), channel_id=1, source_target_pairs={{0,2},{2,0},{4,6},{6,4},{1,3},{3,1},{5,7},{7,5},{8,10},{10,8},{12,... | collective-permute-start | bytes 1572872 | tf_op jit(solution)/shard_map/ppermute | solution.py:844
  284.7 17.2 %collective-permute-start.25 = (bf16[128,2048]{1,0:T(8,128)(2,1)S(1)}, bf16[128,2048]{1,0:T(8,128)(2,1)S(1)}, u32[]{:S(2)}, u32[]{:S(2)}) collective-permute-start(bf16[128,2048]{1,0:T(8,128)(2,1)S(1)} %get-tuple-element.166.refs_7_), channel_id=1, source_target_pairs={{0,2},{2,0},{4,6},{6,4},{1,3},{3,1},{5,7},{7,5},{8,10},{10,8},{12,... | collective-permute-start | bytes 1572872 | tf_op jit(solution)/shard_map/ppermute | solution.py:844
  302.7 221.9 %reduce-scatter.5.cloned.1.call-start = ((), (), s32[]{:S(2)}) async-start(), calls=%async_computation.3 | async-start | bytes 7077888 | tf_op jit(solution)/shard_map/reduce_scatter | solution.py:903
  305.2 16.8 %collective-permute-start.26 = (bf16[128,2048]{1,0:T(8,128)(2,1)}, bf16[128,2048]{1,0:T(8,128)(2,1)S(1)}, u32[]{:S(2)}, u32[]{:S(2)}) collective-permute-start(bf16[128,2048]{1,0:T(8,128)(2,1)} %copy-done.65), channel_id=1, source_target_pairs={{0,2},{2,0},{4,6},{6,4},{1,3},{3,1},{5,7},{7,5},{8,10},{10,8},{12,... | collective-permute-start | bytes 1572872 | tf_op jit(solution)/shard_map/ppermute | solution.py:844
  306.7 21.9 %collective-permute-start.27 = (bf16[128,2048]{1,0:T(8,128)(2,1)S(1)}, bf16[128,2048]{1,0:T(8,128)(2,1)S(1)}, u32[]{:S(2)}, u32[]{:S(2)}) collective-permute-start(bf16[128,2048]{1,0:T(8,128)(2,1)S(1)} %shard_map.425), channel_id=1, source_target_pairs={{0,4},{2,6},{4,0},{6,2},{1,5},{3,7},{5,1},{7,3},{8,12},{10,14},{12... | collective-permute-start | bytes 1572872 | tf_op jit(solution)/shard_map/ppermute | solution.py:844
  332.9 21.5 %collective-permute-start.29 = (bf16[128,2048]{1,0:T(8,128)(2,1)S(1)}, bf16[128,2048]{1,0:T(8,128)(2,1)S(1)}, u32[]{:S(2)}, u32[]{:S(2)}) collective-permute-start(bf16[128,2048]{1,0:T(8,128)(2,1)S(1)} %get-tuple-element.171.refs_3_.refs_1_), channel_id=1, source_target_pairs={{0,4},{2,6},{4,0},{6,2},{1,5},{3,7},{5,1},{7,3},{8,12},{10,14},{12... | collective-permute-start | bytes 1572872 | tf_op jit(solution)/shard_map/ppermute | solution.py:844
  333.0 28.8 %collective-permute-start.28 = (bf16[128,2048]{1,0:T(8,128)(2,1)S(1)}, bf16[128,2048]{1,0:T(8,128)(2,1)S(1)}, u32[]{:S(2)}, u32[]{:S(2)}) collective-permute-start(bf16[128,2048]{1,0:T(8,128)(2,1)S(1)} %get-tuple-element.171.refs_3_.refs_1_), channel_id=1, source_target_pairs={{0,2},{2,0},{4,6},{6,4},{1,3},{3,1},{5,7},{7,5},{8,10},{10,8},{12,... | collective-permute-start | bytes 1572872 | tf_op jit(solution)/shard_map/ppermute | solution.py:844
  354.4 11.3 %collective-permute-start.30 = (bf16[128,2048]{1,0:T(8,128)(2,1)S(1)}, bf16[128,2048]{1,0:T(8,128)(2,1)S(1)}, u32[]{:S(2)}, u32[]{:S(2)}) collective-permute-start(bf16[128,2048]{1,0:T(8,128)(2,1)S(1)} %collective-permute-done.29.refs_3_), channel_id=1, source_target_pairs={{0,2},{2,0},{4,6},{6,4},{1,3},{3,1},{5,7},{7,5},{8,10},{10,8},{12,... | collective-permute-start | bytes 1572872 | tf_op jit(solution)/shard_map/ppermute | solution.py:844
  371.9 11.4 %collective-permute-start.31 = (bf16[512,512]{1,0:T(8,128)(2,1)S(1)}, bf16[512,512]{1,0:T(8,128)(2,1)S(1)}, u32[]{:S(2)}, u32[]{:S(2)}) collective-permute-start(bf16[512,512]{1,0:T(8,128)(2,1)S(1)} %get-tuple-element.176), channel_id=1, source_target_pairs={{0,2},{2,0},{4,6},{6,4},{1,3},{3,1},{5,7},{7,5},{8,10},{10,8},{12,... | collective-permute-start | bytes 1572872 | tf_op jit(solution)/shard_map/ppermute | solution.py:844
  383.3 33.9 %copy-start.44 = (f32[512,256]{1,0:T(8,128)S(1)}, f32[512,256]{1,0:T(8,128)}, u32[]{:S(2)}) copy-start(f32[512,256]{1,0:T(8,128)} %copy-done.43) | copy-start | bytes 1572868
  383.4 19.0 %collective-permute-start.32 = (bf16[512,512]{1,0:T(8,128)(2,1)S(1)}, bf16[512,512]{1,0:T(8,128)(2,1)S(1)}, u32[]{:S(2)}, u32[]{:S(2)}) collective-permute-start(bf16[512,512]{1,0:T(8,128)(2,1)S(1)} %get-tuple-element.177), channel_id=1, source_target_pairs={{0,2},{2,0},{4,6},{6,4},{1,3},{3,1},{5,7},{7,5},{8,10},{10,8},{12,... | collective-permute-start | bytes 1572872 | tf_op jit(solution)/shard_map/ppermute | solution.py:844
  383.5 23.9 %collective-permute-start.33 = (bf16[512,512]{1,0:T(8,128)(2,1)S(1)}, bf16[512,512]{1,0:T(8,128)(2,1)S(1)}, u32[]{:S(2)}, u32[]{:S(2)}) collective-permute-start(bf16[512,512]{1,0:T(8,128)(2,1)S(1)} %shard_map.430), channel_id=1, source_target_pairs={{0,4},{2,6},{4,0},{6,2},{1,5},{3,7},{5,1},{7,3},{8,12},{10,14},{12... | collective-permute-start | bytes 1572872 | tf_op jit(solution)/shard_map/ppermute | solution.py:844
  394.8 22.4 %collective-permute-start.34 = (bf16[512,512]{1,0:T(8,128)(2,1)S(1)}, bf16[512,512]{1,0:T(8,128)(2,1)S(1)}, u32[]{:S(2)}, u32[]{:S(2)}) collective-permute-start(bf16[512,512]{1,0:T(8,128)(2,1)S(1)} %get-tuple-element.186), channel_id=1, source_target_pairs={{1,0},{3,2},{5,4},{7,6},{9,8},{11,10},{13,12},{15,14},{17,16},{19,... | collective-permute-start | bytes 1572872 | tf_op jit(solution)/shard_map/ppermute | solution.py:1367
  439.6 16.8 %collective-permute-start.38 = (bf16[576,512]{1,0:T(8,128)(2,1)}, bf16[576,512]{1,0:T(8,128)(2,1)}, u32[]{:S(2)}, u32[]{:S(2)}) collective-permute-start(bf16[576,512]{1,0:T(8,128)(2,1)} %get-tuple-element.205), channel_id=1, source_target_pairs={{0,6},{2,0},{4,2},{6,4},{1,7},{3,1},{5,3},{7,5},{8,14},{10,8},{12,... | collective-permute-start | bytes 1769480 | tf_op jit(solution)/shard_map/ppermute | solution.py:878
  440.7 52.6 %collective-permute-start.39 = (bf16[576,512]{1,0:T(8,128)(2,1)}, bf16[576,512]{1,0:T(8,128)(2,1)}, u32[]{:S(2)}, u32[]{:S(2)}) collective-permute-start(bf16[576,512]{1,0:T(8,128)(2,1)} %get-tuple-element.207), channel_id=1, source_target_pairs={{0,4},{2,6},{4,0},{6,2},{1,5},{3,7},{5,1},{7,3},{8,12},{10,14},{12... | collective-permute-start | bytes 1769480 | tf_op jit(solution)/shard_map/ppermute | solution.py:878
  441.9 52.4 %collective-permute-start.40 = (bf16[576,512]{1,0:T(8,128)(2,1)}, bf16[576,512]{1,0:T(8,128)(2,1)}, u32[]{:S(2)}, u32[]{:S(2)}) collective-permute-start(bf16[576,512]{1,0:T(8,128)(2,1)} %get-tuple-element.208), channel_id=1, source_target_pairs={{0,2},{2,4},{4,6},{6,0},{1,3},{3,5},{5,7},{7,1},{8,10},{10,12},{12... | collective-permute-start | bytes 1769480 | tf_op jit(solution)/shard_map/ppermute | solution.py:878
  448.9 52.1 %copy-start.52 = (f32[512,1]{1,0:T(8,128)S(1)}, f32[512,1]{1,0:T(8,128)}, u32[]{:S(2)}) copy-start(f32[512,1]{1,0:T(8,128)} %copy-done.51) | copy-start | bytes 6148
  451.1 57.9 %collective-permute-start.35 = (bf16[512,512]{1,0:T(8,128)(2,1)S(1)}, bf16[512,512]{1,0:T(8,128)(2,1)S(1)}, u32[]{:S(2)}, u32[]{:S(2)}) collective-permute-start(bf16[512,512]{1,0:T(8,128)(2,1)S(1)} %get-tuple-element.198), channel_id=1, source_target_pairs={{0,2},{2,0},{4,6},{6,4},{1,3},{3,1},{5,7},{7,5},{8,10},{10,8},{12,... | collective-permute-start | bytes 1572872 | tf_op jit(solution)/shard_map/ppermute | solution.py:844
  456.4 40.5 %collective-permute-start.44 = (f32[34,128]{1,0:T(8,128)S(1)}, f32[34,128]{1,0:T(8,128)S(1)}, u32[]{:S(2)}, u32[]{:S(2)}) collective-permute-start(f32[34,128]{1,0:T(8,128)S(1)} %maximum_bitcast_fusion), channel_id=1, source_target_pairs={{0,8},{8,0},{16,24},{24,16},{1,9},{9,1},{17,25},{25,17},{2,10},{10... | collective-permute-start | bytes 52232 | tf_op jit(solution)/shard_map/ppermute | solution.py:844
  496.7 29.8 %collective-permute-start.53 = (bf16[192,512]{1,0:T(8,128)(2,1)}, bf16[192,512]{1,0:T(8,128)(2,1)S(1)}, u32[]{:S(2)}, u32[]{:S(2)}) collective-permute-start(bf16[192,512]{1,0:T(8,128)(2,1)} %get-tuple-element.231), channel_id=1, source_target_pairs={{0,8},{8,16},{16,24},{24,0},{1,9},{9,17},{17,25},{25,1},{2,10},{10... | collective-permute-start | bytes 589832 | tf_op jit(solution)/shard_map/ppermute | solution.py:893
  497.0 4.0 collective-permute-start.45
  501.0 3.8 collective-permute-start.46
  504.7 3.8 collective-permute-start.47
  508.6 15.8 %collective-permute-start.48 = (f32[38,128]{1,0:T(8,128)S(1)}, f32[38,128]{1,0:T(8,128)S(1)}, u32[]{:S(2)}, u32[]{:S(2)}) collective-permute-start(f32[38,128]{1,0:T(8,128)S(1)} %add.107), channel_id=1, source_target_pairs={{0,4},{2,6},{4,0},{6,2},{1,5},{3,7},{5,1},{7,3},{8,12},{10,14},{12... | collective-permute-start | bytes 58376 | tf_op jit(solution)/shard_map/ppermute | solution.py:844
  509.1 46.7 %collective-permute-start.36 = (bf16[512,512]{1,0:T(8,128)(2,1)}, bf16[512,512]{1,0:T(8,128)(2,1)}, u32[]{:S(2)}, u32[]{:S(2)}) collective-permute-start(bf16[512,512]{1,0:T(8,128)(2,1)} %copy-done.64), channel_id=1, source_target_pairs={{0,2},{2,0},{4,6},{6,4},{1,3},{3,1},{5,7},{7,5},{8,10},{10,8},{12,... | collective-permute-start | bytes 1572872 | tf_op jit(solution)/shard_map/ppermute | solution.py:844
  509.2 46.6 %collective-permute-start.37 = (bf16[512,512]{1,0:T(8,128)(2,1)S(1)}, bf16[512,512]{1,0:T(8,128)(2,1)}, u32[]{:S(2)}, u32[]{:S(2)}) collective-permute-start(bf16[512,512]{1,0:T(8,128)(2,1)S(1)} %shard_map.438), channel_id=1, source_target_pairs={{0,4},{2,6},{4,0},{6,2},{1,5},{3,7},{5,1},{7,3},{8,12},{10,14},{12... | collective-permute-start | bytes 1572872 | tf_op jit(solution)/shard_map/ppermute | solution.py:844
  515.0 12.8 %collective-permute-start.54 = (bf16[192,512]{1,0:T(8,128)(2,1)S(1)}, bf16[192,512]{1,0:T(8,128)(2,1)S(1)}, u32[]{:S(2)}, u32[]{:S(2)}) collective-permute-start(bf16[192,512]{1,0:T(8,128)(2,1)S(1)} %copy-done.69), channel_id=1, source_target_pairs={{0,16},{8,24},{16,0},{24,8},{1,17},{9,25},{17,1},{25,9},{2,18},{10... | collective-permute-start | bytes 589832 | tf_op jit(solution)/shard_map/ppermute | solution.py:893
  524.4 6.7 %collective-permute-start.55 = (bf16[192,512]{1,0:T(8,128)(2,1)S(1)}, bf16[192,512]{1,0:T(8,128)(2,1)S(1)}, u32[]{:S(2)}, u32[]{:S(2)}) collective-permute-start(bf16[192,512]{1,0:T(8,128)(2,1)S(1)} %copy-done.67), channel_id=1, source_target_pairs={{0,24},{8,0},{16,8},{24,16},{1,25},{9,1},{17,9},{25,17},{2,26},{10... | collective-permute-start | bytes 589832 | tf_op jit(solution)/shard_map/ppermute | solution.py:893
  526.5 6.2 %collective-permute-start.49 = (bf16[64,512]{1,0:T(8,128)(2,1)S(1)}, bf16[64,512]{1,0:T(8,128)(2,1)S(1)}, u32[]{:S(2)}, u32[]{:S(2)}) collective-permute-start(bf16[64,512]{1,0:T(8,128)(2,1)S(1)} %get-tuple-element.221), channel_id=1, source_target_pairs={{0,0},{2,8},{4,16},{6,24},{8,2},{10,10},{12,18},{14,26},{16,4},{18... | collective-permute-start | bytes 196616 | tf_op jit(solution)/shard_map/ppermute | solution.py:1134
  527.8 10.4 %collective-permute-start.50 = (bf16[64,512]{1,0:T(8,128)(2,1)S(1)}, bf16[64,512]{1,0:T(8,128)(2,1)S(1)}, u32[]{:S(2)}, u32[]{:S(2)}) collective-permute-start(bf16[64,512]{1,0:T(8,128)(2,1)S(1)} %get-tuple-element.222), channel_id=1, source_target_pairs={{0,2},{2,10},{4,18},{6,26},{8,4},{10,12},{12,20},{14,28},{16,6},{1... | collective-permute-start | bytes 196616 | tf_op jit(solution)/shard_map/ppermute | solution.py:1134
  531.2 9.1 %collective-permute-start.51 = (bf16[64,512]{1,0:T(8,128)(2,1)S(1)}, bf16[64,512]{1,0:T(8,128)(2,1)S(1)}, u32[]{:S(2)}, u32[]{:S(2)}) collective-permute-start(bf16[64,512]{1,0:T(8,128)(2,1)S(1)} %get-tuple-element.223), channel_id=1, source_target_pairs={{0,4},{2,12},{4,20},{6,28},{8,6},{10,14},{12,22},{14,30},{16,0},{1... | collective-permute-start | bytes 196616 | tf_op jit(solution)/shard_map/ppermute | solution.py:1134
  532.7 10.0 %collective-permute-start.52 = (bf16[64,512]{1,0:T(8,128)(2,1)S(1)}, bf16[64,512]{1,0:T(8,128)(2,1)S(1)}, u32[]{:S(2)}, u32[]{:S(2)}) collective-permute-start(bf16[64,512]{1,0:T(8,128)(2,1)S(1)} %get-tuple-element.224), channel_id=1, source_target_pairs={{0,6},{2,14},{4,22},{6,30},{8,0},{10,8},{12,16},{14,24},{16,2},{18... | collective-permute-start | bytes 196616 | tf_op jit(solution)/shard_map/ppermute | solution.py:1134
  538.2 16.5 %collective-permute-start.41 = (bf16[128,512]{1,0:T(8,128)(2,1)}, bf16[128,512]{1,0:T(8,128)(2,1)S(1)}, u32[]{:S(2)}, u32[]{:S(2)}) collective-permute-start(bf16[128,512]{1,0:T(8,128)(2,1)} %get-tuple-element.211), channel_id=1, source_target_pairs={{0,6},{2,0},{4,2},{6,4},{1,7},{3,1},{5,3},{7,5},{8,14},{10,8},{12,... | collective-permute-start | bytes 393224 | tf_op jit(solution)/shard_map/ppermute | solution.py:878
  540.2 15.4 %collective-permute-start.42 = (bf16[128,512]{1,0:T(8,128)(2,1)S(1)}, bf16[128,512]{1,0:T(8,128)(2,1)S(1)}, u32[]{:S(2)}, u32[]{:S(2)}) collective-permute-start(bf16[128,512]{1,0:T(8,128)(2,1)S(1)} %get-tuple-element.212), channel_id=1, source_target_pairs={{0,4},{2,6},{4,0},{6,2},{1,5},{3,7},{5,1},{7,3},{8,12},{10,14},{12... | collective-permute-start | bytes 393224 | tf_op jit(solution)/shard_map/ppermute | solution.py:878
  542.7 12.9 %collective-permute-start.43 = (bf16[128,512]{1,0:T(8,128)(2,1)S(1)}, bf16[128,512]{1,0:T(8,128)(2,1)S(1)}, u32[]{:S(2)}, u32[]{:S(2)}) collective-permute-start(bf16[128,512]{1,0:T(8,128)(2,1)S(1)} %get-tuple-element.213), channel_id=1, source_target_pairs={{0,2},{2,4},{4,6},{6,0},{1,3},{3,5},{5,7},{7,1},{8,10},{10,12},{12... | collective-permute-start | bytes 393224 | tf_op jit(solution)/shard_map/ppermute | solution.py:878
  (77 other events, 399.1 us)
Sparse Core Ops, SparseCore 0:
  58.5 43.7 all-gather.4
  127.5 109.0 all-gather.6
  302.8 133.6 reduce-scatter.2
  439.8 59.5 reduce-scatter.4

commit v4 on v3

--- a/solution.py
+++ b/solution.py
@@ -976,7 +976,7 @@
     )
 
 
-def regroup(parts, source, target, cuts, after=()):
+def regroup(parts, source, target, cuts, after=(), top=0):
     size = len(parts)
     sources = [source(k) for k in range(size)]
     targets = [target(k) for k in range(size)]
@@ -986,7 +986,7 @@
         places, ins = refs[: 2 * size], refs[2 * size : 3 * size]
         outs, held = refs[3 * size : -1], refs[-1]
         for k in range(size):
-            held[places[k][0]] = ins[k][...]
+            held[places[k][0]] = ins[k][top:, :]
         for i, (first, n) in enumerate(zip(starts, cuts)):
             for k in range(size):
                 outs[i * size + k][...] = held[places[size + k][0], first : first + n]
@@ -997,7 +997,7 @@
         [shape((n, width), BF) for n in cuts for _ in range(size)],
         parts,
         sources + targets,
-        scratch=[pltpu.VMEM((size, rows, width), BF)],
+        scratch=[pltpu.VMEM((size, rows - top, width), BF)],
         after=after,
     )
     return [outs[i * size : (i + 1) * size] for i in range(len(cuts))]
@@ -1135,14 +1135,16 @@
     return result
 
 
-def out_pieces(messages, inner, z):
+def out_pieces(messages, inner, z, after=()):
     size = len(messages)
     quarter = quarter_index()
     parts = regroup(
-        [m[-inner:] for m in messages],
+        messages,
         lambda k: ahead(z, k, size),
         lambda k: ahead(quarter, k, size),
         [inner],
+        after,
+        messages[0].shape[0] - inner,
     )[0]
     return along_quarters(parts, True)
 
@@ -1181,7 +1183,7 @@
     return m, v, w
 
 
-def place_columns(messages, rows, cuts, z):
+def place_columns(messages, rows, cuts, z, after=()):
     size = len(messages)
 
     def kernel(z, *refs):
@@ -1196,7 +1198,7 @@
                     at = at + w
 
     out = [shape((rows, size * sum(w for _, _, w in cut)), BF) for cut in cuts]
-    return call(kernel, out, messages, [z])
+    return call(kernel, out, messages, [z], after=after)
 
 
 def flat(values):
@@ -1233,8 +1235,8 @@
 def adamw(weight, moment, second, grad, rate, decay):
     moment_new = BETA_ONE * moment + (1.0 - BETA_ONE) * grad
     second_new = BETA_TWO * second + (1.0 - BETA_TWO) * grad * grad
-    first_hat = moment_new / (1.0 - BETA_ONE**STEP)
-    second_hat = second_new / (1.0 - BETA_TWO**STEP)
+    first_hat = moment_new * (1.0 / (1.0 - BETA_ONE**STEP))
+    second_hat = second_new * (1.0 / (1.0 - BETA_TWO**STEP))
     weight_new = weight - rate * (first_hat / (jnp.sqrt(second_hat) + ADAM_EPS) + decay * weight)
     return (moment_new, second_new, weight_new)
 
@@ -1410,17 +1412,19 @@
 
     down_new = update_out(
         (down_weight, down_moment, down_second),
-        out_pieces(feed_messages, down_inner, z),
+        out_pieces(feed_messages, down_inner, z, [gain_part]),
         RATES[4],
         quarter_place,
     )
+    attention_pieces, output_pieces = split_attention(
+        attention_total, 1, in_rows, output_inner, z
+    )
     cut = [(t, 0, COLUMNS) for t in range(gateup_terms)]
-    (gateup_total,) = place_columns(feed_messages, in_rows, [cut], z)
-    gateup_new, gateup_flat = update_pair(
+    (gateup_total,) = place_columns(
+        feed_messages, in_rows, [cut], z, attention_pieces[:1]
+    )
+    gateup_new, _ = update_pair(
         (gateup_weight, gateup_moment, gateup_second), gateup_total, RATES[3]
-    )
-    attention_pieces, output_pieces = split_attention(
-        attention_total, 1, in_rows, output_inner, z, [gateup_flat]
     )
     output_pieces = turned_back(output_pieces)
     attention_messages = along_row(attention_pieces, False)

time: 582 us -> 585 us (level)
  starting transfers between devices: 124 us -> 134 us
  waiting for transfers between devices: 229 us -> 221 us
    ppermute x4, starting transfers between devices: 10.3 us -> 20.9 us  [turned_back(): result.append(lax.ppermute(piece, ('dp', 'row'), pairs))]
    ppermute x15, waiting for transfers between devices: 39.9 us -> 31 us  [along_row(): lax.ppermute(p, 'row', [(i, (i + sign * k) % size) for i in range(size)])]
    unnamed x162 -> x178, local copies, waits for them, and re-layouts: 32.6 us -> 35 us
  transfers between devices with their start and end apart: 60 -> 60, of which waited for: 24 -> 26; matrix products, arithmetic and copies ran while one was open for 2% -> 1% of each run, Pallas kernels for 22% -> 23%
where the time goes in v4:
time: 585 us; the launch traced here: 576 us
  waiting for transfers between devices  221 us (38%)
  Pallas kernels  159 us (27%)
  starting transfers between devices  134 us (23%)
  local copies, waits for them, and re-layouts  38.6 us (7%)
  between operations  15.3 us (3%)
  other arithmetic  7.4 us (1%)
    ppermute x29, waiting for transfers between devices, swap(): lax.ppermute(value, axis, [(i, i ^ step) for i in range(lax.axis_size(axi...  156 us
    pallas_call x39, Pallas kernels, call(): pl.pallas_call(run, grid_spec=pltpu.PrefetchScalarGridSpec(num_scalar_pre...  143 us
    ppermute x29, starting transfers between devices, swap(): lax.ppermute(value, axis, [(i, i ^ step) for i in range(lax.axis_size(axi...  68.2 us
    unnamed x178, local copies, waits for them, and re-layouts  35 us
    ppermute x15, starting transfers between devices, along_row(): lax.ppermute(p, 'row', [(i, (i + sign * k) % size) for i in range(size)])  34.9 us
    ppermute x15, waiting for transfers between devices, along_row(): lax.ppermute(p, 'row', [(i, (i + sign * k) % size) for i in range(size)])  31 us
    ppermute x4, starting transfers between devices, turned_back(): result.append(lax.ppermute(piece, ('dp', 'row'), pairs))  20.9 us
    ppermute x1, waiting for transfers between devices, body(): lax.ppermute(keys_values, 'col', [(i, i + 1) for i in range(cols - 1)])  14.9 us
  transfers between devices with their start and end apart: 60, of which 26 were waited for; matrix products, arithmetic and copies ran while one was open for 1% of the time, Pallas kernels for 23%

profile of v4, /device:TPU:0, one launch (start us, length us, event | category | flops | bytes accessed | tf_op | source)
XLA Modules:
  0.0 575.8 jit_solution(9116728058507595673)
XLA Ops:
  7.2 4.1 collective-permute-start.1
  11.3 2.4 shard_map.407
  13.8 2.3 shard_map.408
  20.6 3.5 collective-permute-done.6.refs_9_
  25.9 3.5 collective-permute-start.5
  34.0 12.0 %collective-permute-start.10 = (bf16[64,512]{1,0:T(8,128)(2,1)S(1)}, bf16[64,512]{1,0:T(8,128)(2,1)S(1)}, u32[]{:S(2)}, u32[]{:S(2)}) collective-permute-start(bf16[64,512]{1,0:T(8,128)(2,1)S(1)} %get-tuple-element.140), channel_id=1, source_target_pairs={{0,4},{2,6},{4,0},{6,2},{1,5},{3,7},{5,1},{7,3},{8,12},{10,14},{12... | collective-permute-start | bytes 196616 | tf_op jit(solution)/shard_map/ppermute | solution.py:878
  46.0 3.7 collective-permute-start.11
  49.7 3.1 shard_map.410
  55.4 2.1 shard_map.411.refs_5_
  59.4 2.9 collective-permute-start.14
  64.4 46.5 %collective-permute-done.refs_2_ = bf16[512,512]{1,0:T(8,128)(2,1)S(1)} collective-permute-done((bf16[512,512]{1,0:T(8,128)(2,1)S(1)}, bf16[512,512]{1,0:T(8,128)(2,1)S(1)}, u32[]{:S(2)}, u32[]{:S(2)}) %collective-permute-start) | collective-permute-done | bytes 524320 | tf_op jit(solution)/shard_map/ppermute | solution.py:844
  111.0 11.1 %collective-permute-done.2.refs_4_ = bf16[512,512]{1,0:T(8,128)(2,1)S(1)} collective-permute-done((bf16[512,512]{1,0:T(8,128)(2,1)}, bf16[512,512]{1,0:T(8,128)(2,1)S(1)}, u32[]{:S(2)}, u32[]{:S(2)}) %collective-permute-start.2) | collective-permute-done | bytes 524320 | tf_op jit(solution)/shard_map/ppermute | solution.py:844
  122.1 2.2 shard_map.412.refs_5_.refs_0_.refs_4_.refs_3_
  133.7 7.8 %shard_map.415 = (bf16[512,2048]{1,0:T(8,128)(2,1)S(1)}, f32[512,1]{1,0:T(8,128)S(1)}, f32[512,512]{1,0:T(8,128)S(1)}, f32[512,256]{1,0:T(8,128)S(1)}, bf16[512,...) custom-call(bf16[512,2048]{1,0:T(8,128)(2,1)S(1)} %copy-done.1, f32[1,2048]{1,0:T(1,128)S(1)} %bitcast.102, ...), custom_call_target="tpu_custom_call" | custom-call | tf_op jit(solution)/shard_map/pallas_call | solution.py:215
  146.2 3.6 collective-permute-start.15
  149.9 6.5 %collective-permute-done.17.refs_4_.refs_3_ = bf16[512,512]{1,0:T(8,128)(2,1)} collective-permute-done((bf16[512,512]{1,0:T(8,128)(2,1)}, bf16[512,512]{1,0:T(8,128)(2,1)}, u32[]{:S(2)}, u32[]{:S(2)}) %collective-permute-start.17) | collective-permute-done | bytes 524320 | tf_op jit(solution)/shard_map/ppermute | solution.py:844
  157.3 14.9 %collective-permute-done.15.refs_7_.refs_8_ = bf16[512,512]{1,0:T(8,128)(2,1)S(1)} collective-permute-done((bf16[512,512]{1,0:T(8,128)(2,1)S(1)}, bf16[512,512]{1,0:T(8,128)(2,1)S(1)}, u32[]{:S(2)}, u32[]{:S(2)}) %collective-permute-start.15) | collective-permute-done | bytes 524320 | tf_op jit(solution)/shard_map/ppermute | solution.py:1331
  174.2 7.3 %shard_map.416 = (bf16[512,512]{1,0:T(8,128)(2,1)S(1)}, f32[4,512,1]{2,1,0:T(8,128)S(1)}) custom-call(s32[1]{0:T(128)} %bitcast.1.refs_0_, s32[512,1]{1,0:T(8,128)S(1)} %copy-done.18, s32[1,512]{1,0:T(1,128)S(1)} %bitcast.105, s32[1,512]{1,0:T(1,128)S(1)} %bitcast.107, bf16[512,512]{1,0:T(8,128)(2,1)S(1)} %copy-done.26, ...), custom_call_target="tpu_custom_call" | custom-call | tf_op jit(solution)/shard_map/pallas_call | solution.py:93
  181.6 4.4 shard_map.417
  186.0 11.8 %collective-permute-done.19.refs_1_ = bf16[128,2048]{1,0:T(8,128)(2,1)S(1)} collective-permute-done((bf16[128,2048]{1,0:T(8,128)(2,1)S(1)}, bf16[128,2048]{1,0:T(8,128)(2,1)S(1)}, u32[]{:S(2)}, u32[]{:S(2)}) %collective-permute-start.19) | collective-permute-done | bytes 524320 | tf_op jit(solution)/shard_map/ppermute | solution.py:844
  198.0 3.0 collective-permute-start.21
  201.1 18.8 %collective-permute-done.20.refs_2_ = bf16[128,2048]{1,0:T(8,128)(2,1)S(1)} collective-permute-done((bf16[128,2048]{1,0:T(8,128)(2,1)S(1)}, bf16[128,2048]{1,0:T(8,128)(2,1)S(1)}, u32[]{:S(2)}, u32[]{:S(2)}) %collective-permute-start.20) | collective-permute-done | bytes 524320 | tf_op jit(solution)/shard_map/ppermute | solution.py:844
  223.4 16.5 %collective-permute-start.22 = (bf16[128,2048]{1,0:T(8,128)(2,1)}, bf16[128,2048]{1,0:T(8,128)(2,1)}, u32[]{:S(2)}, u32[]{:S(2)}) collective-permute-start(bf16[128,2048]{1,0:T(8,128)(2,1)} %get-tuple-element.159.refs_0_), channel_id=1, source_target_pairs={{0,2},{2,0},{4,6},{6,4},{1,3},{3,1},{5,7},{7,5},{8,10},{10,8},{12,... | collective-permute-start | bytes 1572872 | tf_op jit(solution)/shard_map/ppermute | solution.py:844
  240.3 9.7 %collective-permute-start.24 = (bf16[128,2048]{1,0:T(8,128)(2,1)}, bf16[128,2048]{1,0:T(8,128)(2,1)}, u32[]{:S(2)}, u32[]{:S(2)}) collective-permute-start(bf16[128,2048]{1,0:T(8,128)(2,1)} %collective-permute-done.23.refs_2_), channel_id=1, source_target_pairs={{0,2},{2,0},{4,6},{6,4},{1,3},{3,1},{5,7},{7,5},{8,10},{10,8},{12,... | collective-permute-start | bytes 1572872 | tf_op jit(solution)/shard_map/ppermute | solution.py:844
  250.0 2.6 shard_map.420.refs_0_.refs_6_
  255.5 6.8 %shard_map.421.refs_5_ = f32[512,1536]{1,0:T(8,128)S(1)} custom-call(bf16[512,2048]{1,0:T(8,128)(2,1)S(1)} %copy-done.3, bf16[2,4,2304,512]{3,2,1,0:T(8,128)(2,1)} %bitcast.110, bf16[128,2048]{1,0:T(8,128)(2,1)} %collective-permute-done.23.refs_2_), custom_call_target="tpu_custom_call" | custom-call | tf_op jit(solution)/shard_map/pallas_call | solution.py:215
  262.3 11.6 %shard_map.422 = (bf16[512,1536]{1,0:T(8,128)(2,1)S(1)}, bf16[512,3072]{1,0:T(8,128)(2,1)S(1)}) custom-call(bf16[128,2048]{1,0:T(8,128)(2,1)} %get-tuple-element.159.refs_0_, bf16[128,2048]{1,0:T(8,128)(2,1)} %collective-permute-done.22.refs_1_, bf16[128,2048]{1,0:T(8,128)(2,1)} %collective-permute-done.23.refs_2_, ...), custom_call_target="tpu_custom_call" | custom-call | tf_op jit(solution)/shard_map/pallas_call | solution.py:215
  274.0 10.0 %shard_map.423 = (f32[128,2048]{1,0:T(8,128)S(1)}, bf16[128,2048]{1,0:T(8,128)(2,1)S(1)}, bf16[128,2048]{1,0:T(8,128)(2,1)S(1)}, bf16[128,2048]{1,0:T(8,128)(2,1)S(1)}) custom-call(bf16[512,3072]{1,0:T(8,128)(2,1)S(1)} %get-tuple-element.162.refs_0_.refs_4_, bf16[2,4,2304,512]{3,2,1,0:T(8,128)(2,1)} %bitcast.112), custom_call_target="tpu_custom_call" | custom-call | tf_op jit(solution)/shard_map/pallas_call | solution.py:215
  284.8 17.2 %shard_map.424 = bf16[2,4,2304,512]{3,2,1,0:T(8,128)(2,1)} custom-call(bf16[128,2048]{1,0:T(8,128)(2,1)} %get-tuple-element.159.refs_0_, bf16[128,2048]{1,0:T(8,128)(2,1)} %collective-permute-done.22.refs_1_, bf16[128,2048]{1,0:T(8,128)(2,1)} %collective-permute-done.23.refs_2_, bf16[128,2048]{1,0:T(8,128)(2,1)} %collective-permute-done.24.refs_3_, ...), custom_call_target="tpu_custom_call" | custom-call | tf_op jit(solution)/shard_map/pallas_call | solution.py:215
  306.8 2.3 collective-permute-start.27
  309.1 12.8 %collective-permute-done.26.refs_1_ = bf16[128,2048]{1,0:T(8,128)(2,1)S(1)} collective-permute-done((bf16[128,2048]{1,0:T(8,128)(2,1)}, bf16[128,2048]{1,0:T(8,128)(2,1)S(1)}, u32[]{:S(2)}, u32[]{:S(2)}) %collective-permute-start.26) | collective-permute-done | bytes 524320 | tf_op jit(solution)/shard_map/ppermute | solution.py:844
  321.9 6.8 %collective-permute-done.27.refs_2_ = bf16[128,2048]{1,0:T(8,128)(2,1)S(1)} collective-permute-done((bf16[128,2048]{1,0:T(8,128)(2,1)S(1)}, bf16[128,2048]{1,0:T(8,128)(2,1)S(1)}, u32[]{:S(2)}, u32[]{:S(2)}) %collective-permute-start.27) | collective-permute-done | bytes 524320 | tf_op jit(solution)/shard_map/ppermute | solution.py:844
  329.5 3.5 shard_map.426
  333.2 7.9 %collective-permute-start.28 = (bf16[128,2048]{1,0:T(8,128)(2,1)S(1)}, bf16[128,2048]{1,0:T(8,128)(2,1)S(1)}, u32[]{:S(2)}, u32[]{:S(2)}) collective-permute-start(bf16[128,2048]{1,0:T(8,128)(2,1)S(1)} %get-tuple-element.171.refs_3_.refs_1_), channel_id=1, source_target_pairs={{0,2},{2,0},{4,6},{6,4},{1,3},{3,1},{5,7},{7,5},{8,10},{10,8},{12,... | collective-permute-start | bytes 1572872 | tf_op jit(solution)/shard_map/ppermute | solution.py:844
  341.1 13.5 %collective-permute-done.29.refs_3_ = bf16[128,2048]{1,0:T(8,128)(2,1)S(1)} collective-permute-done((bf16[128,2048]{1,0:T(8,128)(2,1)S(1)}, bf16[128,2048]{1,0:T(8,128)(2,1)S(1)}, u32[]{:S(2)}, u32[]{:S(2)}) %collective-permute-start.29) | collective-permute-done | bytes 524320 | tf_op jit(solution)/shard_map/ppermute | solution.py:844
  354.6 6.0 %shard_map.427.refs_6_.refs_1_ = bf16[512,2048]{1,0:T(8,128)(2,1)S(1)} custom-call(bf16[512,1536]{1,0:T(8,128)(2,1)S(1)} %copy-done.11, f32[128,2048]{1,0:T(8,128)S(1)} %copy-done.15, bf16[2,4,2304,512]{3,2,1,0:T(8,128)(2,1)} %bitcast.113, bf16[128,2048]{1,0:T(8,128)(2,1)S(1)} %get-tuple-element.171.refs_3_.refs_1_), custom_call_target="tpu_custom_call" | custom-call | tf_op jit(solution)/shard_map/pallas_call | solution.py:215
  362.0 3.9 collective-permute-done.30.refs_4_
  365.9 4.2 shard_map.428
  373.0 9.2 %shard_map.432 = (f32[512,512]{1,0:T(8,128)S(1)}, f32[512,256]{1,0:T(8,128)S(1)}, f32[512,256]{1,0:T(8,128)S(1)}, bf16[512,512]{1,0:T(8,128)(2,1)S(1)}) custom-call(s32[1]{0:T(128)} %bitcast.1.refs_0_, s32[512,1]{1,0:T(8,128)S(1)} %copy-done.19, s32[1,512]{1,0:T(1,128)S(1)} %bitcast.106, s32[1,512]{1,0:T(1,128)S(1)} %bitcast.108, ...), custom_call_target="tpu_custom_call" | custom-call | tf_op jit(solution)/shard_map/pallas_call | solution.py:163
  383.7 11.2 %collective-permute-start.33 = (bf16[512,512]{1,0:T(8,128)(2,1)S(1)}, bf16[512,512]{1,0:T(8,128)(2,1)S(1)}, u32[]{:S(2)}, u32[]{:S(2)}) collective-permute-start(bf16[512,512]{1,0:T(8,128)(2,1)S(1)} %shard_map.430), channel_id=1, source_target_pairs={{0,4},{2,6},{4,0},{6,2},{1,5},{3,7},{5,1},{7,3},{8,12},{10,14},{12... | collective-permute-start | bytes 1572872 | tf_op jit(solution)/shard_map/ppermute | solution.py:844
  396.2 6.6 %collective-permute-done.32.refs_1_ = bf16[512,512]{1,0:T(8,128)(2,1)S(1)} collective-permute-done((bf16[512,512]{1,0:T(8,128)(2,1)S(1)}, bf16[512,512]{1,0:T(8,128)(2,1)S(1)}, u32[]{:S(2)}, u32[]{:S(2)}) %collective-permute-start.32) | collective-permute-done | bytes 524320 | tf_op jit(solution)/shard_map/ppermute | solution.py:844
  402.8 4.7 collective-permute-done.33.refs_2_
  408.7 8.7 %collective-permute-done.34.refs_5_ = bf16[512,512]{1,0:T(8,128)(2,1)S(1)} collective-permute-done((bf16[512,512]{1,0:T(8,128)(2,1)S(1)}, bf16[512,512]{1,0:T(8,128)(2,1)S(1)}, u32[]{:S(2)}, u32[]{:S(2)}) %collective-permute-start.34) | collective-permute-done | bytes 524320 | tf_op jit(solution)/shard_map/ppermute | solution.py:1369
  417.4 2.6 shard_map.433
  420.0 9.7 %shard_map.434 = bf16[2,4,768,512]{3,2,1,0:T(8,128)(2,1)} custom-call(bf16[512,2048]{1,0:T(8,128)(2,1)S(1)} %copy-done.31, bf16[512,1024]{1,0:T(8,128)(2,1)S(1)} %get-tuple-element.187.refs_1_, bf16[512,512]{1,0:T(8,128)(2,1)S(1)} %copy-done.24, bf16[512,2048]{1,0:T(8,128)(2,1)S(1)} %copy-done.9), custom_call_target="tpu_custom_call" | custom-call | tf_op jit(solution)/shard_map/pallas_call | solution.py:215
  430.7 5.9 %reduce-scatter.3.cloned.1.call-done.refs_1_ = bf16[2304,512]{1,0:T(8,128)(2,1)} async-done(((bf16[18432,512]{1,0:T(8,128)(2,1)}), bf16[2304,512]{1,0:T(8,128)(2,1)}) %reduce-scatter.3.cloned.1.call-update) | async-done | bytes 2359312 | tf_op jit(solution)/shard_map/reduce_scatter | solution.py:903
  442.0 6.2 %shard_map.436 = (bf16[512,2048]{1,0:T(8,128)(2,1)S(1)}, f32[512,1]{1,0:T(8,128)S(1)}, f32[1,2048]{1,0:T(1,128)S(1)}) custom-call(s32[1]{0:T(128)} %bitcast.refs_0_, bf16[512,1024]{1,0:T(8,128)(2,1)S(1)} %copy-done.13, bf16[2,4,768,512]{3,2,1,0:T(8,128)(2,1)} %bitcast.117, bf16[512,2048]{1,0:T(8,128)(2,1)S(1)} %copy-done.1, f32[512,1]{1,0:T(8,128)S(1)} %copy-done.35, ...), custom_call_target="tpu_custom_call" | custom-call | tf_op jit(solution)/shard_map/pallas_call | solution.py:215
  451.1 2.3 collective-permute-start.35
  453.5 2.9 collective-permute-done.41.refs_2_.refs_9_
  458.9 2.4 collective-permute-done.43
  461.3 4.0 collective-permute-done.44
  465.3 28.1 %collective-permute-done.51.refs_3_.refs_10_ = bf16[576,512]{1,0:T(8,128)(2,1)} collective-permute-done((bf16[576,512]{1,0:T(8,128)(2,1)}, bf16[576,512]{1,0:T(8,128)(2,1)}, u32[]{:S(2)}, u32[]{:S(2)}) %collective-permute-start.51) | collective-permute-done | bytes 589856 | tf_op jit(solution)/shard_map/ppermute | solution.py:878
  493.4 2.1 shard_map.446
  497.1 3.8 collective-permute-done.45
  502.4 1.7 collective-permute-start.37
  511.1 2.8 collective-permute-start.48
  513.9 2.3 collective-permute-start.49
  516.2 15.2 %collective-permute-start.50 = (bf16[64,512]{1,0:T(8,128)(2,1)S(1)}, bf16[64,512]{1,0:T(8,128)(2,1)S(1)}, u32[]{:S(2)}, u32[]{:S(2)}) collective-permute-start(bf16[64,512]{1,0:T(8,128)(2,1)S(1)} %get-tuple-element.220), channel_id=1, source_target_pairs={{0,6},{2,14},{4,22},{6,30},{8,0},{10,8},{12,16},{14,24},{16,2},{18... | collective-permute-start | bytes 196616 | tf_op jit(solution)/shard_map/ppermute | solution.py:1134
  533.4 3.0 collective-permute-start.39
  536.4 2.0 collective-permute-start.40
  538.6 5.9 %shard_map.447 = (f32[768,512]{1,0:T(8,128)}, f32[768,512]{1,0:T(8,128)}, f32[768,512]{1,0:T(8,128)}) custom-call(s32[1]{0:T(128)} %bitcast.15.refs_0_.refs_1_, bf16[192,512]{1,0:T(8,128)(2,1)S(1)} %get-tuple-element.230.refs_1_, bf16[192,512]{1,0:T(8,128)(2,1)} %collective-permute-done.53.refs_2_, bf16[192,512]{1,0:T(8,128)(2,1)S(1)} %collective-permute-done.54.refs_3_, ...), custom_call_target="tpu_custom_call" | custom-call | tf_op jit(solution)/shard_map/pallas_call | solution.py:215
  547.6 8.2 %shard_map.445 = (f32[6144,128]{1,0:T(8,128)}, f32[6144,128]{1,0:T(8,128)}, f32[6144,128]{1,0:T(8,128)}) custom-call(bf16[6144,128]{1,0:T(8,128)(2,1)} %reshape.288.refs_0_, f32[6144,128]{1,0:T(8,128)} %bitcast.99, f32[6144,128]{1,0:T(8,128)} %bitcast.120, f32[6144,128]{1,0:T(8,128)} %bitcast.121), custom_call_target="tpu_custom_call" | custom-call | tf_op jit(solution)/shard_map/pallas_call | solution.py:215
  555.8 3.9 shard_map.443
  565.1 3.7 shard_map.442
  (319 shorter events, 88.4 us)
Async XLA Ops:
  7.2 126.5 %all-gather.5.cloned.1.call-start = ((), (), s32[]{:S(2)}) async-start(), calls=%async_computation.4 | async-start | bytes 7077888 | tf_op jit(solution)/shard_map/all_gather | solution.py:897
  7.2 48.1 %collective-permute-start.1 = (bf16[512,512]{1,0:T(8,128)(2,1)}, bf16[512,512]{1,0:T(8,128)(2,1)}, u32[]{:S(2)}, u32[]{:S(2)}) collective-permute-start(bf16[512,512]{1,0:T(8,128)(2,1)} %refs_1_.7), channel_id=1, source_target_pairs={{0,4},{2,6},{4,0},{6,2},{1,5},{3,7},{5,1},{7,3},{8,12},{10,14},{12... | collective-permute-start | bytes 1572872 | tf_op jit(solution)/shard_map/ppermute | solution.py:844
  11.3 38.4 %copy-start.7 = (f32[128,2,3072]{2,1,0:T(2,128)S(1)}, f32[128,2,3072]{2,1,0:T(2,128)}, u32[]{:S(2)}) copy-start(f32[128,2,3072]{2,1,0:T(2,128)} %refs_1_.6) | copy-start | bytes 9437188
  16.1 8.1 %collective-permute-start.6 = (bf16[256,512]{1,0:T(8,128)(2,1)S(1)}, bf16[256,512]{1,0:T(8,128)(2,1)S(1)}, u32[]{:S(2)}, u32[]{:S(2)}) collective-permute-start(bf16[256,512]{1,0:T(8,128)(2,1)S(1)} %get-tuple-element.135), channel_id=1, source_target_pairs={{0,8},{8,16},{16,24},{24,0},{1,9},{9,17},{17,25},{25,1},{2,10},{10... | collective-permute-start | bytes 786440 | tf_op jit(solution)/shard_map/ppermute | solution.py:893
  16.1 9.2 %collective-permute-start.7 = (bf16[256,512]{1,0:T(8,128)(2,1)S(1)}, bf16[256,512]{1,0:T(8,128)(2,1)S(1)}, u32[]{:S(2)}, u32[]{:S(2)}) collective-permute-start(bf16[256,512]{1,0:T(8,128)(2,1)S(1)} %get-tuple-element.136), channel_id=1, source_target_pairs={{0,16},{8,24},{16,0},{24,8},{1,17},{9,25},{17,1},{25,9},{2,18},{10... | collective-permute-start | bytes 786440 | tf_op jit(solution)/shard_map/ppermute | solution.py:893
  17.6 11.9 %collective-permute-start.8 = (bf16[256,512]{1,0:T(8,128)(2,1)}, bf16[256,512]{1,0:T(8,128)(2,1)}, u32[]{:S(2)}, u32[]{:S(2)}) collective-permute-start(bf16[256,512]{1,0:T(8,128)(2,1)} %get-tuple-element.137), channel_id=1, source_target_pairs={{0,24},{8,0},{16,8},{24,16},{1,25},{9,1},{17,9},{25,17},{2,26},{10... | collective-permute-start | bytes 786440 | tf_op jit(solution)/shard_map/ppermute | solution.py:893
  19.0 15.0 %collective-permute-start.3 = (bf16[128,512]{1,0:T(8,128)(2,1)}, bf16[128,512]{1,0:T(8,128)(2,1)}, u32[]{:S(2)}, u32[]{:S(2)}) collective-permute-start(bf16[128,512]{1,0:T(8,128)(2,1)} %get-tuple-element.131), channel_id=1, source_target_pairs={{0,2},{2,4},{4,6},{6,0},{1,3},{3,5},{5,7},{7,1},{8,10},{10,12},{12... | collective-permute-start | bytes 393224 | tf_op jit(solution)/shard_map/ppermute | solution.py:878
  24.8 21.2 %collective-permute-start.4 = (bf16[128,512]{1,0:T(8,128)(2,1)}, bf16[128,512]{1,0:T(8,128)(2,1)}, u32[]{:S(2)}, u32[]{:S(2)}) collective-permute-start(bf16[128,512]{1,0:T(8,128)(2,1)} %get-tuple-element.132), channel_id=1, source_target_pairs={{0,4},{2,6},{4,0},{6,2},{1,5},{3,7},{5,1},{7,3},{8,12},{10,14},{12... | collective-permute-start | bytes 393224 | tf_op jit(solution)/shard_map/ppermute | solution.py:878
  25.9 29.4 %collective-permute-start.5 = (bf16[128,512]{1,0:T(8,128)(2,1)}, bf16[128,512]{1,0:T(8,128)(2,1)}, u32[]{:S(2)}, u32[]{:S(2)}) collective-permute-start(bf16[128,512]{1,0:T(8,128)(2,1)} %get-tuple-element.133), channel_id=1, source_target_pairs={{0,6},{2,0},{4,2},{6,4},{1,7},{3,1},{5,3},{7,5},{8,14},{10,8},{12,... | collective-permute-start | bytes 393224 | tf_op jit(solution)/shard_map/ppermute | solution.py:878
  32.5 22.9 %collective-permute-start.9 = (bf16[64,512]{1,0:T(8,128)(2,1)S(1)}, bf16[64,512]{1,0:T(8,128)(2,1)S(1)}, u32[]{:S(2)}, u32[]{:S(2)}) collective-permute-start(bf16[64,512]{1,0:T(8,128)(2,1)S(1)} %get-tuple-element.139), channel_id=1, source_target_pairs={{0,2},{2,4},{4,6},{6,0},{1,3},{3,5},{5,7},{7,1},{8,10},{10,12},{12... | collective-permute-start | bytes 196616 | tf_op jit(solution)/shard_map/ppermute | solution.py:878
  34.0 21.3 %collective-permute-start.10 = (bf16[64,512]{1,0:T(8,128)(2,1)S(1)}, bf16[64,512]{1,0:T(8,128)(2,1)S(1)}, u32[]{:S(2)}, u32[]{:S(2)}) collective-permute-start(bf16[64,512]{1,0:T(8,128)(2,1)S(1)} %get-tuple-element.140), channel_id=1, source_target_pairs={{0,4},{2,6},{4,0},{6,2},{1,5},{3,7},{5,1},{7,3},{8,12},{10,14},{12... | collective-permute-start | bytes 196616 | tf_op jit(solution)/shard_map/ppermute | solution.py:878
  46.0 9.3 %collective-permute-start.11 = (bf16[64,512]{1,0:T(8,128)(2,1)S(1)}, bf16[64,512]{1,0:T(8,128)(2,1)S(1)}, u32[]{:S(2)}, u32[]{:S(2)}) collective-permute-start(bf16[64,512]{1,0:T(8,128)(2,1)S(1)} %get-tuple-element.141), channel_id=1, source_target_pairs={{0,6},{2,0},{4,2},{6,4},{1,7},{3,1},{5,3},{7,5},{8,14},{10,8},{12,... | collective-permute-start | bytes 196616 | tf_op jit(solution)/shard_map/ppermute | solution.py:878
  58.4 195.6 %all-gather.7.cloned.1.call-start = ((), (), s32[]{:S(2)}) async-start(), calls=%async_computation.5 | async-start | bytes 21233664 | tf_op jit(solution)/shard_map/all_gather | solution.py:897
  58.4 67.2 %collective-permute-start.12 = (bf16[576,512]{1,0:T(8,128)(2,1)S(1)}, bf16[576,512]{1,0:T(8,128)(2,1)S(1)}, u32[]{:S(2)}, u32[]{:S(2)}) collective-permute-start(bf16[576,512]{1,0:T(8,128)(2,1)S(1)} %copy-done.75), channel_id=1, source_target_pairs={{0,2},{2,4},{4,6},{6,0},{1,3},{3,5},{5,7},{7,1},{8,10},{10,12},{12... | collective-permute-start | bytes 1769480 | tf_op jit(solution)/shard_map/ppermute | solution.py:878
  58.5 67.1 %collective-permute-start.13 = (bf16[576,512]{1,0:T(8,128)(2,1)S(1)}, bf16[576,512]{1,0:T(8,128)(2,1)S(1)}, u32[]{:S(2)}, u32[]{:S(2)}) collective-permute-start(bf16[576,512]{1,0:T(8,128)(2,1)S(1)} %copy-done.73), channel_id=1, source_target_pairs={{0,4},{2,6},{4,0},{6,2},{1,5},{3,7},{5,1},{7,3},{8,12},{10,14},{12... | collective-permute-start | bytes 1769480 | tf_op jit(solution)/shard_map/ppermute | solution.py:878
  59.4 66.2 %copy-start.22 = (bf16[576,512]{1,0:T(8,128)(2,1)S(1)}, bf16[576,512]{1,0:T(8,128)(2,1)}, u32[]{:S(2)}) copy-start(bf16[576,512]{1,0:T(8,128)(2,1)} %copy-done.21) | copy-start | bytes 1769476
  59.4 66.2 %collective-permute-start.14 = (bf16[576,512]{1,0:T(8,128)(2,1)S(1)}, bf16[576,512]{1,0:T(8,128)(2,1)S(1)}, u32[]{:S(2)}, u32[]{:S(2)}) collective-permute-start(bf16[576,512]{1,0:T(8,128)(2,1)S(1)} %copy-done.71), channel_id=1, source_target_pairs={{0,6},{2,0},{4,2},{6,4},{1,7},{3,1},{5,3},{7,5},{8,14},{10,8},{12,... | collective-permute-start | bytes 1769480 | tf_op jit(solution)/shard_map/ppermute | solution.py:878
  62.4 48.6 %collective-permute-start = (bf16[512,512]{1,0:T(8,128)(2,1)S(1)}, bf16[512,512]{1,0:T(8,128)(2,1)S(1)}, u32[]{:S(2)}, u32[]{:S(2)}) collective-permute-start(bf16[512,512]{1,0:T(8,128)(2,1)S(1)} %copy-done.28), channel_id=1, source_target_pairs={{0,2},{2,0},{4,6},{6,4},{1,3},{3,1},{5,7},{7,5},{8,10},{10,8},{12,... | collective-permute-start | bytes 1572872 | tf_op jit(solution)/shard_map/ppermute | solution.py:844
  62.9 59.1 %collective-permute-start.2 = (bf16[512,512]{1,0:T(8,128)(2,1)}, bf16[512,512]{1,0:T(8,128)(2,1)S(1)}, u32[]{:S(2)}, u32[]{:S(2)}) collective-permute-start(bf16[512,512]{1,0:T(8,128)(2,1)} %collective-permute-done.1.refs_10_.refs_3_), channel_id=1, source_target_pairs={{0,2},{2,0},{4,6},{6,4},{1,3},{3,1},{5,7},{7,5},{8,10},{10,8},{12,... | collective-permute-start | bytes 1572872 | tf_op jit(solution)/shard_map/ppermute | solution.py:844
  127.3 309.3 %reduce-scatter.3.cloned.1.call-start = ((), (), s32[]{:S(2)}) async-start(), calls=%async_computation.2 | async-start | bytes 21233664 | tf_op jit(solution)/shard_map/reduce_scatter | solution.py:903
  130.9 25.5 %collective-permute-start.17 = (bf16[512,512]{1,0:T(8,128)(2,1)}, bf16[512,512]{1,0:T(8,128)(2,1)}, u32[]{:S(2)}, u32[]{:S(2)}) collective-permute-start(bf16[512,512]{1,0:T(8,128)(2,1)} %shard_map.414.refs_6_.refs_1_), channel_id=1, source_target_pairs={{0,4},{2,6},{4,0},{6,2},{1,5},{3,7},{5,1},{7,3},{8,12},{10,14},{12... | collective-permute-start | bytes 1572872 | tf_op jit(solution)/shard_map/ppermute | solution.py:844
  146.2 26.1 %collective-permute-start.15 = (bf16[512,512]{1,0:T(8,128)(2,1)S(1)}, bf16[512,512]{1,0:T(8,128)(2,1)S(1)}, u32[]{:S(2)}, u32[]{:S(2)}) collective-permute-start(bf16[512,512]{1,0:T(8,128)(2,1)S(1)} %get-tuple-element.151.refs_5_.refs_6_), channel_id=1, source_target_pairs={{0,1},{2,3},{4,5},{6,7},{8,9},{10,11},{12,13},{14,15},{16,17},{18,... | collective-permute-start | bytes 1572872 | tf_op jit(solution)/shard_map/ppermute | solution.py:1331
  149.8 31.8 %collective-permute-start.16 = (bf16[512,512]{1,0:T(8,128)(2,1)}, bf16[512,512]{1,0:T(8,128)(2,1)}, u32[]{:S(2)}, u32[]{:S(2)}) collective-permute-start(bf16[512,512]{1,0:T(8,128)(2,1)} %shard_map.414.refs_6_.refs_1_), channel_id=1, source_target_pairs={{0,2},{2,0},{4,6},{6,4},{1,3},{3,1},{5,7},{7,5},{8,10},{10,8},{12,... | collective-permute-start | bytes 1572872 | tf_op jit(solution)/shard_map/ppermute | solution.py:844
  156.4 25.1 %collective-permute-start.18 = (bf16[512,512]{1,0:T(8,128)(2,1)}, bf16[512,512]{1,0:T(8,128)(2,1)}, u32[]{:S(2)}, u32[]{:S(2)}) collective-permute-start(bf16[512,512]{1,0:T(8,128)(2,1)} %collective-permute-done.17.refs_4_.refs_3_), channel_id=1, source_target_pairs={{0,2},{2,0},{4,6},{6,4},{1,3},{3,1},{5,7},{7,5},{8,10},{10,8},{12,... | collective-permute-start | bytes 1572872 | tf_op jit(solution)/shard_map/ppermute | solution.py:844
  186.0 11.9 %collective-permute-start.19 = (bf16[128,2048]{1,0:T(8,128)(2,1)S(1)}, bf16[128,2048]{1,0:T(8,128)(2,1)S(1)}, u32[]{:S(2)}, u32[]{:S(2)}) collective-permute-start(bf16[128,2048]{1,0:T(8,128)(2,1)S(1)} %get-tuple-element.156), channel_id=1, source_target_pairs={{0,2},{2,0},{4,6},{6,4},{1,3},{3,1},{5,7},{7,5},{8,10},{10,8},{12,... | collective-permute-start | bytes 1572872 | tf_op jit(solution)/shard_map/ppermute | solution.py:844
  198.0 21.9 %collective-permute-start.20 = (bf16[128,2048]{1,0:T(8,128)(2,1)S(1)}, bf16[128,2048]{1,0:T(8,128)(2,1)S(1)}, u32[]{:S(2)}, u32[]{:S(2)}) collective-permute-start(bf16[128,2048]{1,0:T(8,128)(2,1)S(1)} %get-tuple-element.157.refs_5_), channel_id=1, source_target_pairs={{0,2},{2,0},{4,6},{6,4},{1,3},{3,1},{5,7},{7,5},{8,10},{10,8},{12,... | collective-permute-start | bytes 1572872 | tf_op jit(solution)/shard_map/ppermute | solution.py:844
  198.0 21.8 %collective-permute-start.21 = (bf16[128,2048]{1,0:T(8,128)(2,1)S(1)}, bf16[128,2048]{1,0:T(8,128)(2,1)S(1)}, u32[]{:S(2)}, u32[]{:S(2)}) collective-permute-start(bf16[128,2048]{1,0:T(8,128)(2,1)S(1)} %shard_map.418), channel_id=1, source_target_pairs={{0,4},{2,6},{4,0},{6,2},{1,5},{3,7},{5,1},{7,3},{8,12},{10,14},{12... | collective-permute-start | bytes 1572872 | tf_op jit(solution)/shard_map/ppermute | solution.py:844
  222.1 18.2 %collective-permute-start.23 = (bf16[128,2048]{1,0:T(8,128)(2,1)}, bf16[128,2048]{1,0:T(8,128)(2,1)}, u32[]{:S(2)}, u32[]{:S(2)}) collective-permute-start(bf16[128,2048]{1,0:T(8,128)(2,1)} %get-tuple-element.159.refs_0_), channel_id=1, source_target_pairs={{0,4},{2,6},{4,0},{6,2},{1,5},{3,7},{5,1},{7,3},{8,12},{10,14},{12... | collective-permute-start | bytes 1572872 | tf_op jit(solution)/shard_map/ppermute | solution.py:844
  223.4 39.0 %collective-permute-start.22 = (bf16[128,2048]{1,0:T(8,128)(2,1)}, bf16[128,2048]{1,0:T(8,128)(2,1)}, u32[]{:S(2)}, u32[]{:S(2)}) collective-permute-start(bf16[128,2048]{1,0:T(8,128)(2,1)} %get-tuple-element.159.refs_0_), channel_id=1, source_target_pairs={{0,2},{2,0},{4,6},{6,4},{1,3},{3,1},{5,7},{7,5},{8,10},{10,8},{12,... | collective-permute-start | bytes 1572872 | tf_op jit(solution)/shard_map/ppermute | solution.py:844
  240.3 22.0 %collective-permute-start.24 = (bf16[128,2048]{1,0:T(8,128)(2,1)}, bf16[128,2048]{1,0:T(8,128)(2,1)}, u32[]{:S(2)}, u32[]{:S(2)}) collective-permute-start(bf16[128,2048]{1,0:T(8,128)(2,1)} %collective-permute-done.23.refs_2_), channel_id=1, source_target_pairs={{0,2},{2,0},{4,6},{6,4},{1,3},{3,1},{5,7},{7,5},{8,10},{10,8},{12,... | collective-permute-start | bytes 1572872 | tf_op jit(solution)/shard_map/ppermute | solution.py:844
  284.8 17.2 %collective-permute-start.25 = (bf16[128,2048]{1,0:T(8,128)(2,1)S(1)}, bf16[128,2048]{1,0:T(8,128)(2,1)S(1)}, u32[]{:S(2)}, u32[]{:S(2)}) collective-permute-start(bf16[128,2048]{1,0:T(8,128)(2,1)S(1)} %get-tuple-element.166.refs_7_), channel_id=1, source_target_pairs={{0,2},{2,0},{4,6},{6,4},{1,3},{3,1},{5,7},{7,5},{8,10},{10,8},{12,... | collective-permute-start | bytes 1572872 | tf_op jit(solution)/shard_map/ppermute | solution.py:844
  302.8 203.1 %reduce-scatter.5.cloned.1.call-start = ((), (), s32[]{:S(2)}) async-start(), calls=%async_computation.3 | async-start | bytes 7077888 | tf_op jit(solution)/shard_map/reduce_scatter | solution.py:903
  305.3 16.7 %collective-permute-start.26 = (bf16[128,2048]{1,0:T(8,128)(2,1)}, bf16[128,2048]{1,0:T(8,128)(2,1)S(1)}, u32[]{:S(2)}, u32[]{:S(2)}) collective-permute-start(bf16[128,2048]{1,0:T(8,128)(2,1)} %copy-done.77), channel_id=1, source_target_pairs={{0,2},{2,0},{4,6},{6,4},{1,3},{3,1},{5,7},{7,5},{8,10},{10,8},{12,... | collective-permute-start | bytes 1572872 | tf_op jit(solution)/shard_map/ppermute | solution.py:844
  306.8 21.9 %collective-permute-start.27 = (bf16[128,2048]{1,0:T(8,128)(2,1)S(1)}, bf16[128,2048]{1,0:T(8,128)(2,1)S(1)}, u32[]{:S(2)}, u32[]{:S(2)}) collective-permute-start(bf16[128,2048]{1,0:T(8,128)(2,1)S(1)} %shard_map.425), channel_id=1, source_target_pairs={{0,4},{2,6},{4,0},{6,2},{1,5},{3,7},{5,1},{7,3},{8,12},{10,14},{12... | collective-permute-start | bytes 1572872 | tf_op jit(solution)/shard_map/ppermute | solution.py:844
  333.1 21.5 %collective-permute-start.29 = (bf16[128,2048]{1,0:T(8,128)(2,1)S(1)}, bf16[128,2048]{1,0:T(8,128)(2,1)S(1)}, u32[]{:S(2)}, u32[]{:S(2)}) collective-permute-start(bf16[128,2048]{1,0:T(8,128)(2,1)S(1)} %get-tuple-element.171.refs_3_.refs_1_), channel_id=1, source_target_pairs={{0,4},{2,6},{4,0},{6,2},{1,5},{3,7},{5,1},{7,3},{8,12},{10,14},{12... | collective-permute-start | bytes 1572872 | tf_op jit(solution)/shard_map/ppermute | solution.py:844
  333.2 28.8 %collective-permute-start.28 = (bf16[128,2048]{1,0:T(8,128)(2,1)S(1)}, bf16[128,2048]{1,0:T(8,128)(2,1)S(1)}, u32[]{:S(2)}, u32[]{:S(2)}) collective-permute-start(bf16[128,2048]{1,0:T(8,128)(2,1)S(1)} %get-tuple-element.171.refs_3_.refs_1_), channel_id=1, source_target_pairs={{0,2},{2,0},{4,6},{6,4},{1,3},{3,1},{5,7},{7,5},{8,10},{10,8},{12,... | collective-permute-start | bytes 1572872 | tf_op jit(solution)/shard_map/ppermute | solution.py:844
  354.6 11.3 %collective-permute-start.30 = (bf16[128,2048]{1,0:T(8,128)(2,1)S(1)}, bf16[128,2048]{1,0:T(8,128)(2,1)S(1)}, u32[]{:S(2)}, u32[]{:S(2)}) collective-permute-start(bf16[128,2048]{1,0:T(8,128)(2,1)S(1)} %collective-permute-done.29.refs_3_), channel_id=1, source_target_pairs={{0,2},{2,0},{4,6},{6,4},{1,3},{3,1},{5,7},{7,5},{8,10},{10,8},{12,... | collective-permute-start | bytes 1572872 | tf_op jit(solution)/shard_map/ppermute | solution.py:844
  372.1 11.3 %collective-permute-start.31 = (bf16[512,512]{1,0:T(8,128)(2,1)S(1)}, bf16[512,512]{1,0:T(8,128)(2,1)S(1)}, u32[]{:S(2)}, u32[]{:S(2)}) collective-permute-start(bf16[512,512]{1,0:T(8,128)(2,1)S(1)} %get-tuple-element.176), channel_id=1, source_target_pairs={{0,2},{2,0},{4,6},{6,4},{1,3},{3,1},{5,7},{7,5},{8,10},{10,8},{12,... | collective-permute-start | bytes 1572872 | tf_op jit(solution)/shard_map/ppermute | solution.py:844
  383.5 19.2 %collective-permute-start.32 = (bf16[512,512]{1,0:T(8,128)(2,1)S(1)}, bf16[512,512]{1,0:T(8,128)(2,1)S(1)}, u32[]{:S(2)}, u32[]{:S(2)}) collective-permute-start(bf16[512,512]{1,0:T(8,128)(2,1)S(1)} %get-tuple-element.177), channel_id=1, source_target_pairs={{0,2},{2,0},{4,6},{6,4},{1,3},{3,1},{5,7},{7,5},{8,10},{10,8},{12,... | collective-permute-start | bytes 1572872 | tf_op jit(solution)/shard_map/ppermute | solution.py:844
  383.7 23.8 %collective-permute-start.33 = (bf16[512,512]{1,0:T(8,128)(2,1)S(1)}, bf16[512,512]{1,0:T(8,128)(2,1)S(1)}, u32[]{:S(2)}, u32[]{:S(2)}) collective-permute-start(bf16[512,512]{1,0:T(8,128)(2,1)S(1)} %shard_map.430), channel_id=1, source_target_pairs={{0,4},{2,6},{4,0},{6,2},{1,5},{3,7},{5,1},{7,3},{8,12},{10,14},{12... | collective-permute-start | bytes 1572872 | tf_op jit(solution)/shard_map/ppermute | solution.py:844
  394.9 22.5 %collective-permute-start.34 = (bf16[512,512]{1,0:T(8,128)(2,1)S(1)}, bf16[512,512]{1,0:T(8,128)(2,1)S(1)}, u32[]{:S(2)}, u32[]{:S(2)}) collective-permute-start(bf16[512,512]{1,0:T(8,128)(2,1)S(1)} %get-tuple-element.186), channel_id=1, source_target_pairs={{1,0},{3,2},{5,4},{7,6},{9,8},{11,10},{13,12},{15,14},{17,16},{19,... | collective-permute-start | bytes 1572872 | tf_op jit(solution)/shard_map/ppermute | solution.py:1369
  439.7 16.7 %collective-permute-start.41 = (bf16[576,512]{1,0:T(8,128)(2,1)}, bf16[576,512]{1,0:T(8,128)(2,1)S(1)}, u32[]{:S(2)}, u32[]{:S(2)}) collective-permute-start(bf16[576,512]{1,0:T(8,128)(2,1)} %get-tuple-element.210), channel_id=1, source_target_pairs={{0,6},{2,0},{4,2},{6,4},{1,7},{3,1},{5,3},{7,5},{8,14},{10,8},{12,... | collective-permute-start | bytes 1769480 | tf_op jit(solution)/shard_map/ppermute | solution.py:878
  440.8 52.6 %collective-permute-start.51 = (bf16[576,512]{1,0:T(8,128)(2,1)}, bf16[576,512]{1,0:T(8,128)(2,1)}, u32[]{:S(2)}, u32[]{:S(2)}) collective-permute-start(bf16[576,512]{1,0:T(8,128)(2,1)} %get-tuple-element.225), channel_id=1, source_target_pairs={{0,4},{2,6},{4,0},{6,2},{1,5},{3,7},{5,1},{7,3},{8,12},{10,14},{12... | collective-permute-start | bytes 1769480 | tf_op jit(solution)/shard_map/ppermute | solution.py:878
  442.0 51.5 %collective-permute-start.52 = (bf16[576,512]{1,0:T(8,128)(2,1)}, bf16[576,512]{1,0:T(8,128)(2,1)}, u32[]{:S(2)}, u32[]{:S(2)}) collective-permute-start(bf16[576,512]{1,0:T(8,128)(2,1)} %get-tuple-element.226), channel_id=1, source_target_pairs={{0,2},{2,4},{4,6},{6,0},{1,3},{3,5},{5,7},{7,1},{8,10},{10,12},{12... | collective-permute-start | bytes 1769480 | tf_op jit(solution)/shard_map/ppermute | solution.py:878
  448.9 47.9 %copy-start.54 = (f32[512,1]{1,0:T(8,128)S(1)}, f32[512,1]{1,0:T(8,128)}, u32[]{:S(2)}) copy-start(f32[512,1]{1,0:T(8,128)} %copy-done.53) | copy-start | bytes 6148
  451.1 51.1 %collective-permute-start.35 = (bf16[512,512]{1,0:T(8,128)(2,1)S(1)}, bf16[512,512]{1,0:T(8,128)(2,1)S(1)}, u32[]{:S(2)}, u32[]{:S(2)}) collective-permute-start(bf16[512,512]{1,0:T(8,128)(2,1)S(1)} %get-tuple-element.198), channel_id=1, source_target_pairs={{0,2},{2,0},{4,6},{6,4},{1,3},{3,1},{5,7},{7,5},{8,10},{10,8},{12,... | collective-permute-start | bytes 1572872 | tf_op jit(solution)/shard_map/ppermute | solution.py:844
  456.3 1.2 collective-permute-start.42
  457.5 3.8 collective-permute-start.43
  461.3 4.0 collective-permute-start.44
  493.4 37.9 %copy-start.87 = (f32[2,128]{1,0:T(2,128)S(1)}, f32[2,128]{1,0:T(2,128)}, u32[]{:S(2)}) copy-start(f32[2,128]{1,0:T(2,128)} %param.46) | copy-start | bytes 3076
  496.8 11.6 %collective-permute-start.53 = (bf16[192,512]{1,0:T(8,128)(2,1)}, bf16[192,512]{1,0:T(8,128)(2,1)}, u32[]{:S(2)}, u32[]{:S(2)}) collective-permute-start(bf16[192,512]{1,0:T(8,128)(2,1)} %get-tuple-element.231), channel_id=1, source_target_pairs={{0,8},{8,16},{16,24},{24,0},{1,9},{9,17},{17,25},{25,1},{2,10},{10... | collective-permute-start | bytes 589832 | tf_op jit(solution)/shard_map/ppermute | solution.py:893
  497.0 3.8 collective-permute-start.45
  500.9 4.7 collective-permute-start.46
  502.3 58.7 %collective-permute-start.36 = (bf16[512,512]{1,0:T(8,128)(2,1)}, bf16[512,512]{1,0:T(8,128)(2,1)}, u32[]{:S(2)}, u32[]{:S(2)}) collective-permute-start(bf16[512,512]{1,0:T(8,128)(2,1)} %copy-done.76), channel_id=1, source_target_pairs={{0,2},{2,0},{4,6},{6,4},{1,3},{3,1},{5,7},{7,5},{8,10},{10,8},{12,... | collective-permute-start | bytes 1572872 | tf_op jit(solution)/shard_map/ppermute | solution.py:844
  502.4 58.6 %collective-permute-start.37 = (bf16[512,512]{1,0:T(8,128)(2,1)S(1)}, bf16[512,512]{1,0:T(8,128)(2,1)}, u32[]{:S(2)}, u32[]{:S(2)}) collective-permute-start(bf16[512,512]{1,0:T(8,128)(2,1)S(1)} %shard_map.438), channel_id=1, source_target_pairs={{0,4},{2,6},{4,0},{6,2},{1,5},{3,7},{5,1},{7,3},{8,12},{10,14},{12... | collective-permute-start | bytes 1572872 | tf_op jit(solution)/shard_map/ppermute | solution.py:844
  504.1 7.1 %collective-permute-start.54 = (bf16[192,512]{1,0:T(8,128)(2,1)}, bf16[192,512]{1,0:T(8,128)(2,1)S(1)}, u32[]{:S(2)}, u32[]{:S(2)}) collective-permute-start(bf16[192,512]{1,0:T(8,128)(2,1)} %copy-done.79), channel_id=1, source_target_pairs={{0,16},{8,24},{16,0},{24,8},{1,17},{9,25},{17,1},{25,9},{2,18},{10... | collective-permute-start | bytes 589832 | tf_op jit(solution)/shard_map/ppermute | solution.py:893
  505.6 8.3 %collective-permute-start.55 = (bf16[192,512]{1,0:T(8,128)(2,1)}, bf16[192,512]{1,0:T(8,128)(2,1)S(1)}, u32[]{:S(2)}, u32[]{:S(2)}) collective-permute-start(bf16[192,512]{1,0:T(8,128)(2,1)} %copy-done.78), channel_id=1, source_target_pairs={{0,24},{8,0},{16,8},{24,16},{1,25},{9,1},{17,9},{25,17},{2,26},{10... | collective-permute-start | bytes 589832 | tf_op jit(solution)/shard_map/ppermute | solution.py:893
  508.5 7.8 %collective-permute-start.47 = (bf16[64,512]{1,0:T(8,128)(2,1)S(1)}, bf16[64,512]{1,0:T(8,128)(2,1)S(1)}, u32[]{:S(2)}, u32[]{:S(2)}) collective-permute-start(bf16[64,512]{1,0:T(8,128)(2,1)S(1)} %get-tuple-element.217), channel_id=1, source_target_pairs={{0,0},{2,8},{4,16},{6,24},{8,2},{10,10},{12,18},{14,26},{16,4},{18... | collective-permute-start | bytes 196616 | tf_op jit(solution)/shard_map/ppermute | solution.py:1134
  511.1 21.0 %collective-permute-start.48 = (bf16[64,512]{1,0:T(8,128)(2,1)S(1)}, bf16[64,512]{1,0:T(8,128)(2,1)S(1)}, u32[]{:S(2)}, u32[]{:S(2)}) collective-permute-start(bf16[64,512]{1,0:T(8,128)(2,1)S(1)} %get-tuple-element.218), channel_id=1, source_target_pairs={{0,2},{2,10},{4,18},{6,26},{8,4},{10,12},{12,20},{14,28},{16,6},{1... | collective-permute-start | bytes 196616 | tf_op jit(solution)/shard_map/ppermute | solution.py:1134
  513.9 19.5 %collective-permute-start.49 = (bf16[64,512]{1,0:T(8,128)(2,1)S(1)}, bf16[64,512]{1,0:T(8,128)(2,1)S(1)}, u32[]{:S(2)}, u32[]{:S(2)}) collective-permute-start(bf16[64,512]{1,0:T(8,128)(2,1)S(1)} %get-tuple-element.219), channel_id=1, source_target_pairs={{0,4},{2,12},{4,20},{6,28},{8,6},{10,14},{12,22},{14,30},{16,0},{1... | collective-permute-start | bytes 196616 | tf_op jit(solution)/shard_map/ppermute | solution.py:1134
  516.2 20.2 %collective-permute-start.50 = (bf16[64,512]{1,0:T(8,128)(2,1)S(1)}, bf16[64,512]{1,0:T(8,128)(2,1)S(1)}, u32[]{:S(2)}, u32[]{:S(2)}) collective-permute-start(bf16[64,512]{1,0:T(8,128)(2,1)S(1)} %get-tuple-element.220), channel_id=1, source_target_pairs={{0,6},{2,14},{4,22},{6,30},{8,0},{10,8},{12,16},{14,24},{16,2},{18... | collective-permute-start | bytes 196616 | tf_op jit(solution)/shard_map/ppermute | solution.py:1134
  532.1 27.6 %collective-permute-start.38 = (bf16[128,512]{1,0:T(8,128)(2,1)}, bf16[128,512]{1,0:T(8,128)(2,1)}, u32[]{:S(2)}, u32[]{:S(2)}) collective-permute-start(bf16[128,512]{1,0:T(8,128)(2,1)} %get-tuple-element.203), channel_id=1, source_target_pairs={{0,6},{2,0},{4,2},{6,4},{1,7},{3,1},{5,3},{7,5},{8,14},{10,8},{12,... | collective-permute-start | bytes 393224 | tf_op jit(solution)/shard_map/ppermute | solution.py:878
  533.4 26.3 %collective-permute-start.39 = (bf16[128,512]{1,0:T(8,128)(2,1)}, bf16[128,512]{1,0:T(8,128)(2,1)}, u32[]{:S(2)}, u32[]{:S(2)}) collective-permute-start(bf16[128,512]{1,0:T(8,128)(2,1)} %get-tuple-element.204), channel_id=1, source_target_pairs={{0,4},{2,6},{4,0},{6,2},{1,5},{3,7},{5,1},{7,3},{8,12},{10,14},{12... | collective-permute-start | bytes 393224 | tf_op jit(solution)/shard_map/ppermute | solution.py:878
  536.4 23.3 %collective-permute-start.40 = (bf16[128,512]{1,0:T(8,128)(2,1)}, bf16[128,512]{1,0:T(8,128)(2,1)}, u32[]{:S(2)}, u32[]{:S(2)}) collective-permute-start(bf16[128,512]{1,0:T(8,128)(2,1)} %get-tuple-element.205), channel_id=1, source_target_pairs={{0,2},{2,4},{4,6},{6,0},{1,3},{3,5},{5,7},{7,1},{8,10},{10,12},{12... | collective-permute-start | bytes 393224 | tf_op jit(solution)/shard_map/ppermute | solution.py:878
  (85 other events, 538.5 us)
Sparse Core Ops, SparseCore 0:
  58.5 43.7 all-gather.4
  127.5 109.0 all-gather.6
  302.9 133.6 reduce-scatter.2
  439.8 59.5 reduce-scatter.4

commit v5 on v4

--- a/solution.py
+++ b/solution.py
@@ -856,8 +856,8 @@
     return along_row([own] * lax.axis_size("row"), True)
 
 
-def scatter_pieces(pieces):
-    sent = add_parts([pieces[2], swap(pieces[3], "row", 1)], BF)
+def scatter_pieces(pieces, after=()):
+    sent = add_parts([pieces[2], swap(pieces[3], "row", 1)], BF, after)
     direct, sent = lax.optimization_barrier((pieces[1], sent))
     return [pieces[0], swap(direct, "row", 1), swap(sent, "row", 2)], sent
 
@@ -1397,14 +1397,19 @@
         feed_pieces[:1],
     )
     input_pieces = take_apart(input_part, z, False)
-    input_parts, _ = scatter_pieces(input_pieces)
+    attention_pieces = split_shard(attention_total, 1, in_rows, output_inner, z)
+    attention_messages = along_row(attention_pieces, False)
+    input_parts, _ = scatter_pieces(input_pieces, attention_messages[1:2])
     feed_messages = along_row(feed_pieces, False)
     norm_part = jnp.concatenate([first_gain_grad, second_gain_grad])
     norm_part = norm_part.reshape(2, dp, size, rest).transpose(0, 2, 1, 3).reshape(2, MODEL_WIDTH)
     gain_part = jnp.concatenate([norm_part.reshape(-1), head_part.reshape(-1)]).reshape(-1, 128)
-    gain_part, feed_messages[1] = lax.optimization_barrier((gain_part, feed_messages[1]))
+    gain_part, feed_messages[1], input_parts[0] = lax.optimization_barrier(
+        (gain_part, feed_messages[1], input_parts[0])
+    )
     gain_part = add_along(gain_part, ("dp", "col"))
     small = jnp.concatenate([gain_part, inner_part.reshape(-1, 128)])
+    small, feed_messages[2] = lax.optimization_barrier((small, feed_messages[2]))
     small = add_along(small, ("row",)).reshape(-1)
     inner = small[gain_part.size :][:, None]
     norm_total = small[: norm_part.size].reshape(norm_part.shape)
@@ -1416,9 +1421,6 @@
         RATES[4],
         quarter_place,
     )
-    attention_pieces, output_pieces = split_attention(
-        attention_total, 1, in_rows, output_inner, z
-    )
     cut = [(t, 0, COLUMNS) for t in range(gateup_terms)]
     (gateup_total,) = place_columns(
         feed_messages, in_rows, [cut], z, attention_pieces[:1]
@@ -1426,10 +1428,11 @@
     gateup_new, _ = update_pair(
         (gateup_weight, gateup_moment, gateup_second), gateup_total, RATES[3]
     )
-    output_pieces = turned_back(output_pieces)
-    attention_messages = along_row(attention_pieces, False)
     output_new = update_out(
-        (output_weight, output_moment, output_second), output_pieces, RATES[2], z
+        (output_weight, output_moment, output_second),
+        out_pieces(attention_messages, output_inner, z),
+        RATES[2],
+        quarter_place,
     )
     query_total, keyval_total = place_columns(
         attention_messages,

time: 585 us -> 571 us (0.976)
  starting transfers between devices: 134 us -> 116 us
    ppermute x4 -> x0, starting transfers between devices: 20.9 us -> none  [turned_back(): result.append(lax.ppermute(piece, ('dp', 'row'), pairs))]
    pallas_call x39 -> x40, Pallas kernels: 143 us -> 146 us  [call(): pl.pallas_call(run, grid_spec=pltpu.PrefetchScalarGridSpec(num_scalar_pre...]
    unnamed x178 -> x166, local copies, waits for them, and re-layouts: 35 us -> 36.8 us
  transfers between devices with their start and end apart: 60 -> 59, of which waited for: 26 -> 25; matrix products, arithmetic and copies ran while one was open for 1% -> 2% of each run, Pallas kernels for 23% -> 24%
where the time goes in v5:
time: 571 us; the launch traced here: 562 us
  waiting for transfers between devices  220 us (39%)
  Pallas kernels  162 us (28%)
  starting transfers between devices  116 us (20%)
  local copies, waits for them, and re-layouts  41.1 us (7%)
  between operations  15.2 us (3%)
  other arithmetic  7.6 us (1%)
    ppermute x29, waiting for transfers between devices, swap(): lax.ppermute(value, axis, [(i, i ^ step) for i in range(lax.axis_size(axi...  156 us
    pallas_call x40, Pallas kernels, call(): pl.pallas_call(run, grid_spec=pltpu.PrefetchScalarGridSpec(num_scalar_pre...  146 us
    ppermute x29, starting transfers between devices, swap(): lax.ppermute(value, axis, [(i, i ^ step) for i in range(lax.axis_size(axi...  67.7 us
    unnamed x166, local copies, waits for them, and re-layouts  36.8 us
    ppermute x15, starting transfers between devices, along_row(): lax.ppermute(p, 'row', [(i, (i + sign * k) % size) for i in range(size)])  34.7 us
    ppermute x15, waiting for transfers between devices, along_row(): lax.ppermute(p, 'row', [(i, (i + sign * k) % size) for i in range(size)])  30.6 us
    ppermute x1, waiting for transfers between devices, body(): lax.ppermute(keys_values, 'col', [(i, i + 1) for i in range(cols - 1)])  14.9 us
  transfers between devices with their start and end apart: 59, of which 25 were waited for; matrix products, arithmetic and copies ran while one was open for 2% of the time, Pallas kernels for 24%

profile of v5, /device:TPU:0, one launch (start us, length us, event | category | flops | bytes accessed | tf_op | source)
XLA Modules:
  0.0 562.4 jit_solution(15421693678663124124)
XLA Ops:
  7.2 4.1 collective-permute-start.1
  11.3 2.4 shard_map.407
  13.8 2.3 shard_map.408
  20.6 3.5 collective-permute-done.6.refs_9_
  25.9 3.5 collective-permute-start.5
  34.0 12.0 %collective-permute-start.10 = (bf16[64,512]{1,0:T(8,128)(2,1)S(1)}, bf16[64,512]{1,0:T(8,128)(2,1)S(1)}, u32[]{:S(2)}, u32[]{:S(2)}) collective-permute-start(bf16[64,512]{1,0:T(8,128)(2,1)S(1)} %get-tuple-element.143), channel_id=1, source_target_pairs={{0,4},{2,6},{4,0},{6,2},{1,5},{3,7},{5,1},{7,3},{8,12},{10,14},{12... | collective-permute-start | bytes 196616 | tf_op jit(solution)/shard_map/ppermute | solution.py:878
  46.0 3.7 collective-permute-start.11
  49.7 3.1 shard_map.410
  55.4 2.1 shard_map.411.refs_5_
  59.4 2.9 collective-permute-start.14
  64.4 46.5 %collective-permute-done.refs_2_ = bf16[512,512]{1,0:T(8,128)(2,1)S(1)} collective-permute-done((bf16[512,512]{1,0:T(8,128)(2,1)S(1)}, bf16[512,512]{1,0:T(8,128)(2,1)S(1)}, u32[]{:S(2)}, u32[]{:S(2)}) %collective-permute-start) | collective-permute-done | bytes 524320 | tf_op jit(solution)/shard_map/ppermute | solution.py:844
  111.0 11.1 %collective-permute-done.2.refs_4_ = bf16[512,512]{1,0:T(8,128)(2,1)S(1)} collective-permute-done((bf16[512,512]{1,0:T(8,128)(2,1)}, bf16[512,512]{1,0:T(8,128)(2,1)S(1)}, u32[]{:S(2)}, u32[]{:S(2)}) %collective-permute-start.2) | collective-permute-done | bytes 524320 | tf_op jit(solution)/shard_map/ppermute | solution.py:844
  122.1 2.2 shard_map.412.refs_5_.refs_0_.refs_4_.refs_3_
  125.7 1.6 shard_map.413.refs_2_
  133.7 7.8 %shard_map.415 = (bf16[512,2048]{1,0:T(8,128)(2,1)S(1)}, f32[512,1]{1,0:T(8,128)S(1)}, f32[512,512]{1,0:T(8,128)S(1)}, f32[512,256]{1,0:T(8,128)S(1)}, bf16[512,...) custom-call(bf16[512,2048]{1,0:T(8,128)(2,1)S(1)} %copy-done.1, f32[1,2048]{1,0:T(1,128)S(1)} %bitcast.102, ...), custom_call_target="tpu_custom_call" | custom-call | tf_op jit(solution)/shard_map/pallas_call | solution.py:215
  146.2 3.6 collective-permute-start.15
  149.9 6.5 %collective-permute-done.17.refs_4_.refs_3_ = bf16[512,512]{1,0:T(8,128)(2,1)} collective-permute-done((bf16[512,512]{1,0:T(8,128)(2,1)}, bf16[512,512]{1,0:T(8,128)(2,1)}, u32[]{:S(2)}, u32[]{:S(2)}) %collective-permute-start.17) | collective-permute-done | bytes 524320 | tf_op jit(solution)/shard_map/ppermute | solution.py:844
  157.3 14.9 %collective-permute-done.15.refs_7_.refs_8_ = bf16[512,512]{1,0:T(8,128)(2,1)S(1)} collective-permute-done((bf16[512,512]{1,0:T(8,128)(2,1)S(1)}, bf16[512,512]{1,0:T(8,128)(2,1)S(1)}, u32[]{:S(2)}, u32[]{:S(2)}) %collective-permute-start.15) | collective-permute-done | bytes 524320 | tf_op jit(solution)/shard_map/ppermute | solution.py:1331
  174.2 7.3 %shard_map.416 = (bf16[512,512]{1,0:T(8,128)(2,1)S(1)}, f32[4,512,1]{2,1,0:T(8,128)S(1)}) custom-call(s32[1]{0:T(128)} %bitcast.1.refs_0_, s32[512,1]{1,0:T(8,128)S(1)} %copy-done.18, s32[1,512]{1,0:T(1,128)S(1)} %bitcast.105, s32[1,512]{1,0:T(1,128)S(1)} %bitcast.107, bf16[512,512]{1,0:T(8,128)(2,1)S(1)} %copy-done.26, ...), custom_call_target="tpu_custom_call" | custom-call | tf_op jit(solution)/shard_map/pallas_call | solution.py:93
  181.6 4.4 shard_map.417
  186.0 11.8 %collective-permute-done.19.refs_1_ = bf16[128,2048]{1,0:T(8,128)(2,1)S(1)} collective-permute-done((bf16[128,2048]{1,0:T(8,128)(2,1)S(1)}, bf16[128,2048]{1,0:T(8,128)(2,1)S(1)}, u32[]{:S(2)}, u32[]{:S(2)}) %collective-permute-start.19) | collective-permute-done | bytes 524320 | tf_op jit(solution)/shard_map/ppermute | solution.py:844
  198.0 3.0 collective-permute-start.21
  201.1 18.8 %collective-permute-done.20.refs_2_ = bf16[128,2048]{1,0:T(8,128)(2,1)S(1)} collective-permute-done((bf16[128,2048]{1,0:T(8,128)(2,1)S(1)}, bf16[128,2048]{1,0:T(8,128)(2,1)S(1)}, u32[]{:S(2)}, u32[]{:S(2)}) %collective-permute-start.20) | collective-permute-done | bytes 524320 | tf_op jit(solution)/shard_map/ppermute | solution.py:844
  223.4 16.5 %collective-permute-start.22 = (bf16[128,2048]{1,0:T(8,128)(2,1)}, bf16[128,2048]{1,0:T(8,128)(2,1)}, u32[]{:S(2)}, u32[]{:S(2)}) collective-permute-start(bf16[128,2048]{1,0:T(8,128)(2,1)} %get-tuple-element.162.refs_0_), channel_id=1, source_target_pairs={{0,2},{2,0},{4,6},{6,4},{1,3},{3,1},{5,7},{7,5},{8,10},{10,8},{12,... | collective-permute-start | bytes 1572872 | tf_op jit(solution)/shard_map/ppermute | solution.py:844
  240.3 9.7 %collective-permute-start.24 = (bf16[128,2048]{1,0:T(8,128)(2,1)}, bf16[128,2048]{1,0:T(8,128)(2,1)}, u32[]{:S(2)}, u32[]{:S(2)}) collective-permute-start(bf16[128,2048]{1,0:T(8,128)(2,1)} %collective-permute-done.23.refs_2_), channel_id=1, source_target_pairs={{0,2},{2,0},{4,6},{6,4},{1,3},{3,1},{5,7},{7,5},{8,10},{10,8},{12,... | collective-permute-start | bytes 1572872 | tf_op jit(solution)/shard_map/ppermute | solution.py:844
  250.0 2.6 shard_map.420.refs_0_.refs_6_
  255.5 6.8 %shard_map.421.refs_5_ = f32[512,1536]{1,0:T(8,128)S(1)} custom-call(bf16[512,2048]{1,0:T(8,128)(2,1)S(1)} %copy-done.3, bf16[2,4,2304,512]{3,2,1,0:T(8,128)(2,1)} %bitcast.110, bf16[128,2048]{1,0:T(8,128)(2,1)} %collective-permute-done.23.refs_2_), custom_call_target="tpu_custom_call" | custom-call | tf_op jit(solution)/shard_map/pallas_call | solution.py:215
  262.3 11.6 %shard_map.422 = (bf16[512,1536]{1,0:T(8,128)(2,1)S(1)}, bf16[512,3072]{1,0:T(8,128)(2,1)S(1)}) custom-call(bf16[128,2048]{1,0:T(8,128)(2,1)} %get-tuple-element.162.refs_0_, bf16[128,2048]{1,0:T(8,128)(2,1)} %collective-permute-done.22.refs_1_, bf16[128,2048]{1,0:T(8,128)(2,1)} %collective-permute-done.23.refs_2_, ...), custom_call_target="tpu_custom_call" | custom-call | tf_op jit(solution)/shard_map/pallas_call | solution.py:215
  274.0 10.0 %shard_map.423 = (f32[128,2048]{1,0:T(8,128)S(1)}, bf16[128,2048]{1,0:T(8,128)(2,1)S(1)}, bf16[128,2048]{1,0:T(8,128)(2,1)S(1)}, bf16[128,2048]{1,0:T(8,128)(2,1)S(1)}) custom-call(bf16[512,3072]{1,0:T(8,128)(2,1)S(1)} %get-tuple-element.165.refs_0_.refs_4_, bf16[2,4,2304,512]{3,2,1,0:T(8,128)(2,1)} %bitcast.112), custom_call_target="tpu_custom_call" | custom-call | tf_op jit(solution)/shard_map/pallas_call | solution.py:215
  284.8 17.2 %shard_map.424 = bf16[2,4,2304,512]{3,2,1,0:T(8,128)(2,1)} custom-call(bf16[128,2048]{1,0:T(8,128)(2,1)} %get-tuple-element.162.refs_0_, bf16[128,2048]{1,0:T(8,128)(2,1)} %collective-permute-done.22.refs_1_, bf16[128,2048]{1,0:T(8,128)(2,1)} %collective-permute-done.23.refs_2_, bf16[128,2048]{1,0:T(8,128)(2,1)} %collective-permute-done.24.refs_3_, ...), custom_call_target="tpu_custom_call" | custom-call | tf_op jit(solution)/shard_map/pallas_call | solution.py:215
  306.8 2.3 collective-permute-start.27
  309.1 12.8 %collective-permute-done.26.refs_1_ = bf16[128,2048]{1,0:T(8,128)(2,1)S(1)} collective-permute-done((bf16[128,2048]{1,0:T(8,128)(2,1)}, bf16[128,2048]{1,0:T(8,128)(2,1)S(1)}, u32[]{:S(2)}, u32[]{:S(2)}) %collective-permute-start.26) | collective-permute-done | bytes 524320 | tf_op jit(solution)/shard_map/ppermute | solution.py:844
  321.9 6.8 %collective-permute-done.27.refs_2_ = bf16[128,2048]{1,0:T(8,128)(2,1)S(1)} collective-permute-done((bf16[128,2048]{1,0:T(8,128)(2,1)S(1)}, bf16[128,2048]{1,0:T(8,128)(2,1)S(1)}, u32[]{:S(2)}, u32[]{:S(2)}) %collective-permute-start.27) | collective-permute-done | bytes 524320 | tf_op jit(solution)/shard_map/ppermute | solution.py:844
  329.5 3.5 shard_map.426
  333.2 7.9 %collective-permute-start.28 = (bf16[128,2048]{1,0:T(8,128)(2,1)S(1)}, bf16[128,2048]{1,0:T(8,128)(2,1)S(1)}, u32[]{:S(2)}, u32[]{:S(2)}) collective-permute-start(bf16[128,2048]{1,0:T(8,128)(2,1)S(1)} %get-tuple-element.174.refs_3_.refs_1_), channel_id=1, source_target_pairs={{0,2},{2,0},{4,6},{6,4},{1,3},{3,1},{5,7},{7,5},{8,10},{10,8},{12,... | collective-permute-start | bytes 1572872 | tf_op jit(solution)/shard_map/ppermute | solution.py:844
  341.1 13.5 %collective-permute-done.29.refs_3_ = bf16[128,2048]{1,0:T(8,128)(2,1)S(1)} collective-permute-done((bf16[128,2048]{1,0:T(8,128)(2,1)S(1)}, bf16[128,2048]{1,0:T(8,128)(2,1)S(1)}, u32[]{:S(2)}, u32[]{:S(2)}) %collective-permute-start.29) | collective-permute-done | bytes 524320 | tf_op jit(solution)/shard_map/ppermute | solution.py:844
  354.6 6.0 %shard_map.427.refs_6_.refs_1_ = bf16[512,2048]{1,0:T(8,128)(2,1)S(1)} custom-call(bf16[512,1536]{1,0:T(8,128)(2,1)S(1)} %copy-done.11, f32[128,2048]{1,0:T(8,128)S(1)} %copy-done.15, bf16[2,4,2304,512]{3,2,1,0:T(8,128)(2,1)} %bitcast.113, bf16[128,2048]{1,0:T(8,128)(2,1)S(1)} %get-tuple-element.174.refs_3_.refs_1_), custom_call_target="tpu_custom_call" | custom-call | tf_op jit(solution)/shard_map/pallas_call | solution.py:215
  362.0 3.9 collective-permute-done.30.refs_4_
  365.9 4.2 shard_map.428
  373.0 9.2 %shard_map.432 = (f32[512,512]{1,0:T(8,128)S(1)}, f32[512,256]{1,0:T(8,128)S(1)}, f32[512,256]{1,0:T(8,128)S(1)}, bf16[512,512]{1,0:T(8,128)(2,1)S(1)}) custom-call(s32[1]{0:T(128)} %bitcast.1.refs_0_, s32[512,1]{1,0:T(8,128)S(1)} %copy-done.19, s32[1,512]{1,0:T(1,128)S(1)} %bitcast.106, s32[1,512]{1,0:T(1,128)S(1)} %bitcast.108, ...), custom_call_target="tpu_custom_call" | custom-call | tf_op jit(solution)/shard_map/pallas_call | solution.py:163
  383.7 11.2 %collective-permute-start.33 = (bf16[512,512]{1,0:T(8,128)(2,1)S(1)}, bf16[512,512]{1,0:T(8,128)(2,1)S(1)}, u32[]{:S(2)}, u32[]{:S(2)}) collective-permute-start(bf16[512,512]{1,0:T(8,128)(2,1)S(1)} %shard_map.430), channel_id=1, source_target_pairs={{0,4},{2,6},{4,0},{6,2},{1,5},{3,7},{5,1},{7,3},{8,12},{10,14},{12... | collective-permute-start | bytes 1572872 | tf_op jit(solution)/shard_map/ppermute | solution.py:844
  396.2 6.6 %collective-permute-done.32.refs_1_ = bf16[512,512]{1,0:T(8,128)(2,1)S(1)} collective-permute-done((bf16[512,512]{1,0:T(8,128)(2,1)S(1)}, bf16[512,512]{1,0:T(8,128)(2,1)S(1)}, u32[]{:S(2)}, u32[]{:S(2)}) %collective-permute-start.32) | collective-permute-done | bytes 524320 | tf_op jit(solution)/shard_map/ppermute | solution.py:844
  402.8 4.7 collective-permute-done.33.refs_2_
  408.6 8.7 %collective-permute-done.34.refs_5_ = bf16[512,512]{1,0:T(8,128)(2,1)S(1)} collective-permute-done((bf16[512,512]{1,0:T(8,128)(2,1)S(1)}, bf16[512,512]{1,0:T(8,128)(2,1)S(1)}, u32[]{:S(2)}, u32[]{:S(2)}) %collective-permute-start.34) | collective-permute-done | bytes 524320 | tf_op jit(solution)/shard_map/ppermute | solution.py:1369
  417.4 2.6 shard_map.433
  420.0 9.7 %shard_map.434 = bf16[2,4,768,512]{3,2,1,0:T(8,128)(2,1)} custom-call(bf16[512,2048]{1,0:T(8,128)(2,1)S(1)} %copy-done.33, bf16[512,1024]{1,0:T(8,128)(2,1)S(1)} %get-tuple-element.190.refs_1_, bf16[512,512]{1,0:T(8,128)(2,1)S(1)} %copy-done.24, bf16[512,2048]{1,0:T(8,128)(2,1)S(1)} %copy-done.9), custom_call_target="tpu_custom_call" | custom-call | tf_op jit(solution)/shard_map/pallas_call | solution.py:215
  430.7 5.9 %reduce-scatter.3.cloned.1.call-done.refs_1_ = bf16[2304,512]{1,0:T(8,128)(2,1)} async-done(((bf16[18432,512]{1,0:T(8,128)(2,1)}), bf16[2304,512]{1,0:T(8,128)(2,1)}) %reduce-scatter.3.cloned.1.call-update) | async-done | bytes 2359312 | tf_op jit(solution)/shard_map/reduce_scatter | solution.py:903
  436.7 1.7 copy-done.20
  442.0 6.3 %shard_map.436 = (bf16[512,2048]{1,0:T(8,128)(2,1)S(1)}, f32[512,1]{1,0:T(8,128)S(1)}, f32[1,2048]{1,0:T(1,128)S(1)}) custom-call(s32[1]{0:T(128)} %bitcast.refs_0_, bf16[512,1024]{1,0:T(8,128)(2,1)S(1)} %copy-done.13, bf16[2,4,768,512]{3,2,1,0:T(8,128)(2,1)} %bitcast.117, bf16[512,2048]{1,0:T(8,128)(2,1)S(1)} %copy-done.1, f32[512,1]{1,0:T(8,128)S(1)} %copy-done.37, ...), custom_call_target="tpu_custom_call" | custom-call | tf_op jit(solution)/shard_map/pallas_call | solution.py:215
  450.4 1.9 copy-done.29
  452.3 1.8 shard_map.437
  457.7 2.5 collective-permute-done.43
  460.3 3.8 collective-permute-done.44
  464.2 29.2 %collective-permute-done.45.refs_3_.refs_10_ = bf16[576,512]{1,0:T(8,128)(2,1)} collective-permute-done((bf16[576,512]{1,0:T(8,128)(2,1)}, bf16[576,512]{1,0:T(8,128)(2,1)}, u32[]{:S(2)}, u32[]{:S(2)}) %collective-permute-start.45) | collective-permute-done | bytes 589856 | tf_op jit(solution)/shard_map/ppermute | solution.py:878
  493.4 3.8 collective-permute-done.46
  497.3 2.1 shard_map.447
  505.5 4.5 collective-permute-start.37
  512.6 1.6 collective-permute-start.40
  516.2 3.7 collective-permute-start.38
  521.7 6.0 %shard_map.448 = (f32[768,512]{1,0:T(8,128)}, f32[768,512]{1,0:T(8,128)}, f32[768,512]{1,0:T(8,128)}) custom-call(s32[1]{0:T(128)} %bitcast.15.refs_0_, bf16[192,512]{1,0:T(8,128)(2,1)S(1)} %get-tuple-element.236.refs_1_, bf16[192,512]{1,0:T(8,128)(2,1)S(1)} %collective-permute-done.52.refs_2_, bf16[192,512]{1,0:T(8,128)(2,1)} %collective-permute-done.53.refs_3_, ...), custom_call_target="tpu_custom_call" | custom-call | tf_op jit(solution)/shard_map/pallas_call | solution.py:215
  529.0 1.7 reshape.296.refs_0_
  530.7 8.2 %shard_map.446 = (f32[6144,128]{1,0:T(8,128)}, f32[6144,128]{1,0:T(8,128)}, f32[6144,128]{1,0:T(8,128)}) custom-call(bf16[6144,128]{1,0:T(8,128)(2,1)} %reshape.296.refs_0_, f32[6144,128]{1,0:T(8,128)} %bitcast.99, f32[6144,128]{1,0:T(8,128)} %bitcast.120, f32[6144,128]{1,0:T(8,128)} %bitcast.121), custom_call_target="tpu_custom_call" | custom-call | tf_op jit(solution)/shard_map/pallas_call | solution.py:215
  545.1 3.7 shard_map.442
  548.9 3.9 shard_map.444
  (306 shorter events, 87.3 us)
Async XLA Ops:
  7.2 126.5 %all-gather.5.cloned.1.call-start = ((), (), s32[]{:S(2)}) async-start(), calls=%async_computation.4 | async-start | bytes 7077888 | tf_op jit(solution)/shard_map/all_gather | solution.py:897
  7.2 48.1 %collective-permute-start.1 = (bf16[512,512]{1,0:T(8,128)(2,1)}, bf16[512,512]{1,0:T(8,128)(2,1)}, u32[]{:S(2)}, u32[]{:S(2)}) collective-permute-start(bf16[512,512]{1,0:T(8,128)(2,1)} %refs_1_.7), channel_id=1, source_target_pairs={{0,4},{2,6},{4,0},{6,2},{1,5},{3,7},{5,1},{7,3},{8,12},{10,14},{12... | collective-permute-start | bytes 1572872 | tf_op jit(solution)/shard_map/ppermute | solution.py:844
  11.3 38.4 %copy-start.7 = (f32[128,2,3072]{2,1,0:T(2,128)S(1)}, f32[128,2,3072]{2,1,0:T(2,128)}, u32[]{:S(2)}) copy-start(f32[128,2,3072]{2,1,0:T(2,128)} %refs_1_.6) | copy-start | bytes 9437188
  16.1 8.1 %collective-permute-start.6 = (bf16[256,512]{1,0:T(8,128)(2,1)S(1)}, bf16[256,512]{1,0:T(8,128)(2,1)S(1)}, u32[]{:S(2)}, u32[]{:S(2)}) collective-permute-start(bf16[256,512]{1,0:T(8,128)(2,1)S(1)} %get-tuple-element.138), channel_id=1, source_target_pairs={{0,8},{8,16},{16,24},{24,0},{1,9},{9,17},{17,25},{25,1},{2,10},{10... | collective-permute-start | bytes 786440 | tf_op jit(solution)/shard_map/ppermute | solution.py:893
  16.1 9.2 %collective-permute-start.7 = (bf16[256,512]{1,0:T(8,128)(2,1)S(1)}, bf16[256,512]{1,0:T(8,128)(2,1)S(1)}, u32[]{:S(2)}, u32[]{:S(2)}) collective-permute-start(bf16[256,512]{1,0:T(8,128)(2,1)S(1)} %get-tuple-element.139), channel_id=1, source_target_pairs={{0,16},{8,24},{16,0},{24,8},{1,17},{9,25},{17,1},{25,9},{2,18},{10... | collective-permute-start | bytes 786440 | tf_op jit(solution)/shard_map/ppermute | solution.py:893
  17.6 11.9 %collective-permute-start.8 = (bf16[256,512]{1,0:T(8,128)(2,1)}, bf16[256,512]{1,0:T(8,128)(2,1)}, u32[]{:S(2)}, u32[]{:S(2)}) collective-permute-start(bf16[256,512]{1,0:T(8,128)(2,1)} %get-tuple-element.140), channel_id=1, source_target_pairs={{0,24},{8,0},{16,8},{24,16},{1,25},{9,1},{17,9},{25,17},{2,26},{10... | collective-permute-start | bytes 786440 | tf_op jit(solution)/shard_map/ppermute | solution.py:893
  19.0 15.0 %collective-permute-start.3 = (bf16[128,512]{1,0:T(8,128)(2,1)}, bf16[128,512]{1,0:T(8,128)(2,1)}, u32[]{:S(2)}, u32[]{:S(2)}) collective-permute-start(bf16[128,512]{1,0:T(8,128)(2,1)} %get-tuple-element.134), channel_id=1, source_target_pairs={{0,2},{2,4},{4,6},{6,0},{1,3},{3,5},{5,7},{7,1},{8,10},{10,12},{12... | collective-permute-start | bytes 393224 | tf_op jit(solution)/shard_map/ppermute | solution.py:878
  24.8 21.2 %collective-permute-start.4 = (bf16[128,512]{1,0:T(8,128)(2,1)}, bf16[128,512]{1,0:T(8,128)(2,1)}, u32[]{:S(2)}, u32[]{:S(2)}) collective-permute-start(bf16[128,512]{1,0:T(8,128)(2,1)} %get-tuple-element.135), channel_id=1, source_target_pairs={{0,4},{2,6},{4,0},{6,2},{1,5},{3,7},{5,1},{7,3},{8,12},{10,14},{12... | collective-permute-start | bytes 393224 | tf_op jit(solution)/shard_map/ppermute | solution.py:878
  25.9 29.4 %collective-permute-start.5 = (bf16[128,512]{1,0:T(8,128)(2,1)}, bf16[128,512]{1,0:T(8,128)(2,1)}, u32[]{:S(2)}, u32[]{:S(2)}) collective-permute-start(bf16[128,512]{1,0:T(8,128)(2,1)} %get-tuple-element.136), channel_id=1, source_target_pairs={{0,6},{2,0},{4,2},{6,4},{1,7},{3,1},{5,3},{7,5},{8,14},{10,8},{12,... | collective-permute-start | bytes 393224 | tf_op jit(solution)/shard_map/ppermute | solution.py:878
  32.5 22.9 %collective-permute-start.9 = (bf16[64,512]{1,0:T(8,128)(2,1)S(1)}, bf16[64,512]{1,0:T(8,128)(2,1)S(1)}, u32[]{:S(2)}, u32[]{:S(2)}) collective-permute-start(bf16[64,512]{1,0:T(8,128)(2,1)S(1)} %get-tuple-element.142), channel_id=1, source_target_pairs={{0,2},{2,4},{4,6},{6,0},{1,3},{3,5},{5,7},{7,1},{8,10},{10,12},{12... | collective-permute-start | bytes 196616 | tf_op jit(solution)/shard_map/ppermute | solution.py:878
  34.0 21.3 %collective-permute-start.10 = (bf16[64,512]{1,0:T(8,128)(2,1)S(1)}, bf16[64,512]{1,0:T(8,128)(2,1)S(1)}, u32[]{:S(2)}, u32[]{:S(2)}) collective-permute-start(bf16[64,512]{1,0:T(8,128)(2,1)S(1)} %get-tuple-element.143), channel_id=1, source_target_pairs={{0,4},{2,6},{4,0},{6,2},{1,5},{3,7},{5,1},{7,3},{8,12},{10,14},{12... | collective-permute-start | bytes 196616 | tf_op jit(solution)/shard_map/ppermute | solution.py:878
  46.0 9.3 %collective-permute-start.11 = (bf16[64,512]{1,0:T(8,128)(2,1)S(1)}, bf16[64,512]{1,0:T(8,128)(2,1)S(1)}, u32[]{:S(2)}, u32[]{:S(2)}) collective-permute-start(bf16[64,512]{1,0:T(8,128)(2,1)S(1)} %get-tuple-element.144), channel_id=1, source_target_pairs={{0,6},{2,0},{4,2},{6,4},{1,7},{3,1},{5,3},{7,5},{8,14},{10,8},{12,... | collective-permute-start | bytes 196616 | tf_op jit(solution)/shard_map/ppermute | solution.py:878
  58.4 195.6 %all-gather.7.cloned.1.call-start = ((), (), s32[]{:S(2)}) async-start(), calls=%async_computation.5 | async-start | bytes 21233664 | tf_op jit(solution)/shard_map/all_gather | solution.py:897
  58.4 67.2 %collective-permute-start.12 = (bf16[576,512]{1,0:T(8,128)(2,1)S(1)}, bf16[576,512]{1,0:T(8,128)(2,1)S(1)}, u32[]{:S(2)}, u32[]{:S(2)}) collective-permute-start(bf16[576,512]{1,0:T(8,128)(2,1)S(1)} %copy-done.67), channel_id=1, source_target_pairs={{0,2},{2,4},{4,6},{6,0},{1,3},{3,5},{5,7},{7,1},{8,10},{10,12},{12... | collective-permute-start | bytes 1769480 | tf_op jit(solution)/shard_map/ppermute | solution.py:878
  58.5 67.1 %collective-permute-start.13 = (bf16[576,512]{1,0:T(8,128)(2,1)S(1)}, bf16[576,512]{1,0:T(8,128)(2,1)S(1)}, u32[]{:S(2)}, u32[]{:S(2)}) collective-permute-start(bf16[576,512]{1,0:T(8,128)(2,1)S(1)} %copy-done.65), channel_id=1, source_target_pairs={{0,4},{2,6},{4,0},{6,2},{1,5},{3,7},{5,1},{7,3},{8,12},{10,14},{12... | collective-permute-start | bytes 1769480 | tf_op jit(solution)/shard_map/ppermute | solution.py:878
  59.4 66.2 %copy-start.22 = (bf16[576,512]{1,0:T(8,128)(2,1)S(1)}, bf16[576,512]{1,0:T(8,128)(2,1)}, u32[]{:S(2)}) copy-start(bf16[576,512]{1,0:T(8,128)(2,1)} %copy-done.21) | copy-start | bytes 1769476
  59.4 66.2 %collective-permute-start.14 = (bf16[576,512]{1,0:T(8,128)(2,1)S(1)}, bf16[576,512]{1,0:T(8,128)(2,1)S(1)}, u32[]{:S(2)}, u32[]{:S(2)}) collective-permute-start(bf16[576,512]{1,0:T(8,128)(2,1)S(1)} %copy-done.63), channel_id=1, source_target_pairs={{0,6},{2,0},{4,2},{6,4},{1,7},{3,1},{5,3},{7,5},{8,14},{10,8},{12,... | collective-permute-start | bytes 1769480 | tf_op jit(solution)/shard_map/ppermute | solution.py:878
  62.4 48.6 %collective-permute-start = (bf16[512,512]{1,0:T(8,128)(2,1)S(1)}, bf16[512,512]{1,0:T(8,128)(2,1)S(1)}, u32[]{:S(2)}, u32[]{:S(2)}) collective-permute-start(bf16[512,512]{1,0:T(8,128)(2,1)S(1)} %copy-done.30), channel_id=1, source_target_pairs={{0,2},{2,0},{4,6},{6,4},{1,3},{3,1},{5,7},{7,5},{8,10},{10,8},{12,... | collective-permute-start | bytes 1572872 | tf_op jit(solution)/shard_map/ppermute | solution.py:844
  62.9 59.1 %collective-permute-start.2 = (bf16[512,512]{1,0:T(8,128)(2,1)}, bf16[512,512]{1,0:T(8,128)(2,1)S(1)}, u32[]{:S(2)}, u32[]{:S(2)}) collective-permute-start(bf16[512,512]{1,0:T(8,128)(2,1)} %collective-permute-done.1.refs_10_.refs_3_), channel_id=1, source_target_pairs={{0,2},{2,0},{4,6},{6,4},{1,3},{3,1},{5,7},{7,5},{8,10},{10,8},{12,... | collective-permute-start | bytes 1572872 | tf_op jit(solution)/shard_map/ppermute | solution.py:844
  127.3 309.3 %reduce-scatter.3.cloned.1.call-start = ((), (), s32[]{:S(2)}) async-start(), calls=%async_computation.2 | async-start | bytes 21233664 | tf_op jit(solution)/shard_map/reduce_scatter | solution.py:903
  130.9 25.5 %collective-permute-start.17 = (bf16[512,512]{1,0:T(8,128)(2,1)}, bf16[512,512]{1,0:T(8,128)(2,1)}, u32[]{:S(2)}, u32[]{:S(2)}) collective-permute-start(bf16[512,512]{1,0:T(8,128)(2,1)} %shard_map.414.refs_6_.refs_1_), channel_id=1, source_target_pairs={{0,4},{2,6},{4,0},{6,2},{1,5},{3,7},{5,1},{7,3},{8,12},{10,14},{12... | collective-permute-start | bytes 1572872 | tf_op jit(solution)/shard_map/ppermute | solution.py:844
  146.2 26.1 %collective-permute-start.15 = (bf16[512,512]{1,0:T(8,128)(2,1)S(1)}, bf16[512,512]{1,0:T(8,128)(2,1)S(1)}, u32[]{:S(2)}, u32[]{:S(2)}) collective-permute-start(bf16[512,512]{1,0:T(8,128)(2,1)S(1)} %get-tuple-element.154.refs_5_.refs_6_), channel_id=1, source_target_pairs={{0,1},{2,3},{4,5},{6,7},{8,9},{10,11},{12,13},{14,15},{16,17},{18,... | collective-permute-start | bytes 1572872 | tf_op jit(solution)/shard_map/ppermute | solution.py:1331
  149.8 31.8 %collective-permute-start.16 = (bf16[512,512]{1,0:T(8,128)(2,1)}, bf16[512,512]{1,0:T(8,128)(2,1)}, u32[]{:S(2)}, u32[]{:S(2)}) collective-permute-start(bf16[512,512]{1,0:T(8,128)(2,1)} %shard_map.414.refs_6_.refs_1_), channel_id=1, source_target_pairs={{0,2},{2,0},{4,6},{6,4},{1,3},{3,1},{5,7},{7,5},{8,10},{10,8},{12,... | collective-permute-start | bytes 1572872 | tf_op jit(solution)/shard_map/ppermute | solution.py:844
  156.4 25.1 %collective-permute-start.18 = (bf16[512,512]{1,0:T(8,128)(2,1)}, bf16[512,512]{1,0:T(8,128)(2,1)}, u32[]{:S(2)}, u32[]{:S(2)}) collective-permute-start(bf16[512,512]{1,0:T(8,128)(2,1)} %collective-permute-done.17.refs_4_.refs_3_), channel_id=1, source_target_pairs={{0,2},{2,0},{4,6},{6,4},{1,3},{3,1},{5,7},{7,5},{8,10},{10,8},{12,... | collective-permute-start | bytes 1572872 | tf_op jit(solution)/shard_map/ppermute | solution.py:844
  186.0 11.9 %collective-permute-start.19 = (bf16[128,2048]{1,0:T(8,128)(2,1)S(1)}, bf16[128,2048]{1,0:T(8,128)(2,1)S(1)}, u32[]{:S(2)}, u32[]{:S(2)}) collective-permute-start(bf16[128,2048]{1,0:T(8,128)(2,1)S(1)} %get-tuple-element.159), channel_id=1, source_target_pairs={{0,2},{2,0},{4,6},{6,4},{1,3},{3,1},{5,7},{7,5},{8,10},{10,8},{12,... | collective-permute-start | bytes 1572872 | tf_op jit(solution)/shard_map/ppermute | solution.py:844
  198.0 21.9 %collective-permute-start.20 = (bf16[128,2048]{1,0:T(8,128)(2,1)S(1)}, bf16[128,2048]{1,0:T(8,128)(2,1)S(1)}, u32[]{:S(2)}, u32[]{:S(2)}) collective-permute-start(bf16[128,2048]{1,0:T(8,128)(2,1)S(1)} %get-tuple-element.160.refs_5_), channel_id=1, source_target_pairs={{0,2},{2,0},{4,6},{6,4},{1,3},{3,1},{5,7},{7,5},{8,10},{10,8},{12,... | collective-permute-start | bytes 1572872 | tf_op jit(solution)/shard_map/ppermute | solution.py:844
  198.0 21.8 %collective-permute-start.21 = (bf16[128,2048]{1,0:T(8,128)(2,1)S(1)}, bf16[128,2048]{1,0:T(8,128)(2,1)S(1)}, u32[]{:S(2)}, u32[]{:S(2)}) collective-permute-start(bf16[128,2048]{1,0:T(8,128)(2,1)S(1)} %shard_map.418), channel_id=1, source_target_pairs={{0,4},{2,6},{4,0},{6,2},{1,5},{3,7},{5,1},{7,3},{8,12},{10,14},{12... | collective-permute-start | bytes 1572872 | tf_op jit(solution)/shard_map/ppermute | solution.py:844
  222.1 18.2 %collective-permute-start.23 = (bf16[128,2048]{1,0:T(8,128)(2,1)}, bf16[128,2048]{1,0:T(8,128)(2,1)}, u32[]{:S(2)}, u32[]{:S(2)}) collective-permute-start(bf16[128,2048]{1,0:T(8,128)(2,1)} %get-tuple-element.162.refs_0_), channel_id=1, source_target_pairs={{0,4},{2,6},{4,0},{6,2},{1,5},{3,7},{5,1},{7,3},{8,12},{10,14},{12... | collective-permute-start | bytes 1572872 | tf_op jit(solution)/shard_map/ppermute | solution.py:844
  223.4 39.0 %collective-permute-start.22 = (bf16[128,2048]{1,0:T(8,128)(2,1)}, bf16[128,2048]{1,0:T(8,128)(2,1)}, u32[]{:S(2)}, u32[]{:S(2)}) collective-permute-start(bf16[128,2048]{1,0:T(8,128)(2,1)} %get-tuple-element.162.refs_0_), channel_id=1, source_target_pairs={{0,2},{2,0},{4,6},{6,4},{1,3},{3,1},{5,7},{7,5},{8,10},{10,8},{12,... | collective-permute-start | bytes 1572872 | tf_op jit(solution)/shard_map/ppermute | solution.py:844
  240.3 22.0 %collective-permute-start.24 = (bf16[128,2048]{1,0:T(8,128)(2,1)}, bf16[128,2048]{1,0:T(8,128)(2,1)}, u32[]{:S(2)}, u32[]{:S(2)}) collective-permute-start(bf16[128,2048]{1,0:T(8,128)(2,1)} %collective-permute-done.23.refs_2_), channel_id=1, source_target_pairs={{0,2},{2,0},{4,6},{6,4},{1,3},{3,1},{5,7},{7,5},{8,10},{10,8},{12,... | collective-permute-start | bytes 1572872 | tf_op jit(solution)/shard_map/ppermute | solution.py:844
  284.8 17.2 %collective-permute-start.25 = (bf16[128,2048]{1,0:T(8,128)(2,1)S(1)}, bf16[128,2048]{1,0:T(8,128)(2,1)S(1)}, u32[]{:S(2)}, u32[]{:S(2)}) collective-permute-start(bf16[128,2048]{1,0:T(8,128)(2,1)S(1)} %get-tuple-element.169.refs_7_), channel_id=1, source_target_pairs={{0,2},{2,0},{4,6},{6,4},{1,3},{3,1},{5,7},{7,5},{8,10},{10,8},{12,... | collective-permute-start | bytes 1572872 | tf_op jit(solution)/shard_map/ppermute | solution.py:844
  302.8 199.4 %reduce-scatter.5.cloned.1.call-start = ((), (), s32[]{:S(2)}) async-start(), calls=%async_computation.3 | async-start | bytes 7077888 | tf_op jit(solution)/shard_map/reduce_scatter | solution.py:903
  305.3 16.7 %collective-permute-start.26 = (bf16[128,2048]{1,0:T(8,128)(2,1)}, bf16[128,2048]{1,0:T(8,128)(2,1)S(1)}, u32[]{:S(2)}, u32[]{:S(2)}) collective-permute-start(bf16[128,2048]{1,0:T(8,128)(2,1)} %copy-done.68), channel_id=1, source_target_pairs={{0,2},{2,0},{4,6},{6,4},{1,3},{3,1},{5,7},{7,5},{8,10},{10,8},{12,... | collective-permute-start | bytes 1572872 | tf_op jit(solution)/shard_map/ppermute | solution.py:844
  306.8 21.9 %collective-permute-start.27 = (bf16[128,2048]{1,0:T(8,128)(2,1)S(1)}, bf16[128,2048]{1,0:T(8,128)(2,1)S(1)}, u32[]{:S(2)}, u32[]{:S(2)}) collective-permute-start(bf16[128,2048]{1,0:T(8,128)(2,1)S(1)} %shard_map.425), channel_id=1, source_target_pairs={{0,4},{2,6},{4,0},{6,2},{1,5},{3,7},{5,1},{7,3},{8,12},{10,14},{12... | collective-permute-start | bytes 1572872 | tf_op jit(solution)/shard_map/ppermute | solution.py:844
  333.1 21.5 %collective-permute-start.29 = (bf16[128,2048]{1,0:T(8,128)(2,1)S(1)}, bf16[128,2048]{1,0:T(8,128)(2,1)S(1)}, u32[]{:S(2)}, u32[]{:S(2)}) collective-permute-start(bf16[128,2048]{1,0:T(8,128)(2,1)S(1)} %get-tuple-element.174.refs_3_.refs_1_), channel_id=1, source_target_pairs={{0,4},{2,6},{4,0},{6,2},{1,5},{3,7},{5,1},{7,3},{8,12},{10,14},{12... | collective-permute-start | bytes 1572872 | tf_op jit(solution)/shard_map/ppermute | solution.py:844
  333.2 28.8 %collective-permute-start.28 = (bf16[128,2048]{1,0:T(8,128)(2,1)S(1)}, bf16[128,2048]{1,0:T(8,128)(2,1)S(1)}, u32[]{:S(2)}, u32[]{:S(2)}) collective-permute-start(bf16[128,2048]{1,0:T(8,128)(2,1)S(1)} %get-tuple-element.174.refs_3_.refs_1_), channel_id=1, source_target_pairs={{0,2},{2,0},{4,6},{6,4},{1,3},{3,1},{5,7},{7,5},{8,10},{10,8},{12,... | collective-permute-start | bytes 1572872 | tf_op jit(solution)/shard_map/ppermute | solution.py:844
  354.6 11.3 %collective-permute-start.30 = (bf16[128,2048]{1,0:T(8,128)(2,1)S(1)}, bf16[128,2048]{1,0:T(8,128)(2,1)S(1)}, u32[]{:S(2)}, u32[]{:S(2)}) collective-permute-start(bf16[128,2048]{1,0:T(8,128)(2,1)S(1)} %collective-permute-done.29.refs_3_), channel_id=1, source_target_pairs={{0,2},{2,0},{4,6},{6,4},{1,3},{3,1},{5,7},{7,5},{8,10},{10,8},{12,... | collective-permute-start | bytes 1572872 | tf_op jit(solution)/shard_map/ppermute | solution.py:844
  372.1 11.3 %collective-permute-start.31 = (bf16[512,512]{1,0:T(8,128)(2,1)S(1)}, bf16[512,512]{1,0:T(8,128)(2,1)S(1)}, u32[]{:S(2)}, u32[]{:S(2)}) collective-permute-start(bf16[512,512]{1,0:T(8,128)(2,1)S(1)} %get-tuple-element.179), channel_id=1, source_target_pairs={{0,2},{2,0},{4,6},{6,4},{1,3},{3,1},{5,7},{7,5},{8,10},{10,8},{12,... | collective-permute-start | bytes 1572872 | tf_op jit(solution)/shard_map/ppermute | solution.py:844
  383.5 19.2 %collective-permute-start.32 = (bf16[512,512]{1,0:T(8,128)(2,1)S(1)}, bf16[512,512]{1,0:T(8,128)(2,1)S(1)}, u32[]{:S(2)}, u32[]{:S(2)}) collective-permute-start(bf16[512,512]{1,0:T(8,128)(2,1)S(1)} %get-tuple-element.180), channel_id=1, source_target_pairs={{0,2},{2,0},{4,6},{6,4},{1,3},{3,1},{5,7},{7,5},{8,10},{10,8},{12,... | collective-permute-start | bytes 1572872 | tf_op jit(solution)/shard_map/ppermute | solution.py:844
  383.7 23.7 %collective-permute-start.33 = (bf16[512,512]{1,0:T(8,128)(2,1)S(1)}, bf16[512,512]{1,0:T(8,128)(2,1)S(1)}, u32[]{:S(2)}, u32[]{:S(2)}) collective-permute-start(bf16[512,512]{1,0:T(8,128)(2,1)S(1)} %shard_map.430), channel_id=1, source_target_pairs={{0,4},{2,6},{4,0},{6,2},{1,5},{3,7},{5,1},{7,3},{8,12},{10,14},{12... | collective-permute-start | bytes 1572872 | tf_op jit(solution)/shard_map/ppermute | solution.py:844
  394.9 22.5 %collective-permute-start.34 = (bf16[512,512]{1,0:T(8,128)(2,1)S(1)}, bf16[512,512]{1,0:T(8,128)(2,1)S(1)}, u32[]{:S(2)}, u32[]{:S(2)}) collective-permute-start(bf16[512,512]{1,0:T(8,128)(2,1)S(1)} %get-tuple-element.189), channel_id=1, source_target_pairs={{1,0},{3,2},{5,4},{7,6},{9,8},{11,10},{13,12},{15,14},{17,16},{19,... | collective-permute-start | bytes 1572872 | tf_op jit(solution)/shard_map/ppermute | solution.py:1369
  439.7 15.5 %collective-permute-start.35 = (bf16[576,512]{1,0:T(8,128)(2,1)}, bf16[576,512]{1,0:T(8,128)(2,1)S(1)}, u32[]{:S(2)}, u32[]{:S(2)}) collective-permute-start(bf16[576,512]{1,0:T(8,128)(2,1)} %get-tuple-element.200), channel_id=1, source_target_pairs={{0,6},{2,0},{4,2},{6,4},{1,7},{3,1},{5,3},{7,5},{8,14},{10,8},{12,... | collective-permute-start | bytes 1769480 | tf_op jit(solution)/shard_map/ppermute | solution.py:878
  440.8 52.6 %collective-permute-start.45 = (bf16[576,512]{1,0:T(8,128)(2,1)}, bf16[576,512]{1,0:T(8,128)(2,1)}, u32[]{:S(2)}, u32[]{:S(2)}) collective-permute-start(bf16[576,512]{1,0:T(8,128)(2,1)} %get-tuple-element.217), channel_id=1, source_target_pairs={{0,4},{2,6},{4,0},{6,2},{1,5},{3,7},{5,1},{7,3},{8,12},{10,14},{12... | collective-permute-start | bytes 1769480 | tf_op jit(solution)/shard_map/ppermute | solution.py:878
  442.0 55.3 %collective-permute-start.51 = (bf16[576,512]{1,0:T(8,128)(2,1)}, bf16[576,512]{1,0:T(8,128)(2,1)}, u32[]{:S(2)}, u32[]{:S(2)}) collective-permute-start(bf16[576,512]{1,0:T(8,128)(2,1)} %get-tuple-element.232), channel_id=1, source_target_pairs={{0,2},{2,4},{4,6},{6,0},{1,3},{3,5},{5,7},{7,1},{8,10},{10,12},{12... | collective-permute-start | bytes 1769480 | tf_op jit(solution)/shard_map/ppermute | solution.py:878
  454.9 55.0 %copy-start.77 = (f32[2,2048]{1,0:T(2,128)S(1)}, f32[2,2048]{1,0:T(2,128)}, u32[]{:S(2)}) copy-start(f32[2,2048]{1,0:T(2,128)} %param.42) | copy-start | bytes 49156
  454.9 55.0 %copy-start.78 = (f32[2,2048]{1,0:T(2,128)S(1)}, f32[2,2048]{1,0:T(2,128)}, u32[]{:S(2)}) copy-start(f32[2,2048]{1,0:T(2,128)} %param.44) | copy-start | bytes 49156
  454.9 55.0 %copy-start.79 = (f32[2,2048]{1,0:T(2,128)S(1)}, f32[2,2048]{1,0:T(2,128)}, u32[]{:S(2)}) copy-start(f32[2,2048]{1,0:T(2,128)} %param.43) | copy-start | bytes 49156
  455.2 1.2 collective-permute-start.42
  456.4 3.8 collective-permute-start.43
  460.2 4.0 collective-permute-start.44
  493.4 3.8 collective-permute-start.46
  497.2 5.0 collective-permute-start.47
  497.2 15.4 %collective-permute-start.36 = (bf16[512,512]{1,0:T(8,128)(2,1)}, bf16[512,512]{1,0:T(8,128)(2,1)S(1)}, u32[]{:S(2)}, u32[]{:S(2)}) collective-permute-start(bf16[512,512]{1,0:T(8,128)(2,1)} %get-tuple-element.206), channel_id=1, source_target_pairs={{0,2},{2,0},{4,6},{6,4},{1,3},{3,1},{5,7},{7,5},{8,10},{10,8},{12,... | collective-permute-start | bytes 1572872 | tf_op jit(solution)/shard_map/ppermute | solution.py:844
  499.4 16.8 %collective-permute-start.52 = (bf16[192,512]{1,0:T(8,128)(2,1)}, bf16[192,512]{1,0:T(8,128)(2,1)S(1)}, u32[]{:S(2)}, u32[]{:S(2)}) collective-permute-start(bf16[192,512]{1,0:T(8,128)(2,1)} %get-tuple-element.237), channel_id=1, source_target_pairs={{0,8},{8,16},{16,24},{24,0},{1,9},{9,17},{17,25},{25,1},{2,10},{10... | collective-permute-start | bytes 589832 | tf_op jit(solution)/shard_map/ppermute | solution.py:893
  499.4 20.5 %collective-permute-start.53 = (bf16[192,512]{1,0:T(8,128)(2,1)}, bf16[192,512]{1,0:T(8,128)(2,1)}, u32[]{:S(2)}, u32[]{:S(2)}) collective-permute-start(bf16[192,512]{1,0:T(8,128)(2,1)} %get-tuple-element.238), channel_id=1, source_target_pairs={{0,16},{8,24},{16,0},{24,8},{1,17},{9,25},{17,1},{25,9},{2,18},{10... | collective-permute-start | bytes 589832 | tf_op jit(solution)/shard_map/ppermute | solution.py:893
  500.8 20.9 %collective-permute-start.54 = (bf16[192,512]{1,0:T(8,128)(2,1)}, bf16[192,512]{1,0:T(8,128)(2,1)}, u32[]{:S(2)}, u32[]{:S(2)}) collective-permute-start(bf16[192,512]{1,0:T(8,128)(2,1)} %get-tuple-element.239), channel_id=1, source_target_pairs={{0,24},{8,0},{16,8},{24,16},{1,25},{9,1},{17,9},{25,17},{2,26},{10... | collective-permute-start | bytes 589832 | tf_op jit(solution)/shard_map/ppermute | solution.py:893
  505.5 9.8 %collective-permute-start.37 = (bf16[192,512]{1,0:T(8,128)(2,1)}, bf16[192,512]{1,0:T(8,128)(2,1)S(1)}, u32[]{:S(2)}, u32[]{:S(2)}) collective-permute-start(bf16[192,512]{1,0:T(8,128)(2,1)} %get-tuple-element.208), channel_id=1, source_target_pairs={{0,6},{2,0},{4,2},{6,4},{1,7},{3,1},{5,3},{7,5},{8,14},{10,8},{12,... | collective-permute-start | bytes 589832 | tf_op jit(solution)/shard_map/ppermute | solution.py:878
  512.6 26.3 %collective-permute-start.40 = (bf16[192,512]{1,0:T(8,128)(2,1)}, bf16[192,512]{1,0:T(8,128)(2,1)S(1)}, u32[]{:S(2)}, u32[]{:S(2)}) collective-permute-start(bf16[192,512]{1,0:T(8,128)(2,1)} %copy-done.70), channel_id=1, source_target_pairs={{0,4},{2,6},{4,0},{6,2},{1,5},{3,7},{5,1},{7,3},{8,12},{10,14},{12... | collective-permute-start | bytes 589832 | tf_op jit(solution)/shard_map/ppermute | solution.py:878
  515.3 23.6 %collective-permute-start.41 = (bf16[192,512]{1,0:T(8,128)(2,1)}, bf16[192,512]{1,0:T(8,128)(2,1)}, u32[]{:S(2)}, u32[]{:S(2)}) collective-permute-start(bf16[192,512]{1,0:T(8,128)(2,1)} %copy-done.69), channel_id=1, source_target_pairs={{0,2},{2,4},{4,6},{6,0},{1,3},{3,5},{5,7},{7,1},{8,10},{10,12},{12... | collective-permute-start | bytes 589832 | tf_op jit(solution)/shard_map/ppermute | solution.py:878
  516.2 36.6 %collective-permute-start.38 = (bf16[512,512]{1,0:T(8,128)(2,1)}, bf16[512,512]{1,0:T(8,128)(2,1)}, u32[]{:S(2)}, u32[]{:S(2)}) collective-permute-start(bf16[512,512]{1,0:T(8,128)(2,1)} %get-tuple-element.209), channel_id=1, source_target_pairs={{0,2},{2,0},{4,6},{6,4},{1,3},{3,1},{5,7},{7,5},{8,10},{10,8},{12,... | collective-permute-start | bytes 1572872 | tf_op jit(solution)/shard_map/ppermute | solution.py:844
  519.9 32.9 %collective-permute-start.39 = (bf16[512,512]{1,0:T(8,128)(2,1)}, bf16[512,512]{1,0:T(8,128)(2,1)}, u32[]{:S(2)}, u32[]{:S(2)}) collective-permute-start(bf16[512,512]{1,0:T(8,128)(2,1)} %shard_map.439), channel_id=1, source_target_pairs={{0,4},{2,6},{4,0},{6,2},{1,5},{3,7},{5,1},{7,3},{8,12},{10,14},{12... | collective-permute-start | bytes 1572872 | tf_op jit(solution)/shard_map/ppermute | solution.py:844
  539.9 9.0 %collective-permute-start.48 = (bf16[64,512]{1,0:T(8,128)(2,1)S(1)}, bf16[64,512]{1,0:T(8,128)(2,1)S(1)}, u32[]{:S(2)}, u32[]{:S(2)}) collective-permute-start(bf16[64,512]{1,0:T(8,128)(2,1)S(1)} %get-tuple-element.224), channel_id=1, source_target_pairs={{0,8},{8,16},{16,24},{24,0},{1,9},{9,17},{17,25},{25,1},{2,10},{10... | collective-permute-start | bytes 196616 | tf_op jit(solution)/shard_map/ppermute | solution.py:893
  540.0 8.9 %collective-permute-start.49 = (bf16[64,512]{1,0:T(8,128)(2,1)S(1)}, bf16[64,512]{1,0:T(8,128)(2,1)S(1)}, u32[]{:S(2)}, u32[]{:S(2)}) collective-permute-start(bf16[64,512]{1,0:T(8,128)(2,1)S(1)} %get-tuple-element.225), channel_id=1, source_target_pairs={{0,16},{8,24},{16,0},{24,8},{1,17},{9,25},{17,1},{25,9},{2,18},{10... | collective-permute-start | bytes 196616 | tf_op jit(solution)/shard_map/ppermute | solution.py:893
  541.2 7.7 %collective-permute-start.50 = (bf16[64,512]{1,0:T(8,128)(2,1)S(1)}, bf16[64,512]{1,0:T(8,128)(2,1)S(1)}, u32[]{:S(2)}, u32[]{:S(2)}) collective-permute-start(bf16[64,512]{1,0:T(8,128)(2,1)S(1)} %get-tuple-element.226), channel_id=1, source_target_pairs={{0,24},{8,0},{16,8},{24,16},{1,25},{9,1},{17,9},{25,17},{2,26},{10... | collective-permute-start | bytes 196616 | tf_op jit(solution)/shard_map/ppermute | solution.py:893
  (78 other events, 494.5 us)
Sparse Core Ops, SparseCore 0:
  58.5 43.7 all-gather.4
  127.5 109.0 all-gather.6
  302.9 133.6 reduce-scatter.2
  439.9 59.5 reduce-scatter.4

commit v6 on v5

--- a/solution.py
+++ b/solution.py
@@ -348,6 +348,7 @@
         [blocked((block, width), lambda i, z: (i, 0))],
         [blocked((block, dp * rest), index)] * size,
         after=after,
+        hbm=2**20,
     )
 
 
@@ -1079,60 +1080,8 @@
         [shard],
         [z],
         after=after,
-    )
-
-
-def split_attention(shard, terms, rows, inner, z, after=()):
-    size, dp = lax.axis_size("row"), lax.axis_size("dp")
-    rest = MODEL_WIDTH // (size * dp)
-    steps = MODEL_WIDTH // COLUMNS
-    base = terms * size * rows
-    quarter = quarter_index()
-    if rest % 128:
-        ins = shard[:base].reshape(terms, size, rows, COLUMNS).transpose(1, 0, 2, 3)
-        ins = jnp.take(ins, behind(z, jnp.arange(size), size), axis=0)
-        outs = shard[base:].reshape(steps, inner, COLUMNS).transpose(1, 0, 2)
-        outs = outs.reshape(inner, dp, size, rest)
-        outs = jnp.take(outs, ahead(quarter, jnp.arange(size), size), axis=2)
-        return (
-            [ins[k].reshape(-1, COLUMNS) for k in range(size)],
-            [outs[:, :, k].reshape(inner, COLUMNS) for k in range(size)],
-        )
-
-    def kernel(z, quarter, full, *outs):
-        for k in range(size):
-            at = behind(z[0], k, size)
-            for t in range(terms):
-                first = pl.multiple_of((t * size + at) * rows, rows)
-                outs[k][t * rows : (t + 1) * rows, :] = full[pl.ds(first, rows), :]
-            place = pl.multiple_of(ahead(quarter[0], k, size) * rest, rest)
-            for d in range(dp):
-                part = full[base + d * inner : base + (d + 1) * inner, pl.ds(place, rest)]
-                outs[size + k][:, d * rest : (d + 1) * rest] = part
-
-    pieces = call(
-        kernel,
-        [shape((terms * rows, COLUMNS), BF)] * size + [shape((inner, COLUMNS), BF)] * size,
-        [shard],
-        [z, quarter],
-        after=after,
-    )
-    return pieces[:size], pieces[size:]
-
-
-def turned_back(pieces):
-    size = len(pieces)
-    per = lax.axis_size("dp") // size
-    result = []
-    for k, piece in enumerate(pieces):
-        pairs = []
-        for q in range(size):
-            for r in range(per):
-                for z in range(size):
-                    target = (z * per + r) * size + (q + k) % size
-                    pairs.append(((q * per + r) * size + z, target))
-        result.append(lax.ppermute(piece, ("dp", "row"), pairs))
-    return result
+        hbm=2**19,
+    )
 
 
 def out_pieces(messages, inner, z, after=()):
@@ -1160,6 +1109,17 @@
 def update_out(state, pieces, rate, place):
     size = len(pieces)
     rows, width = pieces[0].shape
+    if rows * width <= 2**15:
+
+        def whole(q, *refs):
+            for k in range(size):
+                own = pl.ds(pl.multiple_of(behind(q[0], k, size) * rows, rows), rows)
+                update([ref.at[own, :] for ref in refs[size:]], refs[k][...].astype(F32), rate)
+
+        w, m, v = call(
+            whole, [shape(state[0].shape, F32)] * 3, list(pieces) + list(state), [place]
+        )
+        return m, v, w
 
     def kernel(q, *refs):
         k = pl.program_id(0)
@@ -1209,7 +1169,7 @@
 def update_pair(state, grad, rate):
     rows, two, width = state[0].shape
     total = rows * two * width // 128
-    steps = 4 if total % 64 == 0 else 1
+    steps = 4 if total >= 4096 else 2
 
     def kernel(grad, *refs):
         update(refs, grad[...].astype(F32), rate)

time: 571 us -> 571 us (level)
    unnamed x166 -> x164, local copies, waits for them, and re-layouts: 36.8 us -> 31.3 us
  transfers between devices with their start and end apart: 59 -> 59, of which waited for: 25 -> 26; matrix products, arithmetic and copies ran while one was open for 2% -> 2% of each run, Pallas kernels for 24% -> 25%
where the time goes in v6:
time: 571 us; the launch traced here: 562 us
  waiting for transfers between devices  223 us (39%)
  Pallas kernels  166 us (29%)
  starting transfers between devices  115 us (20%)
  local copies, waits for them, and re-layouts  35.6 us (6%)
  between operations  15.2 us (3%)
  other arithmetic  7.6 us (1%)
    ppermute x29, waiting for transfers between devices, swap(): lax.ppermute(value, axis, [(i, i ^ step) for i in range(lax.axis_size(axi...  158 us
    pallas_call x40, Pallas kernels, call(): pl.pallas_call(run, grid_spec=pltpu.PrefetchScalarGridSpec(num_scalar_pre...  149 us
    ppermute x29, starting transfers between devices, swap(): lax.ppermute(value, axis, [(i, i ^ step) for i in range(lax.axis_size(axi...  67.4 us
    ppermute x15, starting transfers between devices, along_row(): lax.ppermute(p, 'row', [(i, (i + sign * k) % size) for i in range(size)])  34.1 us
    unnamed x164, local copies, waits for them, and re-layouts  31.3 us
    ppermute x15, waiting for transfers between devices, along_row(): lax.ppermute(p, 'row', [(i, (i + sign * k) % size) for i in range(size)])  31.2 us
    ppermute x1, waiting for transfers between devices, body(): lax.ppermute(keys_values, 'col', [(i, i + 1) for i in range(cols - 1)])  14.9 us
  transfers between devices with their start and end apart: 59, of which 26 were waited for; matrix products, arithmetic and copies ran while one was open for 2% of the time, Pallas kernels for 25%

profile of v6, /device:TPU:0, one launch (start us, length us, event | category | flops | bytes accessed | tf_op | source)
XLA Modules:
  0.0 562.1 jit_solution(596728425817009992)
XLA Ops:
  7.2 4.1 collective-permute-start.1
  11.3 2.4 shard_map.407
  13.8 2.3 shard_map.408
  20.6 3.5 collective-permute-done.6.refs_9_
  25.9 3.5 collective-permute-start.5
  34.0 12.0 %collective-permute-start.10 = (bf16[64,512]{1,0:T(8,128)(2,1)S(1)}, bf16[64,512]{1,0:T(8,128)(2,1)S(1)}, u32[]{:S(2)}, u32[]{:S(2)}) collective-permute-start(bf16[64,512]{1,0:T(8,128)(2,1)S(1)} %get-tuple-element.143), channel_id=1, source_target_pairs={{0,4},{2,6},{4,0},{6,2},{1,5},{3,7},{5,1},{7,3},{8,12},{10,14},{12... | collective-permute-start | bytes 196616 | tf_op jit(solution)/shard_map/ppermute | solution.py:879
  46.0 3.7 collective-permute-start.11
  49.7 3.1 shard_map.410
  55.4 2.1 shard_map.411.refs_5_
  59.4 2.9 collective-permute-start.14
  64.4 46.5 %collective-permute-done.refs_2_ = bf16[512,512]{1,0:T(8,128)(2,1)S(1)} collective-permute-done((bf16[512,512]{1,0:T(8,128)(2,1)S(1)}, bf16[512,512]{1,0:T(8,128)(2,1)S(1)}, u32[]{:S(2)}, u32[]{:S(2)}) %collective-permute-start) | collective-permute-done | bytes 524320 | tf_op jit(solution)/shard_map/ppermute | solution.py:845
  111.0 11.1 %collective-permute-done.2.refs_4_ = bf16[512,512]{1,0:T(8,128)(2,1)S(1)} collective-permute-done((bf16[512,512]{1,0:T(8,128)(2,1)}, bf16[512,512]{1,0:T(8,128)(2,1)S(1)}, u32[]{:S(2)}, u32[]{:S(2)}) %collective-permute-start.2) | collective-permute-done | bytes 524320 | tf_op jit(solution)/shard_map/ppermute | solution.py:845
  122.1 2.2 shard_map.412.refs_5_.refs_0_.refs_4_.refs_3_
  133.7 7.8 %shard_map.415 = (bf16[512,2048]{1,0:T(8,128)(2,1)S(1)}, f32[512,1]{1,0:T(8,128)S(1)}, f32[512,512]{1,0:T(8,128)S(1)}, f32[512,256]{1,0:T(8,128)S(1)}, bf16[512,...) custom-call(bf16[512,2048]{1,0:T(8,128)(2,1)S(1)} %copy-done.1, f32[1,2048]{1,0:T(1,128)S(1)} %bitcast.102, ...), custom_call_target="tpu_custom_call" | custom-call | tf_op jit(solution)/shard_map/pallas_call | solution.py:215
  146.2 3.6 collective-permute-start.15
  149.9 6.5 %collective-permute-done.17.refs_4_.refs_3_ = bf16[512,512]{1,0:T(8,128)(2,1)} collective-permute-done((bf16[512,512]{1,0:T(8,128)(2,1)}, bf16[512,512]{1,0:T(8,128)(2,1)}, u32[]{:S(2)}, u32[]{:S(2)}) %collective-permute-start.17) | collective-permute-done | bytes 524320 | tf_op jit(solution)/shard_map/ppermute | solution.py:845
  157.3 14.9 %collective-permute-done.15.refs_7_.refs_8_ = bf16[512,512]{1,0:T(8,128)(2,1)S(1)} collective-permute-done((bf16[512,512]{1,0:T(8,128)(2,1)S(1)}, bf16[512,512]{1,0:T(8,128)(2,1)S(1)}, u32[]{:S(2)}, u32[]{:S(2)}) %collective-permute-start.15) | collective-permute-done | bytes 524320 | tf_op jit(solution)/shard_map/ppermute | solution.py:1291
  174.2 7.3 %shard_map.416 = (bf16[512,512]{1,0:T(8,128)(2,1)S(1)}, f32[4,512,1]{2,1,0:T(8,128)S(1)}) custom-call(s32[1]{0:T(128)} %bitcast.1.refs_0_, s32[512,1]{1,0:T(8,128)S(1)} %copy-done.17, s32[1,512]{1,0:T(1,128)S(1)} %bitcast.105, s32[1,512]{1,0:T(1,128)S(1)} %bitcast.107, bf16[512,512]{1,0:T(8,128)(2,1)S(1)} %copy-done.24, ...), custom_call_target="tpu_custom_call" | custom-call | tf_op jit(solution)/shard_map/pallas_call | solution.py:93
  181.6 4.4 shard_map.417
  186.0 11.8 %collective-permute-done.19.refs_1_ = bf16[128,2048]{1,0:T(8,128)(2,1)S(1)} collective-permute-done((bf16[128,2048]{1,0:T(8,128)(2,1)S(1)}, bf16[128,2048]{1,0:T(8,128)(2,1)S(1)}, u32[]{:S(2)}, u32[]{:S(2)}) %collective-permute-start.19) | collective-permute-done | bytes 524320 | tf_op jit(solution)/shard_map/ppermute | solution.py:845
  198.0 3.0 collective-permute-start.21
  201.1 18.8 %collective-permute-done.20.refs_2_ = bf16[128,2048]{1,0:T(8,128)(2,1)S(1)} collective-permute-done((bf16[128,2048]{1,0:T(8,128)(2,1)S(1)}, bf16[128,2048]{1,0:T(8,128)(2,1)S(1)}, u32[]{:S(2)}, u32[]{:S(2)}) %collective-permute-start.20) | collective-permute-done | bytes 524320 | tf_op jit(solution)/shard_map/ppermute | solution.py:845
  223.4 16.5 %collective-permute-start.22 = (bf16[128,2048]{1,0:T(8,128)(2,1)}, bf16[128,2048]{1,0:T(8,128)(2,1)}, u32[]{:S(2)}, u32[]{:S(2)}) collective-permute-start(bf16[128,2048]{1,0:T(8,128)(2,1)} %get-tuple-element.162.refs_0_), channel_id=1, source_target_pairs={{0,2},{2,0},{4,6},{6,4},{1,3},{3,1},{5,7},{7,5},{8,10},{10,8},{12,... | collective-permute-start | bytes 1572872 | tf_op jit(solution)/shard_map/ppermute | solution.py:845
  240.3 9.7 %collective-permute-start.24 = (bf16[128,2048]{1,0:T(8,128)(2,1)}, bf16[128,2048]{1,0:T(8,128)(2,1)}, u32[]{:S(2)}, u32[]{:S(2)}) collective-permute-start(bf16[128,2048]{1,0:T(8,128)(2,1)} %collective-permute-done.23.refs_2_), channel_id=1, source_target_pairs={{0,2},{2,0},{4,6},{6,4},{1,3},{3,1},{5,7},{7,5},{8,10},{10,8},{12,... | collective-permute-start | bytes 1572872 | tf_op jit(solution)/shard_map/ppermute | solution.py:845
  250.0 2.6 shard_map.420.refs_0_.refs_6_
  255.5 6.8 %shard_map.421.refs_5_ = f32[512,1536]{1,0:T(8,128)S(1)} custom-call(bf16[512,2048]{1,0:T(8,128)(2,1)S(1)} %copy-done.3, bf16[2,4,2304,512]{3,2,1,0:T(8,128)(2,1)} %bitcast.110, bf16[128,2048]{1,0:T(8,128)(2,1)} %collective-permute-done.23.refs_2_), custom_call_target="tpu_custom_call" | custom-call | tf_op jit(solution)/shard_map/pallas_call | solution.py:215
  262.3 11.6 %shard_map.422 = (bf16[512,1536]{1,0:T(8,128)(2,1)S(1)}, bf16[512,3072]{1,0:T(8,128)(2,1)S(1)}) custom-call(bf16[128,2048]{1,0:T(8,128)(2,1)} %get-tuple-element.162.refs_0_, bf16[128,2048]{1,0:T(8,128)(2,1)} %collective-permute-done.22.refs_1_, bf16[128,2048]{1,0:T(8,128)(2,1)} %collective-permute-done.23.refs_2_, ...), custom_call_target="tpu_custom_call" | custom-call | tf_op jit(solution)/shard_map/pallas_call | solution.py:215
  274.0 10.0 %shard_map.423 = (f32[128,2048]{1,0:T(8,128)S(1)}, bf16[128,2048]{1,0:T(8,128)(2,1)S(1)}, bf16[128,2048]{1,0:T(8,128)(2,1)S(1)}, bf16[128,2048]{1,0:T(8,128)(2,1)S(1)}) custom-call(bf16[512,3072]{1,0:T(8,128)(2,1)S(1)} %get-tuple-element.165.refs_0_.refs_4_, bf16[2,4,2304,512]{3,2,1,0:T(8,128)(2,1)} %bitcast.112), custom_call_target="tpu_custom_call" | custom-call | tf_op jit(solution)/shard_map/pallas_call | solution.py:215
  284.8 17.2 %shard_map.424 = bf16[2,4,2304,512]{3,2,1,0:T(8,128)(2,1)} custom-call(bf16[128,2048]{1,0:T(8,128)(2,1)} %get-tuple-element.162.refs_0_, bf16[128,2048]{1,0:T(8,128)(2,1)} %collective-permute-done.22.refs_1_, bf16[128,2048]{1,0:T(8,128)(2,1)} %collective-permute-done.23.refs_2_, bf16[128,2048]{1,0:T(8,128)(2,1)} %collective-permute-done.24.refs_3_, ...), custom_call_target="tpu_custom_call" | custom-call | tf_op jit(solution)/shard_map/pallas_call | solution.py:215
  306.8 2.3 collective-permute-start.27
  309.1 12.8 %collective-permute-done.26.refs_1_ = bf16[128,2048]{1,0:T(8,128)(2,1)S(1)} collective-permute-done((bf16[128,2048]{1,0:T(8,128)(2,1)}, bf16[128,2048]{1,0:T(8,128)(2,1)S(1)}, u32[]{:S(2)}, u32[]{:S(2)}) %collective-permute-start.26) | collective-permute-done | bytes 524320 | tf_op jit(solution)/shard_map/ppermute | solution.py:845
  321.9 6.8 %collective-permute-done.27.refs_2_ = bf16[128,2048]{1,0:T(8,128)(2,1)S(1)} collective-permute-done((bf16[128,2048]{1,0:T(8,128)(2,1)S(1)}, bf16[128,2048]{1,0:T(8,128)(2,1)S(1)}, u32[]{:S(2)}, u32[]{:S(2)}) %collective-permute-start.27) | collective-permute-done | bytes 524320 | tf_op jit(solution)/shard_map/ppermute | solution.py:845
  329.5 3.5 shard_map.426
  333.2 7.9 %collective-permute-start.28 = (bf16[128,2048]{1,0:T(8,128)(2,1)S(1)}, bf16[128,2048]{1,0:T(8,128)(2,1)S(1)}, u32[]{:S(2)}, u32[]{:S(2)}) collective-permute-start(bf16[128,2048]{1,0:T(8,128)(2,1)S(1)} %get-tuple-element.174.refs_3_.refs_1_), channel_id=1, source_target_pairs={{0,2},{2,0},{4,6},{6,4},{1,3},{3,1},{5,7},{7,5},{8,10},{10,8},{12,... | collective-permute-start | bytes 1572872 | tf_op jit(solution)/shard_map/ppermute | solution.py:845
  341.1 13.5 %collective-permute-done.29.refs_3_ = bf16[128,2048]{1,0:T(8,128)(2,1)S(1)} collective-permute-done((bf16[128,2048]{1,0:T(8,128)(2,1)S(1)}, bf16[128,2048]{1,0:T(8,128)(2,1)S(1)}, u32[]{:S(2)}, u32[]{:S(2)}) %collective-permute-start.29) | collective-permute-done | bytes 524320 | tf_op jit(solution)/shard_map/ppermute | solution.py:845
  354.6 6.0 %shard_map.427.refs_6_.refs_1_ = bf16[512,2048]{1,0:T(8,128)(2,1)S(1)} custom-call(bf16[512,1536]{1,0:T(8,128)(2,1)S(1)} %copy-done.10, f32[128,2048]{1,0:T(8,128)S(1)} %copy-done.14, bf16[2,4,2304,512]{3,2,1,0:T(8,128)(2,1)} %bitcast.113, bf16[128,2048]{1,0:T(8,128)(2,1)S(1)} %get-tuple-element.174.refs_3_.refs_1_), custom_call_target="tpu_custom_call" | custom-call | tf_op jit(solution)/shard_map/pallas_call | solution.py:215
  362.0 3.9 collective-permute-done.30.refs_4_
  365.9 4.2 shard_map.428
  371.5 2.7 shard_map.429
  374.3 9.3 %shard_map.432 = (f32[512,512]{1,0:T(8,128)S(1)}, f32[512,256]{1,0:T(8,128)S(1)}, f32[512,256]{1,0:T(8,128)S(1)}, bf16[512,512]{1,0:T(8,128)(2,1)S(1)}) custom-call(s32[1]{0:T(128)} %bitcast.1.refs_0_, s32[512,1]{1,0:T(8,128)S(1)} %copy-done.18, s32[1,512]{1,0:T(1,128)S(1)} %bitcast.106, s32[1,512]{1,0:T(1,128)S(1)} %bitcast.108, ...), custom_call_target="tpu_custom_call" | custom-call | tf_op jit(solution)/shard_map/pallas_call | solution.py:163
  383.6 2.5 collective-permute-done.31.refs_1_
  386.3 10.7 %collective-permute-start.33 = (bf16[512,512]{1,0:T(8,128)(2,1)S(1)}, bf16[512,512]{1,0:T(8,128)(2,1)S(1)}, u32[]{:S(2)}, u32[]{:S(2)}) collective-permute-start(bf16[512,512]{1,0:T(8,128)(2,1)S(1)} %shard_map.430), channel_id=1, source_target_pairs={{0,4},{2,6},{4,0},{6,2},{1,5},{3,7},{5,1},{7,3},{8,12},{10,14},{12... | collective-permute-start | bytes 1572872 | tf_op jit(solution)/shard_map/ppermute | solution.py:845
  398.3 6.9 %collective-permute-done.32.refs_1_ = bf16[512,512]{1,0:T(8,128)(2,1)S(1)} collective-permute-done((bf16[512,512]{1,0:T(8,128)(2,1)S(1)}, bf16[512,512]{1,0:T(8,128)(2,1)S(1)}, u32[]{:S(2)}, u32[]{:S(2)}) %collective-permute-start.32) | collective-permute-done | bytes 524320 | tf_op jit(solution)/shard_map/ppermute | solution.py:845
  405.1 4.3 collective-permute-done.33.refs_2_
  410.6 11.4 %collective-permute-done.34.refs_5_ = bf16[512,512]{1,0:T(8,128)(2,1)S(1)} collective-permute-done((bf16[512,512]{1,0:T(8,128)(2,1)S(1)}, bf16[512,512]{1,0:T(8,128)(2,1)S(1)}, u32[]{:S(2)}, u32[]{:S(2)}) %collective-permute-start.34) | collective-permute-done | bytes 524320 | tf_op jit(solution)/shard_map/ppermute | solution.py:1329
  422.0 2.6 shard_map.433
  424.6 9.7 %shard_map.434 = bf16[2,4,768,512]{3,2,1,0:T(8,128)(2,1)} custom-call(bf16[512,2048]{1,0:T(8,128)(2,1)S(1)} %copy-done.31, bf16[512,1024]{1,0:T(8,128)(2,1)S(1)} %get-tuple-element.190.refs_1_, bf16[512,512]{1,0:T(8,128)(2,1)S(1)} %copy-done.22, bf16[512,2048]{1,0:T(8,128)(2,1)S(1)} %copy-done.8), custom_call_target="tpu_custom_call" | custom-call | tf_op jit(solution)/shard_map/pallas_call | solution.py:215
  435.3 3.3 reduce-scatter.3.cloned.1.call-done.refs_1_
  438.7 3.2 shard_map.435
  444.2 6.2 %shard_map.436 = (bf16[512,2048]{1,0:T(8,128)(2,1)S(1)}, f32[512,1]{1,0:T(8,128)S(1)}, f32[1,2048]{1,0:T(1,128)S(1)}) custom-call(s32[1]{0:T(128)} %bitcast.refs_0_, bf16[512,1024]{1,0:T(8,128)(2,1)S(1)} %copy-done.12, bf16[2,4,768,512]{3,2,1,0:T(8,128)(2,1)} %bitcast.117, bf16[512,2048]{1,0:T(8,128)(2,1)S(1)} %copy-done.1, f32[512,1]{1,0:T(8,128)S(1)} %copy-done.35, ...), custom_call_target="tpu_custom_call" | custom-call | tf_op jit(solution)/shard_map/pallas_call | solution.py:215
  452.6 3.9 shard_map.437
  460.2 2.2 collective-permute-done.43
  462.6 3.7 collective-permute-done.44
  466.3 29.3 %collective-permute-done.45.refs_3_.refs_10_ = bf16[576,512]{1,0:T(8,128)(2,1)} collective-permute-done((bf16[576,512]{1,0:T(8,128)(2,1)}, bf16[576,512]{1,0:T(8,128)(2,1)}, u32[]{:S(2)}, u32[]{:S(2)}) %collective-permute-start.45) | collective-permute-done | bytes 589856 | tf_op jit(solution)/shard_map/ppermute | solution.py:879
  495.5 3.8 collective-permute-done.46
  499.4 2.1 shard_map.447
  504.7 1.9 shard_map.438
  507.9 4.6 collective-permute-start.37
  516.0 1.8 collective-permute-done.37.refs_2_.refs_9_
  518.7 3.0 collective-permute-start.38
  521.7 1.9 collective-permute-start.39
  524.2 6.0 %shard_map.448 = (f32[768,512]{1,0:T(8,128)}, f32[768,512]{1,0:T(8,128)}, f32[768,512]{1,0:T(8,128)}) custom-call(s32[1]{0:T(128)} %bitcast.15.refs_0_, bf16[192,512]{1,0:T(8,128)(2,1)S(1)} %get-tuple-element.236.refs_1_, bf16[192,512]{1,0:T(8,128)(2,1)S(1)} %collective-permute-done.52.refs_2_, bf16[192,512]{1,0:T(8,128)(2,1)} %collective-permute-done.53.refs_3_, ...), custom_call_target="tpu_custom_call" | custom-call | tf_op jit(solution)/shard_map/pallas_call | solution.py:215
  533.2 8.2 %shard_map.446 = (f32[6144,128]{1,0:T(8,128)}, f32[6144,128]{1,0:T(8,128)}, f32[6144,128]{1,0:T(8,128)}) custom-call(bf16[6144,128]{1,0:T(8,128)(2,1)} %reshape.296.refs_0_, f32[6144,128]{1,0:T(8,128)} %bitcast.99, f32[6144,128]{1,0:T(8,128)} %bitcast.120, f32[6144,128]{1,0:T(8,128)} %bitcast.121), custom_call_target="tpu_custom_call" | custom-call | tf_op jit(solution)/shard_map/pallas_call | solution.py:215
  547.2 2.5 shard_map.442
  (304 shorter events, 86.2 us)
Async XLA Ops:
  7.2 126.5 %all-gather.5.cloned.1.call-start = ((), (), s32[]{:S(2)}) async-start(), calls=%async_computation.4 | async-start | bytes 7077888 | tf_op jit(solution)/shard_map/all_gather | solution.py:898
  7.2 48.1 %collective-permute-start.1 = (bf16[512,512]{1,0:T(8,128)(2,1)}, bf16[512,512]{1,0:T(8,128)(2,1)}, u32[]{:S(2)}, u32[]{:S(2)}) collective-permute-start(bf16[512,512]{1,0:T(8,128)(2,1)} %refs_1_.7), channel_id=1, source_target_pairs={{0,4},{2,6},{4,0},{6,2},{1,5},{3,7},{5,1},{7,3},{8,12},{10,14},{12... | collective-permute-start | bytes 1572872 | tf_op jit(solution)/shard_map/ppermute | solution.py:845
  11.3 38.4 %copy-start.6 = (f32[128,2,3072]{2,1,0:T(2,128)S(1)}, f32[128,2,3072]{2,1,0:T(2,128)}, u32[]{:S(2)}) copy-start(f32[128,2,3072]{2,1,0:T(2,128)} %refs_1_.6) | copy-start | bytes 9437188
  16.1 8.1 %collective-permute-start.6 = (bf16[256,512]{1,0:T(8,128)(2,1)S(1)}, bf16[256,512]{1,0:T(8,128)(2,1)S(1)}, u32[]{:S(2)}, u32[]{:S(2)}) collective-permute-start(bf16[256,512]{1,0:T(8,128)(2,1)S(1)} %get-tuple-element.138), channel_id=1, source_target_pairs={{0,8},{8,16},{16,24},{24,0},{1,9},{9,17},{17,25},{25,1},{2,10},{10... | collective-permute-start | bytes 786440 | tf_op jit(solution)/shard_map/ppermute | solution.py:894
  16.1 9.2 %collective-permute-start.7 = (bf16[256,512]{1,0:T(8,128)(2,1)S(1)}, bf16[256,512]{1,0:T(8,128)(2,1)S(1)}, u32[]{:S(2)}, u32[]{:S(2)}) collective-permute-start(bf16[256,512]{1,0:T(8,128)(2,1)S(1)} %get-tuple-element.139), channel_id=1, source_target_pairs={{0,16},{8,24},{16,0},{24,8},{1,17},{9,25},{17,1},{25,9},{2,18},{10... | collective-permute-start | bytes 786440 | tf_op jit(solution)/shard_map/ppermute | solution.py:894
  17.6 11.9 %collective-permute-start.8 = (bf16[256,512]{1,0:T(8,128)(2,1)}, bf16[256,512]{1,0:T(8,128)(2,1)}, u32[]{:S(2)}, u32[]{:S(2)}) collective-permute-start(bf16[256,512]{1,0:T(8,128)(2,1)} %get-tuple-element.140), channel_id=1, source_target_pairs={{0,24},{8,0},{16,8},{24,16},{1,25},{9,1},{17,9},{25,17},{2,26},{10... | collective-permute-start | bytes 786440 | tf_op jit(solution)/shard_map/ppermute | solution.py:894
  19.0 15.0 %collective-permute-start.3 = (bf16[128,512]{1,0:T(8,128)(2,1)}, bf16[128,512]{1,0:T(8,128)(2,1)}, u32[]{:S(2)}, u32[]{:S(2)}) collective-permute-start(bf16[128,512]{1,0:T(8,128)(2,1)} %get-tuple-element.134), channel_id=1, source_target_pairs={{0,2},{2,4},{4,6},{6,0},{1,3},{3,5},{5,7},{7,1},{8,10},{10,12},{12... | collective-permute-start | bytes 393224 | tf_op jit(solution)/shard_map/ppermute | solution.py:879
  24.8 21.2 %collective-permute-start.4 = (bf16[128,512]{1,0:T(8,128)(2,1)}, bf16[128,512]{1,0:T(8,128)(2,1)}, u32[]{:S(2)}, u32[]{:S(2)}) collective-permute-start(bf16[128,512]{1,0:T(8,128)(2,1)} %get-tuple-element.135), channel_id=1, source_target_pairs={{0,4},{2,6},{4,0},{6,2},{1,5},{3,7},{5,1},{7,3},{8,12},{10,14},{12... | collective-permute-start | bytes 393224 | tf_op jit(solution)/shard_map/ppermute | solution.py:879
  25.9 29.4 %collective-permute-start.5 = (bf16[128,512]{1,0:T(8,128)(2,1)}, bf16[128,512]{1,0:T(8,128)(2,1)}, u32[]{:S(2)}, u32[]{:S(2)}) collective-permute-start(bf16[128,512]{1,0:T(8,128)(2,1)} %get-tuple-element.136), channel_id=1, source_target_pairs={{0,6},{2,0},{4,2},{6,4},{1,7},{3,1},{5,3},{7,5},{8,14},{10,8},{12,... | collective-permute-start | bytes 393224 | tf_op jit(solution)/shard_map/ppermute | solution.py:879
  32.5 22.9 %collective-permute-start.9 = (bf16[64,512]{1,0:T(8,128)(2,1)S(1)}, bf16[64,512]{1,0:T(8,128)(2,1)S(1)}, u32[]{:S(2)}, u32[]{:S(2)}) collective-permute-start(bf16[64,512]{1,0:T(8,128)(2,1)S(1)} %get-tuple-element.142), channel_id=1, source_target_pairs={{0,2},{2,4},{4,6},{6,0},{1,3},{3,5},{5,7},{7,1},{8,10},{10,12},{12... | collective-permute-start | bytes 196616 | tf_op jit(solution)/shard_map/ppermute | solution.py:879
  34.0 21.3 %collective-permute-start.10 = (bf16[64,512]{1,0:T(8,128)(2,1)S(1)}, bf16[64,512]{1,0:T(8,128)(2,1)S(1)}, u32[]{:S(2)}, u32[]{:S(2)}) collective-permute-start(bf16[64,512]{1,0:T(8,128)(2,1)S(1)} %get-tuple-element.143), channel_id=1, source_target_pairs={{0,4},{2,6},{4,0},{6,2},{1,5},{3,7},{5,1},{7,3},{8,12},{10,14},{12... | collective-permute-start | bytes 196616 | tf_op jit(solution)/shard_map/ppermute | solution.py:879
  46.0 9.3 %collective-permute-start.11 = (bf16[64,512]{1,0:T(8,128)(2,1)S(1)}, bf16[64,512]{1,0:T(8,128)(2,1)S(1)}, u32[]{:S(2)}, u32[]{:S(2)}) collective-permute-start(bf16[64,512]{1,0:T(8,128)(2,1)S(1)} %get-tuple-element.144), channel_id=1, source_target_pairs={{0,6},{2,0},{4,2},{6,4},{1,7},{3,1},{5,3},{7,5},{8,14},{10,8},{12,... | collective-permute-start | bytes 196616 | tf_op jit(solution)/shard_map/ppermute | solution.py:879
  58.4 195.6 %all-gather.7.cloned.1.call-start = ((), (), s32[]{:S(2)}) async-start(), calls=%async_computation.5 | async-start | bytes 21233664 | tf_op jit(solution)/shard_map/all_gather | solution.py:898
  58.4 67.2 %collective-permute-start.12 = (bf16[576,512]{1,0:T(8,128)(2,1)S(1)}, bf16[576,512]{1,0:T(8,128)(2,1)S(1)}, u32[]{:S(2)}, u32[]{:S(2)}) collective-permute-start(bf16[576,512]{1,0:T(8,128)(2,1)S(1)} %copy-done.66), channel_id=1, source_target_pairs={{0,2},{2,4},{4,6},{6,0},{1,3},{3,5},{5,7},{7,1},{8,10},{10,12},{12... | collective-permute-start | bytes 1769480 | tf_op jit(solution)/shard_map/ppermute | solution.py:879
  58.5 67.1 %collective-permute-start.13 = (bf16[576,512]{1,0:T(8,128)(2,1)S(1)}, bf16[576,512]{1,0:T(8,128)(2,1)S(1)}, u32[]{:S(2)}, u32[]{:S(2)}) collective-permute-start(bf16[576,512]{1,0:T(8,128)(2,1)S(1)} %copy-done.64), channel_id=1, source_target_pairs={{0,4},{2,6},{4,0},{6,2},{1,5},{3,7},{5,1},{7,3},{8,12},{10,14},{12... | collective-permute-start | bytes 1769480 | tf_op jit(solution)/shard_map/ppermute | solution.py:879
  59.4 66.2 %copy-start.20 = (bf16[576,512]{1,0:T(8,128)(2,1)S(1)}, bf16[576,512]{1,0:T(8,128)(2,1)}, u32[]{:S(2)}) copy-start(bf16[576,512]{1,0:T(8,128)(2,1)} %copy-done.19) | copy-start | bytes 1769476
  59.4 66.2 %collective-permute-start.14 = (bf16[576,512]{1,0:T(8,128)(2,1)S(1)}, bf16[576,512]{1,0:T(8,128)(2,1)S(1)}, u32[]{:S(2)}, u32[]{:S(2)}) collective-permute-start(bf16[576,512]{1,0:T(8,128)(2,1)S(1)} %copy-done.62), channel_id=1, source_target_pairs={{0,6},{2,0},{4,2},{6,4},{1,7},{3,1},{5,3},{7,5},{8,14},{10,8},{12,... | collective-permute-start | bytes 1769480 | tf_op jit(solution)/shard_map/ppermute | solution.py:879
  62.4 48.6 %collective-permute-start = (bf16[512,512]{1,0:T(8,128)(2,1)S(1)}, bf16[512,512]{1,0:T(8,128)(2,1)S(1)}, u32[]{:S(2)}, u32[]{:S(2)}) collective-permute-start(bf16[512,512]{1,0:T(8,128)(2,1)S(1)} %copy-done.28), channel_id=1, source_target_pairs={{0,2},{2,0},{4,6},{6,4},{1,3},{3,1},{5,7},{7,5},{8,10},{10,8},{12,... | collective-permute-start | bytes 1572872 | tf_op jit(solution)/shard_map/ppermute | solution.py:845
  62.9 59.1 %collective-permute-start.2 = (bf16[512,512]{1,0:T(8,128)(2,1)}, bf16[512,512]{1,0:T(8,128)(2,1)S(1)}, u32[]{:S(2)}, u32[]{:S(2)}) collective-permute-start(bf16[512,512]{1,0:T(8,128)(2,1)} %collective-permute-done.1.refs_10_.refs_3_), channel_id=1, source_target_pairs={{0,2},{2,0},{4,6},{6,4},{1,3},{3,1},{5,7},{7,5},{8,10},{10,8},{12,... | collective-permute-start | bytes 1572872 | tf_op jit(solution)/shard_map/ppermute | solution.py:845
  127.3 311.3 %reduce-scatter.3.cloned.1.call-start = ((), (), s32[]{:S(2)}) async-start(), calls=%async_computation.2 | async-start | bytes 21233664 | tf_op jit(solution)/shard_map/reduce_scatter | solution.py:904
  130.9 25.5 %collective-permute-start.17 = (bf16[512,512]{1,0:T(8,128)(2,1)}, bf16[512,512]{1,0:T(8,128)(2,1)}, u32[]{:S(2)}, u32[]{:S(2)}) collective-permute-start(bf16[512,512]{1,0:T(8,128)(2,1)} %shard_map.414.refs_6_.refs_1_), channel_id=1, source_target_pairs={{0,4},{2,6},{4,0},{6,2},{1,5},{3,7},{5,1},{7,3},{8,12},{10,14},{12... | collective-permute-start | bytes 1572872 | tf_op jit(solution)/shard_map/ppermute | solution.py:845
  146.2 26.1 %collective-permute-start.15 = (bf16[512,512]{1,0:T(8,128)(2,1)S(1)}, bf16[512,512]{1,0:T(8,128)(2,1)S(1)}, u32[]{:S(2)}, u32[]{:S(2)}) collective-permute-start(bf16[512,512]{1,0:T(8,128)(2,1)S(1)} %get-tuple-element.154.refs_5_.refs_6_), channel_id=1, source_target_pairs={{0,1},{2,3},{4,5},{6,7},{8,9},{10,11},{12,13},{14,15},{16,17},{18,... | collective-permute-start | bytes 1572872 | tf_op jit(solution)/shard_map/ppermute | solution.py:1291
  149.8 31.8 %collective-permute-start.16 = (bf16[512,512]{1,0:T(8,128)(2,1)}, bf16[512,512]{1,0:T(8,128)(2,1)}, u32[]{:S(2)}, u32[]{:S(2)}) collective-permute-start(bf16[512,512]{1,0:T(8,128)(2,1)} %shard_map.414.refs_6_.refs_1_), channel_id=1, source_target_pairs={{0,2},{2,0},{4,6},{6,4},{1,3},{3,1},{5,7},{7,5},{8,10},{10,8},{12,... | collective-permute-start | bytes 1572872 | tf_op jit(solution)/shard_map/ppermute | solution.py:845
  156.4 25.1 %collective-permute-start.18 = (bf16[512,512]{1,0:T(8,128)(2,1)}, bf16[512,512]{1,0:T(8,128)(2,1)}, u32[]{:S(2)}, u32[]{:S(2)}) collective-permute-start(bf16[512,512]{1,0:T(8,128)(2,1)} %collective-permute-done.17.refs_4_.refs_3_), channel_id=1, source_target_pairs={{0,2},{2,0},{4,6},{6,4},{1,3},{3,1},{5,7},{7,5},{8,10},{10,8},{12,... | collective-permute-start | bytes 1572872 | tf_op jit(solution)/shard_map/ppermute | solution.py:845
  186.0 11.9 %collective-permute-start.19 = (bf16[128,2048]{1,0:T(8,128)(2,1)S(1)}, bf16[128,2048]{1,0:T(8,128)(2,1)S(1)}, u32[]{:S(2)}, u32[]{:S(2)}) collective-permute-start(bf16[128,2048]{1,0:T(8,128)(2,1)S(1)} %get-tuple-element.159), channel_id=1, source_target_pairs={{0,2},{2,0},{4,6},{6,4},{1,3},{3,1},{5,7},{7,5},{8,10},{10,8},{12,... | collective-permute-start | bytes 1572872 | tf_op jit(solution)/shard_map/ppermute | solution.py:845
  198.0 21.9 %collective-permute-start.20 = (bf16[128,2048]{1,0:T(8,128)(2,1)S(1)}, bf16[128,2048]{1,0:T(8,128)(2,1)S(1)}, u32[]{:S(2)}, u32[]{:S(2)}) collective-permute-start(bf16[128,2048]{1,0:T(8,128)(2,1)S(1)} %get-tuple-element.160.refs_5_), channel_id=1, source_target_pairs={{0,2},{2,0},{4,6},{6,4},{1,3},{3,1},{5,7},{7,5},{8,10},{10,8},{12,... | collective-permute-start | bytes 1572872 | tf_op jit(solution)/shard_map/ppermute | solution.py:845
  198.0 21.8 %collective-permute-start.21 = (bf16[128,2048]{1,0:T(8,128)(2,1)S(1)}, bf16[128,2048]{1,0:T(8,128)(2,1)S(1)}, u32[]{:S(2)}, u32[]{:S(2)}) collective-permute-start(bf16[128,2048]{1,0:T(8,128)(2,1)S(1)} %shard_map.418), channel_id=1, source_target_pairs={{0,4},{2,6},{4,0},{6,2},{1,5},{3,7},{5,1},{7,3},{8,12},{10,14},{12... | collective-permute-start | bytes 1572872 | tf_op jit(solution)/shard_map/ppermute | solution.py:845
  222.1 18.2 %collective-permute-start.23 = (bf16[128,2048]{1,0:T(8,128)(2,1)}, bf16[128,2048]{1,0:T(8,128)(2,1)}, u32[]{:S(2)}, u32[]{:S(2)}) collective-permute-start(bf16[128,2048]{1,0:T(8,128)(2,1)} %get-tuple-element.162.refs_0_), channel_id=1, source_target_pairs={{0,4},{2,6},{4,0},{6,2},{1,5},{3,7},{5,1},{7,3},{8,12},{10,14},{12... | collective-permute-start | bytes 1572872 | tf_op jit(solution)/shard_map/ppermute | solution.py:845
  223.4 39.0 %collective-permute-start.22 = (bf16[128,2048]{1,0:T(8,128)(2,1)}, bf16[128,2048]{1,0:T(8,128)(2,1)}, u32[]{:S(2)}, u32[]{:S(2)}) collective-permute-start(bf16[128,2048]{1,0:T(8,128)(2,1)} %get-tuple-element.162.refs_0_), channel_id=1, source_target_pairs={{0,2},{2,0},{4,6},{6,4},{1,3},{3,1},{5,7},{7,5},{8,10},{10,8},{12,... | collective-permute-start | bytes 1572872 | tf_op jit(solution)/shard_map/ppermute | solution.py:845
  240.3 22.0 %collective-permute-start.24 = (bf16[128,2048]{1,0:T(8,128)(2,1)}, bf16[128,2048]{1,0:T(8,128)(2,1)}, u32[]{:S(2)}, u32[]{:S(2)}) collective-permute-start(bf16[128,2048]{1,0:T(8,128)(2,1)} %collective-permute-done.23.refs_2_), channel_id=1, source_target_pairs={{0,2},{2,0},{4,6},{6,4},{1,3},{3,1},{5,7},{7,5},{8,10},{10,8},{12,... | collective-permute-start | bytes 1572872 | tf_op jit(solution)/shard_map/ppermute | solution.py:845
  284.8 17.2 %collective-permute-start.25 = (bf16[128,2048]{1,0:T(8,128)(2,1)S(1)}, bf16[128,2048]{1,0:T(8,128)(2,1)S(1)}, u32[]{:S(2)}, u32[]{:S(2)}) collective-permute-start(bf16[128,2048]{1,0:T(8,128)(2,1)S(1)} %get-tuple-element.169.refs_7_), channel_id=1, source_target_pairs={{0,2},{2,0},{4,6},{6,4},{1,3},{3,1},{5,7},{7,5},{8,10},{10,8},{12,... | collective-permute-start | bytes 1572872 | tf_op jit(solution)/shard_map/ppermute | solution.py:845
  302.8 201.9 %reduce-scatter.5.cloned.1.call-start = ((), (), s32[]{:S(2)}) async-start(), calls=%async_computation.3 | async-start | bytes 7077888 | tf_op jit(solution)/shard_map/reduce_scatter | solution.py:904
  305.3 16.7 %collective-permute-start.26 = (bf16[128,2048]{1,0:T(8,128)(2,1)}, bf16[128,2048]{1,0:T(8,128)(2,1)S(1)}, u32[]{:S(2)}, u32[]{:S(2)}) collective-permute-start(bf16[128,2048]{1,0:T(8,128)(2,1)} %copy-done.67), channel_id=1, source_target_pairs={{0,2},{2,0},{4,6},{6,4},{1,3},{3,1},{5,7},{7,5},{8,10},{10,8},{12,... | collective-permute-start | bytes 1572872 | tf_op jit(solution)/shard_map/ppermute | solution.py:845
  306.8 21.9 %collective-permute-start.27 = (bf16[128,2048]{1,0:T(8,128)(2,1)S(1)}, bf16[128,2048]{1,0:T(8,128)(2,1)S(1)}, u32[]{:S(2)}, u32[]{:S(2)}) collective-permute-start(bf16[128,2048]{1,0:T(8,128)(2,1)S(1)} %shard_map.425), channel_id=1, source_target_pairs={{0,4},{2,6},{4,0},{6,2},{1,5},{3,7},{5,1},{7,3},{8,12},{10,14},{12... | collective-permute-start | bytes 1572872 | tf_op jit(solution)/shard_map/ppermute | solution.py:845
  333.1 21.5 %collective-permute-start.29 = (bf16[128,2048]{1,0:T(8,128)(2,1)S(1)}, bf16[128,2048]{1,0:T(8,128)(2,1)S(1)}, u32[]{:S(2)}, u32[]{:S(2)}) collective-permute-start(bf16[128,2048]{1,0:T(8,128)(2,1)S(1)} %get-tuple-element.174.refs_3_.refs_1_), channel_id=1, source_target_pairs={{0,4},{2,6},{4,0},{6,2},{1,5},{3,7},{5,1},{7,3},{8,12},{10,14},{12... | collective-permute-start | bytes 1572872 | tf_op jit(solution)/shard_map/ppermute | solution.py:845
  333.2 28.8 %collective-permute-start.28 = (bf16[128,2048]{1,0:T(8,128)(2,1)S(1)}, bf16[128,2048]{1,0:T(8,128)(2,1)S(1)}, u32[]{:S(2)}, u32[]{:S(2)}) collective-permute-start(bf16[128,2048]{1,0:T(8,128)(2,1)S(1)} %get-tuple-element.174.refs_3_.refs_1_), channel_id=1, source_target_pairs={{0,2},{2,0},{4,6},{6,4},{1,3},{3,1},{5,7},{7,5},{8,10},{10,8},{12,... | collective-permute-start | bytes 1572872 | tf_op jit(solution)/shard_map/ppermute | solution.py:845
  354.6 11.3 %collective-permute-start.30 = (bf16[128,2048]{1,0:T(8,128)(2,1)S(1)}, bf16[128,2048]{1,0:T(8,128)(2,1)S(1)}, u32[]{:S(2)}, u32[]{:S(2)}) collective-permute-start(bf16[128,2048]{1,0:T(8,128)(2,1)S(1)} %collective-permute-done.29.refs_3_), channel_id=1, source_target_pairs={{0,2},{2,0},{4,6},{6,4},{1,3},{3,1},{5,7},{7,5},{8,10},{10,8},{12,... | collective-permute-start | bytes 1572872 | tf_op jit(solution)/shard_map/ppermute | solution.py:845
  374.2 11.9 %collective-permute-start.31 = (bf16[512,512]{1,0:T(8,128)(2,1)S(1)}, bf16[512,512]{1,0:T(8,128)(2,1)S(1)}, u32[]{:S(2)}, u32[]{:S(2)}) collective-permute-start(bf16[512,512]{1,0:T(8,128)(2,1)S(1)} %get-tuple-element.179), channel_id=1, source_target_pairs={{0,2},{2,0},{4,6},{6,4},{1,3},{3,1},{5,7},{7,5},{8,10},{10,8},{12,... | collective-permute-start | bytes 1572872 | tf_op jit(solution)/shard_map/ppermute | solution.py:845
  386.2 18.9 %collective-permute-start.32 = (bf16[512,512]{1,0:T(8,128)(2,1)S(1)}, bf16[512,512]{1,0:T(8,128)(2,1)S(1)}, u32[]{:S(2)}, u32[]{:S(2)}) collective-permute-start(bf16[512,512]{1,0:T(8,128)(2,1)S(1)} %get-tuple-element.180), channel_id=1, source_target_pairs={{0,2},{2,0},{4,6},{6,4},{1,3},{3,1},{5,7},{7,5},{8,10},{10,8},{12,... | collective-permute-start | bytes 1572872 | tf_op jit(solution)/shard_map/ppermute | solution.py:845
  386.3 23.1 %collective-permute-start.33 = (bf16[512,512]{1,0:T(8,128)(2,1)S(1)}, bf16[512,512]{1,0:T(8,128)(2,1)S(1)}, u32[]{:S(2)}, u32[]{:S(2)}) collective-permute-start(bf16[512,512]{1,0:T(8,128)(2,1)S(1)} %shard_map.430), channel_id=1, source_target_pairs={{0,4},{2,6},{4,0},{6,2},{1,5},{3,7},{5,1},{7,3},{8,12},{10,14},{12... | collective-permute-start | bytes 1572872 | tf_op jit(solution)/shard_map/ppermute | solution.py:845
  397.0 25.0 %collective-permute-start.34 = (bf16[512,512]{1,0:T(8,128)(2,1)S(1)}, bf16[512,512]{1,0:T(8,128)(2,1)S(1)}, u32[]{:S(2)}, u32[]{:S(2)}) collective-permute-start(bf16[512,512]{1,0:T(8,128)(2,1)S(1)} %get-tuple-element.189), channel_id=1, source_target_pairs={{1,0},{3,2},{5,4},{7,6},{9,8},{11,10},{13,12},{15,14},{17,16},{19,... | collective-permute-start | bytes 1572872 | tf_op jit(solution)/shard_map/ppermute | solution.py:1329
  441.9 15.5 %collective-permute-start.35 = (bf16[576,512]{1,0:T(8,128)(2,1)}, bf16[576,512]{1,0:T(8,128)(2,1)S(1)}, u32[]{:S(2)}, u32[]{:S(2)}) collective-permute-start(bf16[576,512]{1,0:T(8,128)(2,1)} %get-tuple-element.200), channel_id=1, source_target_pairs={{0,6},{2,0},{4,2},{6,4},{1,7},{3,1},{5,3},{7,5},{8,14},{10,8},{12,... | collective-permute-start | bytes 1769480 | tf_op jit(solution)/shard_map/ppermute | solution.py:879
  442.3 53.2 %collective-permute-start.45 = (bf16[576,512]{1,0:T(8,128)(2,1)}, bf16[576,512]{1,0:T(8,128)(2,1)}, u32[]{:S(2)}, u32[]{:S(2)}) collective-permute-start(bf16[576,512]{1,0:T(8,128)(2,1)} %get-tuple-element.217), channel_id=1, source_target_pairs={{0,4},{2,6},{4,0},{6,2},{1,5},{3,7},{5,1},{7,3},{8,12},{10,14},{12... | collective-permute-start | bytes 1769480 | tf_op jit(solution)/shard_map/ppermute | solution.py:879
  444.1 55.3 %collective-permute-start.51 = (bf16[576,512]{1,0:T(8,128)(2,1)}, bf16[576,512]{1,0:T(8,128)(2,1)}, u32[]{:S(2)}, u32[]{:S(2)}) collective-permute-start(bf16[576,512]{1,0:T(8,128)(2,1)} %get-tuple-element.232), channel_id=1, source_target_pairs={{0,2},{2,4},{4,6},{6,0},{1,3},{3,5},{5,7},{7,1},{8,10},{10,12},{12... | collective-permute-start | bytes 1769480 | tf_op jit(solution)/shard_map/ppermute | solution.py:879
  457.3 55.2 %copy-start.76 = (f32[2,2048]{1,0:T(2,128)S(1)}, f32[2,2048]{1,0:T(2,128)}, u32[]{:S(2)}) copy-start(f32[2,2048]{1,0:T(2,128)} %param.42) | copy-start | bytes 49156
  457.3 55.2 %copy-start.77 = (f32[2,2048]{1,0:T(2,128)S(1)}, f32[2,2048]{1,0:T(2,128)}, u32[]{:S(2)}) copy-start(f32[2,2048]{1,0:T(2,128)} %param.44) | copy-start | bytes 49156
  457.3 55.2 %copy-start.78 = (f32[2,2048]{1,0:T(2,128)S(1)}, f32[2,2048]{1,0:T(2,128)}, u32[]{:S(2)}) copy-start(f32[2,2048]{1,0:T(2,128)} %param.43) | copy-start | bytes 49156
  457.4 1.2 collective-permute-start.42
  458.6 3.8 collective-permute-start.43
  462.4 3.8 collective-permute-start.44
  495.5 3.8 collective-permute-start.46
  499.3 5.3 collective-permute-start.47
  499.3 15.8 %collective-permute-start.36 = (bf16[512,512]{1,0:T(8,128)(2,1)}, bf16[512,512]{1,0:T(8,128)(2,1)S(1)}, u32[]{:S(2)}, u32[]{:S(2)}) collective-permute-start(bf16[512,512]{1,0:T(8,128)(2,1)} %get-tuple-element.206), channel_id=1, source_target_pairs={{0,2},{2,0},{4,6},{6,4},{1,3},{3,1},{5,7},{7,5},{8,10},{10,8},{12,... | collective-permute-start | bytes 1572872 | tf_op jit(solution)/shard_map/ppermute | solution.py:845
  501.5 17.2 %collective-permute-start.52 = (bf16[192,512]{1,0:T(8,128)(2,1)}, bf16[192,512]{1,0:T(8,128)(2,1)S(1)}, u32[]{:S(2)}, u32[]{:S(2)}) collective-permute-start(bf16[192,512]{1,0:T(8,128)(2,1)} %get-tuple-element.237), channel_id=1, source_target_pairs={{0,8},{8,16},{16,24},{24,0},{1,9},{9,17},{17,25},{25,1},{2,10},{10... | collective-permute-start | bytes 589832 | tf_op jit(solution)/shard_map/ppermute | solution.py:894
  501.6 20.2 %collective-permute-start.53 = (bf16[192,512]{1,0:T(8,128)(2,1)}, bf16[192,512]{1,0:T(8,128)(2,1)}, u32[]{:S(2)}, u32[]{:S(2)}) collective-permute-start(bf16[192,512]{1,0:T(8,128)(2,1)} %get-tuple-element.238), channel_id=1, source_target_pairs={{0,16},{8,24},{16,0},{24,8},{1,17},{9,25},{17,1},{25,9},{2,18},{10... | collective-permute-start | bytes 589832 | tf_op jit(solution)/shard_map/ppermute | solution.py:894
  503.2 20.9 %collective-permute-start.54 = (bf16[192,512]{1,0:T(8,128)(2,1)}, bf16[192,512]{1,0:T(8,128)(2,1)}, u32[]{:S(2)}, u32[]{:S(2)}) collective-permute-start(bf16[192,512]{1,0:T(8,128)(2,1)} %get-tuple-element.239), channel_id=1, source_target_pairs={{0,24},{8,0},{16,8},{24,16},{1,25},{9,1},{17,9},{25,17},{2,26},{10... | collective-permute-start | bytes 589832 | tf_op jit(solution)/shard_map/ppermute | solution.py:894
  507.9 9.9 %collective-permute-start.37 = (bf16[192,512]{1,0:T(8,128)(2,1)}, bf16[192,512]{1,0:T(8,128)(2,1)S(1)}, u32[]{:S(2)}, u32[]{:S(2)}) collective-permute-start(bf16[192,512]{1,0:T(8,128)(2,1)} %get-tuple-element.208), channel_id=1, source_target_pairs={{0,6},{2,0},{4,2},{6,4},{1,7},{3,1},{5,3},{7,5},{8,14},{10,8},{12,... | collective-permute-start | bytes 589832 | tf_op jit(solution)/shard_map/ppermute | solution.py:879
  515.1 26.2 %collective-permute-start.40 = (bf16[192,512]{1,0:T(8,128)(2,1)}, bf16[192,512]{1,0:T(8,128)(2,1)S(1)}, u32[]{:S(2)}, u32[]{:S(2)}) collective-permute-start(bf16[192,512]{1,0:T(8,128)(2,1)} %copy-done.69), channel_id=1, source_target_pairs={{0,4},{2,6},{4,0},{6,2},{1,5},{3,7},{5,1},{7,3},{8,12},{10,14},{12... | collective-permute-start | bytes 589832 | tf_op jit(solution)/shard_map/ppermute | solution.py:879
  517.8 23.6 %collective-permute-start.41 = (bf16[192,512]{1,0:T(8,128)(2,1)}, bf16[192,512]{1,0:T(8,128)(2,1)}, u32[]{:S(2)}, u32[]{:S(2)}) collective-permute-start(bf16[192,512]{1,0:T(8,128)(2,1)} %copy-done.68), channel_id=1, source_target_pairs={{0,2},{2,4},{4,6},{6,0},{1,3},{3,5},{5,7},{7,1},{8,10},{10,12},{12... | collective-permute-start | bytes 589832 | tf_op jit(solution)/shard_map/ppermute | solution.py:879
  518.7 32.6 %collective-permute-start.38 = (bf16[512,512]{1,0:T(8,128)(2,1)}, bf16[512,512]{1,0:T(8,128)(2,1)}, u32[]{:S(2)}, u32[]{:S(2)}) collective-permute-start(bf16[512,512]{1,0:T(8,128)(2,1)} %get-tuple-element.209), channel_id=1, source_target_pairs={{0,2},{2,0},{4,6},{6,4},{1,3},{3,1},{5,7},{7,5},{8,10},{10,8},{12,... | collective-permute-start | bytes 1572872 | tf_op jit(solution)/shard_map/ppermute | solution.py:845
  521.7 30.9 %collective-permute-start.39 = (bf16[512,512]{1,0:T(8,128)(2,1)}, bf16[512,512]{1,0:T(8,128)(2,1)}, u32[]{:S(2)}, u32[]{:S(2)}) collective-permute-start(bf16[512,512]{1,0:T(8,128)(2,1)} %shard_map.439), channel_id=1, source_target_pairs={{0,4},{2,6},{4,0},{6,2},{1,5},{3,7},{5,1},{7,3},{8,12},{10,14},{12... | collective-permute-start | bytes 1572872 | tf_op jit(solution)/shard_map/ppermute | solution.py:845
  542.4 7.3 %collective-permute-start.48 = (bf16[64,512]{1,0:T(8,128)(2,1)S(1)}, bf16[64,512]{1,0:T(8,128)(2,1)S(1)}, u32[]{:S(2)}, u32[]{:S(2)}) collective-permute-start(bf16[64,512]{1,0:T(8,128)(2,1)S(1)} %get-tuple-element.224), channel_id=1, source_target_pairs={{0,8},{8,16},{16,24},{24,0},{1,9},{9,17},{17,25},{25,1},{2,10},{10... | collective-permute-start | bytes 196616 | tf_op jit(solution)/shard_map/ppermute | solution.py:894
  542.4 7.3 %collective-permute-start.49 = (bf16[64,512]{1,0:T(8,128)(2,1)S(1)}, bf16[64,512]{1,0:T(8,128)(2,1)S(1)}, u32[]{:S(2)}, u32[]{:S(2)}) collective-permute-start(bf16[64,512]{1,0:T(8,128)(2,1)S(1)} %get-tuple-element.225), channel_id=1, source_target_pairs={{0,16},{8,24},{16,0},{24,8},{1,17},{9,25},{17,1},{25,9},{2,18},{10... | collective-permute-start | bytes 196616 | tf_op jit(solution)/shard_map/ppermute | solution.py:894
  543.3 6.5 %collective-permute-start.50 = (bf16[64,512]{1,0:T(8,128)(2,1)S(1)}, bf16[64,512]{1,0:T(8,128)(2,1)S(1)}, u32[]{:S(2)}, u32[]{:S(2)}) collective-permute-start(bf16[64,512]{1,0:T(8,128)(2,1)S(1)} %get-tuple-element.226), channel_id=1, source_target_pairs={{0,24},{8,0},{16,8},{24,16},{1,25},{9,1},{17,9},{25,17},{2,26},{10... | collective-permute-start | bytes 196616 | tf_op jit(solution)/shard_map/ppermute | solution.py:894
  (77 other events, 506.9 us)
Sparse Core Ops, SparseCore 0:
  58.5 43.7 all-gather.4
  127.5 109.0 all-gather.6
  302.9 135.6 reduce-scatter.2
  441.9 59.3 reduce-scatter.4

commit v7 on v6

--- a/solution.py
+++ b/solution.py
@@ -1109,7 +1109,7 @@
 def update_out(state, pieces, rate, place):
     size = len(pieces)
     rows, width = pieces[0].shape
-    if rows * width <= 2**15:
+    if rows * width <= 2**17:
 
         def whole(q, *refs):
             for k in range(size):
@@ -1117,7 +1117,7 @@
                 update([ref.at[own, :] for ref in refs[size:]], refs[k][...].astype(F32), rate)
 
         w, m, v = call(
-            whole, [shape(state[0].shape, F32)] * 3, list(pieces) + list(state), [place]
+            whole, [shape(state[0].shape, F32)] * 3, list(pieces) + list(state), [place], vmem=32
         )
         return m, v, w
 
@@ -1169,7 +1169,7 @@
 def update_pair(state, grad, rate):
     rows, two, width = state[0].shape
     total = rows * two * width // 128
-    steps = 4 if total >= 4096 else 2
+    steps = 2
 
     def kernel(grad, *refs):
         update(refs, grad[...].astype(F32), rate)
@@ -1184,6 +1184,7 @@
         [spec] * 4,
         [spec] * 3,
         hbm=2**19,
+        vmem=32,
     )
     w, m, v = [
         n.reshape(rows, width // 128, two, 128).transpose(0, 2, 1, 3).reshape(rows, two, width)

time: 571 us -> 574 us (level)
    unnamed x164 -> x178, local copies, waits for them, and re-layouts: 31.3 us -> 36.9 us
  transfers between devices with their start and end apart: 59 -> 59, of which waited for: 26 -> 24; matrix products, arithmetic and copies ran while one was open for 2% -> 2% of each run, Pallas kernels for 25% -> 25%
where the time goes in v7:
time: 574 us; the launch traced here: 565 us
  waiting for transfers between devices  220 us (38%)
  Pallas kernels  166 us (29%)
  starting transfers between devices  114 us (20%)
  local copies, waits for them, and re-layouts  41.2 us (7%)
  between operations  15.3 us (3%)
  other arithmetic  8.46 us (1%)
    ppermute x29, waiting for transfers between devices, swap(): lax.ppermute(value, axis, [(i, i ^ step) for i in range(lax.axis_size(axi...  157 us
    pallas_call x40, Pallas kernels, call(): pl.pallas_call(run, grid_spec=pltpu.PrefetchScalarGridSpec(num_scalar_pre...  149 us
    ppermute x29, starting transfers between devices, swap(): lax.ppermute(value, axis, [(i, i ^ step) for i in range(lax.axis_size(axi...  67 us
    unnamed x178, local copies, waits for them, and re-layouts  36.9 us
    ppermute x15, starting transfers between devices, along_row(): lax.ppermute(p, 'row', [(i, (i + sign * k) % size) for i in range(size)])  33.3 us
    ppermute x15, waiting for transfers between devices, along_row(): lax.ppermute(p, 'row', [(i, (i + sign * k) % size) for i in range(size)])  28.4 us
    ppermute x1, waiting for transfers between devices, body(): lax.ppermute(keys_values, 'col', [(i, i + 1) for i in range(cols - 1)])  15 us
    ppermute x1, waiting for transfers between devices, body(): far = lax.ppermute(far_sent, 'col', [(i + 1, i) for i in range(cols - 1)])  11.7 us
  transfers between devices with their start and end apart: 59, of which 24 were waited for; matrix products, arithmetic and copies ran while one was open for 2% of the time, Pallas kernels for 25%

profile of v7, /device:TPU:0, one launch (start us, length us, event | category | flops | bytes accessed | tf_op | source)
XLA Modules:
  0.0 564.8 jit_solution(10158091761189550466)
XLA Ops:
  7.2 4.1 collective-permute-start.1
  11.3 2.4 shard_map.407
  13.8 2.3 shard_map.408
  20.6 3.5 collective-permute-done.6.refs_9_
  25.9 3.5 collective-permute-start.5
  34.0 12.0 %collective-permute-start.10 = (bf16[64,512]{1,0:T(8,128)(2,1)S(1)}, bf16[64,512]{1,0:T(8,128)(2,1)S(1)}, u32[]{:S(2)}, u32[]{:S(2)}) collective-permute-start(bf16[64,512]{1,0:T(8,128)(2,1)S(1)} %get-tuple-element.143), channel_id=1, source_target_pairs={{0,4},{2,6},{4,0},{6,2},{1,5},{3,7},{5,1},{7,3},{8,12},{10,14},{12... | collective-permute-start | bytes 196616 | tf_op jit(solution)/shard_map/ppermute | solution.py:879
  46.0 3.7 collective-permute-start.11
  49.7 3.1 shard_map.410
  55.4 2.1 shard_map.411.refs_5_
  59.4 2.9 collective-permute-start.14
  64.4 46.5 %collective-permute-done.refs_2_ = bf16[512,512]{1,0:T(8,128)(2,1)S(1)} collective-permute-done((bf16[512,512]{1,0:T(8,128)(2,1)S(1)}, bf16[512,512]{1,0:T(8,128)(2,1)S(1)}, u32[]{:S(2)}, u32[]{:S(2)}) %collective-permute-start) | collective-permute-done | bytes 524320 | tf_op jit(solution)/shard_map/ppermute | solution.py:845
  111.0 11.1 %collective-permute-done.2.refs_4_ = bf16[512,512]{1,0:T(8,128)(2,1)S(1)} collective-permute-done((bf16[512,512]{1,0:T(8,128)(2,1)}, bf16[512,512]{1,0:T(8,128)(2,1)S(1)}, u32[]{:S(2)}, u32[]{:S(2)}) %collective-permute-start.2) | collective-permute-done | bytes 524320 | tf_op jit(solution)/shard_map/ppermute | solution.py:845
  122.1 2.2 shard_map.412.refs_5_.refs_0_.refs_4_.refs_3_
  133.7 7.9 %shard_map.415 = (bf16[512,2048]{1,0:T(8,128)(2,1)S(1)}, f32[512,1]{1,0:T(8,128)S(1)}, f32[512,512]{1,0:T(8,128)S(1)}, f32[512,256]{1,0:T(8,128)S(1)}, bf16[512,...) custom-call(bf16[512,2048]{1,0:T(8,128)(2,1)S(1)} %copy-done.1, f32[1,2048]{1,0:T(1,128)S(1)} %bitcast.102, ...), custom_call_target="tpu_custom_call" | custom-call | tf_op jit(solution)/shard_map/pallas_call | solution.py:215
  146.2 3.6 collective-permute-start.15
  149.9 6.5 %collective-permute-done.17.refs_4_.refs_3_ = bf16[512,512]{1,0:T(8,128)(2,1)} collective-permute-done((bf16[512,512]{1,0:T(8,128)(2,1)}, bf16[512,512]{1,0:T(8,128)(2,1)}, u32[]{:S(2)}, u32[]{:S(2)}) %collective-permute-start.17) | collective-permute-done | bytes 524320 | tf_op jit(solution)/shard_map/ppermute | solution.py:845
  157.3 15.0 %collective-permute-done.15.refs_7_.refs_8_ = bf16[512,512]{1,0:T(8,128)(2,1)S(1)} collective-permute-done((bf16[512,512]{1,0:T(8,128)(2,1)S(1)}, bf16[512,512]{1,0:T(8,128)(2,1)S(1)}, u32[]{:S(2)}, u32[]{:S(2)}) %collective-permute-start.15) | collective-permute-done | bytes 524320 | tf_op jit(solution)/shard_map/ppermute | solution.py:1292
  174.3 7.3 %shard_map.416 = (bf16[512,512]{1,0:T(8,128)(2,1)S(1)}, f32[4,512,1]{2,1,0:T(8,128)S(1)}) custom-call(s32[1]{0:T(128)} %bitcast.1.refs_0_, s32[512,1]{1,0:T(8,128)S(1)} %copy-done.18, s32[1,512]{1,0:T(1,128)S(1)} %bitcast.105, s32[1,512]{1,0:T(1,128)S(1)} %bitcast.107, bf16[512,512]{1,0:T(8,128)(2,1)S(1)} %copy-done.25, ...), custom_call_target="tpu_custom_call" | custom-call | tf_op jit(solution)/shard_map/pallas_call | solution.py:93
  181.6 4.4 shard_map.417
  186.1 11.8 %collective-permute-done.19.refs_1_ = bf16[128,2048]{1,0:T(8,128)(2,1)S(1)} collective-permute-done((bf16[128,2048]{1,0:T(8,128)(2,1)S(1)}, bf16[128,2048]{1,0:T(8,128)(2,1)S(1)}, u32[]{:S(2)}, u32[]{:S(2)}) %collective-permute-start.19) | collective-permute-done | bytes 524320 | tf_op jit(solution)/shard_map/ppermute | solution.py:845
  198.1 3.0 collective-permute-start.21
  201.1 18.8 %collective-permute-done.20.refs_2_ = bf16[128,2048]{1,0:T(8,128)(2,1)S(1)} collective-permute-done((bf16[128,2048]{1,0:T(8,128)(2,1)S(1)}, bf16[128,2048]{1,0:T(8,128)(2,1)S(1)}, u32[]{:S(2)}, u32[]{:S(2)}) %collective-permute-start.20) | collective-permute-done | bytes 524320 | tf_op jit(solution)/shard_map/ppermute | solution.py:845
  223.4 16.5 %collective-permute-start.22 = (bf16[128,2048]{1,0:T(8,128)(2,1)}, bf16[128,2048]{1,0:T(8,128)(2,1)}, u32[]{:S(2)}, u32[]{:S(2)}) collective-permute-start(bf16[128,2048]{1,0:T(8,128)(2,1)} %get-tuple-element.162.refs_0_), channel_id=1, source_target_pairs={{0,2},{2,0},{4,6},{6,4},{1,3},{3,1},{5,7},{7,5},{8,10},{10,8},{12,... | collective-permute-start | bytes 1572872 | tf_op jit(solution)/shard_map/ppermute | solution.py:845
  240.3 9.7 %collective-permute-start.24 = (bf16[128,2048]{1,0:T(8,128)(2,1)}, bf16[128,2048]{1,0:T(8,128)(2,1)}, u32[]{:S(2)}, u32[]{:S(2)}) collective-permute-start(bf16[128,2048]{1,0:T(8,128)(2,1)} %collective-permute-done.23.refs_2_), channel_id=1, source_target_pairs={{0,2},{2,0},{4,6},{6,4},{1,3},{3,1},{5,7},{7,5},{8,10},{10,8},{12,... | collective-permute-start | bytes 1572872 | tf_op jit(solution)/shard_map/ppermute | solution.py:845
  250.1 2.6 shard_map.420.refs_0_.refs_6_
  255.6 6.8 %shard_map.421.refs_5_ = f32[512,1536]{1,0:T(8,128)S(1)} custom-call(bf16[512,2048]{1,0:T(8,128)(2,1)S(1)} %copy-done.3, bf16[2,4,2304,512]{3,2,1,0:T(8,128)(2,1)} %bitcast.110, bf16[128,2048]{1,0:T(8,128)(2,1)} %collective-permute-done.23.refs_2_), custom_call_target="tpu_custom_call" | custom-call | tf_op jit(solution)/shard_map/pallas_call | solution.py:215
  262.5 11.6 %shard_map.422 = (bf16[512,1536]{1,0:T(8,128)(2,1)S(1)}, bf16[512,3072]{1,0:T(8,128)(2,1)S(1)}) custom-call(bf16[128,2048]{1,0:T(8,128)(2,1)} %get-tuple-element.162.refs_0_, bf16[128,2048]{1,0:T(8,128)(2,1)} %collective-permute-done.22.refs_1_, bf16[128,2048]{1,0:T(8,128)(2,1)} %collective-permute-done.23.refs_2_, ...), custom_call_target="tpu_custom_call" | custom-call | tf_op jit(solution)/shard_map/pallas_call | solution.py:215
  274.1 10.0 %shard_map.423 = (f32[128,2048]{1,0:T(8,128)S(1)}, bf16[128,2048]{1,0:T(8,128)(2,1)S(1)}, bf16[128,2048]{1,0:T(8,128)(2,1)S(1)}, bf16[128,2048]{1,0:T(8,128)(2,1)S(1)}) custom-call(bf16[512,3072]{1,0:T(8,128)(2,1)S(1)} %get-tuple-element.165.refs_0_.refs_4_, bf16[2,4,2304,512]{3,2,1,0:T(8,128)(2,1)} %bitcast.112), custom_call_target="tpu_custom_call" | custom-call | tf_op jit(solution)/shard_map/pallas_call | solution.py:215
  284.9 17.2 %shard_map.424 = bf16[2,4,2304,512]{3,2,1,0:T(8,128)(2,1)} custom-call(bf16[128,2048]{1,0:T(8,128)(2,1)} %get-tuple-element.162.refs_0_, bf16[128,2048]{1,0:T(8,128)(2,1)} %collective-permute-done.22.refs_1_, bf16[128,2048]{1,0:T(8,128)(2,1)} %collective-permute-done.23.refs_2_, bf16[128,2048]{1,0:T(8,128)(2,1)} %collective-permute-done.24.refs_3_, ...), custom_call_target="tpu_custom_call" | custom-call | tf_op jit(solution)/shard_map/pallas_call | solution.py:215
  307.0 2.2 collective-permute-start.27
  309.2 12.7 %collective-permute-done.26.refs_1_ = bf16[128,2048]{1,0:T(8,128)(2,1)S(1)} collective-permute-done((bf16[128,2048]{1,0:T(8,128)(2,1)}, bf16[128,2048]{1,0:T(8,128)(2,1)S(1)}, u32[]{:S(2)}, u32[]{:S(2)}) %collective-permute-start.26) | collective-permute-done | bytes 524320 | tf_op jit(solution)/shard_map/ppermute | solution.py:845
  321.9 7.1 %collective-permute-done.27.refs_2_ = bf16[128,2048]{1,0:T(8,128)(2,1)S(1)} collective-permute-done((bf16[128,2048]{1,0:T(8,128)(2,1)S(1)}, bf16[128,2048]{1,0:T(8,128)(2,1)S(1)}, u32[]{:S(2)}, u32[]{:S(2)}) %collective-permute-start.27) | collective-permute-done | bytes 524320 | tf_op jit(solution)/shard_map/ppermute | solution.py:845
  329.8 3.6 shard_map.426
  333.6 7.6 %collective-permute-start.28 = (bf16[128,2048]{1,0:T(8,128)(2,1)S(1)}, bf16[128,2048]{1,0:T(8,128)(2,1)S(1)}, u32[]{:S(2)}, u32[]{:S(2)}) collective-permute-start(bf16[128,2048]{1,0:T(8,128)(2,1)S(1)} %get-tuple-element.174.refs_3_.refs_1_), channel_id=1, source_target_pairs={{0,2},{2,0},{4,6},{6,4},{1,3},{3,1},{5,7},{7,5},{8,10},{10,8},{12,... | collective-permute-start | bytes 1572872 | tf_op jit(solution)/shard_map/ppermute | solution.py:845
  341.2 13.8 %collective-permute-done.29.refs_3_ = bf16[128,2048]{1,0:T(8,128)(2,1)S(1)} collective-permute-done((bf16[128,2048]{1,0:T(8,128)(2,1)S(1)}, bf16[128,2048]{1,0:T(8,128)(2,1)S(1)}, u32[]{:S(2)}, u32[]{:S(2)}) %collective-permute-start.29) | collective-permute-done | bytes 524320 | tf_op jit(solution)/shard_map/ppermute | solution.py:845
  355.0 6.0 %shard_map.427.refs_6_.refs_1_ = bf16[512,2048]{1,0:T(8,128)(2,1)S(1)} custom-call(bf16[512,1536]{1,0:T(8,128)(2,1)S(1)} %copy-done.10, f32[128,2048]{1,0:T(8,128)S(1)} %copy-done.15, bf16[2,4,2304,512]{3,2,1,0:T(8,128)(2,1)} %bitcast.113, bf16[128,2048]{1,0:T(8,128)(2,1)S(1)} %get-tuple-element.174.refs_3_.refs_1_), custom_call_target="tpu_custom_call" | custom-call | tf_op jit(solution)/shard_map/pallas_call | solution.py:215
  362.4 3.9 collective-permute-done.30.refs_4_
  366.3 4.2 shard_map.428
  371.8 2.8 shard_map.429
  374.8 9.3 %shard_map.432 = (f32[512,512]{1,0:T(8,128)S(1)}, f32[512,256]{1,0:T(8,128)S(1)}, f32[512,256]{1,0:T(8,128)S(1)}, bf16[512,512]{1,0:T(8,128)(2,1)S(1)}) custom-call(s32[1]{0:T(128)} %bitcast.1.refs_0_, s32[512,1]{1,0:T(8,128)S(1)} %copy-done.19, s32[1,512]{1,0:T(1,128)S(1)} %bitcast.106, s32[1,512]{1,0:T(1,128)S(1)} %bitcast.108, ...), custom_call_target="tpu_custom_call" | custom-call | tf_op jit(solution)/shard_map/pallas_call | solution.py:163
  384.1 2.4 collective-permute-done.31.refs_1_
  386.8 10.4 %collective-permute-start.33 = (bf16[512,512]{1,0:T(8,128)(2,1)S(1)}, bf16[512,512]{1,0:T(8,128)(2,1)S(1)}, u32[]{:S(2)}, u32[]{:S(2)}) collective-permute-start(bf16[512,512]{1,0:T(8,128)(2,1)S(1)} %shard_map.430), channel_id=1, source_target_pairs={{0,4},{2,6},{4,0},{6,2},{1,5},{3,7},{5,1},{7,3},{8,12},{10,14},{12... | collective-permute-start | bytes 1572872 | tf_op jit(solution)/shard_map/ppermute | solution.py:845
  398.4 7.5 %collective-permute-done.32.refs_1_ = bf16[512,512]{1,0:T(8,128)(2,1)S(1)} collective-permute-done((bf16[512,512]{1,0:T(8,128)(2,1)S(1)}, bf16[512,512]{1,0:T(8,128)(2,1)S(1)}, u32[]{:S(2)}, u32[]{:S(2)}) %collective-permute-start.32) | collective-permute-done | bytes 524320 | tf_op jit(solution)/shard_map/ppermute | solution.py:845
  406.0 3.5 collective-permute-done.33.refs_2_
  410.7 11.7 %collective-permute-done.34.refs_5_ = bf16[512,512]{1,0:T(8,128)(2,1)S(1)} collective-permute-done((bf16[512,512]{1,0:T(8,128)(2,1)S(1)}, bf16[512,512]{1,0:T(8,128)(2,1)S(1)}, u32[]{:S(2)}, u32[]{:S(2)}) %collective-permute-start.34) | collective-permute-done | bytes 524320 | tf_op jit(solution)/shard_map/ppermute | solution.py:1330
  422.5 2.7 shard_map.433
  425.2 9.7 %shard_map.434 = bf16[2,4,768,512]{3,2,1,0:T(8,128)(2,1)} custom-call(bf16[512,2048]{1,0:T(8,128)(2,1)S(1)} %copy-done.32, bf16[512,1024]{1,0:T(8,128)(2,1)S(1)} %get-tuple-element.190.refs_1_, bf16[512,512]{1,0:T(8,128)(2,1)S(1)} %copy-done.23, bf16[512,2048]{1,0:T(8,128)(2,1)S(1)} %copy-done.8), custom_call_target="tpu_custom_call" | custom-call | tf_op jit(solution)/shard_map/pallas_call | solution.py:215
  435.9 3.0 reduce-scatter.3.cloned.1.call-done.refs_1_
  439.0 3.2 shard_map.435
  444.5 6.2 %shard_map.436 = (bf16[512,2048]{1,0:T(8,128)(2,1)S(1)}, f32[512,1]{1,0:T(8,128)S(1)}, f32[1,2048]{1,0:T(1,128)S(1)}) custom-call(s32[1]{0:T(128)} %bitcast.refs_0_, bf16[512,1024]{1,0:T(8,128)(2,1)S(1)} %copy-done.13, bf16[2,4,768,512]{3,2,1,0:T(8,128)(2,1)} %bitcast.117, bf16[512,2048]{1,0:T(8,128)(2,1)S(1)} %copy-done.1, f32[512,1]{1,0:T(8,128)S(1)} %copy-done.38, ...), custom_call_target="tpu_custom_call" | custom-call | tf_op jit(solution)/shard_map/pallas_call | solution.py:215
  452.7 3.8 shard_map.437
  461.9 2.1 collective-permute-done.43
  464.2 4.0 collective-permute-done.44
  468.2 27.6 %collective-permute-done.45.refs_3_.refs_10_ = bf16[576,512]{1,0:T(8,128)(2,1)} collective-permute-done((bf16[576,512]{1,0:T(8,128)(2,1)}, bf16[576,512]{1,0:T(8,128)(2,1)}, u32[]{:S(2)}, u32[]{:S(2)}) %collective-permute-start.45) | collective-permute-done | bytes 589856 | tf_op jit(solution)/shard_map/ppermute | solution.py:879
  495.8 3.8 collective-permute-done.46
  499.7 2.1 shard_map.447
  505.5 1.9 shard_map.438
  508.8 4.6 collective-permute-start.37
  518.7 2.0 shard_map.439
  520.8 2.8 collective-permute-start.38
  523.6 2.0 collective-permute-start.39
  528.6 4.7 shard_map.448
  536.3 7.9 %shard_map.446 = (f32[6144,128]{1,0:T(8,128)}, f32[6144,128]{1,0:T(8,128)}, f32[6144,128]{1,0:T(8,128)}) custom-call(bf16[6144,128]{1,0:T(8,128)(2,1)} %reshape.296.refs_0_, f32[6144,128]{1,0:T(8,128)} %bitcast.99, f32[6144,128]{1,0:T(8,128)} %bitcast.120, f32[6144,128]{1,0:T(8,128)} %bitcast.121), custom_call_target="tpu_custom_call" | custom-call | tf_op jit(solution)/shard_map/pallas_call | solution.py:215
  551.2 2.5 shard_map.442
  (318 shorter events, 91.4 us)
Async XLA Ops:
  7.2 126.5 %all-gather.5.cloned.1.call-start = ((), (), s32[]{:S(2)}) async-start(), calls=%async_computation.4 | async-start | bytes 7077888 | tf_op jit(solution)/shard_map/all_gather | solution.py:898
  7.2 48.1 %collective-permute-start.1 = (bf16[512,512]{1,0:T(8,128)(2,1)}, bf16[512,512]{1,0:T(8,128)(2,1)}, u32[]{:S(2)}, u32[]{:S(2)}) collective-permute-start(bf16[512,512]{1,0:T(8,128)(2,1)} %refs_1_.7), channel_id=1, source_target_pairs={{0,4},{2,6},{4,0},{6,2},{1,5},{3,7},{5,1},{7,3},{8,12},{10,14},{12... | collective-permute-start | bytes 1572872 | tf_op jit(solution)/shard_map/ppermute | solution.py:845
  11.3 38.4 %copy-start.6 = (f32[128,2,3072]{2,1,0:T(2,128)S(1)}, f32[128,2,3072]{2,1,0:T(2,128)}, u32[]{:S(2)}) copy-start(f32[128,2,3072]{2,1,0:T(2,128)} %refs_1_.6) | copy-start | bytes 9437188
  16.1 8.1 %collective-permute-start.6 = (bf16[256,512]{1,0:T(8,128)(2,1)S(1)}, bf16[256,512]{1,0:T(8,128)(2,1)S(1)}, u32[]{:S(2)}, u32[]{:S(2)}) collective-permute-start(bf16[256,512]{1,0:T(8,128)(2,1)S(1)} %get-tuple-element.138), channel_id=1, source_target_pairs={{0,8},{8,16},{16,24},{24,0},{1,9},{9,17},{17,25},{25,1},{2,10},{10... | collective-permute-start | bytes 786440 | tf_op jit(solution)/shard_map/ppermute | solution.py:894
  16.1 9.2 %collective-permute-start.7 = (bf16[256,512]{1,0:T(8,128)(2,1)S(1)}, bf16[256,512]{1,0:T(8,128)(2,1)S(1)}, u32[]{:S(2)}, u32[]{:S(2)}) collective-permute-start(bf16[256,512]{1,0:T(8,128)(2,1)S(1)} %get-tuple-element.139), channel_id=1, source_target_pairs={{0,16},{8,24},{16,0},{24,8},{1,17},{9,25},{17,1},{25,9},{2,18},{10... | collective-permute-start | bytes 786440 | tf_op jit(solution)/shard_map/ppermute | solution.py:894
  17.6 11.9 %collective-permute-start.8 = (bf16[256,512]{1,0:T(8,128)(2,1)}, bf16[256,512]{1,0:T(8,128)(2,1)}, u32[]{:S(2)}, u32[]{:S(2)}) collective-permute-start(bf16[256,512]{1,0:T(8,128)(2,1)} %get-tuple-element.140), channel_id=1, source_target_pairs={{0,24},{8,0},{16,8},{24,16},{1,25},{9,1},{17,9},{25,17},{2,26},{10... | collective-permute-start | bytes 786440 | tf_op jit(solution)/shard_map/ppermute | solution.py:894
  19.0 15.0 %collective-permute-start.3 = (bf16[128,512]{1,0:T(8,128)(2,1)}, bf16[128,512]{1,0:T(8,128)(2,1)}, u32[]{:S(2)}, u32[]{:S(2)}) collective-permute-start(bf16[128,512]{1,0:T(8,128)(2,1)} %get-tuple-element.134), channel_id=1, source_target_pairs={{0,2},{2,4},{4,6},{6,0},{1,3},{3,5},{5,7},{7,1},{8,10},{10,12},{12... | collective-permute-start | bytes 393224 | tf_op jit(solution)/shard_map/ppermute | solution.py:879
  24.8 21.2 %collective-permute-start.4 = (bf16[128,512]{1,0:T(8,128)(2,1)}, bf16[128,512]{1,0:T(8,128)(2,1)}, u32[]{:S(2)}, u32[]{:S(2)}) collective-permute-start(bf16[128,512]{1,0:T(8,128)(2,1)} %get-tuple-element.135), channel_id=1, source_target_pairs={{0,4},{2,6},{4,0},{6,2},{1,5},{3,7},{5,1},{7,3},{8,12},{10,14},{12... | collective-permute-start | bytes 393224 | tf_op jit(solution)/shard_map/ppermute | solution.py:879
  25.9 29.4 %collective-permute-start.5 = (bf16[128,512]{1,0:T(8,128)(2,1)}, bf16[128,512]{1,0:T(8,128)(2,1)}, u32[]{:S(2)}, u32[]{:S(2)}) collective-permute-start(bf16[128,512]{1,0:T(8,128)(2,1)} %get-tuple-element.136), channel_id=1, source_target_pairs={{0,6},{2,0},{4,2},{6,4},{1,7},{3,1},{5,3},{7,5},{8,14},{10,8},{12,... | collective-permute-start | bytes 393224 | tf_op jit(solution)/shard_map/ppermute | solution.py:879
  32.5 22.9 %collective-permute-start.9 = (bf16[64,512]{1,0:T(8,128)(2,1)S(1)}, bf16[64,512]{1,0:T(8,128)(2,1)S(1)}, u32[]{:S(2)}, u32[]{:S(2)}) collective-permute-start(bf16[64,512]{1,0:T(8,128)(2,1)S(1)} %get-tuple-element.142), channel_id=1, source_target_pairs={{0,2},{2,4},{4,6},{6,0},{1,3},{3,5},{5,7},{7,1},{8,10},{10,12},{12... | collective-permute-start | bytes 196616 | tf_op jit(solution)/shard_map/ppermute | solution.py:879
  34.0 21.3 %collective-permute-start.10 = (bf16[64,512]{1,0:T(8,128)(2,1)S(1)}, bf16[64,512]{1,0:T(8,128)(2,1)S(1)}, u32[]{:S(2)}, u32[]{:S(2)}) collective-permute-start(bf16[64,512]{1,0:T(8,128)(2,1)S(1)} %get-tuple-element.143), channel_id=1, source_target_pairs={{0,4},{2,6},{4,0},{6,2},{1,5},{3,7},{5,1},{7,3},{8,12},{10,14},{12... | collective-permute-start | bytes 196616 | tf_op jit(solution)/shard_map/ppermute | solution.py:879
  46.0 9.4 %collective-permute-start.11 = (bf16[64,512]{1,0:T(8,128)(2,1)S(1)}, bf16[64,512]{1,0:T(8,128)(2,1)S(1)}, u32[]{:S(2)}, u32[]{:S(2)}) collective-permute-start(bf16[64,512]{1,0:T(8,128)(2,1)S(1)} %get-tuple-element.144), channel_id=1, source_target_pairs={{0,6},{2,0},{4,2},{6,4},{1,7},{3,1},{5,3},{7,5},{8,14},{10,8},{12,... | collective-permute-start | bytes 196616 | tf_op jit(solution)/shard_map/ppermute | solution.py:879
  58.4 195.7 %all-gather.7.cloned.1.call-start = ((), (), s32[]{:S(2)}) async-start(), calls=%async_computation.5 | async-start | bytes 21233664 | tf_op jit(solution)/shard_map/all_gather | solution.py:898
  58.4 67.2 %collective-permute-start.12 = (bf16[576,512]{1,0:T(8,128)(2,1)S(1)}, bf16[576,512]{1,0:T(8,128)(2,1)S(1)}, u32[]{:S(2)}, u32[]{:S(2)}) collective-permute-start(bf16[576,512]{1,0:T(8,128)(2,1)S(1)} %copy-done.73), channel_id=1, source_target_pairs={{0,2},{2,4},{4,6},{6,0},{1,3},{3,5},{5,7},{7,1},{8,10},{10,12},{12... | collective-permute-start | bytes 1769480 | tf_op jit(solution)/shard_map/ppermute | solution.py:879
  58.5 67.1 %collective-permute-start.13 = (bf16[576,512]{1,0:T(8,128)(2,1)S(1)}, bf16[576,512]{1,0:T(8,128)(2,1)S(1)}, u32[]{:S(2)}, u32[]{:S(2)}) collective-permute-start(bf16[576,512]{1,0:T(8,128)(2,1)S(1)} %copy-done.71), channel_id=1, source_target_pairs={{0,4},{2,6},{4,0},{6,2},{1,5},{3,7},{5,1},{7,3},{8,12},{10,14},{12... | collective-permute-start | bytes 1769480 | tf_op jit(solution)/shard_map/ppermute | solution.py:879
  59.4 66.2 %copy-start.21 = (bf16[576,512]{1,0:T(8,128)(2,1)S(1)}, bf16[576,512]{1,0:T(8,128)(2,1)}, u32[]{:S(2)}) copy-start(bf16[576,512]{1,0:T(8,128)(2,1)} %copy-done.20) | copy-start | bytes 1769476
  59.4 66.2 %collective-permute-start.14 = (bf16[576,512]{1,0:T(8,128)(2,1)S(1)}, bf16[576,512]{1,0:T(8,128)(2,1)S(1)}, u32[]{:S(2)}, u32[]{:S(2)}) collective-permute-start(bf16[576,512]{1,0:T(8,128)(2,1)S(1)} %copy-done.69), channel_id=1, source_target_pairs={{0,6},{2,0},{4,2},{6,4},{1,7},{3,1},{5,3},{7,5},{8,14},{10,8},{12,... | collective-permute-start | bytes 1769480 | tf_op jit(solution)/shard_map/ppermute | solution.py:879
  62.4 48.6 %collective-permute-start = (bf16[512,512]{1,0:T(8,128)(2,1)S(1)}, bf16[512,512]{1,0:T(8,128)(2,1)S(1)}, u32[]{:S(2)}, u32[]{:S(2)}) collective-permute-start(bf16[512,512]{1,0:T(8,128)(2,1)S(1)} %copy-done.29), channel_id=1, source_target_pairs={{0,2},{2,0},{4,6},{6,4},{1,3},{3,1},{5,7},{7,5},{8,10},{10,8},{12,... | collective-permute-start | bytes 1572872 | tf_op jit(solution)/shard_map/ppermute | solution.py:845
  63.0 59.1 %collective-permute-start.2 = (bf16[512,512]{1,0:T(8,128)(2,1)}, bf16[512,512]{1,0:T(8,128)(2,1)S(1)}, u32[]{:S(2)}, u32[]{:S(2)}) collective-permute-start(bf16[512,512]{1,0:T(8,128)(2,1)} %collective-permute-done.1.refs_10_.refs_3_), channel_id=1, source_target_pairs={{0,2},{2,0},{4,6},{6,4},{1,3},{3,1},{5,7},{7,5},{8,10},{10,8},{12,... | collective-permute-start | bytes 1572872 | tf_op jit(solution)/shard_map/ppermute | solution.py:845
  127.3 311.6 %reduce-scatter.3.cloned.1.call-start = ((), (), s32[]{:S(2)}) async-start(), calls=%async_computation.2 | async-start | bytes 21233664 | tf_op jit(solution)/shard_map/reduce_scatter | solution.py:904
  130.9 25.5 %collective-permute-start.17 = (bf16[512,512]{1,0:T(8,128)(2,1)}, bf16[512,512]{1,0:T(8,128)(2,1)}, u32[]{:S(2)}, u32[]{:S(2)}) collective-permute-start(bf16[512,512]{1,0:T(8,128)(2,1)} %shard_map.414.refs_6_.refs_1_), channel_id=1, source_target_pairs={{0,4},{2,6},{4,0},{6,2},{1,5},{3,7},{5,1},{7,3},{8,12},{10,14},{12... | collective-permute-start | bytes 1572872 | tf_op jit(solution)/shard_map/ppermute | solution.py:845
  146.2 26.1 %collective-permute-start.15 = (bf16[512,512]{1,0:T(8,128)(2,1)S(1)}, bf16[512,512]{1,0:T(8,128)(2,1)S(1)}, u32[]{:S(2)}, u32[]{:S(2)}) collective-permute-start(bf16[512,512]{1,0:T(8,128)(2,1)S(1)} %get-tuple-element.154.refs_5_.refs_6_), channel_id=1, source_target_pairs={{0,1},{2,3},{4,5},{6,7},{8,9},{10,11},{12,13},{14,15},{16,17},{18,... | collective-permute-start | bytes 1572872 | tf_op jit(solution)/shard_map/ppermute | solution.py:1292
  149.9 31.7 %collective-permute-start.16 = (bf16[512,512]{1,0:T(8,128)(2,1)}, bf16[512,512]{1,0:T(8,128)(2,1)}, u32[]{:S(2)}, u32[]{:S(2)}) collective-permute-start(bf16[512,512]{1,0:T(8,128)(2,1)} %shard_map.414.refs_6_.refs_1_), channel_id=1, source_target_pairs={{0,2},{2,0},{4,6},{6,4},{1,3},{3,1},{5,7},{7,5},{8,10},{10,8},{12,... | collective-permute-start | bytes 1572872 | tf_op jit(solution)/shard_map/ppermute | solution.py:845
  156.4 25.2 %collective-permute-start.18 = (bf16[512,512]{1,0:T(8,128)(2,1)}, bf16[512,512]{1,0:T(8,128)(2,1)}, u32[]{:S(2)}, u32[]{:S(2)}) collective-permute-start(bf16[512,512]{1,0:T(8,128)(2,1)} %collective-permute-done.17.refs_4_.refs_3_), channel_id=1, source_target_pairs={{0,2},{2,0},{4,6},{6,4},{1,3},{3,1},{5,7},{7,5},{8,10},{10,8},{12,... | collective-permute-start | bytes 1572872 | tf_op jit(solution)/shard_map/ppermute | solution.py:845
  186.0 11.9 %collective-permute-start.19 = (bf16[128,2048]{1,0:T(8,128)(2,1)S(1)}, bf16[128,2048]{1,0:T(8,128)(2,1)S(1)}, u32[]{:S(2)}, u32[]{:S(2)}) collective-permute-start(bf16[128,2048]{1,0:T(8,128)(2,1)S(1)} %get-tuple-element.159), channel_id=1, source_target_pairs={{0,2},{2,0},{4,6},{6,4},{1,3},{3,1},{5,7},{7,5},{8,10},{10,8},{12,... | collective-permute-start | bytes 1572872 | tf_op jit(solution)/shard_map/ppermute | solution.py:845
  198.0 21.9 %collective-permute-start.20 = (bf16[128,2048]{1,0:T(8,128)(2,1)S(1)}, bf16[128,2048]{1,0:T(8,128)(2,1)S(1)}, u32[]{:S(2)}, u32[]{:S(2)}) collective-permute-start(bf16[128,2048]{1,0:T(8,128)(2,1)S(1)} %get-tuple-element.160.refs_5_), channel_id=1, source_target_pairs={{0,2},{2,0},{4,6},{6,4},{1,3},{3,1},{5,7},{7,5},{8,10},{10,8},{12,... | collective-permute-start | bytes 1572872 | tf_op jit(solution)/shard_map/ppermute | solution.py:845
  198.1 21.8 %collective-permute-start.21 = (bf16[128,2048]{1,0:T(8,128)(2,1)S(1)}, bf16[128,2048]{1,0:T(8,128)(2,1)S(1)}, u32[]{:S(2)}, u32[]{:S(2)}) collective-permute-start(bf16[128,2048]{1,0:T(8,128)(2,1)S(1)} %shard_map.418), channel_id=1, source_target_pairs={{0,4},{2,6},{4,0},{6,2},{1,5},{3,7},{5,1},{7,3},{8,12},{10,14},{12... | collective-permute-start | bytes 1572872 | tf_op jit(solution)/shard_map/ppermute | solution.py:845
  222.1 18.2 %collective-permute-start.23 = (bf16[128,2048]{1,0:T(8,128)(2,1)}, bf16[128,2048]{1,0:T(8,128)(2,1)}, u32[]{:S(2)}, u32[]{:S(2)}) collective-permute-start(bf16[128,2048]{1,0:T(8,128)(2,1)} %get-tuple-element.162.refs_0_), channel_id=1, source_target_pairs={{0,4},{2,6},{4,0},{6,2},{1,5},{3,7},{5,1},{7,3},{8,12},{10,14},{12... | collective-permute-start | bytes 1572872 | tf_op jit(solution)/shard_map/ppermute | solution.py:845
  223.4 39.1 %collective-permute-start.22 = (bf16[128,2048]{1,0:T(8,128)(2,1)}, bf16[128,2048]{1,0:T(8,128)(2,1)}, u32[]{:S(2)}, u32[]{:S(2)}) collective-permute-start(bf16[128,2048]{1,0:T(8,128)(2,1)} %get-tuple-element.162.refs_0_), channel_id=1, source_target_pairs={{0,2},{2,0},{4,6},{6,4},{1,3},{3,1},{5,7},{7,5},{8,10},{10,8},{12,... | collective-permute-start | bytes 1572872 | tf_op jit(solution)/shard_map/ppermute | solution.py:845
  240.3 22.1 %collective-permute-start.24 = (bf16[128,2048]{1,0:T(8,128)(2,1)}, bf16[128,2048]{1,0:T(8,128)(2,1)}, u32[]{:S(2)}, u32[]{:S(2)}) collective-permute-start(bf16[128,2048]{1,0:T(8,128)(2,1)} %collective-permute-done.23.refs_2_), channel_id=1, source_target_pairs={{0,2},{2,0},{4,6},{6,4},{1,3},{3,1},{5,7},{7,5},{8,10},{10,8},{12,... | collective-permute-start | bytes 1572872 | tf_op jit(solution)/shard_map/ppermute | solution.py:845
  284.9 17.2 %collective-permute-start.25 = (bf16[128,2048]{1,0:T(8,128)(2,1)S(1)}, bf16[128,2048]{1,0:T(8,128)(2,1)S(1)}, u32[]{:S(2)}, u32[]{:S(2)}) collective-permute-start(bf16[128,2048]{1,0:T(8,128)(2,1)S(1)} %get-tuple-element.169.refs_7_), channel_id=1, source_target_pairs={{0,2},{2,0},{4,6},{6,4},{1,3},{3,1},{5,7},{7,5},{8,10},{10,8},{12,... | collective-permute-start | bytes 1572872 | tf_op jit(solution)/shard_map/ppermute | solution.py:845
  303.0 202.6 %reduce-scatter.5.cloned.1.call-start = ((), (), s32[]{:S(2)}) async-start(), calls=%async_computation.3 | async-start | bytes 7077888 | tf_op jit(solution)/shard_map/reduce_scatter | solution.py:904
  305.4 16.5 %collective-permute-start.26 = (bf16[128,2048]{1,0:T(8,128)(2,1)}, bf16[128,2048]{1,0:T(8,128)(2,1)S(1)}, u32[]{:S(2)}, u32[]{:S(2)}) collective-permute-start(bf16[128,2048]{1,0:T(8,128)(2,1)} %copy-done.75), channel_id=1, source_target_pairs={{0,2},{2,0},{4,6},{6,4},{1,3},{3,1},{5,7},{7,5},{8,10},{10,8},{12,... | collective-permute-start | bytes 1572872 | tf_op jit(solution)/shard_map/ppermute | solution.py:845
  307.0 22.1 %collective-permute-start.27 = (bf16[128,2048]{1,0:T(8,128)(2,1)S(1)}, bf16[128,2048]{1,0:T(8,128)(2,1)S(1)}, u32[]{:S(2)}, u32[]{:S(2)}) collective-permute-start(bf16[128,2048]{1,0:T(8,128)(2,1)S(1)} %shard_map.425), channel_id=1, source_target_pairs={{0,4},{2,6},{4,0},{6,2},{1,5},{3,7},{5,1},{7,3},{8,12},{10,14},{12... | collective-permute-start | bytes 1572872 | tf_op jit(solution)/shard_map/ppermute | solution.py:845
  333.5 21.5 %collective-permute-start.29 = (bf16[128,2048]{1,0:T(8,128)(2,1)S(1)}, bf16[128,2048]{1,0:T(8,128)(2,1)S(1)}, u32[]{:S(2)}, u32[]{:S(2)}) collective-permute-start(bf16[128,2048]{1,0:T(8,128)(2,1)S(1)} %get-tuple-element.174.refs_3_.refs_1_), channel_id=1, source_target_pairs={{0,4},{2,6},{4,0},{6,2},{1,5},{3,7},{5,1},{7,3},{8,12},{10,14},{12... | collective-permute-start | bytes 1572872 | tf_op jit(solution)/shard_map/ppermute | solution.py:845
  333.6 28.8 %collective-permute-start.28 = (bf16[128,2048]{1,0:T(8,128)(2,1)S(1)}, bf16[128,2048]{1,0:T(8,128)(2,1)S(1)}, u32[]{:S(2)}, u32[]{:S(2)}) collective-permute-start(bf16[128,2048]{1,0:T(8,128)(2,1)S(1)} %get-tuple-element.174.refs_3_.refs_1_), channel_id=1, source_target_pairs={{0,2},{2,0},{4,6},{6,4},{1,3},{3,1},{5,7},{7,5},{8,10},{10,8},{12,... | collective-permute-start | bytes 1572872 | tf_op jit(solution)/shard_map/ppermute | solution.py:845
  355.0 11.3 %collective-permute-start.30 = (bf16[128,2048]{1,0:T(8,128)(2,1)S(1)}, bf16[128,2048]{1,0:T(8,128)(2,1)S(1)}, u32[]{:S(2)}, u32[]{:S(2)}) collective-permute-start(bf16[128,2048]{1,0:T(8,128)(2,1)S(1)} %collective-permute-done.29.refs_3_), channel_id=1, source_target_pairs={{0,2},{2,0},{4,6},{6,4},{1,3},{3,1},{5,7},{7,5},{8,10},{10,8},{12,... | collective-permute-start | bytes 1572872 | tf_op jit(solution)/shard_map/ppermute | solution.py:845
  374.7 11.9 %collective-permute-start.31 = (bf16[512,512]{1,0:T(8,128)(2,1)S(1)}, bf16[512,512]{1,0:T(8,128)(2,1)S(1)}, u32[]{:S(2)}, u32[]{:S(2)}) collective-permute-start(bf16[512,512]{1,0:T(8,128)(2,1)S(1)} %get-tuple-element.179), channel_id=1, source_target_pairs={{0,2},{2,0},{4,6},{6,4},{1,3},{3,1},{5,7},{7,5},{8,10},{10,8},{12,... | collective-permute-start | bytes 1572872 | tf_op jit(solution)/shard_map/ppermute | solution.py:845
  386.5 35.9 %copy-start.46 = (f32[512,256]{1,0:T(8,128)S(1)}, f32[512,256]{1,0:T(8,128)}, u32[]{:S(2)}) copy-start(f32[512,256]{1,0:T(8,128)} %copy-done.45) | copy-start | bytes 1572868
  386.7 19.3 %collective-permute-start.32 = (bf16[512,512]{1,0:T(8,128)(2,1)S(1)}, bf16[512,512]{1,0:T(8,128)(2,1)S(1)}, u32[]{:S(2)}, u32[]{:S(2)}) collective-permute-start(bf16[512,512]{1,0:T(8,128)(2,1)S(1)} %get-tuple-element.180), channel_id=1, source_target_pairs={{0,2},{2,0},{4,6},{6,4},{1,3},{3,1},{5,7},{7,5},{8,10},{10,8},{12,... | collective-permute-start | bytes 1572872 | tf_op jit(solution)/shard_map/ppermute | solution.py:845
  386.8 22.8 %collective-permute-start.33 = (bf16[512,512]{1,0:T(8,128)(2,1)S(1)}, bf16[512,512]{1,0:T(8,128)(2,1)S(1)}, u32[]{:S(2)}, u32[]{:S(2)}) collective-permute-start(bf16[512,512]{1,0:T(8,128)(2,1)S(1)} %shard_map.430), channel_id=1, source_target_pairs={{0,4},{2,6},{4,0},{6,2},{1,5},{3,7},{5,1},{7,3},{8,12},{10,14},{12... | collective-permute-start | bytes 1572872 | tf_op jit(solution)/shard_map/ppermute | solution.py:845
  397.1 25.3 %collective-permute-start.34 = (bf16[512,512]{1,0:T(8,128)(2,1)S(1)}, bf16[512,512]{1,0:T(8,128)(2,1)S(1)}, u32[]{:S(2)}, u32[]{:S(2)}) collective-permute-start(bf16[512,512]{1,0:T(8,128)(2,1)S(1)} %get-tuple-element.189), channel_id=1, source_target_pairs={{1,0},{3,2},{5,4},{7,6},{9,8},{11,10},{13,12},{15,14},{17,16},{19,... | collective-permute-start | bytes 1572872 | tf_op jit(solution)/shard_map/ppermute | solution.py:1330
  442.2 16.8 %collective-permute-start.35 = (bf16[576,512]{1,0:T(8,128)(2,1)}, bf16[576,512]{1,0:T(8,128)(2,1)S(1)}, u32[]{:S(2)}, u32[]{:S(2)}) collective-permute-start(bf16[576,512]{1,0:T(8,128)(2,1)} %get-tuple-element.200), channel_id=1, source_target_pairs={{0,6},{2,0},{4,2},{6,4},{1,7},{3,1},{5,3},{7,5},{8,14},{10,8},{12,... | collective-permute-start | bytes 1769480 | tf_op jit(solution)/shard_map/ppermute | solution.py:879
  442.6 53.2 %collective-permute-start.45 = (bf16[576,512]{1,0:T(8,128)(2,1)}, bf16[576,512]{1,0:T(8,128)(2,1)}, u32[]{:S(2)}, u32[]{:S(2)}) collective-permute-start(bf16[576,512]{1,0:T(8,128)(2,1)} %get-tuple-element.217), channel_id=1, source_target_pairs={{0,4},{2,6},{4,0},{6,2},{1,5},{3,7},{5,1},{7,3},{8,12},{10,14},{12... | collective-permute-start | bytes 1769480 | tf_op jit(solution)/shard_map/ppermute | solution.py:879
  444.4 55.3 %collective-permute-start.51 = (bf16[576,512]{1,0:T(8,128)(2,1)}, bf16[576,512]{1,0:T(8,128)(2,1)}, u32[]{:S(2)}, u32[]{:S(2)}) collective-permute-start(bf16[576,512]{1,0:T(8,128)(2,1)} %get-tuple-element.232), channel_id=1, source_target_pairs={{0,2},{2,4},{4,6},{6,0},{1,3},{3,5},{5,7},{7,1},{8,10},{10,12},{12... | collective-permute-start | bytes 1769480 | tf_op jit(solution)/shard_map/ppermute | solution.py:879
  458.9 54.4 %copy-start.84 = (f32[2,2048]{1,0:T(2,128)S(1)}, f32[2,2048]{1,0:T(2,128)}, u32[]{:S(2)}) copy-start(f32[2,2048]{1,0:T(2,128)} %param.42) | copy-start | bytes 49156
  458.9 54.4 %copy-start.85 = (f32[2,2048]{1,0:T(2,128)S(1)}, f32[2,2048]{1,0:T(2,128)}, u32[]{:S(2)}) copy-start(f32[2,2048]{1,0:T(2,128)} %param.44) | copy-start | bytes 49156
  459.0 1.3 collective-permute-start.42
  460.2 3.8 collective-permute-start.43
  464.0 4.2 collective-permute-start.44
  495.8 3.8 collective-permute-start.46
  499.6 5.9 %collective-permute-start.47 = (f32[38,128]{1,0:T(8,128)S(1)}, f32[38,128]{1,0:T(8,128)S(1)}, u32[]{:S(2)}, u32[]{:S(2)}) collective-permute-start(f32[38,128]{1,0:T(8,128)S(1)} %add.113), channel_id=1, source_target_pairs={{0,4},{2,6},{4,0},{6,2},{1,5},{3,7},{5,1},{7,3},{8,12},{10,14},{12... | collective-permute-start | bytes 58376 | tf_op jit(solution)/shard_map/ppermute | solution.py:845
  499.6 17.2 %collective-permute-start.36 = (bf16[512,512]{1,0:T(8,128)(2,1)}, bf16[512,512]{1,0:T(8,128)(2,1)}, u32[]{:S(2)}, u32[]{:S(2)}) collective-permute-start(bf16[512,512]{1,0:T(8,128)(2,1)} %get-tuple-element.206), channel_id=1, source_target_pairs={{0,2},{2,0},{4,6},{6,4},{1,3},{3,1},{5,7},{7,5},{8,10},{10,8},{12,... | collective-permute-start | bytes 1572872 | tf_op jit(solution)/shard_map/ppermute | solution.py:845
  502.5 18.2 %collective-permute-start.52 = (bf16[192,512]{1,0:T(8,128)(2,1)}, bf16[192,512]{1,0:T(8,128)(2,1)}, u32[]{:S(2)}, u32[]{:S(2)}) collective-permute-start(bf16[192,512]{1,0:T(8,128)(2,1)} %get-tuple-element.237), channel_id=1, source_target_pairs={{0,8},{8,16},{16,24},{24,0},{1,9},{9,17},{17,25},{25,1},{2,10},{10... | collective-permute-start | bytes 589832 | tf_op jit(solution)/shard_map/ppermute | solution.py:894
  502.5 21.1 %collective-permute-start.53 = (bf16[192,512]{1,0:T(8,128)(2,1)}, bf16[192,512]{1,0:T(8,128)(2,1)}, u32[]{:S(2)}, u32[]{:S(2)}) collective-permute-start(bf16[192,512]{1,0:T(8,128)(2,1)} %get-tuple-element.238), channel_id=1, source_target_pairs={{0,16},{8,24},{16,0},{24,8},{1,17},{9,25},{17,1},{25,9},{2,18},{10... | collective-permute-start | bytes 589832 | tf_op jit(solution)/shard_map/ppermute | solution.py:894
  504.1 22.2 %collective-permute-start.54 = (bf16[192,512]{1,0:T(8,128)(2,1)}, bf16[192,512]{1,0:T(8,128)(2,1)}, u32[]{:S(2)}, u32[]{:S(2)}) collective-permute-start(bf16[192,512]{1,0:T(8,128)(2,1)} %get-tuple-element.239), channel_id=1, source_target_pairs={{0,24},{8,0},{16,8},{24,16},{1,25},{9,1},{17,9},{25,17},{2,26},{10... | collective-permute-start | bytes 589832 | tf_op jit(solution)/shard_map/ppermute | solution.py:894
  508.8 8.9 %collective-permute-start.37 = (bf16[192,512]{1,0:T(8,128)(2,1)}, bf16[192,512]{1,0:T(8,128)(2,1)S(1)}, u32[]{:S(2)}, u32[]{:S(2)}) collective-permute-start(bf16[192,512]{1,0:T(8,128)(2,1)} %get-tuple-element.208), channel_id=1, source_target_pairs={{0,6},{2,0},{4,2},{6,4},{1,7},{3,1},{5,3},{7,5},{8,14},{10,8},{12,... | collective-permute-start | bytes 589832 | tf_op jit(solution)/shard_map/ppermute | solution.py:879
  516.9 27.3 %collective-permute-start.40 = (bf16[192,512]{1,0:T(8,128)(2,1)}, bf16[192,512]{1,0:T(8,128)(2,1)S(1)}, u32[]{:S(2)}, u32[]{:S(2)}) collective-permute-start(bf16[192,512]{1,0:T(8,128)(2,1)} %copy-done.77), channel_id=1, source_target_pairs={{0,4},{2,6},{4,0},{6,2},{1,5},{3,7},{5,1},{7,3},{8,12},{10,14},{12... | collective-permute-start | bytes 589832 | tf_op jit(solution)/shard_map/ppermute | solution.py:879
  517.7 26.5 %collective-permute-start.41 = (bf16[192,512]{1,0:T(8,128)(2,1)}, bf16[192,512]{1,0:T(8,128)(2,1)}, u32[]{:S(2)}, u32[]{:S(2)}) collective-permute-start(bf16[192,512]{1,0:T(8,128)(2,1)} %copy-done.76), channel_id=1, source_target_pairs={{0,2},{2,4},{4,6},{6,0},{1,3},{3,5},{5,7},{7,1},{8,10},{10,12},{12... | collective-permute-start | bytes 589832 | tf_op jit(solution)/shard_map/ppermute | solution.py:879
  520.8 34.5 %collective-permute-start.38 = (bf16[512,512]{1,0:T(8,128)(2,1)}, bf16[512,512]{1,0:T(8,128)(2,1)}, u32[]{:S(2)}, u32[]{:S(2)}) collective-permute-start(bf16[512,512]{1,0:T(8,128)(2,1)} %copy-done.74), channel_id=1, source_target_pairs={{0,2},{2,0},{4,6},{6,4},{1,3},{3,1},{5,7},{7,5},{8,10},{10,8},{12,... | collective-permute-start | bytes 1572872 | tf_op jit(solution)/shard_map/ppermute | solution.py:845
  523.6 31.7 %collective-permute-start.39 = (bf16[512,512]{1,0:T(8,128)(2,1)}, bf16[512,512]{1,0:T(8,128)(2,1)}, u32[]{:S(2)}, u32[]{:S(2)}) collective-permute-start(bf16[512,512]{1,0:T(8,128)(2,1)} %shard_map.439), channel_id=1, source_target_pairs={{0,4},{2,6},{4,0},{6,2},{1,5},{3,7},{5,1},{7,3},{8,12},{10,14},{12... | collective-permute-start | bytes 1572872 | tf_op jit(solution)/shard_map/ppermute | solution.py:845
  545.8 7.9 %collective-permute-start.48 = (bf16[64,512]{1,0:T(8,128)(2,1)}, bf16[64,512]{1,0:T(8,128)(2,1)S(1)}, u32[]{:S(2)}, u32[]{:S(2)}) collective-permute-start(bf16[64,512]{1,0:T(8,128)(2,1)} %get-tuple-element.224), channel_id=1, source_target_pairs={{0,8},{8,16},{16,24},{24,0},{1,9},{9,17},{17,25},{25,1},{2,10},{10... | collective-permute-start | bytes 196616 | tf_op jit(solution)/shard_map/ppermute | solution.py:894
  545.8 7.9 %collective-permute-start.49 = (bf16[64,512]{1,0:T(8,128)(2,1)}, bf16[64,512]{1,0:T(8,128)(2,1)S(1)}, u32[]{:S(2)}, u32[]{:S(2)}) collective-permute-start(bf16[64,512]{1,0:T(8,128)(2,1)} %get-tuple-element.225), channel_id=1, source_target_pairs={{0,16},{8,24},{16,0},{24,8},{1,17},{9,25},{17,1},{25,9},{2,18},{10... | collective-permute-start | bytes 196616 | tf_op jit(solution)/shard_map/ppermute | solution.py:894
  547.2 6.5 %collective-permute-start.50 = (bf16[64,512]{1,0:T(8,128)(2,1)S(1)}, bf16[64,512]{1,0:T(8,128)(2,1)S(1)}, u32[]{:S(2)}, u32[]{:S(2)}) collective-permute-start(bf16[64,512]{1,0:T(8,128)(2,1)S(1)} %get-tuple-element.226), channel_id=1, source_target_pairs={{0,24},{8,0},{16,8},{24,16},{1,25},{9,1},{17,9},{25,17},{2,26},{10... | collective-permute-start | bytes 196616 | tf_op jit(solution)/shard_map/ppermute | solution.py:894
  (84 other events, 521.1 us)
Sparse Core Ops, SparseCore 0:
  58.5 43.7 all-gather.4
  127.4 109.0 all-gather.6
  303.1 135.7 reduce-scatter.2
  442.1 59.4 reduce-scatter.4
